TPU v7x, 32 devices: a whole 2x2x4 slice. The times are simulated.
32 devices in a mesh: dp: 4 (over y, x), expert: 8 (over z, core).
Axes of the slice: x: 2, y: 2, z: 4, core: 2. Of those that a mesh axis runs over, the one named last changes fastest.
Arguments:
- tokens: bfloat16 [32, 1024, 768], P(('dp', 'expert')), may hold values from -6 to 6
- cotangent: bfloat16 [32, 1024, 768], P(('dp', 'expert')), may hold values from -6 to 6
- lengths: int32 [32], P(('dp', 'expert')), may hold values from 512 to 1024
- routes: int32 [32, 1024], P(('dp', 'expert')), may hold values from 0 to 7
- norm_gain: bfloat16 [768], replicated, may hold values from 0.5 to 1.5
- query_weight: bfloat16 [768, 768], replicated, may hold values from -0.21875 to 0.21875
- key_weight: bfloat16 [768, 768], replicated, may hold values from -0.21875 to 0.21875
- value_weight: bfloat16 [768, 768], replicated, may hold values from -0.21875 to 0.21875
- output_weight: bfloat16 [768, 768], replicated, may hold values from -2.5 to 2.5
- bucket_head_bias: bfloat16 [32, 12], replicated, may hold values from -4 to 4
- ffn_gain: bfloat16 [768], replicated, may hold values from 0.5 to 1.5
- router_weight: bfloat16 [768, 8], replicated, may hold values from -0.15625 to 0.15625
- expert_in: bfloat16 [8, 768, 3072], P('expert'), may hold values from -0.21875 to 0.21875
- expert_out: bfloat16 [8, 3072, 768], P('expert'), as said below
Outputs:
- result: bfloat16 [32, 1024, 768], P(('dp', 'expert'))
- token_grad: float32 [32, 1024, 768], P(('dp', 'expert'))
- norm_gain_grad: float32 [768], replicated
- query_grad: float32 [768, 768], replicated
- key_grad: float32 [768, 768], replicated
- value_grad: float32 [768, 768], replicated
- output_grad: float32 [768, 768], replicated
- bucket_grad: float32 [32, 12], replicated
- ffn_gain_grad: float32 [768], replicated
- router_grad: float32 [768, 8], replicated
- expert_in_grad: float32 [8, 768, 3072], P('expert', None, 'dp')
- expert_output_gradient: float32 [8, 3072, 768], P('expert', 'dp')
Inputs may be any that keep to these rules, and one draw needn't show every extreme that they name: Every entry of expert_out lies within 6 * 8 / sqrt(3072) of zero.
All inputs are finite; a program needn't handle non-finite values.
Results may differ from a plain program's by a relative error of at most 0.015.
Values may be sent and summed in bfloat16 or wider, within the bound.
No kernel may reach another device: no remote copies, remote signals or barrier semaphores. Data moves between devices by JAX's collectives and lax.ppermute only.
A program may use at most 320 MiB of HBM per device.

v0:
```python
import math

import jax
import jax.numpy as jnp
from jax import lax
from jax.sharding import PartitionSpec as P

MAXDIST = 128


EPSILON = 1e-06
NEGATIVE = -1000000000.0


def bucket_table(query_rows, key_rows, query_start, buckets, far_limit):
    exact_limit = buckets // 4
    half_count = buckets // 2
    offset = lax.broadcasted_iota(jnp.int32, (query_rows, key_rows), 1) - (
        lax.broadcasted_iota(jnp.int32, (query_rows, key_rows), 0) + query_start
    )
    distance = jnp.abs(offset)
    bucket_ids = jnp.minimum(distance, exact_limit)
    for bucket_level in range(exact_limit + 1, half_count):
        border = math.ceil(
            exact_limit
            * (far_limit / exact_limit)
            ** ((bucket_level - exact_limit) / (half_count - exact_limit))
        )
        bucket_ids = bucket_ids + (distance >= border).astype(jnp.int32)
    return bucket_ids + jnp.where(offset > 0, half_count, 0).astype(jnp.int32)


def rms_inverse(row_values):
    return lax.rsqrt(jnp.mean(row_values * row_values, axis=-1, keepdims=True) + EPSILON)


def norm_back(row_values, inverse, gain_vector, upstream):
    scaled = gain_vector * upstream
    gain_grad = jnp.sum(upstream * row_values * inverse, axis=0)
    row_grad = inverse * scaled - row_values * inverse * inverse * inverse * jnp.mean(
        scaled * row_values, axis=-1, keepdims=True
    )
    return (row_grad, gain_grad)


def gelu_tanh(values):
    return jax.nn.gelu(values, approximate=True)


def expert_forward(received, expert_in):
    pre_act = jnp.einsum("erd,edf->erf", received, expert_in, preferred_element_type=jnp.float32)
    return (pre_act, gelu_tanh(pre_act).astype(jnp.bfloat16))


def hidden_grad(grad_rows, weight_out, pre_values):
    act_grad = jnp.einsum("erd,efd->erf", grad_rows, weight_out, preferred_element_type=jnp.float32)
    return jax.vjp(gelu_tanh, pre_values)[1](act_grad)[0].astype(jnp.bfloat16)


def on_device(
    tokens,
    cotangent,
    lengths,
    routes,
    norm_gain,
    query_weight,
    key_weight,
    value_weight,
    output_weight,
    bucket_head_bias,
    ffn_gain,
    router_weight,
    expert_in,
    expert_out,
):
    seq_count, seq_len, model_width = tokens.shape
    bucket_count, head_count = bucket_head_bias.shape
    head_width = model_width // head_count
    score_scale = head_width ** (-0.5)
    token_count = seq_count * seq_len
    expert_count = router_weight.shape[1]
    capacity = max(2, 5 * token_count // (4 * expert_count))
    block_rows = min(512, seq_len)
    block_count = seq_len // block_rows
    head_shape = (seq_count, seq_len, head_count, head_width)
    positions = lax.broadcasted_iota(jnp.int32, (seq_count, seq_len), 1)
    live_mask = positions < lengths[:, None]
    live_flat = live_mask.reshape(token_count, 1).astype(jnp.float32)
    inputs = tokens.reshape(token_count, model_width).astype(jnp.float32)
    gain_one = norm_gain.astype(jnp.float32)
    gain_two = ffn_gain.astype(jnp.float32)
    inverse_one = rms_inverse(inputs)
    normed_one = (inputs * inverse_one * gain_one).astype(jnp.bfloat16)
    query_all = (
        jnp.dot(normed_one, query_weight, preferred_element_type=jnp.float32)
        .astype(jnp.bfloat16)
        .reshape(head_shape)
    )
    key_all = (
        jnp.dot(normed_one, key_weight, preferred_element_type=jnp.float32)
        .astype(jnp.bfloat16)
        .reshape(head_shape)
    )
    value_all = (
        jnp.dot(normed_one, value_weight, preferred_element_type=jnp.float32)
        .astype(jnp.bfloat16)
        .reshape(head_shape)
    )
    bucket_iota = lax.broadcasted_iota(jnp.int32, (bucket_count, 1, 1), 0)
    indicator_rows = [
        (
            bucket_table(block_rows, seq_len, block_number * block_rows, bucket_count, MAXDIST)[
                None
            ]
            == bucket_iota
        ).astype(jnp.bfloat16)
        for block_number in range(block_count)
    ]
    biases = [
        jnp.einsum(
            "eou,eg->gou", indicator_block, bucket_head_bias, preferred_element_type=jnp.float32
        )
        for indicator_block in indicator_rows
    ]

    def block_scores(query_block, key_seq, key_live, block_number):
        scores = (
            jnp.einsum("qhd,khd->hqk", query_block, key_seq, preferred_element_type=jnp.float32)
            * score_scale
            + biases[block_number]
        )
        return jnp.where(key_live[None, None, :], scores, NEGATIVE)

    def attend_forward(packed):
        query_seq, key_seq, value_seq, key_live = packed
        outputs = []
        log_parts = []
        for block_number in range(block_count):
            query_block = query_seq[block_number * block_rows : (block_number + 1) * block_rows]
            scores = block_scores(query_block, key_seq, key_live, block_number)
            row_peak = jnp.max(scores, axis=-1, keepdims=True)
            shifted = jnp.exp(scores - row_peak)
            row_total = jnp.sum(shifted, axis=-1, keepdims=True)
            prob_low = (shifted / row_total).astype(jnp.bfloat16)
            outputs.append(
                jnp.einsum(
                    "hqk,khd->qhd", prob_low, value_seq, preferred_element_type=jnp.float32
                ).astype(jnp.bfloat16)
            )
            log_parts.append(row_peak[..., 0] + jnp.log(row_total[..., 0]))
        return (jnp.concatenate(outputs, axis=0), jnp.concatenate(log_parts, axis=1))

    mixed, log_sums = lax.map(attend_forward, (query_all, key_all, value_all, live_mask))
    mixed_flat = mixed.reshape(token_count, model_width)
    resid = inputs + jnp.dot(mixed_flat, output_weight, preferred_element_type=jnp.float32)
    inverse_two = rms_inverse(resid)
    normed_two = (resid * inverse_two * gain_two).astype(jnp.bfloat16)
    logits = jnp.dot(normed_two, router_weight, preferred_element_type=jnp.float32)
    router_probs = jax.nn.softmax(logits, axis=-1)
    flat_routes = routes.reshape(token_count, 1)
    route_onehot = (flat_routes == lax.broadcasted_iota(jnp.int32, (1, expert_count), 1)).astype(
        jnp.float32
    )
    gate_prob = jnp.sum(router_probs * route_onehot, axis=-1, keepdims=True)
    lower_tri = (
        lax.broadcasted_iota(jnp.int32, (token_count, token_count), 0)
        > lax.broadcasted_iota(jnp.int32, (token_count, token_count), 1)
    ).astype(jnp.bfloat16)
    before = jnp.dot(
        lower_tri,
        (route_onehot * live_flat).astype(jnp.bfloat16),
        preferred_element_type=jnp.float32,
    )
    rank = jnp.sum(before * route_onehot, axis=-1).astype(jnp.int32)
    kept = live_mask.reshape(token_count) & (rank < capacity)
    kept_flat = kept.reshape(token_count, 1).astype(jnp.float32)
    slot_index = jnp.where(kept, flat_routes[:, 0] * capacity + rank, expert_count * capacity)
    safe_index = jnp.minimum(slot_index, expert_count * capacity - 1)
    slot_buffer = (
        jnp.zeros((expert_count * capacity + 1, model_width), jnp.bfloat16)
        .at[slot_index]
        .set(normed_two)
    )
    slot_buffer = slot_buffer[: expert_count * capacity].reshape(
        expert_count, capacity, model_width
    )
    received = lax.all_to_all(slot_buffer, "expert", split_axis=0, concat_axis=1, tiled=True)
    pre_act, activated = expert_forward(received, expert_in)
    expert_rows = jnp.einsum(
        "erf,efd->erd", activated, expert_out, preferred_element_type=jnp.float32
    ).astype(jnp.bfloat16)
    home_rows = lax.all_to_all(
        expert_rows, "expert", split_axis=1, concat_axis=0, tiled=True
    ).reshape(expert_count * capacity, model_width)
    gathered = home_rows[safe_index].astype(jnp.float32) * kept_flat
    result = (live_flat * (resid + gate_prob * gathered)).astype(jnp.bfloat16).reshape(tokens.shape)
    upstream = cotangent.reshape(token_count, model_width).astype(jnp.float32) * live_flat
    gate_grad = jnp.sum(upstream * gathered, axis=-1, keepdims=True)
    rows_grad = (gate_prob * upstream).astype(jnp.bfloat16)
    home_grad = (
        jnp.zeros((expert_count * capacity + 1, model_width), jnp.bfloat16)
        .at[slot_index]
        .set(rows_grad)
    )
    home_grad = home_grad[: expert_count * capacity].reshape(expert_count, capacity, model_width)
    grad_rows = lax.all_to_all(home_grad, "expert", split_axis=0, concat_axis=1, tiled=True)
    received_back = lax.all_to_all(slot_buffer, "expert", split_axis=0, concat_axis=1, tiled=True)
    pre_back, activated_back = expert_forward(received_back, expert_in)
    pre_grad = hidden_grad(grad_rows, expert_out, pre_back)
    slot_grad = jnp.einsum(
        "erf,edf->erd", pre_grad, expert_in, preferred_element_type=jnp.float32
    ).astype(jnp.bfloat16)
    back_home = lax.all_to_all(
        slot_grad, "expert", split_axis=1, concat_axis=0, tiled=True
    ).reshape(expert_count * capacity, model_width)
    out_weight_grad = jnp.einsum(
        "erf,erd->efd", activated_back, grad_rows, preferred_element_type=jnp.float32
    )
    in_weight_grad = jnp.einsum(
        "erd,erf->edf", received_back, pre_grad, preferred_element_type=jnp.float32
    )
    expert_in_grad, expert_output_gradient = (
        lax.psum_scatter(
            in_weight_grad.astype(jnp.bfloat16), "dp", scatter_dimension=2, tiled=True
        ).astype(jnp.float32),
        lax.psum_scatter(
            out_weight_grad.astype(jnp.bfloat16), "dp", scatter_dimension=1, tiled=True
        ).astype(jnp.float32),
    )
    logit_grad = (gate_grad * gate_prob * (route_onehot - router_probs)).astype(jnp.bfloat16)
    router_grad = jnp.einsum(
        "td,te->de", normed_two, logit_grad, preferred_element_type=jnp.float32
    )
    normed_two_grad = back_home[safe_index].astype(jnp.float32) * kept_flat
    normed_two_grad = normed_two_grad + jnp.einsum(
        "te,de->td", logit_grad, router_weight, preferred_element_type=jnp.float32
    )
    resid_back, ffn_gain_grad = norm_back(resid, inverse_two, gain_two, normed_two_grad)
    residual_gradient = upstream + resid_back
    attn_grad = residual_gradient.astype(jnp.bfloat16)
    output_grad = jnp.einsum("td,te->de", mixed_flat, attn_grad, preferred_element_type=jnp.float32)
    mixed_grad = (
        jnp.einsum("te,de->td", attn_grad, output_weight, preferred_element_type=jnp.float32)
        .astype(jnp.bfloat16)
        .reshape(head_shape)
    )

    def attend_backward(packed):
        query_seq, key_seq, value_seq, key_live, grad_seq, log_seq = packed
        query_parts = []
        key_sum = jnp.zeros(key_seq.shape, jnp.float32)
        value_sum = jnp.zeros(value_seq.shape, jnp.float32)
        bias_sum_local = jnp.zeros((bucket_count, head_count), jnp.float32)
        for block_number in range(block_count):
            lower_edge = block_number * block_rows
            query_block = query_seq[lower_edge : lower_edge + block_rows]
            grad_block = grad_seq[lower_edge : lower_edge + block_rows]
            scores = block_scores(query_block, key_seq, key_live, block_number)
            prob_rows = jnp.exp(scores - log_seq[:, lower_edge : lower_edge + block_rows, None])
            prob_low = prob_rows.astype(jnp.bfloat16)
            prob_grad = jnp.einsum(
                "qhd,khd->hqk", grad_block, value_seq, preferred_element_type=jnp.float32
            )
            row_delta = jnp.sum(prob_rows * prob_grad, axis=-1, keepdims=True)
            scores_gradient = (prob_rows * (prob_grad - row_delta)).astype(jnp.bfloat16)
            bias_sum_local = bias_sum_local + jnp.einsum(
                "iuf,cuf->ci",
                scores_gradient,
                indicator_rows[block_number],
                preferred_element_type=jnp.float32,
            )
            query_parts.append(
                jnp.einsum(
                    "hqk,khd->qhd", scores_gradient, key_seq, preferred_element_type=jnp.float32
                )
                * score_scale
            )
            key_sum = (
                key_sum
                + jnp.einsum(
                    "hqk,qhd->khd", scores_gradient, query_block, preferred_element_type=jnp.float32
                )
                * score_scale
            )
            value_sum = value_sum + jnp.einsum(
                "hqk,qhd->khd", prob_low, grad_block, preferred_element_type=jnp.float32
            )
        query_back = jnp.concatenate(query_parts, axis=0).astype(jnp.bfloat16)
        return (
            query_back,
            key_sum.astype(jnp.bfloat16),
            value_sum.astype(jnp.bfloat16),
            bias_sum_local,
        )

    query_back, key_back, value_back, bias_parts = lax.map(
        attend_backward, (query_all, key_all, value_all, live_mask, mixed_grad, log_sums)
    )
    bucket_grad = jnp.sum(bias_parts, axis=0)
    query_back = query_back.reshape(token_count, model_width)
    key_back = key_back.reshape(token_count, model_width)
    value_back = value_back.reshape(token_count, model_width)
    query_grad = jnp.einsum("td,te->de", normed_one, query_back, preferred_element_type=jnp.float32)
    key_grad = jnp.einsum("td,te->de", normed_one, key_back, preferred_element_type=jnp.float32)
    value_grad = jnp.einsum("td,te->de", normed_one, value_back, preferred_element_type=jnp.float32)
    normed_one_grad = jnp.einsum(
        "te,de->td", query_back, query_weight, preferred_element_type=jnp.float32
    )
    normed_one_grad = normed_one_grad + jnp.einsum(
        "te,de->td", key_back, key_weight, preferred_element_type=jnp.float32
    )
    normed_one_grad = normed_one_grad + jnp.einsum(
        "te,de->td", value_back, value_weight, preferred_element_type=jnp.float32
    )
    input_back, norm_gain_grad = norm_back(inputs, inverse_one, gain_one, normed_one_grad)
    token_grad = (residual_gradient + input_back).reshape(tokens.shape)
    (
        norm_gain_grad,
        query_grad,
        key_grad,
        value_grad,
        output_grad,
        bucket_grad,
        ffn_gain_grad,
        router_grad,
    ) = lax.psum(
        (
            norm_gain_grad,
            query_grad,
            key_grad,
            value_grad,
            output_grad,
            bucket_grad,
            ffn_gain_grad,
            router_grad,
        ),
        ("dp", "expert"),
    )
    return (
        result,
        token_grad,
        norm_gain_grad,
        query_grad,
        key_grad,
        value_grad,
        output_grad,
        bucket_grad,
        ffn_gain_grad,
        router_grad,
        expert_in_grad,
        expert_output_gradient,
    )


def solution(mesh):
    in_specs = (
        P(("dp", "expert"), None, None),
        P(("dp", "expert"), None, None),
        P(("dp", "expert")),
        P(("dp", "expert"), None),
        P(),
        P(),
        P(),
        P(),
        P(),
        P(),
        P(),
        P(),
        P("expert", None, None),
        P("expert", None, None),
    )
    out_specs = (
        P(("dp", "expert"), None, None),
        P(("dp", "expert"), None, None),
        P(),
        P(),
        P(),
        P(),
        P(),
        P(),
        P(),
        P(),
        P("expert", None, "dp"),
        P("expert", "dp", None),
    )
    return jax.shard_map(
        on_device, mesh=mesh, in_specs=in_specs, out_specs=out_specs, check_vma=False
    )
```

profile of v0, /device:TPU:0, one launch (start us, length us, event | category | flops | bytes accessed | tf_op | source)
XLA Modules:
  0.0 953.1 jit_solution(920907180592065125)
XLA Ops:
  31.7 16.1 %fusion.3 = f32[512,1024,12]{0,2,1:T(8,128)} fusion(s32[512,1024]{0,1:T(8,128)S(1)} %copy-done.19, bf16[32,12]{0,1:T(8,128)(2,1)S(1)} %copy-done.71), kind=kOutput, calls=%fused_computation.9 | convolution fusion | flops 419430400 | bytes 27263744 | tf_op jit(solution)/shard_map/eou,eg->gou/dot_general | solution.py:120
  47.8 30.5 %copy.79 = f32[512,1024,12]{1,0,2:T(8,128)} copy(f32[512,1024,12]{0,2,1:T(8,128)} %fusion.3) | data formatting | bytes 50331648 | tf_op jit(solution)/shard_map/eou,eg->gou/dot_general | solution.py:120
  78.2 15.6 %fusion.1 = f32[512,1024,12]{0,2,1:T(8,128)} fusion(s32[512,1024]{0,1:T(8,128)} %select_add_fusion, bf16[32,12]{0,1:T(8,128)(2,1)S(1)} %copy-done.71), kind=kOutput, calls=%fused_computation.6 | convolution fusion | flops 419430400 | bytes 27263744 | tf_op jit(solution)/shard_map/eou,eg->gou/dot_general | solution.py:120
  93.9 30.4 %copy.80 = f32[512,1024,12]{1,0,2:T(8,128)} copy(f32[512,1024,12]{0,2,1:T(8,128)} %fusion.1) | data formatting | bytes 50331648 | tf_op jit(solution)/shard_map/eou,eg->gou/dot_general | solution.py:120
  124.2 16.4 %fusion.138 = (f32[12,512]{1,0:T(8,128)}, f32[12,512,1024]{2,1,0:T(8,128)}) fusion(f32[512,1024,12]{1,0,2:T(8,128)} %copy.79, bf16[512,12,64]{0,2,1:T(8,128)(2,1)} %bitcast.216, bf16[1024,12,64]{0,2,1:T(8,128)(2,1)S(1)} %bitcast.206, pred[1024]{0:T(1024)(128)(4,1)S(1)} %get-tuple-element.168), kind=kOutput, calls=%fused_computation.190 | convolution fusion | flops 830466048 | bytes 52716544 | tf_op jit(solution)/shard_map/while/body/eval_jaxpr/qhd,khd->hqk/dot_general | solution.py:128
  140.6 11.1 %fusion.10 = f32[12,512]{1,0:T(8,128)S(1)} fusion(f32[12,512,1024]{2,1,0:T(8,128)} %get-tuple-element.157, f32[12,512]{1,0:T(8,128)} %get-tuple-element.156), kind=kLoop, calls=%fused_computation.30 | loop fusion | flops 12576768 | bytes 25214976 | tf_op jit(solution)/shard_map/while/body/eval_jaxpr/reduce_sum | solution.py:143
  151.7 11.5 %fusion.99 = bf16[512,12,64]{0,2,1:T(8,128)(2,1)} fusion(bf16[1024,12,64]{0,2,1:T(8,128)(2,1)S(1)} %bitcast.225, f32[12,512,1024]{2,1,0:T(8,128)} %get-tuple-element.157, f32[12,512]{1,0:T(8,128)S(1)} %fusion.10, f32[12,512]{1,0:T(8,128)S(1)} %copy-done.47), kind=kOutput, calls=%fused_computation.138 | convolution fusion | flops 824573952 | bytes 27574272 | tf_op jit(solution)/shard_map/while/body/eval_jaxpr/hqk,khd->qhd/dot_general | solution.py:146
  163.2 16.3 %fusion.137 = (f32[12,512]{1,0:T(8,128)}, f32[12,512,1024]{2,1,0:T(8,128)}) fusion(f32[512,1024,12]{1,0,2:T(8,128)} %copy.80, bf16[512,12,64]{0,2,1:T(8,128)(2,1)S(1)} %bitcast.214, bf16[1024,12,64]{0,2,1:T(8,128)(2,1)S(1)} %bitcast.207, pred[1024]{0:T(1024)(128)(4,1)S(1)} %get-tuple-element.168), kind=kOutput, calls=%fused_computation.189 | convolution fusion | flops 830466048 | bytes 52716544 | tf_op jit(solution)/shard_map/while/body/eval_jaxpr/qhd,khd->hqk/dot_general | solution.py:128
  179.5 11.1 %fusion.11 = f32[12,512]{1,0:T(8,128)S(1)} fusion(f32[12,512,1024]{2,1,0:T(8,128)} %get-tuple-element.155, f32[12,512]{1,0:T(8,128)} %get-tuple-element.154), kind=kLoop, calls=%fused_computation.31 | loop fusion | flops 12576768 | bytes 25214976 | tf_op jit(solution)/shard_map/while/body/eval_jaxpr/reduce_sum | solution.py:143
  190.6 10.5 %fusion.100 = bf16[512,12,64]{0,2,1:T(8,128)(2,1)S(1)} fusion(bf16[1024,12,64]{0,2,1:T(8,128)(2,1)S(1)} %bitcast.226, f32[12,512,1024]{2,1,0:T(8,128)} %get-tuple-element.155, f32[12,512]{1,0:T(8,128)S(1)} %fusion.11, f32[12,512]{1,0:T(8,128)S(1)} %copy-done.49), kind=kOutput, calls=%fused_computation.139 | convolution fusion | flops 824573952 | bytes 27574272 | tf_op jit(solution)/shard_map/while/body/eval_jaxpr/hqk,khd->qhd/dot_general | solution.py:146
  208.8 7.2 scatter_custom_fusion
  217.6 52.9 %all_to_all.16 = bf16[8,160,768]{2,1,0:T(8,128)(2,1)S(1)} all-to-all(bf16[8,160,768]{2,1,0:T(8,128)(2,1)S(1)} %bitcast.218), channel_id=1, replica_groups=mesh['dp'=4,'expert'=8] {'expert'}, dimensions={0} | all-to-all | bytes 3932160 | tf_op jit(solution)/shard_map/all_to_all | solution.py:187
  271.7 8.3 fusion.34
  280.1 9.6 %fusion.69 = bf16[1,1280,768]{2,1,0:T(8,128)(2,1)S(1)} fusion(bf16[1,3072,768]{2,1,0:T(8,128)(2,1)S(1)} %bitcast.251, f32[1280,3072]{1,0:T(8,128)S(1)} %fusion.34), kind=kOutput, calls=%fused_computation.100 | convolution fusion | flops 6076170240 | bytes 22413312 | tf_op jit(solution)/shard_map/erf,efd->erd/dot_general | solution.py:189
  289.7 15.1 %copy.109 = bf16[1,1280,768]{2,0,1:T(2,128)(2,1)} copy(bf16[1,1280,768]{2,1,0:T(8,128)(2,1)S(1)} %fusion.69) | data formatting | bytes 3932160 | tf_op jit(solution)/shard_map/convert_element_type | solution.py:191
  305.3 13.7 %reduce = bf16[1280,768]{1,0:T(8,128)(2,1)} reduce(bf16[1280,1,768]{2,1,0:T(2,128)(2,1)} %bitcast.210, bf16[]{:T(256)} %broadcast.450), dimensions={1}, to_apply=%bitcast.194.reduce_sub_computation | reduce | bytes 3932162
  319.1 5.8 reshape.456
  324.8 4.5 all-to-all-start.1
  332.6 43.0 %all-to-all-done.1 = bf16[8,2,61440]{2,1,0:T(2,128)(2,1)} async-done(((bf16[8,2,61440]{2,1,0:T(2,128)(2,1)}), bf16[8,2,61440]{2,1,0:T(2,128)(2,1)}, u32[]{:S(2)}, u32[]{:S(2)}) %all-to-all-start.1) | async-done | bytes 1966112 | tf_op jit(solution)/shard_map/all_to_all | solution.py:192
  375.5 6.7 reshape.457
  384.7 5.2 gather_fusion
  398.6 6.3 scatter_custom_fusion.1
  405.1 48.9 %all_to_all.17 = bf16[8,160,768]{2,1,0:T(8,128)(2,1)S(1)} all-to-all(bf16[8,160,768]{2,1,0:T(8,128)(2,1)S(1)} %bitcast.219), channel_id=1, replica_groups=mesh['dp'=4,'expert'=8] {'expert'}, dimensions={0} | all-to-all | bytes 3932160 | tf_op jit(solution)/shard_map/all_to_all | solution.py:206
  454.0 13.2 %fusion.37 = bf16[1,3072,768]{2,1,0:T(8,128)(2,1)} fusion(bf16[1280,768]{1,0:T(8,128)(2,1)S(1)} %bitcast.234, f32[1280,3072]{1,0:T(8,128)} %copy-done.79), kind=kOutput, calls=%fused_computation.58 | convolution fusion | flops 6077546496 | bytes 22413312 | tf_op jit(solution)/shard_map/erf,erd->efd/dot_general | solution.py:216
  467.2 17.8 %fusion.20 = bf16[1280,3072]{1,0:T(8,128)(2,1)S(1)} fusion(f32[1280,3072]{1,0:T(8,128)} %copy-done.79, bf16[1280,768]{1,0:T(8,128)(2,1)S(1)} %bitcast.235, bf16[1,3072,768]{2,1,0:T(8,128)(2,1)} %param.27), kind=kOutput, calls=%fused_computation.40 | convolution fusion | flops 6118440960 | bytes 30277632 | tf_op jit(solution)/shard_map/erd,efd->erf/dot_general | solution.py:56
  485.1 11.7 %fusion.72 = bf16[1,1280,768]{2,1,0:T(8,128)(2,1)S(1)} fusion(bf16[1280,3072]{1,0:T(8,128)(2,1)S(1)} %fusion.20, bf16[1,768,3072]{2,1,0:T(8,128)(2,1)} %param.26), kind=kOutput, calls=%fused_computation.101 | convolution fusion | flops 6040780800 | bytes 14548992 | tf_op jit(solution)/shard_map/erf,edf->erd/dot_general | solution.py:210
  496.8 15.1 %copy.108 = bf16[1,1280,768]{2,0,1:T(2,128)(2,1)} copy(bf16[1,1280,768]{2,1,0:T(8,128)(2,1)S(1)} %fusion.72) | data formatting | bytes 3932160 | tf_op jit(solution)/shard_map/convert_element_type | solution.py:212
  511.9 12.5 %reduce.1 = bf16[1280,768]{1,0:T(8,128)(2,1)S(1)} reduce(bf16[1280,1,768]{2,1,0:T(2,128)(2,1)} %bitcast.211, bf16[]{:T(256)} %broadcast.450), dimensions={1}, to_apply=%bitcast.193.reduce_sub_computation | reduce | bytes 3932162
  532.4 10.7 %fusion.36 = bf16[1,768,3072]{2,1,0:T(8,128)(2,1)} fusion(bf16[1280,768]{1,0:T(8,128)(2,1)} %bitcast.233, bf16[1280,3072]{1,0:T(8,128)(2,1)} %copy-done.78), kind=kOutput, calls=%fused_computation.57 | convolution fusion | flops 6042157056 | bytes 14548992 | tf_op jit(solution)/shard_map/erd,erf->edf/dot_general | solution.py:219
  543.2 34.1 %all-to-all-done.3 = bf16[8,2,61440]{2,1,0:T(2,128)(2,1)S(1)} async-done(((bf16[8,2,61440]{2,1,0:T(2,128)(2,1)}), bf16[8,2,61440]{2,1,0:T(2,128)(2,1)S(1)}, u32[]{:S(2)}, u32[]{:S(2)}) %all-to-all-start.3) | async-done | bytes 1966112 | tf_op jit(solution)/shard_map/all_to_all | solution.py:213
  577.3 4.5 reshape.459
  584.2 5.2 gather_fusion.1
  591.1 4.0 multiply_reduce_fusion.2
  601.4 20.2 %multiply_reduce_fusion.1 = (f32[12,512]{1,0:T(8,128)}, f32[12,512,1024]{2,1,0:T(8,128)}) fusion(f32[12,512,1024]{2,1,0:T(8,128)} %get-tuple-element.157, f32[12,512]{1,0:T(8,128)} %log_add_fusion.1, bf16[512,12,64]{0,2,1:T(8,128)(2,1)S(1)} %bitcast.220, bf16[1024,12,64]{0,2,1:T(8,128)(2,1)S(1)} %bitcast.227), kind=kOutput, calls=%fused_computation.22 | convolution fusion | flops 824174592 | bytes 52740096 | tf_op jit(solution)/shard_map/while/body/eval_jaxpr/qhd,khd->hqk/dot_general | solution.py:261
  621.7 21.6 %multiply_convert_fusion.1 = bf16[12,512,1024]{2,1,0:T(8,128)(2,1)} fusion(f32[12,512,1024]{2,1,0:T(8,128)} %get-tuple-element.166, f32[12,512,1024]{2,1,0:T(8,128)} %get-tuple-element.157, f32[12,512]{1,0:T(8,128)} %get-tuple-element.165, f32[12,512]{1,0:T(8,128)} %log_add_fusion.1), kind=kLoop, calls=%fused_computation.21 | loop fusion | flops 25165824 | bytes 62963712 | tf_op jit(solution)/shard_map/while/body/eval_jaxpr/convert_element_type | solution.py:265
  643.3 17.3 %multiply_reduce_fusion = (f32[12,512]{1,0:T(8,128)}, f32[12,512,1024]{2,1,0:T(8,128)}) fusion(f32[12,512,1024]{2,1,0:T(8,128)} %get-tuple-element.155, f32[12,512]{1,0:T(8,128)} %log_add_fusion, bf16[512,12,64]{0,2,1:T(8,128)(2,1)} %bitcast.222, bf16[1024,12,64]{0,2,1:T(8,128)(2,1)} %bitcast.224), kind=kOutput, calls=%fused_computation.19 | convolution fusion | flops 824174592 | bytes 52740096 | tf_op jit(solution)/shard_map/while/body/eval_jaxpr/qhd,khd->hqk/dot_general | solution.py:261
  660.6 8.5 multiply_convert_fusion.7
  669.2 21.8 %multiply_convert_fusion = bf16[12,512,1024]{2,1,0:T(8,128)(2,1)} fusion(f32[12,512,1024]{2,1,0:T(8,128)} %get-tuple-element.164, f32[12,512,1024]{2,1,0:T(8,128)} %get-tuple-element.155, f32[12,512]{1,0:T(8,128)S(1)} %copy-done.50, f32[12,512]{1,0:T(8,128)S(1)} %copy-done.46), kind=kLoop, calls=%fused_computation.18 | loop fusion | flops 25165824 | bytes 62963712 | tf_op jit(solution)/shard_map/while/body/eval_jaxpr/convert_element_type | solution.py:265
  690.9 8.6 multiply_convert_fusion.6
  702.5 12.1 %fusion.21 = f32[12,64,1024]{2,1,0:T(8,128)} fusion(bf16[512,12,64]{0,2,1:T(8,128)(2,1)S(1)} %bitcast.223, f32[12,512,1024]{2,1,0:T(8,128)} %get-tuple-element.155, f32[12,512]{1,0:T(8,128)S(1)} %copy-done.46), kind=kOutput, calls=%fused_computation.42 | convolution fusion | flops 817889280 | bytes 29122560 | tf_op jit(solution)/shard_map/while/body/eval_jaxpr/hqk,qhd->khd/dot_general | solution.py:285
  714.6 13.2 %add_convert_fusion = bf16[12,64,1024]{2,1,0:T(8,128)(2,1)} fusion(f32[12,64,1024]{2,1,0:T(8,128)} %fusion.21, bf16[512,12,64]{0,2,1:T(8,128)(2,1)S(1)} %bitcast.221, f32[12,512,1024]{2,1,0:T(8,128)} %get-tuple-element.157, f32[12,512]{1,0:T(8,128)S(1)} %copy-done.45), kind=kOutput, calls=%fused_computation.91 | convolution fusion | flops 819462144 | bytes 30695424 | tf_op jit(solution)/shard_map/while/body/eval_jaxpr/hqk,qhd->khd/dot_general | solution.py:285
  727.9 4.9 fusion.115
  746.7 23.3 %copy.92 = bf16[12,512,1024]{1,0,2:T(8,128)(2,1)} copy(bf16[12,512,1024]{2,1,0:T(8,128)(2,1)} %multiply_convert_fusion.1) | data formatting | bytes 25165824 | tf_op jit(solution)/shard_map/while/body/eval_jaxpr/convert_element_type | solution.py:265
  770.0 23.2 %copy.93 = bf16[12,512,1024]{1,0,2:T(8,128)(2,1)} copy(bf16[12,512,1024]{2,1,0:T(8,128)(2,1)} %multiply_convert_fusion) | data formatting | bytes 25165824 | tf_op jit(solution)/shard_map/while/body/eval_jaxpr/convert_element_type | solution.py:265
  808.4 12.9 %fusion.103 = f32[32,12]{0,1:T(8,128)S(1)} fusion(bf16[12,512,1024]{1,0,2:T(8,128)(2,1)} %copy.92, s32[512,1024]{0,1:T(8,128)S(1)} %copy-done.20), kind=kOutput, calls=%fused_computation.142 | convolution fusion | flops 419430400 | bytes 14681600 | tf_op jit(solution)/shard_map/while/body/eval_jaxpr/iuf,cuf->ci/dot_general | solution.py:266
  821.3 13.4 %fusion.105 = f32[32,12]{0,1:T(8,128)S(1)} fusion(f32[32,12]{0,1:T(8,128)S(1)} %fusion.103, bf16[12,512,1024]{1,0,2:T(8,128)(2,1)} %copy.93, s32[512,1024]{0,1:T(8,128)S(1)} %copy-done.21), kind=kOutput, calls=%fused_computation.144 | convolution fusion | flops 419430784 | bytes 14683136 | tf_op jit(solution)/shard_map/while/body/eval_jaxpr/iuf,cuf->ci/dot_general | solution.py:266
  834.8 39.4 %all-reduce = (f32[768]{0:T(1024)}, f32[32,12]{0,1:T(8,128)}, f32[768]{0:T(1024)}, f32[768,8]{0,1:T(8,128)}) all-reduce(f32[768]{0:T(1024)S(1)} %get-tuple-element.134, f32[32,12]{0,1:T(8,128)S(1)} %fusion.105, f32[768]{0:T(1024)S(1)} %copy-done.72, f32[768,8]{0,1:T(8,128)S(1)} %copy-done.53), channel_id=1, replica_groups=mesh['dp'=4,'expert'=8] {'dp','expert'}, use_global_device_ids=true, to_apply=%region_18.19 | all-reduce | flops 8064 | bytes 64512 | tf_op jit(solution)/shard_map/psum | solution.py:326
  879.9 55.8 %all-reduce.4.cloned.1.call-done = (f32[768,768]{1,0:T(8,128)}, f32[768,768]{1,0:T(8,128)}, f32[768,768]{1,0:T(8,128)}, f32[768,768]{1,0:T(8,128)}) async-done(((f32[768,768]{1,0:T(8,128)}, f32[768,768]{1,0:T(8,128)}, f32[768,768]{1,0:T(8,128)}, f32[768,768]{1,0:T(8,128)}), (f32[768,768]{1,0:T(8,128)}, f32[768,768]{1,0:T(8,128)}, f32[768,768]{1,0:T(8,128)}, ...) | async-done | bytes 9437200 | tf_op jit(solution)/shard_map/psum | solution.py:326
  (253 shorter events, 114.1 us)
Async XLA Ops:
  8.0 17.5 %copy-start = (bf16[768,768]{1,0:T(8,128)(2,1)S(1)}, bf16[768,768]{1,0:T(8,128)(2,1)}, u32[]{:S(2)}) copy-start(bf16[768,768]{1,0:T(8,128)(2,1)} %param.21) | copy-start | bytes 3538948
  8.0 6.4 copy-start.54
  11.3 14.2 %copy-start.59 = (f32[768]{0:T(1024)}, f32[768]{0:T(1024)S(1)}, u32[]{:S(2)}) copy-start(f32[768]{0:T(1024)S(1)} %convert_element_type.332) | copy-start | bytes 9220
  17.7 7.8 copy-start.64
  22.2 140.9 %copy-start.22 = (bf16[512,768]{0,1:T(8,128)(2,1)}, bf16[512,768]{0,1:T(8,128)(2,1)S(1)}, u32[]{:S(2)}) copy-start(bf16[512,768]{0,1:T(8,128)(2,1)S(1)} %get-tuple-element.153) | copy-start | bytes 2359300
  25.5 137.6 %copy-start.3 = (bf16[1024,768]{0,1:T(8,128)(2,1)}, bf16[1024,768]{0,1:T(8,128)(2,1)S(1)}, u32[]{:S(2)}) copy-start(bf16[1024,768]{0,1:T(8,128)(2,1)S(1)} %convolution_convert_fusion.3) | copy-start | bytes 4718596
  25.6 6.1 copy-start.71
  140.6 11.1 %copy-start.26 = (bf16[1024,768]{0,1:T(8,128)(2,1)S(1)}, bf16[1024,768]{0,1:T(8,128)(2,1)}, u32[]{:S(2)}) copy-start(bf16[1024,768]{0,1:T(8,128)(2,1)} %convolution_convert_fusion.5) | copy-start | bytes 4718596
  140.6 11.1 %copy-start.47 = (f32[12,512]{1,0:T(8,128)S(1)}, f32[12,512]{1,0:T(8,128)}, u32[]{:S(2)}) copy-start(f32[12,512]{1,0:T(8,128)} %get-tuple-element.156) | copy-start | bytes 73732
  151.6 11.5 %copy-start.51 = (f32[12,512]{1,0:T(8,128)}, f32[12,512]{1,0:T(8,128)S(1)}, u32[]{:S(2)}) copy-start(f32[12,512]{1,0:T(8,128)S(1)} %fusion.10) | copy-start | bytes 73732
  179.5 11.1 %copy-start.27 = (bf16[1024,768]{0,1:T(8,128)(2,1)S(1)}, bf16[1024,768]{0,1:T(8,128)(2,1)}, u32[]{:S(2)}) copy-start(bf16[1024,768]{0,1:T(8,128)(2,1)} %convolution_convert_fusion.5) | copy-start | bytes 4718596
  179.5 11.1 %copy-start.49 = (f32[12,512]{1,0:T(8,128)S(1)}, f32[12,512]{1,0:T(8,128)}, u32[]{:S(2)}) copy-start(f32[12,512]{1,0:T(8,128)} %get-tuple-element.154) | copy-start | bytes 73732
  190.6 10.5 %copy-start.44 = (bf16[512,12,64]{0,2,1:T(8,128)(2,1)S(1)}, bf16[512,12,64]{0,2,1:T(8,128)(2,1)}, u32[]{:S(2)}) copy-start(bf16[512,12,64]{0,2,1:T(8,128)(2,1)} %fusion.99) | copy-start | bytes 2359300
  207.1 125.0 %copy-start.5 = (bf16[1024,768]{0,1:T(8,128)(2,1)}, bf16[1024,768]{0,1:T(8,128)(2,1)S(1)}, u32[]{:S(2)}) copy-start(bf16[1024,768]{0,1:T(8,128)(2,1)S(1)} %multiply_convert_fusion.5) | copy-start | bytes 4718596
  216.0 64.0 %slice-start.7 = ((s8[4718592]{0:T(1024)(128)(4,1)}), s8[4194304]{0:T(1024)(128)(4,1)S(1)}, s32[]{:S(2)}) async-start(s8[4718592]{0:T(1024)(128)(4,1)} %bitcast.250), calls=%async_computation.16 | async-start | bytes 8388608
  271.7 8.3 slice-start.8
  280.1 9.6 %copy-start.79 = (f32[1280,3072]{1,0:T(8,128)}, f32[1280,3072]{1,0:T(8,128)S(1)}, u32[]{:S(2)}) copy-start(f32[1280,3072]{1,0:T(8,128)S(1)} %fusion.34) | copy-start | bytes 47185924
  324.8 7.3 copy-start.58
  324.8 50.7 %all-to-all-start.1 = ((bf16[8,2,61440]{2,1,0:T(2,128)(2,1)}), bf16[8,2,61440]{2,1,0:T(2,128)(2,1)}, u32[]{:S(2)}, u32[]{:S(2)}) async-start(bf16[8,2,61440]{2,1,0:T(2,128)(2,1)} %reshape.456), calls=%async_computation.1 | async-start | bytes 3932160 | tf_op jit(solution)/shard_map/all_to_all | solution.py:192
  329.3 544.8 %reduce-scatter.5.cloned.1.call-start = ((), (), s32[]{:S(2)}) async-start(), calls=%async_computation.7 | async-start | bytes 5898240 | tf_op jit(solution)/shard_map/reduce_scatter | solution.py:226
  332.4 258.6 %copy-start.39 = (f32[1024,8]{0,1:T(8,128)}, f32[1024,8]{0,1:T(8,128)S(1)}, u32[]{:S(2)}) copy-start(f32[1024,8]{0,1:T(8,128)S(1)} %get-tuple-element.161) | copy-start | bytes 98308
  485.0 11.7 %copy-start.78 = (bf16[1280,3072]{1,0:T(8,128)(2,1)}, bf16[1280,3072]{1,0:T(8,128)(2,1)S(1)}, u32[]{:S(2)}) copy-start(bf16[1280,3072]{1,0:T(8,128)(2,1)S(1)} %fusion.20) | copy-start | bytes 23592964
  524.3 6.8 copy-start.48
  524.4 6.8 copy-start.52
  527.5 49.8 %all-to-all-start.3 = ((bf16[8,2,61440]{2,1,0:T(2,128)(2,1)}), bf16[8,2,61440]{2,1,0:T(2,128)(2,1)S(1)}, u32[]{:S(2)}, u32[]{:S(2)}) async-start(bf16[8,2,61440]{2,1,0:T(2,128)(2,1)} %reshape.458), calls=%async_computation.3 | async-start | bytes 3932160 | tf_op jit(solution)/shard_map/all_to_all | solution.py:213
  531.1 345.9 %reduce-scatter.3.cloned.1.call-start = ((), (), s32[]{:S(2)}) async-start(), calls=%async_computation.6 | async-start | bytes 5898240 | tf_op jit(solution)/shard_map/reduce_scatter | solution.py:223
  543.1 392.5 %all-reduce.4.cloned.1.call-start = ((), (), s32[]{:S(2)}) async-start(), calls=%async_computation.8 | async-start | bytes 18874368 | tf_op jit(solution)/shard_map/psum | solution.py:326
  591.1 4.0 copy-start.2
  643.3 17.3 %copy-start.4 = (bf16[1024,768]{0,1:T(8,128)(2,1)S(1)}, bf16[1024,768]{0,1:T(8,128)(2,1)}, u32[]{:S(2)}) copy-start(bf16[1024,768]{0,1:T(8,128)(2,1)} %copy-done.3) | copy-start | bytes 4718596
  660.6 8.5 copy-start.46
  660.6 8.5 copy-start.50
  669.1 30.5 %copy-start.41 = (bf16[12,64,512]{2,1,0:T(8,128)(2,1)}, bf16[12,64,512]{2,1,0:T(8,128)(2,1)S(1)}, u32[]{:S(2)}) copy-start(bf16[12,64,512]{2,1,0:T(8,128)(2,1)S(1)} %multiply_convert_fusion.7) | copy-start | bytes 2359300
  690.9 8.6 copy-start.10
  690.9 8.7 copy-start.60
  690.9 8.7 copy-start.65
  702.5 12.1 %copy-start.45 = (f32[12,512]{1,0:T(8,128)S(1)}, f32[12,512]{1,0:T(8,128)}, u32[]{:S(2)}) copy-start(f32[12,512]{1,0:T(8,128)} %log_add_fusion.1) | copy-start | bytes 73732
  702.5 30.3 %slice-start.3 = ((s8[12582912]{0:T(1024)(128)(4,1)}), s8[4194304]{0:T(1024)(128)(4,1)S(1)}, s32[]{:S(2)}) async-start(s8[12582912]{0:T(1024)(128)(4,1)} %bitcast.202), calls=%async_computation.12 | async-start | bytes 8388608
  702.5 30.3 %slice-start.4 = ((s8[12582912]{0:T(1024)(128)(4,1)}), s8[4194304]{0:T(1024)(128)(4,1)S(1)}, s32[]{:S(2)}) async-start(s8[12582912]{0:T(1024)(128)(4,1)} %bitcast.202), calls=%async_computation.13 | async-start | bytes 8388608
  714.6 13.2 %copy-start.61 = (f32[768]{0:T(1024)S(1)}, f32[768]{0:T(1024)}, u32[]{:S(2)}) copy-start(f32[768]{0:T(1024)} %copy-done.59) | copy-start | bytes 9220
  714.6 13.3 %copy-start.66 = (f32[1024]{0:T(1024)S(1)}, f32[1024]{0:T(1024)}, u32[]{:S(2)}) copy-start(f32[1024]{0:T(1024)} %copy-done.64) | copy-start | bytes 12292
  714.6 18.2 %slice-start.5 = ((s8[12582912]{0:T(1024)(128)(4,1)}), s8[4194304]{0:T(1024)(128)(4,1)S(1)}, s32[]{:S(2)}) async-start(s8[12582912]{0:T(1024)(128)(4,1)} %bitcast.202), calls=%async_computation.14 | async-start | bytes 8388608
  727.9 4.9 copy-start.24
  727.9 7.2 slice-start
  727.9 7.2 slice-start.1
  770.0 23.2 %copy-start.30 = (bf16[1,1024,768]{1,2,0:T(8,128)(2,1)S(1)}, bf16[1,1024,768]{1,2,0:T(8,128)(2,1)}, u32[]{:S(2)}) copy-start(bf16[1,1024,768]{1,2,0:T(8,128)(2,1)} %get-tuple-element.147) | copy-start | bytes 4718596
  808.4 12.9 %copy-start.21 = (s32[512,1024]{0,1:T(8,128)S(1)}, s32[512,1024]{0,1:T(8,128)}, u32[]{:S(2)}) copy-start(s32[512,1024]{0,1:T(8,128)} %select_add_fusion) | copy-start | bytes 6291460
  821.3 13.4 %copy-start.53 = (f32[768,8]{0,1:T(8,128)S(1)}, f32[768,8]{0,1:T(8,128)}, u32[]{:S(2)}) copy-start(f32[768,8]{0,1:T(8,128)} %fusion.130) | copy-start | bytes 73732
  821.3 13.4 %copy-start.72 = (f32[768]{0:T(1024)S(1)}, f32[768]{0:T(1024)}, u32[]{:S(2)}) copy-start(f32[768]{0:T(1024)} %get-tuple-element.132) | copy-start | bytes 9220
  (46 other events, 117.9 us)
Sparse Core Ops, SparseCore 0:
  467.3 55.9 reduce-scatter.4
  543.2 58.2 reduce-scatter.2
Sparse Core Ops, SparseCore 1:
  744.3 191.2 all-reduce.3
where the time goes:
time: 963 us; the launch traced here: 953 us
  matrix products  307 us (32%)
  local copies, waits for them, and re-layouts  229 us (24%)
  blocking collectives  141 us (15%)
  waiting for transfers between devices  133 us (14%)
  other arithmetic  118 us (12%)
  between operations  17.4 us (2%)
    dot_general x2, local copies, waits for them, and re-layouts, on_device(): jnp.einsum('eou,eg->gou', indicator_block, bucket_head_bias, preferred_el...  60.8 us
    psum x1, waiting for transfers between devices, on_device(): lax.psum((norm_gain_grad, query_grad, key_grad, value_grad, output_grad,...  55.8 us
    unnamed x191, local copies, waits for them, and re-layouts  54.8 us
    all_to_all x1, blocking collectives, on_device(): lax.all_to_all(slot_buffer, 'expert', split_axis=0, concat_axis=1, tiled=...  52.9 us
    all_to_all x1, blocking collectives, on_device(): lax.all_to_all(home_grad, 'expert', split_axis=0, concat_axis=1, tiled=True)  48.9 us
    convert_element_type x2, local copies, waits for them, and re-layouts, attend_backward(): scores_gradient = (prob_rows * (prob_grad - row_delta)).astype(jnp.bfloat16)  46.5 us
    convert_element_type x2, other arithmetic, attend_backward(): scores_gradient = (prob_rows * (prob_grad - row_delta)).astype(jnp.bfloat16)  43.4 us
    all_to_all x1, waiting for transfers between devices, on_device(): lax.all_to_all(expert_rows, 'expert', split_axis=1, concat_axis=0, tiled=...  43 us
  transfers between devices with their start and end apart: 5, of which 3 were waited for; matrix products, arithmetic and copies ran while one was open for 35% of the time, Pallas kernels for 0%

commit v1 on v0

v1 whole, which is shorter than its diff:
```python
import functools
import math

import jax
import jax.numpy as jnp
from jax import lax
from jax.experimental import pallas as pl
from jax.experimental.pallas import tpu as pltpu
from jax.sharding import PartitionSpec as P

BF = jnp.bfloat16
F32 = jnp.float32
MAXDIST = 128
EPSILON = 1e-06
NEGATIVE = -1000000000.0
TILE = 128
LANES = 128
HALF = 64
LINE = 4 * TILE
VMEM_LIMIT = 60 * 1024 * 1024
GELU_ONE = math.sqrt(2.0 / math.pi)
GELU_CUBE = 0.044715


def dot(left, right, left_dim=1, right_dim=0):
    return lax.dot_general(
        left, right, (((left_dim,), (right_dim,)), ((), ())), preferred_element_type=F32
    )


def iota(shape, dim):
    return lax.broadcasted_iota(jnp.int32, shape, dim)


def bucket_of(offset, buckets, far_limit):
    exact_limit = buckets // 4
    half_count = buckets // 2
    distance = jnp.abs(offset)
    bucket_ids = jnp.minimum(distance, exact_limit)
    for bucket_level in range(exact_limit + 1, half_count):
        border = math.ceil(
            exact_limit
            * (far_limit / exact_limit)
            ** ((bucket_level - exact_limit) / (half_count - exact_limit))
        )
        bucket_ids = bucket_ids + (distance >= border).astype(jnp.int32)
    return bucket_ids + jnp.where(offset > 0, half_count, 0).astype(jnp.int32)


def line_buckets(buckets):
    place = jnp.arange(LINE, dtype=jnp.int32)
    offset = jnp.where(place < 3 * TILE, place - TILE, place - TILE - LINE)
    return bucket_of(offset, buckets, MAXDIST)


def whole(shape):
    return pl.BlockSpec(shape, lambda *_: (0,) * len(shape))


def smem():
    return pl.BlockSpec(memory_space=pltpu.SMEM)


def params():
    return pltpu.CompilerParams(vmem_limit_bytes=VMEM_LIMIT)


def shape_of(shape, dtype):
    return jax.ShapeDtypeStruct(shape, dtype)


def cost(flops, bytes_accessed):
    return pl.CostEstimate(flops=int(flops), bytes_accessed=int(bytes_accessed), transcendentals=0)


def inverse_rms(rows):
    return lax.rsqrt(jnp.mean(rows * rows, axis=-1, keepdims=True) + EPSILON)


def send_rows(starts_ref, slot_row, rows, send_refs):
    for number, send_ref in enumerate(send_refs):
        wanted = iota((send_ref.shape[0], slot_row.shape[1]), 0) + starts_ref[number]
        chosen = jnp.where(wanted == slot_row, 1.0, 0.0).astype(BF)
        send_ref[...] = dot(chosen, rows).astype(BF)


def home_rows(slot_column, wanted_row, blocks):
    chosen = jnp.where(slot_column == wanted_row, 1.0, 0.0).astype(BF)
    return dot(chosen, jnp.concatenate(blocks, axis=0))


def slots_kernel(capacity, experts, starts_ref, length_ref, routes_ref, cotangent_ref, slot_ref, *send_refs):
    seq_len = routes_ref.shape[1]
    routes = routes_ref[...]
    live = iota((1, seq_len), 1) < length_ref[0]
    onehot = jnp.where((iota((experts, seq_len), 0) == routes) & live, 1.0, 0.0)
    earlier = jnp.where(iota((seq_len, seq_len), 0) < iota((seq_len, seq_len), 1), 1.0, 0.0)
    before = dot(onehot.astype(BF), earlier.astype(BF))
    rank = jnp.sum(before * onehot, axis=0, keepdims=True).astype(jnp.int32)
    slot = jnp.where(live & (rank < capacity), routes * capacity + rank, -1)
    slot_ref[...] = slot
    send_rows(starts_ref, slot, cotangent_ref[...], send_refs)


def slots_part(starts, lengths, routes, cotangent, capacity, experts, block_rows):
    seq_len, width = cotangent.shape
    count = starts.shape[0]
    return pl.pallas_call(
        functools.partial(slots_kernel, capacity, experts),
        out_shape=[shape_of((1, seq_len), jnp.int32)]
        + [shape_of((block_rows, width), BF)] * count,
        in_specs=[smem(), smem(), pl.BlockSpec(), pl.BlockSpec()],
        compiler_params=params(),
        name="slots",
    )(starts, lengths, routes, cotangent)


def forward_kernel(
    count,
    starts_ref,
    length_ref,
    slot_ref,
    tokens_ref,
    gain_one_ref,
    query_weight_ref,
    key_weight_ref,
    value_weight_ref,
    out_weight_ref,
    line_ref,
    far_ref,
    gain_two_ref,
    *refs,
):
    probs_ref, qkv_ref, normed_ref, mixed_ref, inverse_ref, resid_ref = refs[:6]
    send_refs = refs[6 : 6 + count]
    qkv_s, mixed_s = refs[6 + count :]
    pair = pl.program_id(0)
    pairs = pl.num_programs(0)
    seq_len, width = tokens_ref.shape
    tiles = seq_len // TILE

    @pl.when(pair == 0)
    def _():
        rows = tokens_ref[...].astype(F32)
        normed = (rows * inverse_rms(rows) * gain_one_ref[...]).astype(BF)
        normed_ref[...] = normed
        for part, weight_ref in enumerate((query_weight_ref, key_weight_ref, value_weight_ref)):
            values = dot(normed, weight_ref[...])
            for number in range(width // LANES):
                block = values[:, number * LANES : (number + 1) * LANES].astype(BF)
                if part == 0:
                    block = block * BF(HALF ** (-0.5))
                qkv_s[part, number] = block

    query = qkv_s[0, pair]
    key = qkv_s[1, pair]
    value = qkv_s[2, pair]
    qkv_ref[0, 0] = query
    qkv_ref[1, 0] = key
    qkv_ref[2, 0] = value
    lane = iota((seq_len, LANES), 1)
    row = iota((seq_len, LANES), 0)
    row_tile = row // TILE
    value_wide = jnp.concatenate([value, jnp.ones((seq_len, LANES), BF)], axis=1)
    outs = []
    for half in range(2):
        own = lane < HALF if half == 0 else lane >= HALF
        extra = lane - HALF if half == 0 else lane
        query_wide = jnp.where(
            own, query.astype(F32), jnp.where((extra == 0) | (extra == 1 + row_tile), 1.0, 0.0)
        ).astype(BF)
        query_tile = extra - 1
        far = jnp.where(
            row_tile <= query_tile - 2,
            far_ref[0, half, 0],
            jnp.where(row_tile >= query_tile + 2, far_ref[0, half, 1], 0.0),
        )
        far = jnp.where((query_tile >= 0) & (query_tile < tiles), far, 0.0)
        far = jnp.where((extra == 0) & (row >= length_ref[0]), NEGATIVE, far)
        key_wide = jnp.where(own, key.astype(F32), far).astype(BF)
        line = jnp.broadcast_to(line_ref[0, half : half + 1, :], (TILE, LINE))
        near = pltpu.roll(line, 0, 1, stride=1, stride_axis=0)[:, : 3 * TILE]
        for tile in range(tiles):
            scores = dot(query_wide[tile * TILE : (tile + 1) * TILE], key_wide, 1, 1)
            low = max(tile - 1, 0)
            high = min(tile + 2, tiles)
            parts = []
            if low > 0:
                parts.append(scores[:, : low * TILE])
            parts.append(
                scores[:, low * TILE : high * TILE]
                + near[:, (low - tile + 1) * TILE : (high - tile + 1) * TILE]
            )
            if high < tiles:
                parts.append(scores[:, high * TILE :])
            scores = jnp.concatenate(parts, axis=1)
            peak = jnp.max(scores, axis=-1, keepdims=True)
            probs_ref[half, tile * TILE : (tile + 1) * TILE, :] = jnp.exp(scores - peak).astype(BF)
        outs.append(dot(probs_ref[half], value_wide))
    first = lane < HALF
    inverse_total = 1.0 / jnp.where(first, outs[0][:, LANES:], outs[1][:, LANES:])
    mixed = jnp.where(first, outs[0][:, :LANES], outs[1][:, :LANES]) * inverse_total
    mixed_s[pair] = mixed.astype(BF)
    inverse_ref[0] = inverse_total

    @pl.when(pair == pairs - 1)
    def _():
        mixed_all = jnp.concatenate([mixed_s[number] for number in range(width // LANES)], axis=1)
        mixed_ref[...] = mixed_all
        resid = tokens_ref[...].astype(F32) + dot(mixed_all, out_weight_ref[...])
        resid_ref[...] = resid
        normed = (resid * inverse_rms(resid) * gain_two_ref[...]).astype(BF)
        send_rows(starts_ref, slot_ref[...], normed, send_refs)


def forward_part(starts, lengths, slot, tokens, gain_one, weights, lines, far, gain_two, block_rows):
    seq_len, width = tokens.shape
    pairs = width // LANES
    count = starts.shape[0]
    square = whole((width, width))
    return pl.pallas_call(
        functools.partial(forward_kernel, count),
        grid=(pairs,),
        out_shape=[
            shape_of((2 * pairs, seq_len, seq_len), BF),
            shape_of((3, pairs, seq_len, LANES), BF),
            shape_of((seq_len, width), BF),
            shape_of((seq_len, width), BF),
            shape_of((pairs, seq_len, LANES), F32),
            shape_of((seq_len, width), F32),
        ]
        + [shape_of((block_rows, width), BF)] * count,
        in_specs=[
            smem(),
            smem(),
            whole((1, seq_len)),
            whole((seq_len, width)),
            whole((1, width)),
            square,
            square,
            square,
            square,
            pl.BlockSpec((1, 2, LINE), lambda p: (p, 0, 0)),
            pl.BlockSpec((1, 2, 2), lambda p: (p, 0, 0), memory_space=pltpu.SMEM),
            whole((1, width)),
        ],
        out_specs=[
            pl.BlockSpec((2, seq_len, seq_len), lambda p: (p, 0, 0)),
            pl.BlockSpec((3, 1, seq_len, LANES), lambda p: (0, p, 0, 0)),
            whole((seq_len, width)),
            whole((seq_len, width)),
            pl.BlockSpec((1, seq_len, LANES), lambda p: (p, 0, 0)),
            whole((seq_len, width)),
        ]
        + [whole((block_rows, width))] * count,
        scratch_shapes=[
            pltpu.VMEM((3, pairs, seq_len, LANES), BF),
            pltpu.VMEM((pairs, seq_len, LANES), BF),
        ],
        compiler_params=params(),
        cost_estimate=cost(50e9, 60e6),
        name="attention_forward",
    )(starts, lengths, slot, tokens, gain_one, *weights, lines, far, gain_two)


def expert_kernel(count, expert_ref, *refs):
    row_refs = refs[:count]
    up_refs = refs[count : 2 * count]
    in_ref, out_ref, router_ref = refs[2 * count : 2 * count + 3]
    act_ref, pre_grad_ref, rows_ref, rows_grad_ref, gate_ref, router_grad_ref = refs[
        2 * count + 3 : 2 * count + 9
    ]
    back_refs = refs[2 * count + 9 : 3 * count + 9]
    total_s, gate_grad_s, probs_s = refs[3 * count + 9 :]
    step = pl.program_id(0)
    steps = pl.num_programs(0)
    block_rows = row_refs[0].shape[0]
    rows = rows_ref.shape[0]
    experts = router_ref.shape[1]
    own = iota((rows, experts), 1) == expert_ref[0]

    @pl.when(step == 0)
    def _():
        for number in range(count):
            rows_ref[pl.ds(number * block_rows, block_rows), :] = row_refs[number][...]
        logits = dot(rows_ref[...], router_ref[...])
        raised = jnp.exp(logits - jnp.max(logits, axis=-1, keepdims=True))
        probs = raised / jnp.sum(raised, axis=-1, keepdims=True)
        probs_s[...] = probs
        gate = jnp.sum(jnp.where(own, probs, 0.0), axis=-1, keepdims=True)
        gate_ref[...] = gate
        gate_grad_s[...] = jnp.zeros_like(gate_grad_s)
        total_s[...] = jnp.zeros_like(total_s)
        for number in range(count):
            part = pl.ds(number * block_rows, block_rows)
            rows_grad_ref[part, :] = (
                up_refs[number][...].astype(F32) * gate[number * block_rows : (number + 1) * block_rows]
            ).astype(BF)

    for number in range(count):
        part = pl.ds(number * block_rows, block_rows)
        pre = dot(row_refs[number][...], in_ref[...])
        act_grad = dot(up_refs[number][...], out_ref[...], 1, 1)
        square = pre * pre
        level = 0.5 + 0.5 * jnp.tanh(pre * (GELU_ONE + GELU_ONE * GELU_CUBE * square))
        act = pre * level
        slope = level + act * (1.0 - level) * (2.0 * GELU_ONE + 6.0 * GELU_ONE * GELU_CUBE * square)
        gate_grad_s[part, :] += jnp.sum(act * act_grad, axis=-1, keepdims=True)
        pre_grad = (act_grad * slope * gate_ref[part, :]).astype(BF)
        act_ref[part, :] = act.astype(BF)
        pre_grad_ref[part, :] = pre_grad
        total_s[part, :] += dot(pre_grad, in_ref[...], 1, 1)

    @pl.when(step == steps - 1)
    def _():
        logit_grad = (
            gate_grad_s[...] * gate_ref[...] * (jnp.where(own, 1.0, 0.0) - probs_s[...])
        ).astype(BF)
        router_grad_ref[...] = dot(logit_grad, rows_ref[...], 0, 0)
        back = total_s[...] + dot(logit_grad, router_ref[...], 1, 1)
        for number in range(count):
            back_refs[number][...] = back[number * block_rows : (number + 1) * block_rows].astype(BF)


def expert_part(expert, row_blocks, up_blocks, expert_in, expert_out, router):
    count = len(row_blocks)
    block_rows, width = row_blocks[0].shape
    rows = count * block_rows
    hidden = expert_in.shape[1]
    experts = router.shape[1]
    tile = 512
    block = whole((block_rows, width))
    return pl.pallas_call(
        functools.partial(expert_kernel, count),
        grid=(hidden // tile,),
        out_shape=[
            shape_of((rows, hidden), BF),
            shape_of((rows, hidden), BF),
            shape_of((rows, width), BF),
            shape_of((rows, width), BF),
            shape_of((rows, 1), F32),
            shape_of((experts, width), F32),
        ]
        + [shape_of((block_rows, width), BF)] * count,
        in_specs=[smem()]
        + [block] * (2 * count)
        + [
            pl.BlockSpec((width, tile), lambda f: (0, f)),
            pl.BlockSpec((tile, width), lambda f: (f, 0)),
            whole((width, experts)),
        ],
        out_specs=[
            pl.BlockSpec((rows, tile), lambda f: (0, f)),
            pl.BlockSpec((rows, tile), lambda f: (0, f)),
            whole((rows, width)),
            whole((rows, width)),
            whole((rows, 1)),
            whole((experts, width)),
        ]
        + [block] * count,
        scratch_shapes=[
            pltpu.VMEM((rows, width), F32),
            pltpu.VMEM((rows, 1), F32),
            pltpu.VMEM((rows, experts), F32),
        ],
        compiler_params=params(),
        cost_estimate=cost(18e9, 40e6),
        name="expert_rows",
    )(expert, *row_blocks, *up_blocks, expert_in, expert_out, router)


def weight_grad_kernel(transposed, me_ref, wide_ref, rows_ref, *out_refs):
    step = pl.program_id(0)
    for number, out_ref in enumerate(out_refs):

        @pl.when(step == number)
        def _(out_ref=out_ref):
            if transposed:
                out_ref[...] = dot(wide_ref[...], rows_ref[...], 0, 0).astype(BF)
            else:
                out_ref[...] = dot(rows_ref[...], wide_ref[...], 0, 0).astype(BF)


def weight_grad_part(me, wide, rows, parts, transposed):
    count, width = rows.shape
    hidden = wide.shape[1]
    tile = hidden // parts
    shape = (tile, width) if transposed else (width, tile)
    return pl.pallas_call(
        functools.partial(weight_grad_kernel, transposed),
        grid_spec=pltpu.PrefetchScalarGridSpec(
            num_scalar_prefetch=1,
            grid=(parts,),
            in_specs=[
                pl.BlockSpec((count, tile), lambda s, me_ref: (0, me_ref[0] ^ s)),
                whole((count, width)),
            ],
            out_specs=[whole(shape)] * parts,
        ),
        out_shape=[shape_of(shape, BF)] * parts,
        compiler_params=params(),
        cost_estimate=cost(2 * count * hidden * width, 20e6),
        name="expert_weight_gradient",
    )(me, wide, rows)


def expert_out_kernel(act_ref, out_ref, gate_ref, *refs):
    total_s = refs[-1]
    send_refs = refs[:-1]
    step = pl.program_id(0)

    @pl.when(step == 0)
    def _():
        total_s[...] = jnp.zeros_like(total_s)

    total_s[...] += dot(act_ref[...], out_ref[...])

    @pl.when(step == pl.num_programs(0) - 1)
    def _():
        block_rows = send_refs[0].shape[0]
        for number, send_ref in enumerate(send_refs):
            part = pl.ds(number * block_rows, block_rows)
            send_ref[...] = (total_s[part, :] * gate_ref[part, :]).astype(BF)


def expert_out_part(act, expert_out, gate, count):
    rows, hidden = act.shape
    width = expert_out.shape[1]
    tile = 512
    block_rows = rows // count
    return pl.pallas_call(
        expert_out_kernel,
        grid=(hidden // tile,),
        out_shape=[shape_of((block_rows, width), BF)] * count,
        in_specs=[
            pl.BlockSpec((rows, tile), lambda f: (0, f)),
            pl.BlockSpec((tile, width), lambda f: (f, 0)),
            whole((rows, 1)),
        ],
        out_specs=[whole((block_rows, width))] * count,
        scratch_shapes=[pltpu.VMEM((rows, width), F32)],
        compiler_params=params(),
        cost_estimate=cost(2 * rows * hidden * width, 16e6),
        name="expert_output",
    )(act, expert_out, gate)


def result_kernel(length_ref, slot_ref, wanted_ref, resid_ref, *refs):
    blocks = [ref[...] for ref in refs[:-1]]
    total = resid_ref[...] + home_rows(slot_ref[...], wanted_ref[...], blocks)
    live = iota((total.shape[0], 1), 0) < length_ref[0]
    refs[-1][...] = jnp.where(live, total, 0.0).astype(BF)


def result_part(lengths, slot_column, wanted, resid, blocks):
    return pl.pallas_call(
        result_kernel,
        out_shape=shape_of(resid.shape, BF),
        in_specs=[smem()] + [pl.BlockSpec()] * (3 + len(blocks)),
        compiler_params=params(),
        cost_estimate=cost(2e9, 10e6),
        name="result",
    )(lengths, slot_column, wanted, resid, *blocks)


def middle_kernel(
    length_ref,
    slot_ref,
    wanted_ref,
    resid_ref,
    cotangent_ref,
    mixed_ref,
    out_weight_ref,
    gain_ref,
    *refs,
):
    blocks = [ref[...] for ref in refs[:-4]]
    resid_grad_ref, mixed_grad_ref, out_grad_ref, gain_grad_ref = refs[-4:]
    upstream = home_rows(slot_ref[...], wanted_ref[...], blocks)
    resid = resid_ref[...]
    inverse = inverse_rms(resid)
    scaled = gain_ref[...] * upstream
    gain_grad_ref[...] = jnp.sum(upstream * resid * inverse, axis=0, keepdims=True)
    live = iota((resid.shape[0], 1), 0) < length_ref[0]
    resid_grad = (
        jnp.where(live, cotangent_ref[...].astype(F32), 0.0)
        + inverse * scaled
        - resid * (inverse * inverse * inverse * jnp.mean(scaled * resid, axis=-1, keepdims=True))
    )
    resid_grad_ref[...] = resid_grad
    attn_grad = resid_grad.astype(BF)
    mixed_grad_ref[...] = dot(attn_grad, out_weight_ref[...], 1, 1).astype(BF)
    out_grad_ref[...] = dot(mixed_ref[...], attn_grad, 0, 0).astype(BF)


def middle_part(lengths, slot_column, wanted, resid, cotangent, mixed, out_weight, gain, blocks):
    seq_len, width = resid.shape
    return pl.pallas_call(
        middle_kernel,
        out_shape=[
            shape_of((seq_len, width), F32),
            shape_of((seq_len, width), BF),
            shape_of((width, width), BF),
            shape_of((1, width), F32),
        ],
        in_specs=[smem()] + [pl.BlockSpec()] * (7 + len(blocks)),
        compiler_params=params(),
        cost_estimate=cost(5e9, 20e6),
        name="expert_norm_backward",
    )(lengths, slot_column, wanted, resid, cotangent, mixed, out_weight, gain, *blocks)


def backward_kernel(
    qkv_ref, probs_ref, mixed_ref, grad_ref, inverse_ref, back_ref, line_ref, far_ref, score_s
):
    seq_len = mixed_ref.shape[0]
    tiles = seq_len // TILE
    query = qkv_ref[0, 0]
    key = qkv_ref[1, 0]
    value = qkv_ref[2, 0]
    lane = iota((seq_len, LANES), 1)
    row_tile = iota((seq_len, LANES), 0) // TILE
    scaled = grad_ref[...].astype(F32) * inverse_ref[0]
    product = scaled * mixed_ref[...].astype(F32)
    scaled_low = scaled.astype(BF)
    key_wide = jnp.concatenate([key, jnp.where(lane == row_tile, 1.0, 0.0).astype(BF)], axis=1)
    backward_rows = jnp.where(iota((TILE, TILE), 0) + iota((TILE, TILE), 1) == TILE - 1, 1.0, 0.0)
    query_backs = []
    key_backs = []
    value_backs = []
    for half in range(2):
        own = lane < HALF if half == 0 else lane >= HALF
        extra = lane - HALF if half == 0 else lane
        delta = jnp.sum(jnp.where(own, product, 0.0), axis=-1, keepdims=True)
        high = delta.astype(BF).astype(F32)
        grad_wide = jnp.where(
            own, scaled, jnp.where(extra == 0, -high, jnp.where(extra == 1, high - delta, 0.0))
        ).astype(BF)
        value_wide = jnp.where(
            own, value.astype(F32), jnp.where((extra == 0) | (extra == 1), 1.0, 0.0)
        ).astype(BF)
        near = [jnp.zeros((TILE, TILE), F32) for _ in range(3)]
        for tile in range(tiles):
            part = slice(tile * TILE, (tile + 1) * TILE)
            prob_grad = dot(grad_wide[part], value_wide, 1, 1)
            score_grad = (probs_ref[half, part, :].astype(F32) * prob_grad).astype(BF)
            score_s[half, part, :] = score_grad
            for side in range(3):
                other = tile + side - 1
                if 0 <= other < tiles:
                    near[side] = near[side] + score_grad[
                        :, other * TILE : (other + 1) * TILE
                    ].astype(F32)
        query_wide = dot(score_s[half], key_wide)
        query_backs.append(query_wide[:, :LANES])
        sums = query_wide[:, LANES:]
        far_left = jnp.sum(jnp.where(lane <= row_tile - 2, sums, 0.0), axis=0, keepdims=True)
        far_right = jnp.sum(jnp.where(lane >= row_tile + 2, sums, 0.0), axis=0, keepdims=True)
        far_ref[0, 2 * half : 2 * half + 1, :] = far_left
        far_ref[0, 2 * half + 1 : 2 * half + 2, :] = far_right
        key_backs.append(dot(query, score_s[half], 0, 0))
        value_backs.append(dot(scaled_low, probs_ref[half], 0, 0))
        spread = lax.dot_general(
            backward_rows,
            jnp.concatenate(near, axis=1),
            (((1,), (0,)), ((), ())),
            precision=lax.Precision.HIGHEST,
            preferred_element_type=F32,
        )
        spread = jnp.concatenate([spread, jnp.zeros((TILE, TILE), F32)], axis=1)
        spread = pltpu.roll(spread, 0, 1, stride=1, stride_axis=0)
        line_ref[0, half : half + 1, :] = jnp.sum(spread, axis=0, keepdims=True)
    first = lane < HALF
    back_ref[0] = (jnp.where(first, query_backs[0], query_backs[1]) * HALF ** (-0.5)).astype(BF)
    for place, backs in ((1, key_backs), (2, value_backs)):
        joined = jnp.concatenate([backs[0][:HALF], backs[1][HALF:]], axis=0)
        back_ref[place] = joined.T.astype(BF)


def backward_part(qkv, probs, mixed, mixed_grad, inverse):
    seq_len, width = mixed.shape
    pairs = width // LANES
    column = pl.BlockSpec((seq_len, LANES), lambda p: (0, p))
    return pl.pallas_call(
        backward_kernel,
        grid=(pairs,),
        out_shape=[
            shape_of((3, seq_len, width), BF),
            shape_of((pairs, 2, LINE), F32),
            shape_of((pairs, 4, LANES), F32),
        ],
        in_specs=[
            pl.BlockSpec((3, 1, seq_len, LANES), lambda p: (0, p, 0, 0)),
            pl.BlockSpec((2, seq_len, seq_len), lambda p: (p, 0, 0)),
            column,
            column,
            pl.BlockSpec((1, seq_len, LANES), lambda p: (p, 0, 0)),
        ],
        out_specs=[
            pl.BlockSpec((3, seq_len, LANES), lambda p: (0, 0, p)),
            pl.BlockSpec((1, 2, LINE), lambda p: (p, 0, 0)),
            pl.BlockSpec((1, 4, LANES), lambda p: (p, 0, 0)),
        ],
        scratch_shapes=[pltpu.VMEM((2, seq_len, seq_len), BF)],
        compiler_params=params(),
        cost_estimate=cost(60e9, 60e6),
        name="attention_backward",
    )(qkv, probs, mixed, mixed_grad, inverse)


def projection_grad_kernel(normed_ref, back_ref, out_ref):
    out_ref[0] = dot(normed_ref[...], back_ref[0], 0, 0).astype(BF)


def projection_grad_part(normed, back):
    parts, seq_len, width = back.shape
    return pl.pallas_call(
        projection_grad_kernel,
        grid=(parts,),
        out_shape=shape_of((parts, width, width), BF),
        in_specs=[
            whole((seq_len, width)),
            pl.BlockSpec((1, seq_len, width), lambda p: (p, 0, 0)),
        ],
        out_specs=pl.BlockSpec((1, width, width), lambda p: (p, 0, 0)),
        compiler_params=params(),
        cost_estimate=cost(parts * 2 * seq_len * width * width, 10e6),
        name="projection_gradient",
    )(normed, back)


def token_grad_kernel(
    back_ref, query_weight_ref, key_weight_ref, value_weight_ref, tokens_ref, gain_ref, resid_grad_ref, out_ref, gain_grad_ref
):
    upstream = dot(back_ref[0], query_weight_ref[...], 1, 1)
    upstream += dot(back_ref[1], key_weight_ref[...], 1, 1)
    upstream += dot(back_ref[2], value_weight_ref[...], 1, 1)
    rows = tokens_ref[...].astype(F32)
    inverse = inverse_rms(rows)
    scaled = gain_ref[...] * upstream
    gain_grad_ref[...] = jnp.sum(upstream * rows * inverse, axis=0, keepdims=True)
    out_ref[...] = (
        resid_grad_ref[...]
        + inverse * scaled
        - rows * (inverse * inverse * inverse * jnp.mean(scaled * rows, axis=-1, keepdims=True))
    )


def token_grad_part(back, weights, tokens, gain, resid_grad):
    seq_len, width = tokens.shape
    return pl.pallas_call(
        token_grad_kernel,
        out_shape=[shape_of((seq_len, width), F32), shape_of((1, width), F32)],
        compiler_params=params(),
        cost_estimate=cost(3 * 2 * seq_len * width * width, 16e6),
        name="token_gradient",
    )(back, *weights, tokens, gain, resid_grad)


def swap(values, axis, size, distance):
    return lax.ppermute(values, axis, [(place, place ^ distance) for place in range(size)])


def exchange(blocks, axis, size, capacity):
    if len(blocks) == size:
        return [blocks[0]] + [
            swap(blocks[distance], axis, size, distance) for distance in range(1, size)
        ]
    (rows,) = blocks
    parts = rows.reshape(size, capacity, rows.shape[1])
    return [
        lax.all_to_all(parts, axis, split_axis=0, concat_axis=0, tiled=True).reshape(rows.shape)
    ]


def scatter_sum(parts, axis, size, bits):
    parts = dict(enumerate(parts))
    for number, bit in enumerate(bits):
        last = number == len(bits) - 1
        for distance in [d for d in parts if d & bit]:
            arrived = swap(parts.pop(distance), axis, size, bit)
            total = parts[distance ^ bit].astype(F32) + arrived.astype(F32)
            parts[distance ^ bit] = total if last else total.astype(BF)
    return parts[0]


def stages_of(dp_size, expert_size):
    stages = [("expert", expert_size, (1,))]
    bits = [1 << n for n in range(dp_size.bit_length() - 1)]
    stages += [("dp", dp_size, tuple(bits[n : n + 2])) for n in range(0, len(bits), 2)]
    bits = [1 << n for n in range(1, expert_size.bit_length() - 1)]
    stages += [("expert", expert_size, tuple(bits[n : n + 2])) for n in range(0, len(bits), 2)]
    return stages


def distances_of(bits):
    return [sum(bit for n, bit in enumerate(bits) if (k >> n) & 1) for k in range(1 << len(bits))]


def place_of(axis, bits):
    index = lax.axis_index(axis)
    return sum(((index // bit) % 2) << n for n, bit in enumerate(bits))


def sum_everywhere(values, stages):
    for axis, size, bits in stages:
        distances = distances_of(bits)
        place = place_of(axis, bits)
        rows = values.shape[0] // len(distances)
        total = lax.dynamic_slice_in_dim(values, place * rows, rows, 0).astype(F32)
        for number, distance in list(enumerate(distances))[1:]:
            part = lax.dynamic_slice_in_dim(values, (place ^ number) * rows, rows, 0)
            total = total + swap(part, axis, size, distance).astype(F32)
        values = total.astype(BF)
    for axis, size, bits in reversed(stages):
        distances = distances_of(bits)
        place = place_of(axis, bits)
        rows = values.shape[0]
        joined = jnp.zeros((rows * len(distances),) + values.shape[1:], BF)
        joined = lax.dynamic_update_slice_in_dim(joined, values, place * rows, 0)
        for number, distance in list(enumerate(distances))[1:]:
            arrived = swap(values, axis, size, distance)
            joined = lax.dynamic_update_slice_in_dim(joined, arrived, (place ^ number) * rows, 0)
        values = joined
    return values.astype(F32)


def sum_small(values, stages):
    for axis, size, bits in stages:
        total = values
        for distance in distances_of(bits)[1:]:
            total = total + swap(values, axis, size, distance)
        values = total
    return values


def on_device(
    dp_size,
    expert_size,
    tokens,
    cotangent,
    lengths,
    routes,
    norm_gain,
    query_weight,
    key_weight,
    value_weight,
    output_weight,
    bucket_head_bias,
    ffn_gain,
    router_weight,
    expert_in,
    expert_out,
):
    seq_count, seq_len, width = tokens.shape
    assert seq_count == 1
    buckets, heads = bucket_head_bias.shape
    pairs = heads // 2
    experts = router_weight.shape[1]
    capacity = max(2, 5 * seq_len // (4 * experts))
    expert = lax.axis_index("expert")
    group = lax.axis_index("dp").reshape(1)
    if expert_size <= 8 and capacity % 16 == 0:
        starts = (expert ^ jnp.arange(expert_size, dtype=jnp.int32)) * capacity
        block_rows = capacity
    else:
        starts = jnp.zeros((1,), jnp.int32)
        block_rows = experts * capacity
    count = starts.shape[0]
    wanted = (starts[:, None] + jnp.arange(block_rows, dtype=jnp.int32)[None, :]).reshape(1, -1)
    rows_in = tokens.reshape(seq_len, width)
    upstream = cotangent.reshape(seq_len, width)
    gain_one = norm_gain.astype(F32).reshape(1, width)
    gain_two = ffn_gain.astype(F32).reshape(1, width)
    weight_in = expert_in.reshape(expert_in.shape[1:])
    weight_out = expert_out.reshape(expert_out.shape[1:])
    weights = (query_weight, key_weight, value_weight)

    slot, *up_send = slots_part(starts, lengths, routes, upstream, capacity, experts, block_rows)
    up_blocks = exchange(up_send, "expert", expert_size, capacity)
    slot_column = slot.reshape(seq_len, 1)

    table = bucket_head_bias.astype(F32)
    place_bucket = line_buckets(buckets)
    indicator = (place_bucket[None, :] == jnp.arange(buckets, dtype=jnp.int32)[:, None]).astype(F32)
    lines = lax.dot_general(
        table, indicator, (((0,), (0,)), ((), ())), precision=lax.Precision.HIGHEST
    ).reshape(pairs, 2, LINE)
    far = jnp.stack([table[buckets // 2 - 1], table[buckets - 1]], axis=-1).reshape(pairs, 2, 2)

    probs, qkv, normed, mixed, inverse_total, resid, *row_send = forward_part(
        starts,
        lengths,
        slot,
        rows_in,
        gain_one,
        (*weights, output_weight),
        lines,
        far,
        gain_two,
        block_rows,
    )
    row_blocks = exchange(row_send, "expert", expert_size, capacity)
    act, pre_grad, expert_rows, rows_grad, gate, router_grad, *back_send = expert_part(
        expert.reshape(1), row_blocks, up_blocks, weight_in, weight_out, router_weight
    )
    back_blocks = exchange(back_send, "expert", expert_size, capacity)
    out_parts = weight_grad_part(group, act, rows_grad, dp_size, True)
    in_parts = weight_grad_part(group, pre_grad, expert_rows, dp_size, False)
    bits = [1 << n for n in range(dp_size.bit_length() - 1)]
    expert_out_grad = scatter_sum(out_parts, "dp", dp_size, bits)
    expert_in_grad = scatter_sum(in_parts, "dp", dp_size, bits[::-1])
    result_send = expert_out_part(act, weight_out, gate, count)
    result_blocks = exchange(result_send, "expert", expert_size, capacity)

    resid_grad, mixed_grad, output_grad, ffn_gain_grad = middle_part(
        lengths, slot_column, wanted, resid, upstream, mixed, output_weight, gain_two, back_blocks
    )
    stages = stages_of(dp_size, expert_size)
    output_grad = sum_everywhere(output_grad, stages)
    back, near_sums, far_sums = backward_part(qkv, probs, mixed, mixed_grad, inverse_total)
    projection_grad = projection_grad_part(normed, back)
    projection_grad = sum_everywhere(
        projection_grad.reshape(3 * width, width), stages
    ).reshape(3, width, width)
    token_grad, norm_gain_grad = token_grad_part(back, weights, rows_in, gain_one, resid_grad)
    result = result_part(lengths, slot_column, wanted, resid, result_blocks)

    sum_bucket = bucket_of(jnp.arange(LINE, dtype=jnp.int32) - (2 * TILE - 1), buckets, MAXDIST)
    sum_indicator = sum_bucket[None, :] == jnp.arange(buckets, dtype=jnp.int32)[:, None]
    bucket_grad = lax.dot_general(
        sum_indicator.astype(F32),
        near_sums.reshape(heads, LINE),
        (((1,), (1,)), ((), ())),
        precision=lax.Precision.HIGHEST,
    )
    far_sums = jnp.sum(far_sums, axis=-1).reshape(heads, 2)
    bucket_row = jnp.arange(buckets, dtype=jnp.int32)[:, None]
    bucket_grad = bucket_grad + jnp.where(
        bucket_row == buckets // 2 - 1,
        far_sums[None, :, 0],
        jnp.where(bucket_row == buckets - 1, far_sums[None, :, 1], 0.0),
    )
    small = jnp.concatenate(
        [
            norm_gain_grad,
            ffn_gain_grad,
            router_grad,
            jnp.pad(bucket_grad.T, ((0, 0), (0, width - buckets))),
        ],
        axis=0,
    )
    small = sum_small(small, stages)
    return (
        result.reshape(tokens.shape),
        token_grad.reshape(tokens.shape),
        small[0],
        projection_grad[0],
        projection_grad[1],
        projection_grad[2],
        output_grad,
        small[2 + experts :, :buckets].T,
        small[1],
        small[2 : 2 + experts].T,
        expert_in_grad[None],
        expert_out_grad[None],
    )


def solution(mesh):
    in_specs = (
        P(("dp", "expert"), None, None),
        P(("dp", "expert"), None, None),
        P(("dp", "expert")),
        P(("dp", "expert"), None),
        P(),
        P(),
        P(),
        P(),
        P(),
        P(),
        P(),
        P(),
        P("expert", None, None),
        P("expert", None, None),
    )
    out_specs = (
        P(("dp", "expert"), None, None),
        P(("dp", "expert"), None, None),
        P(),
        P(),
        P(),
        P(),
        P(),
        P(),
        P(),
        P(),
        P("expert", None, "dp"),
        P("expert", "dp", None),
    )
    return jax.shard_map(
        functools.partial(on_device, mesh.shape["dp"], mesh.shape["expert"]),
        mesh=mesh,
        in_specs=in_specs,
        out_specs=out_specs,
        check_vma=False,
    )
```

time: 963 us -> 527 us (0.55)
  matrix products: 307 us -> 1.76 us
  local copies, waits for them, and re-layouts: 229 us -> 18.8 us
  Pallas kernels: 0 us -> 190 us
  blocking collectives: 141 us -> 0 us
  starting transfers between devices: 8.19 us -> 122 us
  other arithmetic: 118 us -> 17.2 us
  waiting for transfers between devices: 133 us -> 171 us
  between operations: 17.4 us -> 2.33 us
    dot_general x38 -> x2, matrix products: 307 us -> 1.76 us  [the longest x1 0.94 us: on_device(): lax.dot_general(sum_indicator.astype(F32), near_sums.reshape(heads, LINE)...]
    pallas_call x0 -> x11, Pallas kernels: none -> 190 us  [the longest x1 43.2 us: forward_part(): pl.pallas_call(functools.partial(forward_kernel, count), grid=(pairs,), o...]
    ppermute x0 -> x69, waiting for transfers between devices: none -> 171 us  [swap(): lax.ppermute(values, axis, [(place, place ^ distance) for place in range(...]
    ppermute x0 -> x69, starting transfers between devices: none -> 122 us  [swap(): lax.ppermute(values, axis, [(place, place ^ distance) for place in range(...]
    all_to_all x2 -> x0, blocking collectives: 102 us -> none  [the longest x1 52.9 us: on_device(): lax.all_to_all(slot_buffer, 'expert', split_axis=0, concat_axis=1, tiled=...]
    convert_element_type x6 -> x0, local copies, waits for them, and re-layouts: 80.9 us -> none  [the longest x2 46.5 us: attend_backward(): scores_gradient = (prob_rows * (prob_grad - row_delta)).astype(jnp.bfloat16)]
    all_to_all x2 -> x0, waiting for transfers between devices: 77.1 us -> none  [the longest x1 43 us: on_device(): lax.all_to_all(expert_rows, 'expert', split_axis=1, concat_axis=0, tiled=...]
    dot_general x2 -> x0, local copies, waits for them, and re-layouts: 60.8 us -> none  [on_device(): jnp.einsum('eou,eg->gou', indicator_block, bucket_head_bias, preferred_el...]
  transfers between devices with their start and end apart: 5 -> 69, of which waited for: 3 -> 25; matrix products, arithmetic and copies ran while one was open for 35% -> 5% of each run, Pallas kernels for 0% -> 19%
where the time goes in v1:
time: 527 us; the launch traced here: 523 us
  Pallas kernels  190 us (36%)
  waiting for transfers between devices  171 us (32%)
  starting transfers between devices  122 us (23%)
  local copies, waits for them, and re-layouts  18.8 us (4%)
  other arithmetic  17.2 us (3%)
    ppermute x69, waiting for transfers between devices, swap(): lax.ppermute(values, axis, [(place, place ^ distance) for place in range(...  171 us
    ppermute x69, starting transfers between devices, swap(): lax.ppermute(values, axis, [(place, place ^ distance) for place in range(...  122 us
    pallas_call x1, Pallas kernels, forward_part(): pl.pallas_call(functools.partial(forward_kernel, count), grid=(pairs,), o...  43.2 us
    pallas_call x1, Pallas kernels, expert_part(): pl.pallas_call(functools.partial(expert_kernel, count), grid=(hidden // t...  41.6 us
    pallas_call x1, Pallas kernels, backward_part(): pl.pallas_call(backward_kernel, grid=(pairs,), out_shape=[shape_of((3, se...  28.4 us
    pallas_call x2, Pallas kernels, weight_grad_part(): pl.pallas_call(functools.partial(weight_grad_kernel, transposed), grid_sp...  23.4 us
    pallas_call x1, Pallas kernels, middle_part(): pl.pallas_call(middle_kernel, out_shape=[shape_of((seq_len, width), F32),...  11.8 us
    pallas_call x1, Pallas kernels, expert_out_part(): pl.pallas_call(expert_out_kernel, grid=(hidden // tile,), out_shape=[shap...  11.6 us
  transfers between devices with their start and end apart: 69, of which 25 were waited for; matrix products, arithmetic and copies ran while one was open for 5% of the time, Pallas kernels for 19%

profile of v1, /device:TPU:0, one launch (start us, length us, event | category | flops | bytes accessed | tf_op | source)
XLA Modules:
  0.0 523.3 jit_solution(17947725825652260625)
XLA Ops:
  7.5 4.8 slots.1
  12.4 43.2 %attention_forward.1 = (bf16[12,1024,1024]{2,1,0:T(8,128)(2,1)}, bf16[3,6,1024,128]{3,2,1,0:T(8,128)(2,1)}, bf16[1024,768]{1,0:T(8,128)(2,1)}, bf16[1024,768]{1,...) custom-call(s32[8]{0:T(128)} %xor_multiply_fusion.starts_ref, ...), custom_call_target="tpu_custom_call" | custom-call | flops 49999998976 | bytes 60000000 | tf_op jit(solution)/shard_map/attention_forward/pallas_call | solution.py:221
  56.1 2.7 collective-permute-start.1
  58.8 2.8 collective-permute-start.3
  61.6 3.6 collective-permute-start.5
  65.2 10.7 %collective-permute-done.1.refs_2_ = bf16[160,768]{1,0:T(8,128)(2,1)S(1)} collective-permute-done((bf16[160,768]{1,0:T(8,128)(2,1)}, bf16[160,768]{1,0:T(8,128)(2,1)S(1)}, u32[]{:S(2)}, u32[]{:S(2)}) %collective-permute-start.1) | collective-permute-done | bytes 245792 | tf_op jit(solution)/shard_map/ppermute | solution.py:661
  76.3 4.3 collective-permute-done.2.refs_3_
  80.6 2.4 collective-permute-start.11
  83.0 25.2 %collective-permute-start.12 = (bf16[160,768]{1,0:T(8,128)(2,1)S(1)}, bf16[160,768]{1,0:T(8,128)(2,1)}, u32[]{:S(2)}, u32[]{:S(2)}) collective-permute-start(bf16[160,768]{1,0:T(8,128)(2,1)S(1)} %copy-done.24), channel_id=1, source_target_pairs={{0,6},{1,7},{2,4},{3,5},{4,2},{5,3},{6,0},{7,1},{8,14},{9,15},{10,... | collective-permute-start | bytes 737288 | tf_op jit(solution)/shard_map/ppermute | solution.py:661
  109.1 22.9 %collective-permute-done.10.refs_12_ = bf16[160,768]{1,0:T(8,128)(2,1)S(1)} collective-permute-done((bf16[160,768]{1,0:T(8,128)(2,1)S(1)}, bf16[160,768]{1,0:T(8,128)(2,1)S(1)}, u32[]{:S(2)}, u32[]{:S(2)}) %collective-permute-start.10) | collective-permute-done | bytes 245792 | tf_op jit(solution)/shard_map/ppermute | solution.py:661
  132.9 3.5 collective-permute-done.11.refs_13_
  142.2 5.1 collective-permute-done.9.refs_11_
  147.4 41.6 %expert_rows.1 = (bf16[1280,3072]{1,0:T(8,128)(2,1)}, bf16[1280,3072]{1,0:T(8,128)(2,1)}, bf16[1280,768]{1,0:T(8,128)(2,1)}, bf16[1280,768]{1,0:T(8,128)(2,1)}, ...) custom-call(s32[1]{0:T(128)} %bitcast.4.expert_ref, ...), custom_call_target="tpu_custom_call" | custom-call | flops 17999998976 | bytes 40000000 | tf_op jit(solution)/shard_map/expert_rows/pallas_call | solution.py:333
  190.9 2.5 collective-permute-start.24
  193.6 11.6 %expert_output.1 = (bf16[160,768]{1,0:T(8,128)(2,1)}, bf16[160,768]{1,0:T(8,128)(2,1)}, bf16[160,768]{1,0:T(8,128)(2,1)}, bf16[160,768]{1,0:T(8,128)(2,1)}, bf16...) custom-call(bf16[1280,3072]{1,0:T(8,128)(2,1)} %get-tuple-element.92.act_r, ...), custom_call_target="tpu_custom_call" | custom-call | flops 6039797760 | bytes 16000000 | tf_op jit(solution)/shard_map/expert_output/pallas_call | solution.py:431
  205.2 11.8 %expert_weight_gradient.3 = (bf16[768,768]{1,0:T(8,128)(2,1)}, bf16[768,768]{1,0:T(8,128)(2,1)}, bf16[768,768]{1,0:T(8,128)(2,1)}, bf16[768,768]{1,0:T(8,128)(2,1)}) custom-call(s32[1]{0:T(128)} %bitcast.12.me_ref, bf16[1280,3072]{1,0:T(8,128)(2,1)} %get-tuple-element.92.act_ref.wide_ref, bf16[1280,768]{1,0:T(8,128)(2,1)} %get-tuple-element.131.rows_ref), custom_call_target="tpu_custom_call" | custom-call | flops 6039797760 | bytes 20000000 | tf_op jit(solution)/shard_map/expert_weight_gradient/pallas_call | solution.py:389
  217.0 3.7 collective-permute-start.26
  220.8 11.6 %expert_weight_gradient.2 = (bf16[768,768]{1,0:T(8,128)(2,1)}, bf16[768,768]{1,0:T(8,128)(2,1)}, bf16[768,768]{1,0:T(8,128)(2,1)}, bf16[768,768]{1,0:T(8,128)(2,1)}) custom-call(s32[1]{0:T(128)} %bitcast.12.me_ref, bf16[1280,3072]{1,0:T(8,128)(2,1)} %get-tuple-element.125.wide_ref, bf16[1280,768]{1,0:T(8,128)(2,1)} %get-tuple-element.126.rows_ref), custom_call_target="tpu_custom_call" | custom-call | flops 6039797760 | bytes 20000000 | tf_op jit(solution)/shard_map/expert_weight_gradient/pallas_call | solution.py:389
  234.4 4.6 collective-permute-start.17
  239.7 11.8 %expert_norm_backward.1 = (f32[1024,768]{1,0:T(8,128)}, bf16[1024,768]{1,0:T(8,128)(2,1)}, bf16[768,768]{1,0:T(8,128)(2,1)}, f32[1,768]{1,0:T(1,128)}) custom-call(s32[1]{0:T(128)S(6)} %copy.65.length_ref, s32[1024,1]{1,0:T(8,128)} %copy.43.slot_ref, s32[1,1280]{1,0:T(1,128)} %add.370.wanted_ref, f32[1024,768]{1,0:T(8,128)} %get-tuple-element.75.resid_ref, ...), custom_call_target="tpu_custom_call" | custom-call | flops 5000000000 | bytes 20000000 | tf_op jit(solution)/shard_map/expert_norm_backward/pallas_call | solution.py:498
  252.7 28.4 %attention_backward.1 = (bf16[3,1024,768]{2,1,0:T(8,128)(2,1)}, f32[6,2,512]{2,1,0:T(2,128)}, f32[6,4,128]{2,1,0:T(4,128)}) custom-call(bf16[3,6,1024,128]{3,2,1,0:T(8,128)(2,1)} %get-tuple-element.102.qkv_ref, bf16[12,1024,1024]{2,1,0:T(8,128)(2,1)} %get-tuple-element.103.probs_ref, bf16[1024,768]{1,0:T(8,128)(2,1)} %get-tuple-element.104.mixed_ref, ...), custom_call_target="tpu_custom_call" | custom-call | flops 60000002048 | bytes 60000000 | tf_op jit(solution)/shard_map/attention_backward/pallas_call | solution.py:584
  284.1 7.8 %projection_gradient.1 = bf16[3,768,768]{2,1,0:T(8,128)(2,1)} custom-call(bf16[1024,768]{1,0:T(8,128)(2,1)} %get-tuple-element.123.normed_ref, bf16[3,1024,768]{2,1,0:T(8,128)(2,1)} %get-tuple-element.115.back_ref), custom_call_target="tpu_custom_call" | custom-call | flops 3623878656 | bytes 10000000 | tf_op jit(solution)/shard_map/projection_gradient/pallas_call | solution.py:617
  292.0 11.2 %token_gradient.1 = (f32[1024,768]{1,0:T(8,128)}, f32[1,768]{1,0:T(1,128)}) custom-call(bf16[3,1024,768]{2,1,0:T(8,128)(2,1)} %get-tuple-element.115.back_ref, bf16[768,768]{1,0:T(8,128)(2,1)} %query_weight_ref.3, bf16[768,768]{1,0:T(8,128)(2,1)} %key_weight_ref.3, bf16[768,768]{1,0:T(8,128)(2,1)} %value_weight_ref.3, bf16[1024,768]{1,0:T(8,128)(2,1)} %bitcast.31, ...), custom_call_target="tpu_custom_call" | custom-call | flops 3623878656 | bytes 16000000 | tf_op jit(solution)/shard_map/token_gradient/pallas_call | solution.py:651
  306.2 5.1 collective-permute-start.18
  312.6 2.3 collective-permute-start.20
  317.7 15.6 %collective-permute-done.18.refs_5_ = bf16[160,768]{1,0:T(8,128)(2,1)} collective-permute-done((bf16[160,768]{1,0:T(8,128)(2,1)}, bf16[160,768]{1,0:T(8,128)(2,1)}, u32[]{:S(2)}, u32[]{:S(2)}) %collective-permute-start.18) | collective-permute-done | bytes 245792 | tf_op jit(solution)/shard_map/ppermute | solution.py:661
  334.3 6.1 %result.1 = bf16[1024,768]{1,0:T(8,128)(2,1)} custom-call(s32[1]{0:T(128)S(6)} %copy.65.length_ref, s32[1024,1]{1,0:T(8,128)} %copy.43.slot_ref, s32[1,1280]{1,0:T(1,128)} %add.370.wanted_ref, f32[1024,768]{1,0:T(8,128)} %get-tuple-element.75.resid_ref, bf16[160,768]{1,0:T(8,128)(2,1)} %get-tuple-element.94.refs_0_, ...), custom_call_target="tpu_custom_call" | custom-call | flops 2000000000 | bytes 10000000 | tf_op jit(solution)/shard_map/result/pallas_call | solution.py:456
  346.4 2.2 collective-permute-done.50
  350.1 2.3 collective-permute-done.51
  354.4 10.1 %collective-permute-start.53 = (bf16[24,768]{1,0:T(8,128)(2,1)S(1)}, bf16[24,768]{1,0:T(8,128)(2,1)S(1)}, u32[]{:S(2)}, u32[]{:S(2)}) collective-permute-start(bf16[24,768]{1,0:T(8,128)(2,1)S(1)} %get-tuple-element.158), channel_id=1, source_target_pairs={{0,2},{1,3},{2,0},{3,1},{4,6},{5,7},{6,4},{7,5},{8,10},{9,11},{10,... | collective-permute-start | bytes 110600 | tf_op jit(solution)/shard_map/ppermute | solution.py:661
  364.5 2.1 collective-permute-start.54
  366.6 2.5 collective-permute-start.55
  372.9 2.1 collective-permute-start.34
  380.7 3.5 collective-permute-start.58
  390.0 1.9 collective-permute-start.64
  393.5 20.0 %collective-permute-done.36 = bf16[288,768]{1,0:T(8,128)(2,1)S(1)} collective-permute-done((bf16[288,768]{1,0:T(8,128)(2,1)S(1)}, bf16[288,768]{1,0:T(8,128)(2,1)S(1)}, u32[]{:S(2)}, u32[]{:S(2)}) %collective-permute-start.36) | collective-permute-done | bytes 442400 | tf_op jit(solution)/shard_map/ppermute | solution.py:661
  414.9 6.2 %collective-permute-done.38 = bf16[288,768]{1,0:T(8,128)(2,1)S(1)} collective-permute-done((bf16[288,768]{1,0:T(8,128)(2,1)S(1)}, bf16[288,768]{1,0:T(8,128)(2,1)S(1)}, u32[]{:S(2)}, u32[]{:S(2)}) %collective-permute-start.38) | collective-permute-done | bytes 442400 | tf_op jit(solution)/shard_map/ppermute | solution.py:661
  423.4 2.5 collective-permute-start.41
  425.9 2.4 collective-permute-done.39
  431.6 4.0 collective-permute-done.60
  435.8 2.8 collective-permute-start.44
  438.6 5.1 collective-permute-done.43
  448.0 7.2 %collective-permute-done.45 = bf16[288,768]{1,0:T(8,128)(2,1)S(1)} collective-permute-done((bf16[288,768]{1,0:T(8,128)(2,1)S(1)}, bf16[288,768]{1,0:T(8,128)(2,1)S(1)}, u32[]{:S(2)}, u32[]{:S(2)}) %collective-permute-start.45) | collective-permute-done | bytes 442400 | tf_op jit(solution)/shard_map/ppermute | solution.py:661
  455.3 11.9 %collective-permute-done.46 = bf16[288,768]{1,0:T(8,128)(2,1)S(1)} collective-permute-done((bf16[288,768]{1,0:T(8,128)(2,1)S(1)}, bf16[288,768]{1,0:T(8,128)(2,1)S(1)}, u32[]{:S(2)}, u32[]{:S(2)}) %collective-permute-start.46) | collective-permute-done | bytes 442400 | tf_op jit(solution)/shard_map/ppermute | solution.py:661
  473.2 19.3 %collective-permute-done.68 = bf16[768,768]{1,0:T(8,128)(2,1)S(1)} collective-permute-done((bf16[768,768]{1,0:T(8,128)(2,1)S(1)}, bf16[768,768]{1,0:T(8,128)(2,1)S(1)}, u32[]{:S(2)}, u32[]{:S(2)}) %collective-permute-start.68) | collective-permute-done | bytes 1179680 | tf_op jit(solution)/shard_map/ppermute | solution.py:661
  494.3 23.0 %collective-permute-done.63 = bf16[768,768]{1,0:T(8,128)(2,1)S(1)} collective-permute-done((bf16[768,768]{1,0:T(8,128)(2,1)S(1)}, bf16[768,768]{1,0:T(8,128)(2,1)S(1)}, u32[]{:S(2)}, u32[]{:S(2)}) %collective-permute-start.63) | collective-permute-done | bytes 1179680 | tf_op jit(solution)/shard_map/ppermute | solution.py:661
  517.3 1.9 add_bitcast_fusion.1
  519.9 3.1 fusion.15
  (254 shorter events, 78.2 us)
Async XLA Ops:
  56.1 19.7 %collective-permute-start.1 = (bf16[160,768]{1,0:T(8,128)(2,1)}, bf16[160,768]{1,0:T(8,128)(2,1)S(1)}, u32[]{:S(2)}, u32[]{:S(2)}) collective-permute-start(bf16[160,768]{1,0:T(8,128)(2,1)} %get-tuple-element.78), channel_id=1, source_target_pairs={{0,2},{1,3},{2,0},{3,1},{4,6},{5,7},{6,4},{7,5},{8,10},{9,11},{10,... | collective-permute-start | bytes 737288 | tf_op jit(solution)/shard_map/ppermute | solution.py:661
  58.8 21.8 %collective-permute-start.2 = (bf16[160,768]{1,0:T(8,128)(2,1)}, bf16[160,768]{1,0:T(8,128)(2,1)S(1)}, u32[]{:S(2)}, u32[]{:S(2)}) collective-permute-start(bf16[160,768]{1,0:T(8,128)(2,1)} %get-tuple-element.79), channel_id=1, source_target_pairs={{0,3},{1,2},{2,1},{3,0},{4,7},{5,6},{6,5},{7,4},{8,11},{9,10},{10,... | collective-permute-start | bytes 737288 | tf_op jit(solution)/shard_map/ppermute | solution.py:661
  58.8 21.8 %collective-permute-start.3 = (bf16[160,768]{1,0:T(8,128)(2,1)}, bf16[160,768]{1,0:T(8,128)(2,1)S(1)}, u32[]{:S(2)}, u32[]{:S(2)}) collective-permute-start(bf16[160,768]{1,0:T(8,128)(2,1)} %get-tuple-element.80), channel_id=1, source_target_pairs={{0,4},{1,5},{2,6},{3,7},{4,0},{5,1},{6,2},{7,3},{8,12},{9,13},{10,... | collective-permute-start | bytes 737288 | tf_op jit(solution)/shard_map/ppermute | solution.py:661
  61.6 21.5 %collective-permute-start.4 = (bf16[160,768]{1,0:T(8,128)(2,1)}, bf16[160,768]{1,0:T(8,128)(2,1)S(1)}, u32[]{:S(2)}, u32[]{:S(2)}) collective-permute-start(bf16[160,768]{1,0:T(8,128)(2,1)} %get-tuple-element.81), channel_id=1, source_target_pairs={{0,5},{1,4},{2,7},{3,6},{4,1},{5,0},{6,3},{7,2},{8,13},{9,12},{10,... | collective-permute-start | bytes 737288 | tf_op jit(solution)/shard_map/ppermute | solution.py:661
  61.6 46.6 %collective-permute-start.5 = (bf16[160,768]{1,0:T(8,128)(2,1)}, bf16[160,768]{1,0:T(8,128)(2,1)S(1)}, u32[]{:S(2)}, u32[]{:S(2)}) collective-permute-start(bf16[160,768]{1,0:T(8,128)(2,1)} %get-tuple-element.82), channel_id=1, source_target_pairs={{0,6},{1,7},{2,4},{3,5},{4,2},{5,3},{6,0},{7,1},{8,14},{9,15},{10,... | collective-permute-start | bytes 737288 | tf_op jit(solution)/shard_map/ppermute | solution.py:661
  75.9 33.1 %collective-permute-start.6 = (bf16[160,768]{1,0:T(8,128)(2,1)}, bf16[160,768]{1,0:T(8,128)(2,1)S(1)}, u32[]{:S(2)}, u32[]{:S(2)}) collective-permute-start(bf16[160,768]{1,0:T(8,128)(2,1)} %get-tuple-element.83), channel_id=1, source_target_pairs={{0,7},{1,6},{2,5},{3,4},{4,3},{5,2},{6,1},{7,0},{8,15},{9,14},{10,... | collective-permute-start | bytes 737288 | tf_op jit(solution)/shard_map/ppermute | solution.py:661
  80.6 51.3 %collective-permute-start.10 = (bf16[160,768]{1,0:T(8,128)(2,1)S(1)}, bf16[160,768]{1,0:T(8,128)(2,1)S(1)}, u32[]{:S(2)}, u32[]{:S(2)}) collective-permute-start(bf16[160,768]{1,0:T(8,128)(2,1)S(1)} %copy-done.33), channel_id=1, source_target_pairs={{0,4},{1,5},{2,6},{3,7},{4,0},{5,1},{6,2},{7,3},{8,12},{9,13},{10,... | collective-permute-start | bytes 737288 | tf_op jit(solution)/shard_map/ppermute | solution.py:661
  80.6 55.7 %collective-permute-start.11 = (bf16[160,768]{1,0:T(8,128)(2,1)S(1)}, bf16[160,768]{1,0:T(8,128)(2,1)S(1)}, u32[]{:S(2)}, u32[]{:S(2)}) collective-permute-start(bf16[160,768]{1,0:T(8,128)(2,1)S(1)} %copy-done.31), channel_id=1, source_target_pairs={{0,5},{1,4},{2,7},{3,6},{4,1},{5,0},{6,3},{7,2},{8,13},{9,12},{10,... | collective-permute-start | bytes 737288 | tf_op jit(solution)/shard_map/ppermute | solution.py:661
  83.0 57.5 %collective-permute-start.12 = (bf16[160,768]{1,0:T(8,128)(2,1)S(1)}, bf16[160,768]{1,0:T(8,128)(2,1)}, u32[]{:S(2)}, u32[]{:S(2)}) collective-permute-start(bf16[160,768]{1,0:T(8,128)(2,1)S(1)} %copy-done.24), channel_id=1, source_target_pairs={{0,6},{1,7},{2,4},{3,5},{4,2},{5,3},{6,0},{7,1},{8,14},{9,15},{10,... | collective-permute-start | bytes 737288 | tf_op jit(solution)/shard_map/ppermute | solution.py:661
  108.2 32.3 %collective-permute-start.13 = (bf16[160,768]{1,0:T(8,128)(2,1)S(1)}, bf16[160,768]{1,0:T(8,128)(2,1)}, u32[]{:S(2)}, u32[]{:S(2)}) collective-permute-start(bf16[160,768]{1,0:T(8,128)(2,1)S(1)} %copy-done.22), channel_id=1, source_target_pairs={{0,7},{1,6},{2,5},{3,4},{4,3},{5,2},{6,1},{7,0},{8,15},{9,14},{10,... | collective-permute-start | bytes 737288 | tf_op jit(solution)/shard_map/ppermute | solution.py:661
  108.9 31.7 %collective-permute-start.7 = (bf16[160,768]{1,0:T(8,128)(2,1)S(1)}, bf16[160,768]{1,0:T(8,128)(2,1)}, u32[]{:S(2)}, u32[]{:S(2)}) collective-permute-start(bf16[160,768]{1,0:T(8,128)(2,1)S(1)} %copy-done.20), channel_id=1, source_target_pairs={{0,1},{1,0},{2,3},{3,2},{4,5},{5,4},{6,7},{7,6},{8,9},{9,8},{10,11... | collective-permute-start | bytes 737288 | tf_op jit(solution)/shard_map/ppermute | solution.py:661
  132.0 10.3 %collective-permute-start.8 = (bf16[160,768]{1,0:T(8,128)(2,1)S(1)}, bf16[160,768]{1,0:T(8,128)(2,1)}, u32[]{:S(2)}, u32[]{:S(2)}) collective-permute-start(bf16[160,768]{1,0:T(8,128)(2,1)S(1)} %copy-done.18), channel_id=1, source_target_pairs={{0,2},{1,3},{2,0},{3,1},{4,6},{5,7},{6,4},{7,5},{8,10},{9,11},{10,... | collective-permute-start | bytes 737288 | tf_op jit(solution)/shard_map/ppermute | solution.py:661
  136.4 10.9 %collective-permute-start.9 = (bf16[160,768]{1,0:T(8,128)(2,1)S(1)}, bf16[160,768]{1,0:T(8,128)(2,1)}, u32[]{:S(2)}, u32[]{:S(2)}) collective-permute-start(bf16[160,768]{1,0:T(8,128)(2,1)S(1)} %copy-done.16), channel_id=1, source_target_pairs={{0,3},{1,2},{2,1},{3,0},{4,7},{5,6},{6,5},{7,4},{8,11},{9,10},{10,... | collective-permute-start | bytes 737288 | tf_op jit(solution)/shard_map/ppermute | solution.py:661
  189.0 28.0 %collective-permute-start.21 = (bf16[160,768]{1,0:T(8,128)(2,1)}, bf16[160,768]{1,0:T(8,128)(2,1)S(1)}, u32[]{:S(2)}, u32[]{:S(2)}) collective-permute-start(bf16[160,768]{1,0:T(8,128)(2,1)} %get-tuple-element.106), channel_id=1, source_target_pairs={{0,1},{1,0},{2,3},{3,2},{4,5},{5,4},{6,7},{7,6},{8,9},{9,8},{10,11... | collective-permute-start | bytes 737288 | tf_op jit(solution)/shard_map/ppermute | solution.py:661
  189.2 31.6 %collective-permute-start.22 = (bf16[160,768]{1,0:T(8,128)(2,1)}, bf16[160,768]{1,0:T(8,128)(2,1)S(1)}, u32[]{:S(2)}, u32[]{:S(2)}) collective-permute-start(bf16[160,768]{1,0:T(8,128)(2,1)} %get-tuple-element.107), channel_id=1, source_target_pairs={{0,2},{1,3},{2,0},{3,1},{4,6},{5,7},{6,4},{7,5},{8,10},{9,11},{10,... | collective-permute-start | bytes 737288 | tf_op jit(solution)/shard_map/ppermute | solution.py:661
  190.0 42.4 %collective-permute-start.23 = (bf16[160,768]{1,0:T(8,128)(2,1)}, bf16[160,768]{1,0:T(8,128)(2,1)S(1)}, u32[]{:S(2)}, u32[]{:S(2)}) collective-permute-start(bf16[160,768]{1,0:T(8,128)(2,1)} %get-tuple-element.108), channel_id=1, source_target_pairs={{0,3},{1,2},{2,1},{3,0},{4,7},{5,6},{6,5},{7,4},{8,11},{9,10},{10,... | collective-permute-start | bytes 737288 | tf_op jit(solution)/shard_map/ppermute | solution.py:661
  190.9 41.9 %collective-permute-start.24 = (bf16[160,768]{1,0:T(8,128)(2,1)}, bf16[160,768]{1,0:T(8,128)(2,1)S(1)}, u32[]{:S(2)}, u32[]{:S(2)}) collective-permute-start(bf16[160,768]{1,0:T(8,128)(2,1)} %get-tuple-element.109), channel_id=1, source_target_pairs={{0,4},{1,5},{2,6},{3,7},{4,0},{5,1},{6,2},{7,3},{8,12},{9,13},{10,... | collective-permute-start | bytes 737288 | tf_op jit(solution)/shard_map/ppermute | solution.py:661
  193.4 39.4 %collective-permute-start.25 = (bf16[160,768]{1,0:T(8,128)(2,1)}, bf16[160,768]{1,0:T(8,128)(2,1)S(1)}, u32[]{:S(2)}, u32[]{:S(2)}) collective-permute-start(bf16[160,768]{1,0:T(8,128)(2,1)} %get-tuple-element.110), channel_id=1, source_target_pairs={{0,5},{1,4},{2,7},{3,6},{4,1},{5,0},{6,3},{7,2},{8,13},{9,12},{10,... | collective-permute-start | bytes 737288 | tf_op jit(solution)/shard_map/ppermute | solution.py:661
  217.0 17.4 %collective-permute-start.26 = (bf16[160,768]{1,0:T(8,128)(2,1)S(1)}, bf16[160,768]{1,0:T(8,128)(2,1)S(1)}, u32[]{:S(2)}, u32[]{:S(2)}) collective-permute-start(bf16[160,768]{1,0:T(8,128)(2,1)S(1)} %copy-done.32), channel_id=1, source_target_pairs={{0,6},{1,7},{2,4},{3,5},{4,2},{5,3},{6,0},{7,1},{8,14},{9,15},{10,... | collective-permute-start | bytes 737288 | tf_op jit(solution)/shard_map/ppermute | solution.py:661
  220.7 18.3 %collective-permute-start.27 = (bf16[160,768]{1,0:T(8,128)(2,1)S(1)}, bf16[160,768]{1,0:T(8,128)(2,1)S(1)}, u32[]{:S(2)}, u32[]{:S(2)}) collective-permute-start(bf16[160,768]{1,0:T(8,128)(2,1)S(1)} %copy-done.30), channel_id=1, source_target_pairs={{0,7},{1,6},{2,5},{3,4},{4,3},{5,2},{6,1},{7,0},{8,15},{9,14},{10,... | collective-permute-start | bytes 737288 | tf_op jit(solution)/shard_map/ppermute | solution.py:661
  232.5 73.7 %collective-permute-start.14 = (bf16[160,768]{1,0:T(8,128)(2,1)}, bf16[160,768]{1,0:T(8,128)(2,1)}, u32[]{:S(2)}, u32[]{:S(2)}) collective-permute-start(bf16[160,768]{1,0:T(8,128)(2,1)} %get-tuple-element.95), channel_id=1, source_target_pairs={{0,1},{1,0},{2,3},{3,2},{4,5},{5,4},{6,7},{7,6},{8,9},{9,8},{10,11... | collective-permute-start | bytes 737288 | tf_op jit(solution)/shard_map/ppermute | solution.py:661
  232.8 78.5 %collective-permute-start.15 = (bf16[160,768]{1,0:T(8,128)(2,1)}, bf16[160,768]{1,0:T(8,128)(2,1)}, u32[]{:S(2)}, u32[]{:S(2)}) collective-permute-start(bf16[160,768]{1,0:T(8,128)(2,1)} %get-tuple-element.96), channel_id=1, source_target_pairs={{0,2},{1,3},{2,0},{3,1},{4,6},{5,7},{6,4},{7,5},{8,10},{9,11},{10,... | collective-permute-start | bytes 737288 | tf_op jit(solution)/shard_map/ppermute | solution.py:661
  232.8 79.8 %collective-permute-start.16 = (bf16[160,768]{1,0:T(8,128)(2,1)}, bf16[160,768]{1,0:T(8,128)(2,1)}, u32[]{:S(2)}, u32[]{:S(2)}) collective-permute-start(bf16[160,768]{1,0:T(8,128)(2,1)} %get-tuple-element.97), channel_id=1, source_target_pairs={{0,3},{1,2},{2,1},{3,0},{4,7},{5,6},{6,5},{7,4},{8,11},{9,10},{10,... | collective-permute-start | bytes 737288 | tf_op jit(solution)/shard_map/ppermute | solution.py:661
  234.4 81.8 %collective-permute-start.17 = (bf16[160,768]{1,0:T(8,128)(2,1)}, bf16[160,768]{1,0:T(8,128)(2,1)}, u32[]{:S(2)}, u32[]{:S(2)}) collective-permute-start(bf16[160,768]{1,0:T(8,128)(2,1)} %get-tuple-element.98), channel_id=1, source_target_pairs={{0,4},{1,5},{2,6},{3,7},{4,0},{5,1},{6,2},{7,3},{8,12},{9,13},{10,... | collective-permute-start | bytes 737288 | tf_op jit(solution)/shard_map/ppermute | solution.py:661
  252.6 87.8 %collective-permute-start.49 = (bf16[384,768]{1,0:T(8,128)(2,1)S(1)}, bf16[384,768]{1,0:T(8,128)(2,1)}, u32[]{:S(2)}, u32[]{:S(2)}) collective-permute-start(bf16[384,768]{1,0:T(8,128)(2,1)S(1)} %constant_dynamic-slice_fusion.6), channel_id=1, source_target_pairs={{0,1},{1,0},{2,3},{3,2},{4,5},{5,4},{6,7},{7,6},{8,9},{9,8},{10,11... | collective-permute-start | bytes 1769480 | tf_op jit(solution)/shard_map/ppermute | solution.py:661
  306.2 27.1 %collective-permute-start.18 = (bf16[160,768]{1,0:T(8,128)(2,1)}, bf16[160,768]{1,0:T(8,128)(2,1)}, u32[]{:S(2)}, u32[]{:S(2)}) collective-permute-start(bf16[160,768]{1,0:T(8,128)(2,1)} %get-tuple-element.99), channel_id=1, source_target_pairs={{0,5},{1,4},{2,7},{3,6},{4,1},{5,0},{6,3},{7,2},{8,13},{9,12},{10,... | collective-permute-start | bytes 737288 | tf_op jit(solution)/shard_map/ppermute | solution.py:661
  311.3 23.0 %collective-permute-start.19 = (bf16[160,768]{1,0:T(8,128)(2,1)}, bf16[160,768]{1,0:T(8,128)(2,1)}, u32[]{:S(2)}, u32[]{:S(2)}) collective-permute-start(bf16[160,768]{1,0:T(8,128)(2,1)} %get-tuple-element.100), channel_id=1, source_target_pairs={{0,6},{1,7},{2,4},{3,5},{4,2},{5,3},{6,0},{7,1},{8,14},{9,15},{10,... | collective-permute-start | bytes 737288 | tf_op jit(solution)/shard_map/ppermute | solution.py:661
  312.6 21.7 %collective-permute-start.20 = (bf16[160,768]{1,0:T(8,128)(2,1)}, bf16[160,768]{1,0:T(8,128)(2,1)}, u32[]{:S(2)}, u32[]{:S(2)}) collective-permute-start(bf16[160,768]{1,0:T(8,128)(2,1)} %get-tuple-element.101), channel_id=1, source_target_pairs={{0,7},{1,6},{2,5},{3,4},{4,3},{5,2},{6,1},{7,0},{8,15},{9,14},{10,... | collective-permute-start | bytes 737288 | tf_op jit(solution)/shard_map/ppermute | solution.py:661
  316.2 73.8 %collective-permute-start.67 = (bf16[768,768]{1,0:T(8,128)(2,1)}, bf16[768,768]{1,0:T(8,128)(2,1)}, u32[]{:S(2)}, u32[]{:S(2)}) collective-permute-start(bf16[768,768]{1,0:T(8,128)(2,1)} %get-tuple-element.135), channel_id=1, source_target_pairs={{0,8},{8,0},{16,24},{24,16},{1,9},{9,1},{17,25},{25,17},{2,10},{10... | collective-permute-start | bytes 3538952 | tf_op jit(solution)/shard_map/ppermute | solution.py:661
  333.3 51.0 %collective-permute-start.35 = (bf16[1152,768]{1,0:T(8,128)(2,1)}, bf16[1152,768]{1,0:T(8,128)(2,1)}, u32[]{:S(2)}, u32[]{:S(2)}) collective-permute-start(bf16[1152,768]{1,0:T(8,128)(2,1)} %constant_dynamic-slice_fusion.13), channel_id=1, source_target_pairs={{0,1},{1,0},{2,3},{3,2},{4,5},{5,4},{6,7},{7,6},{8,9},{9,8},{10,11... | collective-permute-start | bytes 5308424 | tf_op jit(solution)/shard_map/ppermute | solution.py:661
  334.3 10.7 %collective-permute-start.28 = (f32[22,768]{1,0:T(8,128)}, f32[22,768]{1,0:T(8,128)}, u32[]{:S(2)}, u32[]{:S(2)}) collective-permute-start(f32[22,768]{1,0:T(8,128)} %select_maximum_fusion), channel_id=1, source_target_pairs={{0,1},{1,0},{2,3},{3,2},{4,5},{5,4},{6,7},{7,6},{8,9},{9,8},{10,11... | collective-permute-start | bytes 202760 | tf_op jit(solution)/shard_map/ppermute | solution.py:661
  352.4 12.1 %collective-permute-start.30 = (f32[22,768]{1,0:T(8,128)S(1)}, f32[22,768]{1,0:T(8,128)S(1)}, u32[]{:S(2)}, u32[]{:S(2)}) collective-permute-start(f32[22,768]{1,0:T(8,128)S(1)} %fusion.14), channel_id=1, source_target_pairs={{0,16},{8,24},{16,0},{24,8},{1,17},{9,25},{17,1},{25,9},{2,18},{10... | collective-permute-start | bytes 202760 | tf_op jit(solution)/shard_map/ppermute | solution.py:661
  354.2 12.5 %collective-permute-start.31 = (f32[22,768]{1,0:T(8,128)S(1)}, f32[22,768]{1,0:T(8,128)S(1)}, u32[]{:S(2)}, u32[]{:S(2)}) collective-permute-start(f32[22,768]{1,0:T(8,128)S(1)} %fusion.14), channel_id=1, source_target_pairs={{0,24},{8,16},{16,8},{24,0},{1,25},{9,17},{17,9},{25,1},{2,26},{10... | collective-permute-start | bytes 202760 | tf_op jit(solution)/shard_map/ppermute | solution.py:661
  354.4 14.7 %collective-permute-start.53 = (bf16[24,768]{1,0:T(8,128)(2,1)S(1)}, bf16[24,768]{1,0:T(8,128)(2,1)S(1)}, u32[]{:S(2)}, u32[]{:S(2)}) collective-permute-start(bf16[24,768]{1,0:T(8,128)(2,1)S(1)} %get-tuple-element.158), channel_id=1, source_target_pairs={{0,2},{1,3},{2,0},{3,1},{4,6},{5,7},{6,4},{7,5},{8,10},{9,11},{10,... | collective-permute-start | bytes 110600 | tf_op jit(solution)/shard_map/ppermute | solution.py:661
  375.0 98.2 %collective-permute-start.66 = (bf16[768,768]{1,0:T(8,128)(2,1)S(1)}, bf16[768,768]{1,0:T(8,128)(2,1)S(1)}, u32[]{:S(2)}, u32[]{:S(2)}) collective-permute-start(bf16[768,768]{1,0:T(8,128)(2,1)S(1)} %copy-done.13), channel_id=1, source_target_pairs={{0,8},{8,0},{16,24},{24,16},{1,9},{9,1},{17,25},{25,17},{2,10},{10... | collective-permute-start | bytes 3538952 | tf_op jit(solution)/shard_map/ppermute | solution.py:661
  386.4 27.1 %collective-permute-start.36 = (bf16[288,768]{1,0:T(8,128)(2,1)S(1)}, bf16[288,768]{1,0:T(8,128)(2,1)S(1)}, u32[]{:S(2)}, u32[]{:S(2)}) collective-permute-start(bf16[288,768]{1,0:T(8,128)(2,1)S(1)} %get-tuple-element.149), channel_id=1, source_target_pairs={{0,8},{8,0},{16,24},{24,16},{1,9},{9,1},{17,25},{25,17},{2,10},{10... | collective-permute-start | bytes 1327112 | tf_op jit(solution)/shard_map/ppermute | solution.py:661
  386.9 28.0 %collective-permute-start.37 = (bf16[288,768]{1,0:T(8,128)(2,1)S(1)}, bf16[288,768]{1,0:T(8,128)(2,1)S(1)}, u32[]{:S(2)}, u32[]{:S(2)}) collective-permute-start(bf16[288,768]{1,0:T(8,128)(2,1)S(1)} %get-tuple-element.151), channel_id=1, source_target_pairs={{0,16},{8,24},{16,0},{24,8},{1,17},{9,25},{17,1},{25,9},{2,18},{10... | collective-permute-start | bytes 1327112 | tf_op jit(solution)/shard_map/ppermute | solution.py:661
  388.4 32.7 %collective-permute-start.38 = (bf16[288,768]{1,0:T(8,128)(2,1)S(1)}, bf16[288,768]{1,0:T(8,128)(2,1)S(1)}, u32[]{:S(2)}, u32[]{:S(2)}) collective-permute-start(bf16[288,768]{1,0:T(8,128)(2,1)S(1)} %get-tuple-element.150), channel_id=1, source_target_pairs={{0,24},{8,16},{16,8},{24,0},{1,25},{9,17},{17,9},{25,1},{2,26},{10... | collective-permute-start | bytes 1327112 | tf_op jit(solution)/shard_map/ppermute | solution.py:661
  390.0 55.9 %collective-permute-start.64 = (bf16[768,768]{1,0:T(8,128)(2,1)S(1)}, bf16[768,768]{1,0:T(8,128)(2,1)S(1)}, u32[]{:S(2)}, u32[]{:S(2)}) collective-permute-start(bf16[768,768]{1,0:T(8,128)(2,1)S(1)} %copy-done.15), channel_id=1, source_target_pairs={{0,16},{8,24},{16,0},{24,8},{1,17},{9,25},{17,1},{25,9},{2,18},{10... | collective-permute-start | bytes 3538952 | tf_op jit(solution)/shard_map/ppermute | solution.py:661
  428.4 16.2 %collective-permute-start.61 = (bf16[96,768]{1,0:T(8,128)(2,1)S(1)}, bf16[96,768]{1,0:T(8,128)(2,1)S(1)}, u32[]{:S(2)}, u32[]{:S(2)}) collective-permute-start(bf16[96,768]{1,0:T(8,128)(2,1)S(1)} %constant_dynamic-update-slice_fusion.6), channel_id=1, source_target_pairs={{0,24},{8,16},{16,8},{24,0},{1,25},{9,17},{17,9},{25,1},{2,26},{10... | collective-permute-start | bytes 442376 | tf_op jit(solution)/shard_map/ppermute | solution.py:661
  443.7 11.4 %collective-permute-start.45 = (bf16[288,768]{1,0:T(8,128)(2,1)S(1)}, bf16[288,768]{1,0:T(8,128)(2,1)S(1)}, u32[]{:S(2)}, u32[]{:S(2)}) collective-permute-start(bf16[288,768]{1,0:T(8,128)(2,1)S(1)} %constant_dynamic-update-slice_fusion.16), channel_id=1, source_target_pairs={{0,8},{8,0},{16,24},{24,16},{1,9},{9,1},{17,25},{25,17},{2,10},{10... | collective-permute-start | bytes 1327112 | tf_op jit(solution)/shard_map/ppermute | solution.py:661
  444.6 24.9 %collective-permute-start.62 = (bf16[384,768]{1,0:T(8,128)(2,1)S(1)}, bf16[384,768]{1,0:T(8,128)(2,1)S(1)}, u32[]{:S(2)}, u32[]{:S(2)}) collective-permute-start(bf16[384,768]{1,0:T(8,128)(2,1)S(1)} %constant_dynamic-update-slice_fusion.2), channel_id=1, source_target_pairs={{0,1},{1,0},{2,3},{3,2},{4,5},{5,4},{6,7},{7,6},{8,9},{9,8},{10,11... | collective-permute-start | bytes 1769480 | tf_op jit(solution)/shard_map/ppermute | solution.py:661
  444.7 22.5 %collective-permute-start.46 = (bf16[288,768]{1,0:T(8,128)(2,1)S(1)}, bf16[288,768]{1,0:T(8,128)(2,1)S(1)}, u32[]{:S(2)}, u32[]{:S(2)}) collective-permute-start(bf16[288,768]{1,0:T(8,128)(2,1)S(1)} %constant_dynamic-update-slice_fusion.16), channel_id=1, source_target_pairs={{0,16},{8,24},{16,0},{24,8},{1,17},{9,25},{17,1},{25,9},{2,18},{10... | collective-permute-start | bytes 1327112 | tf_op jit(solution)/shard_map/ppermute | solution.py:661
  445.9 22.7 %collective-permute-start.47 = (bf16[288,768]{1,0:T(8,128)(2,1)S(1)}, bf16[288,768]{1,0:T(8,128)(2,1)S(1)}, u32[]{:S(2)}, u32[]{:S(2)}) collective-permute-start(bf16[288,768]{1,0:T(8,128)(2,1)S(1)} %constant_dynamic-update-slice_fusion.16), channel_id=1, source_target_pairs={{0,24},{8,16},{16,8},{24,0},{1,25},{9,17},{17,9},{25,1},{2,26},{10... | collective-permute-start | bytes 1327112 | tf_op jit(solution)/shard_map/ppermute | solution.py:661
  455.2 37.3 %collective-permute-start.68 = (bf16[768,768]{1,0:T(8,128)(2,1)S(1)}, bf16[768,768]{1,0:T(8,128)(2,1)S(1)}, u32[]{:S(2)}, u32[]{:S(2)}) collective-permute-start(bf16[768,768]{1,0:T(8,128)(2,1)S(1)} %add_convert_fusion.1), channel_id=1, source_target_pairs={{0,16},{8,24},{16,0},{24,8},{1,17},{9,25},{17,1},{25,9},{2,18},{10... | collective-permute-start | bytes 3538952 | tf_op jit(solution)/shard_map/ppermute | solution.py:661
  467.2 50.1 %collective-permute-start.63 = (bf16[768,768]{1,0:T(8,128)(2,1)S(1)}, bf16[768,768]{1,0:T(8,128)(2,1)S(1)}, u32[]{:S(2)}, u32[]{:S(2)}) collective-permute-start(bf16[768,768]{1,0:T(8,128)(2,1)S(1)} %copy-done.14), channel_id=1, source_target_pairs={{0,16},{8,24},{16,0},{24,8},{1,17},{9,25},{17,1},{25,9},{2,18},{10... | collective-permute-start | bytes 3538952 | tf_op jit(solution)/shard_map/ppermute | solution.py:661
  468.7 48.6 %collective-permute-start.65 = (bf16[768,768]{1,0:T(8,128)(2,1)S(1)}, bf16[768,768]{1,0:T(8,128)(2,1)S(1)}, u32[]{:S(2)}, u32[]{:S(2)}) collective-permute-start(bf16[768,768]{1,0:T(8,128)(2,1)S(1)} %add_convert_fusion.3), channel_id=1, source_target_pairs={{0,8},{8,0},{16,24},{24,16},{1,9},{9,1},{17,25},{25,17},{2,10},{10... | collective-permute-start | bytes 3538952 | tf_op jit(solution)/shard_map/ppermute | solution.py:661
  469.5 50.2 %collective-permute-start.48 = (bf16[1152,768]{1,0:T(8,128)(2,1)S(1)}, bf16[1152,768]{1,0:T(8,128)(2,1)S(1)}, u32[]{:S(2)}, u32[]{:S(2)}) collective-permute-start(bf16[1152,768]{1,0:T(8,128)(2,1)S(1)} %constant_dynamic-update-slice_fusion.12), channel_id=1, source_target_pairs={{0,1},{1,0},{2,3},{3,2},{4,5},{5,4},{6,7},{7,6},{8,9},{9,8},{10,11... | collective-permute-start | bytes 5308424 | tf_op jit(solution)/shard_map/ppermute | solution.py:661
  (62 other events, 1876.4 us)

commit v2 on v1

v2 whole, which is shorter than its diff:
```python
import functools
import math

import jax
import jax.numpy as jnp
from jax import lax
from jax.experimental import pallas as pl
from jax.experimental.pallas import tpu as pltpu
from jax.sharding import PartitionSpec as P

BF = jnp.bfloat16
F32 = jnp.float32
MAXDIST = 128
EPSILON = 1e-06
NEGATIVE = -1000000000.0
TILE = 128
LANES = 128
HALF = 64
LINE = 4 * TILE
GELU_ONE = math.sqrt(2.0 / math.pi)
GELU_CUBE = 0.044715
SEND_LIMIT = 32


def dot(left, right, left_dim=1, right_dim=0):
    return lax.dot_general(
        left, right, (((left_dim,), (right_dim,)), ((), ())), preferred_element_type=F32
    )


def iota(shape, dim):
    return lax.broadcasted_iota(jnp.int32, shape, dim)


def bucket_of(offset, buckets, far_limit):
    exact_limit = buckets // 4
    half_count = buckets // 2
    distance = jnp.abs(offset)
    bucket_ids = jnp.minimum(distance, exact_limit)
    for bucket_level in range(exact_limit + 1, half_count):
        border = math.ceil(
            exact_limit
            * (far_limit / exact_limit)
            ** ((bucket_level - exact_limit) / (half_count - exact_limit))
        )
        bucket_ids = bucket_ids + (distance >= border).astype(jnp.int32)
    return bucket_ids + jnp.where(offset > 0, half_count, 0).astype(jnp.int32)


def whole(shape):
    return pl.BlockSpec(shape, lambda *_: (0,) * len(shape))


def by_rows(rows, columns):
    return pl.BlockSpec((rows, columns), lambda step: (step, 0))


def add_rows(ref, values):
    @pl.when(pl.program_id(0) == 0)
    def _():
        ref[...] = values

    @pl.when(pl.program_id(0) > 0)
    def _():
        ref[...] += values


def smem():
    return pl.BlockSpec(memory_space=pltpu.SMEM)


def params(mebibytes):
    return pltpu.CompilerParams(vmem_limit_bytes=mebibytes * 1024 * 1024)


def shape_of(shape, dtype):
    return jax.ShapeDtypeStruct(shape, dtype)


def inverse_rms(rows):
    return lax.rsqrt(jnp.mean(rows * rows, axis=-1, keepdims=True) + EPSILON)


def send_rows(expert_ref, slot_row, rows, plan, send_refs):
    block_rows = plan.block_rows
    size = plan.blocks * block_rows
    place = iota((size, 1), 0)
    wanted = place
    if plan.paired:
        for distance in range(plan.blocks):
            first = distance * block_rows
            wanted = jnp.where(
                place >= first, place - first + (expert_ref[0] ^ distance) * block_rows, wanted
            )
    chosen = jnp.where(wanted == slot_row, 1.0, 0.0).astype(BF)
    sent = dot(chosen, rows).astype(BF)
    first = 0
    for send_ref in send_refs:
        send_ref[...] = sent[first : first + send_ref.shape[0]]
        first += send_ref.shape[0]


def home_rows(expert_ref, column, refs, plan):
    block_rows = plan.block_rows
    rows = jnp.concatenate(
        [ref[first : first + block_rows, :] for ref, first in plan.take(refs)], axis=0
    )
    place = iota((1, rows.shape[0]), 1)
    wanted = place
    for distance in range(plan.blocks):
        first = distance * block_rows
        base = (expert_ref[0] ^ distance) * block_rows if plan.paired else 0
        wanted = jnp.where(place >= first, place - first + base, wanted)
    chosen = jnp.where(column[:, :1] == wanted, 1.0, 0.0).astype(BF)
    return dot(chosen, rows)


def slots_kernel(
    capacity, experts, plan, expert_ref, length_ref, routes_ref, cotangent_ref, slot_ref, column_ref, *send_refs
):
    seq_len = routes_ref.shape[1]
    routes = routes_ref[...]
    live = iota((1, seq_len), 1) < length_ref[0]
    onehot = jnp.where((iota((experts, seq_len), 0) == routes) & live, 1.0, 0.0)
    earlier = jnp.where(iota((seq_len, seq_len), 0) < iota((seq_len, seq_len), 1), 1.0, 0.0)
    before = dot(onehot.astype(BF), earlier.astype(BF))
    rank = jnp.sum(before * onehot, axis=0, keepdims=True).astype(jnp.int32)
    slot = jnp.where(live & (rank < capacity), routes * capacity + rank, -1)
    slot_ref[...] = slot
    wide = jnp.broadcast_to(slot.astype(F32), (LANES, seq_len))
    column_ref[...] = wide.T.astype(jnp.int32)
    send_rows(expert_ref, slot, cotangent_ref[...], plan, send_refs)


def slots_part(expert, lengths, routes, cotangent, capacity, experts, plan):
    seq_len, width = cotangent.shape
    return pl.pallas_call(
        functools.partial(slots_kernel, capacity, experts, plan),
        out_shape=[shape_of((1, seq_len), jnp.int32), shape_of((seq_len, LANES), jnp.int32)]
        + [shape_of((rows, width), BF) for rows in plan.arrays],
        in_specs=[smem(), smem(), pl.BlockSpec(), pl.BlockSpec()],
        compiler_params=params(58),
        name="slots",
    )(expert, lengths, routes, cotangent)


def forward_kernel(
    plan,
    expert_ref,
    length_ref,
    slot_ref,
    tokens_ref,
    gain_one_ref,
    query_weight_ref,
    key_weight_ref,
    value_weight_ref,
    out_weight_ref,
    bias_ref,
    gain_two_ref,
    *refs,
):
    probs_ref, qkv_ref, lefts_ref, inverse_ref, resid_ref = refs[:5]
    send_refs = refs[5:-3]
    qkv_s, mixed_s, line_s = refs[-3:]
    pair = pl.program_id(0)
    pairs = pl.num_programs(0)
    seq_len, width = tokens_ref.shape
    tiles = seq_len // TILE

    @pl.when(pair == 0)
    def _():
        buckets = bias_ref.shape[1]
        place = iota((buckets, LINE), 1)
        offset = jnp.where(place < 3 * TILE, place - TILE, place - TILE - LINE)
        chosen = bucket_of(offset, buckets, MAXDIST) == iota((buckets, LINE), 0)
        lines = dot(bias_ref[...], jnp.where(chosen, 1.0, 0.0).astype(BF))
        for number in range(width // LANES):
            line_s[number, 0:2, :] = lines[2 * number : 2 * number + 2]
        rows = tokens_ref[...].astype(F32)
        normed = (rows * inverse_rms(rows) * gain_one_ref[...].astype(F32).reshape(1, width)).astype(BF)
        lefts_ref[0] = normed
        for part, weight_ref in enumerate((query_weight_ref, key_weight_ref, value_weight_ref)):
            values = dot(normed, weight_ref[...])
            for number in range(width // LANES):
                block = values[:, number * LANES : (number + 1) * LANES].astype(BF)
                if part == 0:
                    block = block * BF(HALF ** (-0.5))
                qkv_s[part, number] = block

    query = qkv_s[0, pair]
    key = qkv_s[1, pair]
    value = qkv_s[2, pair]
    qkv_ref[0, 0] = query
    qkv_ref[1, 0] = key
    qkv_ref[2, 0] = value
    lane = iota((seq_len, LANES), 1)
    row = iota((seq_len, LANES), 0)
    row_tile = row // TILE
    value_wide = jnp.concatenate([value, jnp.ones((seq_len, LANES), BF)], axis=1)
    query_wides, key_wides, nears = [], [], []
    for half in range(2):
        own = lane < HALF if half == 0 else lane >= HALF
        extra = lane - HALF if half == 0 else lane
        query_wides.append(
            jnp.where(
                own,
                query.astype(F32),
                jnp.where((extra == 0) | (extra == 1 + row_tile), 1.0, 0.0),
            ).astype(BF)
        )
        query_tile = extra - 1
        line = jnp.broadcast_to(line_s[pair, half : half + 1, :], (TILE, LINE))
        far = jnp.where(
            row_tile <= query_tile - 2,
            line[0:1, 0:1],
            jnp.where(row_tile >= query_tile + 2, line[0:1, 3 * TILE - 1 : 3 * TILE], 0.0),
        )
        far = jnp.where((query_tile >= 0) & (query_tile < tiles), far, 0.0)
        far = jnp.where((extra == 0) & (row >= length_ref[0]), NEGATIVE, far)
        key_wides.append(jnp.where(own, key.astype(F32), far).astype(BF))
        nears.append(pltpu.roll(line, 0, 1, stride=1, stride_axis=0)[:, : 3 * TILE])
    first = lane[:TILE] < HALF
    for tile in range(tiles):
        part = slice(tile * TILE, (tile + 1) * TILE)
        low = max(tile - 1, 0)
        high = min(tile + 2, tiles)
        outs = []
        for half in range(2):
            scores = dot(query_wides[half][part], key_wides[half], 1, 1)
            middle = nears[half][:, (low - tile + 1) * TILE : (high - tile + 1) * TILE]
            pieces = [scores[:, low * TILE : high * TILE] + middle]
            if low > 0:
                pieces.insert(0, scores[:, : low * TILE])
            if high < tiles:
                pieces.append(scores[:, high * TILE :])
            scores = jnp.concatenate(pieces, axis=1)
            peak = jnp.max(scores, axis=-1, keepdims=True)
            raised = jnp.exp(scores - peak).astype(BF)
            probs_ref[half, part, :] = raised
            outs.append(dot(raised, value_wide))
        inverse_total = 1.0 / jnp.where(first, outs[0][:, LANES:], outs[1][:, LANES:])
        mixed = jnp.where(first, outs[0][:, :LANES], outs[1][:, :LANES]) * inverse_total
        mixed_s[pair, part, :] = mixed.astype(BF)
        inverse_ref[0, part, :] = inverse_total

    @pl.when(pair == pairs - 1)
    def _():
        mixed_all = jnp.concatenate([mixed_s[number] for number in range(width // LANES)], axis=1)
        lefts_ref[1] = mixed_all
        resid = tokens_ref[...].astype(F32) + dot(mixed_all, out_weight_ref[...])
        resid_ref[...] = resid
        normed = (resid * inverse_rms(resid) * gain_two_ref[...].astype(F32).reshape(1, width)).astype(BF)
        send_rows(expert_ref, slot_ref[...], normed, plan, send_refs)


def forward_part(expert, lengths, slot, tokens, gain_one, weights, bias, gain_two, plan):
    seq_len, width = tokens.shape
    pairs = width // LANES
    square = whole((width, width))
    return pl.pallas_call(
        functools.partial(forward_kernel, plan),
        grid=(pairs,),
        out_shape=[
            shape_of((2 * pairs, seq_len, seq_len), BF),
            shape_of((3, pairs, seq_len, LANES), BF),
            shape_of((2, seq_len, width), BF),
            shape_of((pairs, seq_len, LANES), F32),
            shape_of((seq_len, width), F32),
        ]
        + [shape_of((rows, width), BF) for rows in plan.arrays],
        in_specs=[
            smem(),
            smem(),
            whole((1, seq_len)),
            whole((seq_len, width)),
            whole((width,)),
            square,
            square,
            square,
            square,
            whole(bias.shape),
            whole((width,)),
        ],
        out_specs=[
            pl.BlockSpec((2, seq_len, seq_len), lambda p: (p, 0, 0)),
            pl.BlockSpec((3, 1, seq_len, LANES), lambda p: (0, p, 0, 0)),
            whole((2, seq_len, width)),
            pl.BlockSpec((1, seq_len, LANES), lambda p: (p, 0, 0)),
            whole((seq_len, width)),
        ]
        + [whole((rows, width)) for rows in plan.arrays],
        scratch_shapes=[
            pltpu.VMEM((3, pairs, seq_len, LANES), BF),
            pltpu.VMEM((pairs, seq_len, LANES), BF),
            pltpu.VMEM((pairs, 8, LINE), F32),
        ],
        compiler_params=params(58),
        name="attention_forward",
    )(expert, lengths, slot, tokens, gain_one, *weights, bias, gain_two)


def expert_up_kernel(plan, out_ref, *refs):
    up_refs = refs[:-2]
    up_ref, act_grad_ref = refs[-2:]

    @pl.when(pl.program_id(0) == 0)
    def _():
        for number, (ref, first) in enumerate(plan.take(up_refs)):
            rows = plan.block_rows
            up_ref[number * rows : (number + 1) * rows, :] = ref[first : first + rows, :]

    act_grad_ref[...] = dot(up_ref[...], out_ref[0], 1, 1).astype(BF)


def expert_up_part(up_arrays, expert_out, plan):
    width = expert_out.shape[2]
    hidden = expert_out.shape[1]
    rows = sum(plan.arrays)
    tile = 512
    return pl.pallas_call(
        functools.partial(expert_up_kernel, plan),
        grid=(hidden // tile,),
        out_shape=[shape_of((rows, width), BF), shape_of((rows, hidden), BF)],
        in_specs=[pl.BlockSpec((1, tile, width), lambda f: (0, f, 0))]
        + [whole(array.shape) for array in up_arrays],
        out_specs=[whole((rows, width)), pl.BlockSpec((rows, tile), lambda f: (0, f))],
        compiler_params=params(28),
        name="expert_activation_gradient",
    )(expert_out, *up_arrays)


def expert_kernel(plan, expert_ref, up_ref, act_grad_ref, in_ref, router_ref, *refs):
    count = len(plan.arrays)
    row_refs = refs[: -(7 + count)]
    act_ref, slope_ref, scaled_ref, rows_grad_ref, gate_ref, logit_grad_ref = refs[
        -(7 + count) : -(1 + count)
    ]
    back_refs, rows_ref = refs[-(1 + count) : -1], refs[-1]
    block_rows = plan.block_rows
    step = pl.program_id(0)
    steps = len(plan.arrays)
    rows, hidden = act_ref.shape
    experts = router_ref.shape[0]
    blocks = plan.take(row_refs)
    for number in range(steps):

        @pl.when(step == number)
        def _(number=number):
            each = len(blocks) // steps
            for place in range(each):
                ref, first = blocks[number * each + place]
                rows_ref[place * block_rows : (place + 1) * block_rows, :] = ref[
                    first : first + block_rows, :
                ]

    own = iota((rows, experts), 1) == expert_ref[0]
    logits = dot(rows_ref[...], router_ref[...], 1, 1)
    raised = jnp.exp(logits - jnp.max(logits, axis=-1, keepdims=True))
    probs = raised / jnp.sum(raised, axis=-1, keepdims=True)
    gate = jnp.sum(jnp.where(own, probs, 0.0), axis=-1, keepdims=True)
    gate_ref[...] = gate
    rows_grad_ref[...] = (up_ref[...].astype(F32) * gate).astype(BF)
    scaled_ref[...] = (rows_ref[...].astype(F32) * gate).astype(BF)
    gate_grad = jnp.zeros((rows, LANES), F32)
    tile = 512
    for first in range(0, hidden, tile):
        part = slice(first, first + tile)
        pre = dot(rows_ref[...], in_ref[0, :, part])
        act_grad = act_grad_ref[:, part]
        square = pre * pre
        level = 0.5 + 0.5 * jnp.tanh(pre * (GELU_ONE + GELU_ONE * GELU_CUBE * square))
        act = (pre * level).astype(BF)
        level = level.astype(BF)
        slope = level + act * (BF(1.0) - level) * (
            BF(2.0 * GELU_ONE) + BF(6.0 * GELU_ONE * GELU_CUBE) * square.astype(BF)
        )
        act_ref[:, part] = act
        product = (act * act_grad).astype(F32)
        for place in range(0, tile, LANES):
            gate_grad += product[:, place : place + LANES]
        slope_ref[:, part] = act_grad * slope
    gate_grad = jnp.sum(gate_grad, axis=-1, keepdims=True)
    logit_grad = gate_grad * (jnp.where(own, 1.0, 0.0) - probs)
    logit_grad_ref[...] = logit_grad.astype(BF)
    logit_grad = (gate * logit_grad).astype(BF)
    back = gate * dot(slope_ref[...], in_ref[0], 1, 1) + dot(logit_grad, router_ref[...])
    back = back.astype(BF)
    for number in range(steps):

        @pl.when(step == number)
        def _(number=number):
            back_refs[number][...] = back


def expert_part(expert, up_rows, act_grad, expert_in, router, row_arrays, plan):
    rows, width = up_rows.shape
    hidden = expert_in.shape[2]
    experts = router.shape[0]
    steps = len(plan.arrays)
    some = rows // steps
    return pl.pallas_call(
        functools.partial(expert_kernel, plan),
        grid=(steps,),
        out_shape=[
            shape_of((rows, hidden), BF),
            shape_of((rows, hidden), BF),
            shape_of((rows, width), BF),
            shape_of((rows, width), BF),
            shape_of((rows, 1), F32),
            shape_of((rows, experts), BF),
        ]
        + [shape_of((count, width), BF) for count in plan.arrays],
        in_specs=[
            smem(),
            by_rows(some, width),
            by_rows(some, hidden),
            whole((1, width, hidden)),
            whole((experts, width)),
        ]
        + [whole(array.shape) for array in row_arrays],
        out_specs=[by_rows(some, columns) for columns in (hidden, hidden, width, width, 1, experts)]
        + [whole((count, width)) for count in plan.arrays],
        scratch_shapes=[pltpu.VMEM((some, width), BF)],
        compiler_params=params(44),
        name="expert_rows",
    )(expert, up_rows, act_grad, expert_in, router, *row_arrays)


def later_sums_kernel(*refs):
    count = len(refs) // 3
    for keep_ref, there_ref, out_ref in zip(refs[:count], refs[count : 2 * count], refs[2 * count :]):
        out_ref[...] = (keep_ref[...].astype(F32) + there_ref[...].astype(F32)).astype(BF)


def later_sums(keeps, theres):
    count, rows, columns = keeps[0].shape
    later = count // 2
    some = rows // 4

    def block(first):
        return pl.BlockSpec((1, some, columns), lambda t, r: (first + t, r, 0))

    return pl.pallas_call(
        later_sums_kernel,
        grid=(later, 4),
        out_shape=[shape_of((later, rows, columns), BF)] * len(keeps),
        in_specs=[block(count - later)] * (2 * len(keeps)),
        out_specs=[block(0)] * len(keeps),
        compiler_params=params(58),
        name="later_sums",
    )(*keeps, *theres)


def weight_grad_kernel(transposed, count, *refs):
    _, wide_refs, rows_refs, out_refs = [refs[n * count : (n + 1) * count] for n in range(4)]
    for turned, wide_ref, rows_ref, out_ref in zip(transposed, wide_refs, rows_refs, out_refs):
        left_ref, right_ref = (wide_ref, rows_ref) if turned else (rows_ref, wide_ref)
        out_ref[0] = dot(left_ref[...], right_ref[...], 0, 0).astype(BF)


def weight_grad_part(parts, terms):
    tiles, wides, rows, transposed = zip(*terms)
    steps = tiles[0].shape[0]
    count, width = rows[0].shape
    tile = wides[0].shape[1] // parts
    shapes = [(tile, width) if turned else (width, tile) for turned in transposed]
    return pl.pallas_call(
        functools.partial(weight_grad_kernel, transposed, len(terms)),
        grid_spec=pltpu.PrefetchScalarGridSpec(
            num_scalar_prefetch=len(terms),
            grid=(steps,),
            in_specs=[
                pl.BlockSpec((count, tile), lambda s, *refs, number=number: (0, refs[number][s]))
                for number in range(len(terms))
            ]
            + [whole((count, width))] * len(terms),
            out_specs=[pl.BlockSpec((1,) + shape, lambda s, *_: (s, 0, 0)) for shape in shapes],
        ),
        out_shape=[shape_of((steps,) + shape, BF) for shape in shapes],
        compiler_params=params(SEND_LIMIT),
        name="expert_weight_gradients",
    )(*tiles, *wides, *rows)


def expert_out_kernel(act_ref, out_ref, gate_ref, *send_refs):
    rows = (dot(act_ref[...], out_ref[0]) * gate_ref[...]).astype(BF)
    for number, send_ref in enumerate(send_refs):

        @pl.when(pl.program_id(0) == number)
        def _(send_ref=send_ref):
            send_ref[...] = rows


def expert_out_part(act, expert_out, gate, plan):
    rows, hidden = act.shape
    width = expert_out.shape[2]
    steps = len(plan.arrays)
    return pl.pallas_call(
        expert_out_kernel,
        grid=(steps,),
        out_shape=[shape_of((count, width), BF) for count in plan.arrays],
        in_specs=[
            by_rows(rows // steps, hidden),
            whole((1, hidden, width)),
            by_rows(rows // steps, 1),
        ],
        out_specs=[whole((count, width)) for count in plan.arrays],
        compiler_params=params(32),
        name="expert_output",
    )(act, expert_out, gate)


ROW_STEPS = 4


def result_kernel(plan, expert_ref, length_ref, column_ref, resid_ref, *refs):
    total = resid_ref[...] + home_rows(expert_ref, column_ref[...], refs[:-1], plan)
    rows = total.shape[0]
    live = iota((rows, 1), 0) + pl.program_id(0) * rows < length_ref[0]
    refs[-1][...] = jnp.where(live, total, 0.0).astype(BF)


def result_part(expert, lengths, column, resid, arrays, plan):
    seq_len, width = resid.shape
    rows = seq_len // ROW_STEPS
    return pl.pallas_call(
        functools.partial(result_kernel, plan),
        grid=(ROW_STEPS,),
        out_shape=shape_of(resid.shape, BF),
        in_specs=[smem(), smem(), by_rows(rows, LANES), by_rows(rows, width)]
        + [whole(array.shape) for array in arrays],
        out_specs=by_rows(rows, width),
        compiler_params=params(58),
        name="result",
    )(expert, lengths, column, resid, *arrays)


def middle_kernel(
    plan,
    expert_ref,
    length_ref,
    column_ref,
    resid_ref,
    cotangent_ref,
    out_weight_ref,
    gain_ref,
    *refs,
):
    resid_grad_ref, mixed_grad_ref, attn_grad_ref, gain_grad_ref = refs[-4:]
    upstream = home_rows(expert_ref, column_ref[...], refs[:-4], plan)
    resid = resid_ref[...]
    rows = resid.shape[0]
    inverse = inverse_rms(resid)
    scaled = gain_ref[...].astype(F32).reshape(1, -1) * upstream
    add_rows(gain_grad_ref, jnp.sum(upstream * resid * inverse, axis=0, keepdims=True))
    live = iota((rows, 1), 0) + pl.program_id(0) * rows < length_ref[0]
    resid_grad = (
        jnp.where(live, cotangent_ref[...].astype(F32), 0.0)
        + inverse * scaled
        - resid * (inverse * inverse * inverse * jnp.mean(scaled * resid, axis=-1, keepdims=True))
    )
    resid_grad_ref[...] = resid_grad
    attn_grad = resid_grad.astype(BF)
    mixed_grad_ref[...] = dot(attn_grad, out_weight_ref[...], 1, 1).astype(BF)
    attn_grad_ref[...] = attn_grad


def middle_part(expert, lengths, column, resid, cotangent, out_weight, gain, arrays, plan):
    seq_len, width = resid.shape
    rows = seq_len // ROW_STEPS
    block = by_rows(rows, width)
    return pl.pallas_call(
        functools.partial(middle_kernel, plan),
        grid=(ROW_STEPS,),
        out_shape=[
            shape_of((seq_len, width), F32),
            shape_of((seq_len, width), BF),
            shape_of((seq_len, width), BF),
            shape_of((1, width), F32),
        ],
        in_specs=[smem(), smem(), by_rows(rows, LANES), block, block, whole((width, width)), whole((width,))]
        + [whole(array.shape) for array in arrays],
        out_specs=[block, block, block, whole((1, width))],
        compiler_params=params(58),
        name="expert_norm_backward",
    )(expert, lengths, column, resid, cotangent, out_weight, gain, *arrays)


def backward_kernel(
    qkv_ref, probs_ref, mixed_ref, grad_ref, attn_grad_ref, inverse_ref, back_ref, line_ref, score_s
):
    seq_len = grad_ref.shape[0]
    back_ref[3] = attn_grad_ref[...]
    tiles = seq_len // TILE
    query = qkv_ref[0, 0]
    key = qkv_ref[1, 0]
    value = qkv_ref[2, 0]
    lane = iota((seq_len, LANES), 1)
    row_tile = iota((seq_len, LANES), 0) // TILE
    scaled = grad_ref[...].astype(F32) * inverse_ref[0]
    product = scaled * mixed_ref[0].astype(F32)
    scaled_low = scaled.astype(BF)
    key_wide = jnp.concatenate([key, jnp.where(lane == row_tile, 1.0, 0.0).astype(BF)], axis=1)
    backward_rows = jnp.where(iota((TILE, TILE), 0) + iota((TILE, TILE), 1) == TILE - 1, 1.0, 0.0)
    query_backs = []
    key_backs = []
    value_backs = []
    for half in range(2):
        own = lane < HALF if half == 0 else lane >= HALF
        extra = lane - HALF if half == 0 else lane
        delta = jnp.sum(jnp.where(own, product, 0.0), axis=-1, keepdims=True)
        high = delta.astype(BF).astype(F32)
        grad_wide = jnp.where(
            own, scaled, jnp.where(extra == 0, -high, jnp.where(extra == 1, high - delta, 0.0))
        ).astype(BF)
        value_wide = jnp.where(
            own, value.astype(F32), jnp.where((extra == 0) | (extra == 1), 1.0, 0.0)
        ).astype(BF)
        near = [jnp.zeros((TILE, TILE), F32) for _ in range(3)]
        for tile in range(tiles):
            part = slice(tile * TILE, (tile + 1) * TILE)
            prob_grad = dot(grad_wide[part], value_wide, 1, 1)
            score_grad = (probs_ref[half, part, :].astype(F32) * prob_grad).astype(BF)
            score_s[half, part, :] = score_grad
            for side in range(3):
                other = tile + side - 1
                if 0 <= other < tiles:
                    near[side] = near[side] + score_grad[
                        :, other * TILE : (other + 1) * TILE
                    ].astype(F32)
        query_wide = dot(score_s[half], key_wide)
        query_backs.append(query_wide[:, :LANES])
        sums = query_wide[:, LANES:]
        far_left = jnp.sum(jnp.where(lane <= row_tile - 2, sums, 0.0), axis=0, keepdims=True)
        far_right = jnp.sum(jnp.where(lane >= row_tile + 2, sums, 0.0), axis=0, keepdims=True)
        line_ref[0, half : half + 1, LINE : LINE + LANES] = far_left
        line_ref[0, half : half + 1, LINE + LANES :] = far_right
        key_backs.append(dot(query, score_s[half], 0, 0))
        value_backs.append(dot(scaled_low, probs_ref[half], 0, 0))
        spread = lax.dot_general(
            backward_rows,
            jnp.concatenate(near, axis=1),
            (((1,), (0,)), ((), ())),
            precision=lax.Precision.HIGHEST,
            preferred_element_type=F32,
        )
        spread = jnp.concatenate([spread, jnp.zeros((TILE, TILE), F32)], axis=1)
        spread = pltpu.roll(spread, 0, 1, stride=1, stride_axis=0)
        line_ref[0, half : half + 1, :LINE] = jnp.sum(spread, axis=0, keepdims=True)
    first = lane < HALF
    back_ref[0] = (jnp.where(first, query_backs[0], query_backs[1]) * HALF ** (-0.5)).astype(BF)
    for place, backs in ((1, key_backs), (2, value_backs)):
        joined = jnp.concatenate([backs[0][:HALF], backs[1][HALF:]], axis=0)
        back_ref[place] = joined.T.astype(BF)


def backward_part(qkv, probs, lefts, mixed_grad, attn_grad, inverse):
    _, seq_len, width = lefts.shape
    pairs = width // LANES
    column = pl.BlockSpec((seq_len, LANES), lambda p: (0, p))
    return pl.pallas_call(
        backward_kernel,
        grid=(pairs,),
        out_shape=[
            shape_of((4, seq_len, width), BF),
            shape_of((pairs, 2, LINE + 2 * LANES), F32),
        ],
        in_specs=[
            pl.BlockSpec((3, 1, seq_len, LANES), lambda p: (0, p, 0, 0)),
            pl.BlockSpec((2, seq_len, seq_len), lambda p: (p, 0, 0)),
            pl.BlockSpec((1, seq_len, LANES), lambda p: (1, 0, p)),
            column,
            column,
            pl.BlockSpec((1, seq_len, LANES), lambda p: (p, 0, 0)),
        ],
        out_specs=[
            pl.BlockSpec((4, seq_len, LANES), lambda p: (0, 0, p)),
            pl.BlockSpec((1, 2, LINE + 2 * LANES), lambda p: (p, 0, 0)),
        ],
        scratch_shapes=[pltpu.VMEM((2, seq_len, seq_len), BF)],
        compiler_params=params(58),
        name="attention_backward",
    )(qkv, probs, lefts, mixed_grad, attn_grad, inverse)


def projection_grad_kernel(left_places_ref, right_places_ref, left_ref, right_ref, out_ref):
    out_ref[...] = dot(left_ref[0], right_ref[0], 0, 0).astype(BF)


def projection_grad_part(left_places, right_places, lefts, rights):
    _, seq_len, width = lefts.shape
    count = left_places.shape[0]
    return pl.pallas_call(
        projection_grad_kernel,
        grid_spec=pltpu.PrefetchScalarGridSpec(
            num_scalar_prefetch=2,
            grid=(count,),
            in_specs=[
                pl.BlockSpec((1, seq_len, width), lambda s, left, right: (left[s], 0, 0)),
                pl.BlockSpec((1, seq_len, width), lambda s, left, right: (right[s], 0, 0)),
            ],
            out_specs=pl.BlockSpec((width, width), lambda s, left, right: (s, 0)),
        ),
        out_shape=shape_of((count * width, width), BF),
        compiler_params=params(58),
        name="projection_gradient",
    )(left_places, right_places, lefts, rights)


def token_grad_kernel(
    back_ref,
    query_weight_ref,
    key_weight_ref,
    value_weight_ref,
    tokens_ref,
    gain_ref,
    resid_grad_ref,
    out_ref,
):
    upstream = None
    for part, weight_ref in enumerate((query_weight_ref, key_weight_ref, value_weight_ref)):
        term = dot(back_ref[part], weight_ref[...], 1, 1)
        upstream = term if upstream is None else upstream + term
    rows = tokens_ref[...].astype(F32)
    inverse = inverse_rms(rows)
    scaled = gain_ref[...].astype(F32).reshape(1, -1) * upstream
    out_ref[...] = (
        resid_grad_ref[...]
        + inverse * scaled
        - rows * (inverse * inverse * inverse * jnp.mean(scaled * rows, axis=-1, keepdims=True))
    )


def token_grad_part(back, weights, tokens, gain, resid_grad):
    seq_len, width = tokens.shape
    rows = seq_len // ROW_STEPS
    block = by_rows(rows, width)
    return pl.pallas_call(
        token_grad_kernel,
        grid=(ROW_STEPS,),
        out_shape=shape_of((seq_len, width), F32),
        in_specs=[pl.BlockSpec((3, rows, width), lambda step: (0, step, 0))]
        + [whole((width, width))] * 3
        + [block, whole((width,)), block],
        out_specs=block,
        compiler_params=params(58),
        name="token_gradient",
    )(back, *weights, tokens, gain, resid_grad)


def swap(values, axis, size, distance):
    return lax.ppermute(values, axis, [(place, place ^ distance) for place in range(size)])


def after(values, *others):
    return lax.optimization_barrier((values, *others))[0]


class Plan:
    def __init__(self, size, capacity, experts):
        self.size = size
        self.capacity = capacity
        self.paired = size == 8 and capacity % 16 == 0
        if self.paired:
            self.block_rows = capacity
            self.blocks = size
            self.arrays = [2 * capacity] * (size // 2)
        else:
            self.block_rows = experts * capacity
            self.blocks = 1
            self.arrays = [experts * capacity]

    def turn(self, rows):
        parts = rows.reshape(self.size, self.capacity, rows.shape[1])
        parts = lax.all_to_all(parts, "expert", split_axis=0, concat_axis=0, tiled=True)
        return parts.reshape(rows.shape)

    def cross(self, arrays):
        if not self.paired:
            return [self.turn(array) for array in arrays]
        return [
            array if k == 0 else swap(array, "expert", self.size, 2 * k)
            for k, array in enumerate(arrays)
        ]

    def finish(self, arrays):
        if not self.paired:
            return arrays
        return [*arrays, *[swap(array, "expert", self.size, 1) for array in arrays]]

    def take(self, refs):
        if not self.paired:
            return [(refs[0], 0)]
        half = len(refs) // 2
        return [
            place for pair in zip(refs[:half], refs[half:]) for place in zip(pair, (0, self.block_rows))
        ]


def stages_of(dp_size, expert_size):
    stages = [("expert", expert_size, (1,))]
    bits = [1 << n for n in range(dp_size.bit_length() - 1)]
    stages += [("dp", dp_size, tuple(bits[n : n + 2])) for n in range(0, len(bits), 2)]
    bits = [1 << n for n in range(1, expert_size.bit_length() - 1)]
    return stages + [("expert", expert_size, tuple(bits[n : n + 2])) for n in range(0, len(bits), 2)]


def distances_of(bits):
    return [sum(bit for n, bit in enumerate(bits) if (k >> n) & 1) for k in range(1 << len(bits))]


def place_of(stage):
    axis, _, bits = stage
    index = lax.axis_index(axis)
    return sum(((index // bit) % 2) << n for n, bit in enumerate(bits))


def share_kernel(inputs, place_ref, *refs):
    in_refs, out_refs = refs[:inputs], refs[inputs:]
    for number, out_ref in enumerate(out_refs):
        rows = out_ref.shape[0]
        if len(out_refs) == 1:
            part = slice(None)
        else:
            part = pl.ds(pl.multiple_of((place_ref[0] ^ number) * rows, rows), rows)
        out_ref[...] = sum(ref[part, :].astype(F32) for ref in in_refs).astype(BF)


def share_one(parts, stage):
    count = 1 if stage is None else 1 << len(stage[2])
    place = jnp.int32(0) if stage is None else place_of(stage)
    rows, width = parts[0].shape[0] // count, parts[0].shape[1]
    if rows % 16:
        total = sum(part.astype(F32) for part in parts).astype(BF)
        return [
            lax.dynamic_slice_in_dim(total, (place ^ number) * rows, rows, 0)
            for number in range(count)
        ]
    return pl.pallas_call(
        functools.partial(share_kernel, len(parts)),
        out_shape=[shape_of((rows, width), BF)] * count,
        in_specs=[smem()] + [pl.BlockSpec()] * len(parts),
        compiler_params=params(58),
        name="share",
    )(place.reshape(1), *parts)


def scatter(parts, stage):
    axis, size, bits = stage
    return [
        part if distance == 0 else swap(part, axis, size, distance)
        for part, distance in zip(parts, distances_of(bits))
    ]


def gather(values, stage):
    axis, size, bits = stage
    return [
        values if distance == 0 else swap(values, axis, size, distance)
        for distance in distances_of(bits)
    ]


def join_kernel(place_ref, *refs):
    out_ref = refs[-1]
    for number, ref in enumerate(refs[:-1]):
        rows = ref.shape[0]
        part = pl.ds(pl.multiple_of((place_ref[0] ^ number) * rows, rows), rows)
        out_ref[part, :] = ref[...]


def join(parts, stage):
    place = place_of(stage)
    rows, width = parts[0].shape
    if rows % 16:
        joined = jnp.zeros((rows * len(parts), width), BF)
        for number, part in enumerate(parts):
            joined = lax.dynamic_update_slice_in_dim(joined, part, (place ^ number) * rows, 0)
        return joined
    return pl.pallas_call(
        join_kernel,
        out_shape=shape_of((rows * len(parts), width), BF),
        in_specs=[smem()] + [pl.BlockSpec()] * len(parts),
        compiler_params=params(58),
        name="join",
    )(place.reshape(1), *parts)


def widen_kernel(place_ref, own_ref, other_ref, *refs):
    weight_refs, out_refs, gain_ref = refs[:-3], refs[-3:-1], refs[-1]
    for number, out_ref in enumerate(out_refs):

        @pl.when(place_ref[0] == number)
        def _(out_ref=out_ref):
            out_ref[...] = own_ref[...].astype(F32)

        @pl.when(place_ref[0] != number)
        def _(out_ref=out_ref):
            out_ref[...] = other_ref[...].astype(F32)

    total = sum(
        jnp.sum(out_ref[...] * weight_ref[...].astype(F32), axis=1, keepdims=True)
        for out_ref, weight_ref in zip(out_refs, weight_refs)
    )
    gain_ref[...] = jnp.broadcast_to(total, (total.shape[0], LANES)).T[:1]


def widen(parts, stage, weights):
    rows, width = parts[0].shape
    some = 2 * LANES
    block = by_rows(some, width)
    return pl.pallas_call(
        widen_kernel,
        grid=(rows // some,),
        out_shape=[shape_of(parts[0].shape, F32)] * 2 + [shape_of((1, rows), F32)],
        in_specs=[smem()] + [block] * (2 + len(weights)),
        out_specs=[block, block, pl.BlockSpec((1, some), lambda step: (0, step))],
        compiler_params=params(58),
        name="widen",
    )(place_of(stage).reshape(1), *parts, *weights)


def halving_order(bits):
    if not bits:
        return [0]
    rest = halving_order(bits[1:])
    return rest + [distance | bits[0] for distance in rest]


def on_device(
    dp_size,
    expert_size,
    tokens,
    cotangent,
    lengths,
    routes,
    norm_gain,
    query_weight,
    key_weight,
    value_weight,
    output_weight,
    bucket_head_bias,
    ffn_gain,
    router_weight,
    expert_in,
    expert_out,
):
    seq_count, seq_len, width = tokens.shape
    assert seq_count == 1
    buckets, heads = bucket_head_bias.shape
    experts = router_weight.shape[1]
    capacity = max(2, 5 * seq_len // (4 * experts))
    plan = Plan(expert_size, capacity, experts)
    expert = lax.axis_index("expert").reshape(1)
    group = lax.axis_index("dp")
    rows_in = tokens.reshape(seq_len, width)
    upstream = cotangent.reshape(seq_len, width)
    weights = (query_weight, key_weight, value_weight)

    slot, column, *up_send = slots_part(expert, lengths, routes, upstream, capacity, experts, plan)
    up_there = plan.cross(up_send)
    probs, qkv, lefts, inverse_total, resid, *row_send = forward_part(
        expert,
        lengths,
        slot,
        rows_in,
        norm_gain,
        (*weights, output_weight),
        bucket_head_bias.T,
        ffn_gain,
        plan,
    )
    row_send, up_there = lax.optimization_barrier((row_send, up_there))
    row_there = plan.cross(row_send)
    up_rows, act_grad = expert_up_part(plan.finish(up_there), expert_out, plan)
    row_there = lax.optimization_barrier((row_there, act_grad))[0]
    act, slope, scaled_rows, rows_grad, gate, logit_grad, *back_send = expert_part(
        expert, up_rows, act_grad, expert_in, router_weight.T, plan.finish(row_there), plan
    )
    router_grad = dot(logit_grad, scaled_rows, 0, 0)
    back_there = plan.cross(back_send)

    bits = [1 << n for n in range(dp_size.bit_length() - 1)]
    half = dp_size // 2
    orders = (bits, bits[::-1])
    tiles = [group ^ jnp.array(halving_order(order), jnp.int32) for order in orders]
    grad_terms = [(act, rows_grad, True), (slope, scaled_rows, False)]
    sends = [
        weight_grad_part(dp_size, [(tile[half:], *term)])[0] for tile, term in zip(tiles, grad_terms)
    ]
    arrived = [swap(send, "dp", dp_size, order[0]) for send, order in zip(sends, orders)]
    keeps = weight_grad_part(
        dp_size, [(tile[:half], *term) for tile, term in zip(tiles, grad_terms)]
    )
    result_send = expert_out_part(act, expert_out, gate, plan)
    back_there = lax.optimization_barrier((back_there, keeps, result_send))[0]
    back_arrays = plan.finish(back_there)

    resid_grad, mixed_grad, attn_grad, ffn_gain_grad = middle_part(
        expert, lengths, column, after(resid, *keeps), upstream, output_weight, ffn_gain, back_arrays, plan
    )
    result_send = lax.optimization_barrier((result_send, back_there))[0]
    result_there = plan.cross(result_send)

    arrived = lax.optimization_barrier((arrived, back_arrays))[0]
    seconds = later_sums(keeps, arrived)
    rests = [list(order[1:]) for order in orders]
    arrived_seconds = [
        swap(send, "dp", dp_size, rest[0]) if rest else None for send, rest in zip(seconds, rests)
    ]
    mixed_grad = after(mixed_grad, *seconds)

    back, lines = backward_part(qkv, probs, lefts, mixed_grad, attn_grad, inverse_total)
    back, result_there, arrived_seconds = lax.optimization_barrier(
        (back, result_there, arrived_seconds)
    )

    sum_bucket = bucket_of(jnp.arange(LINE, dtype=jnp.int32) - (2 * TILE - 1), buckets, MAXDIST)
    sum_indicator = sum_bucket[None, :] == jnp.arange(buckets, dtype=jnp.int32)[:, None]
    lines = jnp.pad(
        lines.reshape(heads, LINE + 2 * LANES), ((0, 0), (0, width - LINE - 2 * LANES))
    )
    small = jnp.concatenate([ffn_gain_grad, router_grad, lines], axis=0)
    stages = stages_of(dp_size, expert_size)
    steps = [
        (axis, size, bit)
        for axis, size, bits in stages[2:] + stages[:1] + stages[1:2]
        for bit in bits
    ]

    def sum_step(small):
        if not steps:
            return small
        return small + swap(small, *steps.pop(0))

    core = place_of(stages[0])
    result_arrays = plan.finish(result_there)

    def gradient(chunk, which, *others):
        left, right = (0 * which, which) if chunk == 0 else (which, 2 + which)
        args = lax.optimization_barrier(((lefts, back), others))[0]
        return projection_grad_part(left.reshape(1), right.reshape(1), *args)

    sent = [gradient(0, 1 - core)]
    sent.append(gradient(1, 1 - core, sent[0]))
    there = [swap(values, *stages[0][:2], 1) for values in sent]
    kept = gradient(0, core, sent[1])
    shares = [share_one([kept, there[0]], stages[1])]
    kept = gradient(1, core, shares[0])
    shares.append(share_one([kept, there[1]], stages[1]))
    moved = [scatter(parts, stages[1]) for parts in shares]
    later_back, small = lax.optimization_barrier((back, small, shares[1]))[:2]
    token_grad = token_grad_part(later_back, weights, rows_in, norm_gain, resid_grad)
    moved[0], token_grad = lax.optimization_barrier((moved[0], token_grad))
    while len(steps) > len(stages[1][2]):
        small = sum_step(small)
    moved[1], small, result_arrays = lax.optimization_barrier((moved[1], small, result_arrays))
    for stage in stages[2:]:
        shares = [share_one(parts, stage) for parts in moved]
        moved = [scatter(parts, stage) for parts in shares]
        while steps:
            small = sum_step(small)
        moved[1], small = lax.optimization_barrier((moved[1], small))
    chunks = [share_one(parts, None)[0] for parts in moved]
    for stage in stages[:1:-1]:
        chunks = [join(gather(values, stage), stage) for values in chunks]
    there = [gather(values, stages[1]) for values in chunks]
    keeps, arrived, arrived_seconds, resid = lax.optimization_barrier(
        (keeps, arrived, arrived_seconds, resid, chunks)
    )[:4]
    result = result_part(expert, lengths, column, resid, result_arrays, plan)
    weight_sums = []
    for rest, keep, term, second in zip(rests, keeps, arrived, arrived_seconds):
        total = keep[: half // 2].astype(F32) + term[: half // 2].astype(F32)
        if rest:
            total = total + second.astype(F32)
        weight_sums.append(total)
    there, weight_sums, result = lax.optimization_barrier((there, weight_sums, result))
    expert_out_grad, expert_in_grad = weight_sums
    chunks = [join(parts, stages[1]) for parts in there]
    pairs_of = [gather(chunk, stages[0]) for chunk in chunks]
    query_grad, key_grad, gain_sum = widen(pairs_of[0], stages[0], (query_weight, key_weight))
    value_grad, output_grad, value_sum = widen(pairs_of[1], stages[0], (value_weight,))
    norm_gain_grad = (gain_sum + value_sum).reshape(width) / norm_gain.astype(F32)

    lines = small[1 + experts :]
    bucket_grad = lax.dot_general(
        sum_indicator.astype(F32),
        lines[:, :LINE],
        (((1,), (1,)), ((), ())),
        precision=lax.Precision.HIGHEST,
    )
    far_sums = jnp.sum(lines[:, LINE : LINE + 2 * LANES].reshape(heads, 2, LANES), axis=-1)
    bucket_row = jnp.arange(buckets, dtype=jnp.int32)[:, None]
    bucket_grad = bucket_grad + jnp.where(
        bucket_row == buckets // 2 - 1,
        far_sums[None, :, 0],
        jnp.where(bucket_row == buckets - 1, far_sums[None, :, 1], 0.0),
    )
    return (
        result.reshape(tokens.shape),
        token_grad.reshape(tokens.shape),
        norm_gain_grad,
        query_grad,
        key_grad,
        value_grad,
        output_grad,
        bucket_grad,
        small[0],
        small[1 : 1 + experts].T,
        expert_in_grad,
        expert_out_grad,
    )


def solution(mesh):
    in_specs = (
        P(("dp", "expert"), None, None),
        P(("dp", "expert"), None, None),
        P(("dp", "expert")),
        P(("dp", "expert"), None),
        P(),
        P(),
        P(),
        P(),
        P(),
        P(),
        P(),
        P(),
        P("expert", None, None),
        P("expert", None, None),
    )
    out_specs = (
        P(("dp", "expert"), None, None),
        P(("dp", "expert"), None, None),
        P(),
        P(),
        P(),
        P(),
        P(),
        P(),
        P(),
        P(),
        P("expert", None, "dp"),
        P("expert", "dp", None),
    )
    return jax.shard_map(
        functools.partial(on_device, mesh.shape["dp"], mesh.shape["expert"]),
        mesh=mesh,
        in_specs=in_specs,
        out_specs=out_specs,
        check_vma=False,
    )
```

time: 527 us -> 390 us (0.74)
  waiting for transfers between devices: 171 us -> 44.7 us
  starting transfers between devices: 122 us -> 91.4 us
  Pallas kernels: 190 us -> 211 us
  other arithmetic: 17.2 us -> 8.6 us
  local copies, waits for them, and re-layouts: 18.8 us -> 27.4 us
    ppermute x69 -> x65, waiting for transfers between devices: 171 us -> 44.7 us  [swap(): lax.ppermute(values, axis, [(place, place ^ distance) for place in range(...]
    ppermute x69 -> x65, starting transfers between devices: 122 us -> 91.4 us  [swap(): lax.ppermute(values, axis, [(place, place ^ distance) for place in range(...]
    unnamed x83 -> x134, local copies, waits for them, and re-layouts: 2.23 us -> 25.8 us
    pallas_call x11 -> x29, Pallas kernels: 190 us -> 211 us  [the longest x1 36.6 us: forward_part(): pl.pallas_call(functools.partial(forward_kernel, plan), grid=(pairs,), ou...]
    convert_element_type x8 -> x0, other arithmetic: 7.77 us -> none  [the longest x4 3.65 us: sum_everywhere(): values = total.astype(BF)]
    add x4 -> x8, other arithmetic: 1.02 us -> 7.87 us  [the longest x2 7.12 us: on_device(): total = total + second.astype(F32)]
    reshape x6 -> x2, local copies, waits for them, and re-layouts: 5.67 us -> 0.05 us  [the longest x1 0.04 us: on_device(): lines.reshape(heads, LINE + 2 * LANES)]
  transfers between devices with their start and end apart: 69 -> 65, of which waited for: 25 -> 14; matrix products, arithmetic and copies ran while one was open for 5% -> 3% of each run, Pallas kernels for 19% -> 41%
where the time goes in v2:
time: 390 us; the launch traced here: 386 us
  Pallas kernels  211 us (54%)
  starting transfers between devices  91.4 us (23%)
  waiting for transfers between devices  44.7 us (11%)
  local copies, waits for them, and re-layouts  27.4 us (7%)
  other arithmetic  8.6 us (2%)
    ppermute x65, starting transfers between devices, swap(): lax.ppermute(values, axis, [(place, place ^ distance) for place in range(...  91.4 us
    ppermute x65, waiting for transfers between devices, swap(): lax.ppermute(values, axis, [(place, place ^ distance) for place in range(...  44.7 us
    pallas_call x1, Pallas kernels, forward_part(): pl.pallas_call(functools.partial(forward_kernel, plan), grid=(pairs,), ou...  36.6 us
    pallas_call x1, Pallas kernels, backward_part(): pl.pallas_call(backward_kernel, grid=(pairs,), out_shape=[shape_of((4, se...  28.7 us
    unnamed x134, local copies, waits for them, and re-layouts  25.8 us
    pallas_call x1, Pallas kernels, expert_part(): pl.pallas_call(functools.partial(expert_kernel, plan), grid=(steps,), out...  24.6 us
    pallas_call x3, Pallas kernels, weight_grad_part(): pl.pallas_call(functools.partial(weight_grad_kernel, transposed, len(term...  17.9 us
    pallas_call x4, Pallas kernels, projection_grad_part(): pl.pallas_call(projection_grad_kernel, grid_spec=pltpu.PrefetchScalarGrid...  17.4 us
  transfers between devices with their start and end apart: 65, of which 14 were waited for; matrix products, arithmetic and copies ran while one was open for 3% of the time, Pallas kernels for 41%

profile of v2, /device:TPU:0, one launch (start us, length us, event | category | flops | bytes accessed | tf_op | source)
XLA Modules:
  0.0 386.3 jit_solution(9850957000382535031)
XLA Ops:
  1.3 5.2 %slots.1 = (s32[1,1024]{1,0:T(1,128)}, s32[1024,128]{1,0:T(8,128)}, bf16[320,768]{1,0:T(8,128)(2,1)}, bf16[320,768]{1,0:T(8,128)(2,1)}, bf16[320,768]{1,0:T(8,128)(2,1)}, /*index=5*/bf16[320,768]{1,0:T(8,128)(2,1)}) custom-call(s32[1]{0:T(128)} %bitcast.3.expert_ref, s32[1]{0:T(128)S(6)} %copy.28.length_ref, s32[1,1024]{1,0:T(1,128)} %routes_ref.1, ...), custom_call_target="tpu_custom_call" | custom-call | tf_op jit(solution)/shard_map/slots/pallas_call | solution.py:137
  6.5 3.0 collective-permute-start
  9.6 2.6 collective-permute-start.1
  12.2 36.6 %attention_forward.1 = (bf16[12,1024,1024]{2,1,0:T(8,128)(2,1)}, bf16[3,6,1024,128]{3,2,1,0:T(8,128)(2,1)}, bf16[2,1024,768]{2,1,0:T(8,128)(2,1)}, f32[6,1024,12...) custom-call(s32[1]{0:T(128)} %bitcast.3.expert_ref, ...), custom_call_target="tpu_custom_call" | custom-call | tf_op jit(solution)/shard_map/attention_forward/pallas_call | solution.py:260
  49.8 6.7 %collective-permute-start.7 = (bf16[320,768]{1,0:T(8,128)(2,1)}, bf16[320,768]{1,0:T(8,128)(2,1)S(1)}, u32[]{:S(2)}, u32[]{:S(2)}) collective-permute-start(bf16[320,768]{1,0:T(8,128)(2,1)} %get-tuple-element.178), channel_id=1, source_target_pairs={{0,2},{1,3},{2,0},{3,1},{4,6},{5,7},{6,4},{7,5},{8,10},{9,11},{10,... | collective-permute-start | bytes 1474568 | tf_op jit(solution)/shard_map/ppermute | solution.py:752
  61.4 2.3 copy-done.2
  65.8 9.6 %expert_activation_gradient.1 = (bf16[1280,768]{1,0:T(8,128)(2,1)S(1)}, bf16[1280,3072]{1,0:T(8,128)(2,1)S(1)}) custom-call(bf16[1,3072,768]{2,1,0:T(8,128)(2,1)S(1)} %copy-done.2, bf16[320,768]{1,0:T(8,128)(2,1)S(1)} %copy-done.15, bf16[320,768]{1,0:T(8,128)(2,1)S(1)} %collective-permute-done.refs_1_, bf16[320,768]{1,0:T(8,128)(2,1)S(1)} %collective-permute-done.1.refs_2_, ...), custom_call_target="tpu_custom_call" | custom-call | tf_op jit(solution)/shard_map/expert_activation_gradient/pallas_call | solution.py:320
  75.3 3.1 copy-done.3
  79.7 14.0 %collective-permute-done.8.refs_2_ = bf16[320,768]{1,0:T(8,128)(2,1)S(1)} collective-permute-done((bf16[320,768]{1,0:T(8,128)(2,1)}, bf16[320,768]{1,0:T(8,128)(2,1)S(1)}, u32[]{:S(2)}, u32[]{:S(2)}) %collective-permute-start.8) | collective-permute-done | bytes 491552 | tf_op jit(solution)/shard_map/ppermute | solution.py:752
  98.7 24.6 %expert_rows.1 = (bf16[1280,3072]{1,0:T(8,128)(2,1)}, bf16[1280,3072]{1,0:T(8,128)(2,1)}, bf16[1280,768]{1,0:T(8,128)(2,1)S(1)}, bf16[1280,768]{1,0:T(8,128)(2,1...) custom-call(s32[1]{0:T(128)} %bitcast.3.expert_ref, ...), custom_call_target="tpu_custom_call" | custom-call | tf_op jit(solution)/shard_map/expert_rows/pallas_call | solution.py:401
  123.3 3.5 copy-done.1
  126.8 4.3 %expert_weight_gradients.5 = bf16[2,768,768]{2,1,0:T(8,128)(2,1)S(1)} custom-call(s32[2]{0:T(128)S(1)} %get-tuple-element.304.refs_0_, bf16[1280,3072]{1,0:T(8,128)(2,1)S(1)} %copy-done.1, bf16[1280,768]{1,0:T(8,128)(2,1)S(1)} %get-tuple-element.188.refs_5_.refs_2_), custom_call_target="tpu_custom_call" | custom-call | tf_op jit(solution)/shard_map/expert_weight_gradients/pallas_call | solution.py:467
  132.8 4.3 %expert_weight_gradients.4 = bf16[2,768,768]{2,1,0:T(8,128)(2,1)S(1)} custom-call(s32[2]{0:T(128)S(1)} %get-tuple-element.306.refs_0_, bf16[1280,3072]{1,0:T(8,128)(2,1)S(1)} %copy-done, bf16[1280,768]{1,0:T(8,128)(2,1)S(1)} %copy-done.4), custom_call_target="tpu_custom_call" | custom-call | tf_op jit(solution)/shard_map/expert_weight_gradients/pallas_call | solution.py:467
  138.7 9.9 %collective-permute-start.14 = (bf16[320,768]{1,0:T(8,128)(2,1)S(1)}, bf16[320,768]{1,0:T(8,128)(2,1)S(1)}, u32[]{:S(2)}, u32[]{:S(2)}) collective-permute-start(bf16[320,768]{1,0:T(8,128)(2,1)S(1)} %get-tuple-element.193), channel_id=1, source_target_pairs={{0,2},{1,3},{2,0},{3,1},{4,6},{5,7},{6,4},{7,5},{8,10},{9,11},{10,... | collective-permute-start | bytes 1474568 | tf_op jit(solution)/shard_map/ppermute | solution.py:752
  151.0 8.2 %expert_output.1 = (bf16[320,768]{1,0:T(8,128)(2,1)S(1)}, bf16[320,768]{1,0:T(8,128)(2,1)}, bf16[320,768]{1,0:T(8,128)(2,1)}, bf16[320,768]{1,0:T(8,128)(2,1)S(1)}) custom-call(bf16[1280,3072]{1,0:T(8,128)(2,1)S(1)} %copy-done, bf16[1,3072,768]{2,1,0:T(8,128)(2,1)S(1)} %bitcast.18, f32[1280,1]{1,0:T(8,128)S(1)} %get-tuple-element.196.gate_ref), custom_call_target="tpu_custom_call" | custom-call | tf_op jit(solution)/shard_map/expert_output/pallas_call | solution.py:498
  159.2 9.2 %expert_weight_gradients.3 = (bf16[2,768,768]{2,1,0:T(8,128)(2,1)S(1)}, bf16[2,768,768]{2,1,0:T(8,128)(2,1)S(1)}) custom-call(s32[2]{0:T(128)S(1)} %get-tuple-element.307.refs_0_, s32[2]{0:T(128)S(1)} %get-tuple-element.305.refs_1_, bf16[1280,3072]{1,0:T(8,128)(2,1)S(1)} %copy-done, bf16[1280,3072]{1,0:T(8,128)(2,1)} %get-tuple-element.186.refs_3_.refs_1_, ...), custom_call_target="tpu_custom_call" | custom-call | tf_op jit(solution)/shard_map/expert_weight_gradients/pallas_call | solution.py:467
  171.3 13.4 %collective-permute-done.15.refs_2_ = bf16[320,768]{1,0:T(8,128)(2,1)S(1)} collective-permute-done((bf16[320,768]{1,0:T(8,128)(2,1)S(1)}, bf16[320,768]{1,0:T(8,128)(2,1)S(1)}, u32[]{:S(2)}, u32[]{:S(2)}) %collective-permute-start.15) | collective-permute-done | bytes 491552 | tf_op jit(solution)/shard_map/ppermute | solution.py:752
  190.3 4.3 %later_sums.1 = (bf16[1,768,768]{2,1,0:T(8,128)(2,1)}, bf16[1,768,768]{2,1,0:T(8,128)(2,1)}) custom-call(bf16[2,768,768]{2,1,0:T(8,128)(2,1)} %copy-done.5, bf16[2,768,768]{2,1,0:T(8,128)(2,1)} %copy-done.7, bf16[2,768,768]{2,1,0:T(8,128)(2,1)} %collective-permute-done.21.refs_2_, bf16[2,768,768]{2,1,0:T(8,128)(2,1)} %collective-permute-done.22.refs_3_), custom_call_target="tpu_custom_call" | custom-call | tf_op jit(solution)/shard_map/later_sums/pallas_call | solution.py:443
  196.6 9.9 %collective-permute-start.23 = (bf16[320,768]{1,0:T(8,128)(2,1)}, bf16[320,768]{1,0:T(8,128)(2,1)S(1)}, u32[]{:S(2)}, u32[]{:S(2)}) collective-permute-start(bf16[320,768]{1,0:T(8,128)(2,1)} %get-tuple-element.215), channel_id=1, source_target_pairs={{0,2},{1,3},{2,0},{3,1},{4,6},{5,7},{6,4},{7,5},{8,10},{9,11},{10,... | collective-permute-start | bytes 1474568 | tf_op jit(solution)/shard_map/ppermute | solution.py:752
  208.9 10.3 %expert_norm_backward.1 = (f32[1024,768]{1,0:T(8,128)}, bf16[1024,768]{1,0:T(8,128)(2,1)}, bf16[1024,768]{1,0:T(8,128)(2,1)}, f32[1,768]{1,0:T(1,128)}) custom-call(s32[1]{0:T(128)} %bitcast.3.expert_ref, s32[1]{0:T(128)S(6)} %copy.28.length_ref, s32[1024,128]{1,0:T(8,128)} %get-tuple-element.161.column_ref, f32[1024,768]{1,0:T(8,128)} %get-tuple-element.274.resid_ref, ...), custom_call_target="tpu_custom_call" | custom-call | tf_op jit(solution)/shard_map/expert_norm_backward/pallas_call | solution.py:572
  219.2 28.7 %attention_backward.1 = (bf16[4,1024,768]{2,1,0:T(8,128)(2,1)}, f32[6,2,768]{2,1,0:T(2,128)}) custom-call(bf16[3,6,1024,128]{3,2,1,0:T(8,128)(2,1)} %get-tuple-element.159.qkv_ref, bf16[12,1024,1024]{2,1,0:T(8,128)(2,1)} %get-tuple-element.160.probs_ref, bf16[2,1024,768]{2,1,0:T(8,128)(2,1)} %get-tuple-element.232.mixed_ref.left_ref, ...), custom_call_target="tpu_custom_call" | custom-call | tf_op jit(solution)/shard_map/attention_backward/pallas_call | solution.py:661
  248.0 4.5 %projection_gradient.4 = bf16[768,768]{1,0:T(8,128)(2,1)} custom-call(s32[1]{0:T(128)} %constant.158.clone.1.left_places_ref.place_ref, s32[1]{0:T(128)} %bitcast.8.right_places_ref.left_places_ref, bf16[2,1024,768]{2,1,0:T(8,128)(2,1)} %get-tuple-element.232.mixed_ref.left_ref, bf16[4,1024,768]{2,1,0:T(8,128)(2,1)} %get-tuple-element.238.right_ref.back_ref), custom_call_target="tpu_custom_call" | custom-call | tf_op jit(solution)/shard_map/projection_gradient/pallas_call | solution.py:693
  252.5 4.3 %projection_gradient.5 = bf16[768,768]{1,0:T(8,128)(2,1)} custom-call(s32[1]{0:T(128)} %bitcast.8.right_places_ref.left_places_ref, s32[1]{0:T(128)} %bitcast.9.right_places_ref, bf16[2,1024,768]{2,1,0:T(8,128)(2,1)} %get-tuple-element.232.mixed_ref.left_ref, bf16[4,1024,768]{2,1,0:T(8,128)(2,1)} %get-tuple-element.238.right_ref.back_ref), custom_call_target="tpu_custom_call" | custom-call | tf_op jit(solution)/shard_map/projection_gradient/pallas_call | solution.py:693
  257.9 4.3 %projection_gradient.6.refs_0_ = bf16[768,768]{1,0:T(8,128)(2,1)} custom-call(s32[1]{0:T(128)} %constant.158.clone.1.left_places_ref.place_ref, s32[1]{0:T(128)} %bitcast.2.right_places_ref.left_places_ref.place_ref, bf16[2,1024,768]{2,1,0:T(8,128)(2,1)} %get-tuple-element.232.mixed_ref.left_ref, bf16[4,1024,768]{2,1,0:T(8,128)(2,1)} %get-tuple-element.238.right_ref.back_ref), custom_call_target="tpu_custom_call" | custom-call | tf_op jit(solution)/shard_map/projection_gradient/pallas_call | solution.py:693
  262.2 2.9 share.6
  267.8 4.3 %projection_gradient.7.refs_0_ = bf16[768,768]{1,0:T(8,128)(2,1)} custom-call(s32[1]{0:T(128)} %bitcast.2.right_places_ref.left_places_ref.place_ref, s32[1]{0:T(128)} %bitcast.10.right_places_ref, bf16[2,1024,768]{2,1,0:T(8,128)(2,1)} %get-tuple-element.232.mixed_ref.left_ref, bf16[4,1024,768]{2,1,0:T(8,128)(2,1)} %get-tuple-element.238.right_ref.back_ref), custom_call_target="tpu_custom_call" | custom-call | tf_op jit(solution)/shard_map/projection_gradient/pallas_call | solution.py:693
  272.1 2.9 share.7
  275.0 3.0 collective-permute-start.45
  278.0 2.9 collective-permute-done.45
  282.4 2.8 collective-permute-start.46
  285.2 2.9 collective-permute-done.46
  291.8 9.6 %token_gradient.1 = f32[1024,768]{1,0:T(8,128)} custom-call(bf16[4,1024,768]{2,1,0:T(8,128)(2,1)} %get-tuple-element.238.right_ref.back_ref, bf16[768,768]{1,0:T(8,128)(2,1)} %refs_0_.2, bf16[768,768]{1,0:T(8,128)(2,1)} %refs_1_.1, bf16[768,768]{1,0:T(8,128)(2,1)} %refs_0_.3, bf16[1024,768]{1,0:T(8,128)(2,1)} %bitcast.21, bf16[768]{0:T(1024)(128)(2,1)} %gain_ref.3, ...), custom_call_target="tpu_custom_call" | custom-call | tf_op jit(solution)/shard_map/token_gradient/pallas_call | solution.py:738
  301.4 2.0 share.8
  309.5 2.0 share.10
  312.4 2.1 collective-permute-start.53
  318.5 2.2 collective-permute-start.56
  320.7 2.3 collective-permute-done.56
  323.0 2.7 collective-permute-start.37
  329.7 2.8 collective-permute-start.58
  343.6 1.9 collective-permute-start.60
  346.0 7.0 %result.1 = bf16[1024,768]{1,0:T(8,128)(2,1)} custom-call(s32[1]{0:T(128)} %bitcast.3.expert_ref, s32[1]{0:T(128)S(6)} %copy.28.length_ref, s32[1024,128]{1,0:T(8,128)} %get-tuple-element.161.column_ref, f32[1024,768]{1,0:T(8,128)} %get-tuple-element.274.resid_ref, bf16[320,768]{1,0:T(8,128)(2,1)} %copy-done.10, bf16[320,768]{1,0:T(8,128)(2,1)} %copy-done.26, ...), custom_call_target="tpu_custom_call" | custom-call | tf_op jit(solution)/shard_map/result/pallas_call | solution.py:526
  353.0 3.6 convert_add_fusion
  357.7 3.6 convert_add_fusion.1
  361.3 3.0 collective-permute-done.62.refs_3_
  365.0 2.3 join.7.own_ref
  367.4 2.3 join.6.own_ref
  373.5 5.0 %widen.3 = (f32[768,768]{1,0:T(8,128)}, f32[768,768]{1,0:T(8,128)}, f32[1,768]{1,0:T(1,128)}) custom-call(s32[1]{0:T(128)} %bitcast.2.right_places_ref.left_places_ref.place_ref, bf16[768,768]{1,0:T(8,128)(2,1)} %join.7.own_ref, bf16[768,768]{1,0:T(8,128)(2,1)} %copy-done.25, bf16[768,768]{1,0:T(8,128)(2,1)} %refs_0_.3), custom_call_target="tpu_custom_call" | custom-call | tf_op jit(solution)/shard_map/widen/pallas_call | solution.py:912
  379.5 5.3 %widen.2 = (f32[768,768]{1,0:T(8,128)}, f32[768,768]{1,0:T(8,128)}, f32[1,768]{1,0:T(1,128)}) custom-call(s32[1]{0:T(128)} %bitcast.2.right_places_ref.left_places_ref.place_ref, bf16[768,768]{1,0:T(8,128)(2,1)} %join.6.own_ref, bf16[768,768]{1,0:T(8,128)(2,1)} %copy-done.24, bf16[768,768]{1,0:T(8,128)(2,1)} %refs_0_.2, bf16[768,768]{1,0:T(8,128)(2,1)} %refs_1_.1), custom_call_target="tpu_custom_call" | custom-call | tf_op jit(solution)/shard_map/widen/pallas_call | solution.py:912
  (270 shorter events, 75.8 us)
Async XLA Ops:
  6.5 42.2 %collective-permute-start = (bf16[320,768]{1,0:T(8,128)(2,1)}, bf16[320,768]{1,0:T(8,128)(2,1)S(1)}, u32[]{:S(2)}, u32[]{:S(2)}) collective-permute-start(bf16[320,768]{1,0:T(8,128)(2,1)} %get-tuple-element.168), channel_id=1, source_target_pairs={{0,2},{1,3},{2,0},{3,1},{4,6},{5,7},{6,4},{7,5},{8,10},{9,11},{10,... | collective-permute-start | bytes 1474568 | tf_op jit(solution)/shard_map/ppermute | solution.py:752
  9.6 39.2 %collective-permute-start.1 = (bf16[320,768]{1,0:T(8,128)(2,1)}, bf16[320,768]{1,0:T(8,128)(2,1)S(1)}, u32[]{:S(2)}, u32[]{:S(2)}) collective-permute-start(bf16[320,768]{1,0:T(8,128)(2,1)} %get-tuple-element.169), channel_id=1, source_target_pairs={{0,4},{1,5},{2,6},{3,7},{4,0},{5,1},{6,2},{7,3},{8,12},{9,13},{10,... | collective-permute-start | bytes 1474568 | tf_op jit(solution)/shard_map/ppermute | solution.py:752
  12.1 36.6 %collective-permute-start.2 = (bf16[320,768]{1,0:T(8,128)(2,1)}, bf16[320,768]{1,0:T(8,128)(2,1)S(1)}, u32[]{:S(2)}, u32[]{:S(2)}) collective-permute-start(bf16[320,768]{1,0:T(8,128)(2,1)} %get-tuple-element.170), channel_id=1, source_target_pairs={{0,6},{1,7},{2,4},{3,5},{4,2},{5,3},{6,0},{7,1},{8,14},{9,15},{10,... | collective-permute-start | bytes 1474568 | tf_op jit(solution)/shard_map/ppermute | solution.py:752
  48.8 10.4 %collective-permute-start.4 = (bf16[320,768]{1,0:T(8,128)(2,1)S(1)}, bf16[320,768]{1,0:T(8,128)(2,1)S(1)}, u32[]{:S(2)}, u32[]{:S(2)}) collective-permute-start(bf16[320,768]{1,0:T(8,128)(2,1)S(1)} %collective-permute-done.refs_1_), channel_id=1, source_target_pairs={{0,1},{1,0},{2,3},{3,2},{4,5},{5,4},{6,7},{7,6},{8,9},{9,8},{10,11... | collective-permute-start | bytes 1474568 | tf_op jit(solution)/shard_map/ppermute | solution.py:752
  49.3 12.0 %collective-permute-start.5 = (bf16[320,768]{1,0:T(8,128)(2,1)S(1)}, bf16[320,768]{1,0:T(8,128)(2,1)}, u32[]{:S(2)}, u32[]{:S(2)}) collective-permute-start(bf16[320,768]{1,0:T(8,128)(2,1)S(1)} %collective-permute-done.1.refs_2_), channel_id=1, source_target_pairs={{0,1},{1,0},{2,3},{3,2},{4,5},{5,4},{6,7},{7,6},{8,9},{9,8},{10,11... | collective-permute-start | bytes 1474568 | tf_op jit(solution)/shard_map/ppermute | solution.py:752
  49.4 11.9 %collective-permute-start.6 = (bf16[320,768]{1,0:T(8,128)(2,1)S(1)}, bf16[320,768]{1,0:T(8,128)(2,1)}, u32[]{:S(2)}, u32[]{:S(2)}) collective-permute-start(bf16[320,768]{1,0:T(8,128)(2,1)S(1)} %collective-permute-done.2.refs_3_), channel_id=1, source_target_pairs={{0,1},{1,0},{2,3},{3,2},{4,5},{5,4},{6,7},{7,6},{8,9},{9,8},{10,11... | collective-permute-start | bytes 1474568 | tf_op jit(solution)/shard_map/ppermute | solution.py:752
  49.8 29.8 %collective-permute-start.7 = (bf16[320,768]{1,0:T(8,128)(2,1)}, bf16[320,768]{1,0:T(8,128)(2,1)S(1)}, u32[]{:S(2)}, u32[]{:S(2)}) collective-permute-start(bf16[320,768]{1,0:T(8,128)(2,1)} %get-tuple-element.178), channel_id=1, source_target_pairs={{0,2},{1,3},{2,0},{3,1},{4,6},{5,7},{6,4},{7,5},{8,10},{9,11},{10,... | collective-permute-start | bytes 1474568 | tf_op jit(solution)/shard_map/ppermute | solution.py:752
  57.4 36.3 %collective-permute-start.8 = (bf16[320,768]{1,0:T(8,128)(2,1)}, bf16[320,768]{1,0:T(8,128)(2,1)S(1)}, u32[]{:S(2)}, u32[]{:S(2)}) collective-permute-start(bf16[320,768]{1,0:T(8,128)(2,1)} %get-tuple-element.179), channel_id=1, source_target_pairs={{0,4},{1,5},{2,6},{3,7},{4,0},{5,1},{6,2},{7,3},{8,12},{9,13},{10,... | collective-permute-start | bytes 1474568 | tf_op jit(solution)/shard_map/ppermute | solution.py:752
  60.0 33.7 %collective-permute-start.9 = (bf16[320,768]{1,0:T(8,128)(2,1)}, bf16[320,768]{1,0:T(8,128)(2,1)S(1)}, u32[]{:S(2)}, u32[]{:S(2)}) collective-permute-start(bf16[320,768]{1,0:T(8,128)(2,1)} %get-tuple-element.180), channel_id=1, source_target_pairs={{0,6},{1,7},{2,4},{3,5},{4,2},{5,3},{6,0},{7,1},{8,14},{9,15},{10,... | collective-permute-start | bytes 1474568 | tf_op jit(solution)/shard_map/ppermute | solution.py:752
  131.2 57.6 %collective-permute-start.22 = (bf16[2,768,768]{2,1,0:T(8,128)(2,1)S(1)}, bf16[2,768,768]{2,1,0:T(8,128)(2,1)}, u32[]{:S(2)}, u32[]{:S(2)}) collective-permute-start(bf16[2,768,768]{2,1,0:T(8,128)(2,1)S(1)} %expert_weight_gradients.5), channel_id=1, source_target_pairs={{0,16},{8,24},{16,0},{24,8},{1,17},{9,25},{17,1},{25,9},{2,18},{10... | collective-permute-start | bytes 7077896 | tf_op jit(solution)/shard_map/ppermute | solution.py:752
  137.1 53.2 %collective-permute-start.21 = (bf16[2,768,768]{2,1,0:T(8,128)(2,1)S(1)}, bf16[2,768,768]{2,1,0:T(8,128)(2,1)}, u32[]{:S(2)}, u32[]{:S(2)}) collective-permute-start(bf16[2,768,768]{2,1,0:T(8,128)(2,1)S(1)} %expert_weight_gradients.4), channel_id=1, source_target_pairs={{0,8},{8,0},{16,24},{24,16},{1,9},{9,1},{17,25},{25,17},{2,10},{10... | collective-permute-start | bytes 7077896 | tf_op jit(solution)/shard_map/ppermute | solution.py:752
  138.7 32.6 %collective-permute-start.14 = (bf16[320,768]{1,0:T(8,128)(2,1)S(1)}, bf16[320,768]{1,0:T(8,128)(2,1)S(1)}, u32[]{:S(2)}, u32[]{:S(2)}) collective-permute-start(bf16[320,768]{1,0:T(8,128)(2,1)S(1)} %get-tuple-element.193), channel_id=1, source_target_pairs={{0,2},{1,3},{2,0},{3,1},{4,6},{5,7},{6,4},{7,5},{8,10},{9,11},{10,... | collective-permute-start | bytes 1474568 | tf_op jit(solution)/shard_map/ppermute | solution.py:752
  148.5 36.1 %collective-permute-start.15 = (bf16[320,768]{1,0:T(8,128)(2,1)S(1)}, bf16[320,768]{1,0:T(8,128)(2,1)S(1)}, u32[]{:S(2)}, u32[]{:S(2)}) collective-permute-start(bf16[320,768]{1,0:T(8,128)(2,1)S(1)} %get-tuple-element.194), channel_id=1, source_target_pairs={{0,4},{1,5},{2,6},{3,7},{4,0},{5,1},{6,2},{7,3},{8,12},{9,13},{10,... | collective-permute-start | bytes 1474568 | tf_op jit(solution)/shard_map/ppermute | solution.py:752
  149.6 35.1 %collective-permute-start.16 = (bf16[320,768]{1,0:T(8,128)(2,1)S(1)}, bf16[320,768]{1,0:T(8,128)(2,1)S(1)}, u32[]{:S(2)}, u32[]{:S(2)}) collective-permute-start(bf16[320,768]{1,0:T(8,128)(2,1)S(1)} %get-tuple-element.195), channel_id=1, source_target_pairs={{0,6},{1,7},{2,4},{3,5},{4,2},{5,3},{6,0},{7,1},{8,14},{9,15},{10,... | collective-permute-start | bytes 1474568 | tf_op jit(solution)/shard_map/ppermute | solution.py:752
  194.6 53.4 %collective-permute-start.26 = (bf16[1,768,768]{2,1,0:T(8,128)(2,1)}, bf16[1,768,768]{2,1,0:T(8,128)(2,1)}, u32[]{:S(2)}, u32[]{:S(2)}) collective-permute-start(bf16[1,768,768]{2,1,0:T(8,128)(2,1)} %get-tuple-element.208), channel_id=1, source_target_pairs={{0,16},{8,24},{16,0},{24,8},{1,17},{9,25},{17,1},{25,9},{2,18},{10... | collective-permute-start | bytes 3538952 | tf_op jit(solution)/shard_map/ppermute | solution.py:752
  195.1 52.9 %collective-permute-start.27 = (bf16[1,768,768]{2,1,0:T(8,128)(2,1)}, bf16[1,768,768]{2,1,0:T(8,128)(2,1)}, u32[]{:S(2)}, u32[]{:S(2)}) collective-permute-start(bf16[1,768,768]{2,1,0:T(8,128)(2,1)} %get-tuple-element.209), channel_id=1, source_target_pairs={{0,8},{8,0},{16,24},{24,16},{1,9},{9,1},{17,25},{25,17},{2,10},{10... | collective-permute-start | bytes 3538952 | tf_op jit(solution)/shard_map/ppermute | solution.py:752
  196.6 51.3 %collective-permute-start.23 = (bf16[320,768]{1,0:T(8,128)(2,1)}, bf16[320,768]{1,0:T(8,128)(2,1)S(1)}, u32[]{:S(2)}, u32[]{:S(2)}) collective-permute-start(bf16[320,768]{1,0:T(8,128)(2,1)} %get-tuple-element.215), channel_id=1, source_target_pairs={{0,2},{1,3},{2,0},{3,1},{4,6},{5,7},{6,4},{7,5},{8,10},{9,11},{10,... | collective-permute-start | bytes 1474568 | tf_op jit(solution)/shard_map/ppermute | solution.py:752
  206.5 41.5 %collective-permute-start.24 = (bf16[320,768]{1,0:T(8,128)(2,1)}, bf16[320,768]{1,0:T(8,128)(2,1)}, u32[]{:S(2)}, u32[]{:S(2)}) collective-permute-start(bf16[320,768]{1,0:T(8,128)(2,1)} %get-tuple-element.216), channel_id=1, source_target_pairs={{0,4},{1,5},{2,6},{3,7},{4,0},{5,1},{6,2},{7,3},{8,12},{9,13},{10,... | collective-permute-start | bytes 1474568 | tf_op jit(solution)/shard_map/ppermute | solution.py:752
  207.5 40.5 %collective-permute-start.25 = (bf16[320,768]{1,0:T(8,128)(2,1)S(1)}, bf16[320,768]{1,0:T(8,128)(2,1)}, u32[]{:S(2)}, u32[]{:S(2)}) collective-permute-start(bf16[320,768]{1,0:T(8,128)(2,1)S(1)} %get-tuple-element.217), channel_id=1, source_target_pairs={{0,6},{1,7},{2,4},{3,5},{4,2},{5,3},{6,0},{7,1},{8,14},{9,15},{10,... | collective-permute-start | bytes 1474568 | tf_op jit(solution)/shard_map/ppermute | solution.py:752
  252.5 9.8 %collective-permute-start.28 = (bf16[768,768]{1,0:T(8,128)(2,1)}, bf16[768,768]{1,0:T(8,128)(2,1)}, u32[]{:S(2)}, u32[]{:S(2)}) collective-permute-start(bf16[768,768]{1,0:T(8,128)(2,1)} %projection_gradient.4), channel_id=1, source_target_pairs={{0,1},{1,0},{2,3},{3,2},{4,5},{5,4},{6,7},{7,6},{8,9},{9,8},{10,11... | collective-permute-start | bytes 3538952 | tf_op jit(solution)/shard_map/ppermute | solution.py:752
  256.8 10.8 %collective-permute-start.32 = (bf16[768,768]{1,0:T(8,128)(2,1)}, bf16[768,768]{1,0:T(8,128)(2,1)}, u32[]{:S(2)}, u32[]{:S(2)}) collective-permute-start(bf16[768,768]{1,0:T(8,128)(2,1)} %projection_gradient.5), channel_id=1, source_target_pairs={{0,1},{1,0},{2,3},{3,2},{4,5},{5,4},{6,7},{7,6},{8,9},{9,8},{10,11... | collective-permute-start | bytes 3538952 | tf_op jit(solution)/shard_map/ppermute | solution.py:752
  257.3 17.7 %collective-permute-start.49 = (bf16[320,768]{1,0:T(8,128)(2,1)S(1)}, bf16[320,768]{1,0:T(8,128)(2,1)}, u32[]{:S(2)}, u32[]{:S(2)}) collective-permute-start(bf16[320,768]{1,0:T(8,128)(2,1)S(1)} %collective-permute-done.23.refs_1_), channel_id=1, source_target_pairs={{0,1},{1,0},{2,3},{3,2},{4,5},{5,4},{6,7},{7,6},{8,9},{9,8},{10,11... | collective-permute-start | bytes 1474568 | tf_op jit(solution)/shard_map/ppermute | solution.py:752
  257.8 24.6 %collective-permute-start.50 = (bf16[320,768]{1,0:T(8,128)(2,1)}, bf16[320,768]{1,0:T(8,128)(2,1)}, u32[]{:S(2)}, u32[]{:S(2)}) collective-permute-start(bf16[320,768]{1,0:T(8,128)(2,1)} %collective-permute-done.24.refs_2_), channel_id=1, source_target_pairs={{0,1},{1,0},{2,3},{3,2},{4,5},{5,4},{6,7},{7,6},{8,9},{9,8},{10,11... | collective-permute-start | bytes 1474568 | tf_op jit(solution)/shard_map/ppermute | solution.py:752
  265.1 23.6 %collective-permute-start.29 = (bf16[192,768]{1,0:T(8,128)(2,1)}, bf16[192,768]{1,0:T(8,128)(2,1)}, u32[]{:S(2)}, u32[]{:S(2)}) collective-permute-start(bf16[192,768]{1,0:T(8,128)(2,1)} %get-tuple-element.226), channel_id=1, source_target_pairs={{0,8},{8,0},{16,24},{24,16},{1,9},{9,1},{17,25},{25,17},{2,10},{10... | collective-permute-start | bytes 884744 | tf_op jit(solution)/shard_map/ppermute | solution.py:752
  265.6 24.5 %collective-permute-start.30 = (bf16[192,768]{1,0:T(8,128)(2,1)}, bf16[192,768]{1,0:T(8,128)(2,1)S(1)}, u32[]{:S(2)}, u32[]{:S(2)}) collective-permute-start(bf16[192,768]{1,0:T(8,128)(2,1)} %get-tuple-element.227), channel_id=1, source_target_pairs={{0,16},{8,24},{16,0},{24,8},{1,17},{9,25},{17,1},{25,9},{2,18},{10... | collective-permute-start | bytes 884744 | tf_op jit(solution)/shard_map/ppermute | solution.py:752
  267.6 35.8 %collective-permute-start.51 = (bf16[320,768]{1,0:T(8,128)(2,1)}, bf16[320,768]{1,0:T(8,128)(2,1)S(1)}, u32[]{:S(2)}, u32[]{:S(2)}) collective-permute-start(bf16[320,768]{1,0:T(8,128)(2,1)} %collective-permute-done.25.refs_3_), channel_id=1, source_target_pairs={{0,1},{1,0},{2,3},{3,2},{4,5},{5,4},{6,7},{7,6},{8,9},{9,8},{10,11... | collective-permute-start | bytes 1474568 | tf_op jit(solution)/shard_map/ppermute | solution.py:752
  280.9 10.7 %collective-permute-start.31 = (bf16[192,768]{1,0:T(8,128)(2,1)S(1)}, bf16[192,768]{1,0:T(8,128)(2,1)S(1)}, u32[]{:S(2)}, u32[]{:S(2)}) collective-permute-start(bf16[192,768]{1,0:T(8,128)(2,1)S(1)} %copy-done.64), channel_id=1, source_target_pairs={{0,24},{8,16},{16,8},{24,0},{1,25},{9,17},{17,9},{25,1},{2,26},{10... | collective-permute-start | bytes 884744 | tf_op jit(solution)/shard_map/ppermute | solution.py:752
  288.1 18.4 %collective-permute-start.42 = (bf16[192,768]{1,0:T(8,128)(2,1)}, bf16[192,768]{1,0:T(8,128)(2,1)S(1)}, u32[]{:S(2)}, u32[]{:S(2)}) collective-permute-start(bf16[192,768]{1,0:T(8,128)(2,1)} %get-tuple-element.235), channel_id=1, source_target_pairs={{0,8},{8,0},{16,24},{24,16},{1,9},{9,1},{17,25},{25,17},{2,10},{10... | collective-permute-start | bytes 884744 | tf_op jit(solution)/shard_map/ppermute | solution.py:752
  288.7 19.2 %collective-permute-start.43 = (bf16[192,768]{1,0:T(8,128)(2,1)}, bf16[192,768]{1,0:T(8,128)(2,1)S(1)}, u32[]{:S(2)}, u32[]{:S(2)}) collective-permute-start(bf16[192,768]{1,0:T(8,128)(2,1)} %get-tuple-element.236), channel_id=1, source_target_pairs={{0,16},{8,24},{16,0},{24,8},{1,17},{9,25},{17,1},{25,9},{2,18},{10... | collective-permute-start | bytes 884744 | tf_op jit(solution)/shard_map/ppermute | solution.py:752
  290.2 17.8 %collective-permute-start.44 = (bf16[192,768]{1,0:T(8,128)(2,1)}, bf16[192,768]{1,0:T(8,128)(2,1)S(1)}, u32[]{:S(2)}, u32[]{:S(2)}) collective-permute-start(bf16[192,768]{1,0:T(8,128)(2,1)} %get-tuple-element.237), channel_id=1, source_target_pairs={{0,24},{8,16},{16,8},{24,0},{1,25},{9,17},{17,9},{25,1},{2,26},{10... | collective-permute-start | bytes 884744 | tf_op jit(solution)/shard_map/ppermute | solution.py:752
  291.7 13.2 %collective-permute-start.47 = (f32[21,768]{1,0:T(8,128)S(1)}, f32[21,768]{1,0:T(8,128)S(1)}, u32[]{:S(2)}, u32[]{:S(2)}) collective-permute-start(f32[21,768]{1,0:T(8,128)S(1)} %add.158), channel_id=1, source_target_pairs={{0,1},{1,0},{2,3},{3,2},{4,5},{5,4},{6,7},{7,6},{8,9},{9,8},{10,11... | collective-permute-start | bytes 193544 | tf_op jit(solution)/shard_map/ppermute | solution.py:752
  303.4 9.0 %collective-permute-start.33 = (bf16[48,768]{1,0:T(8,128)(2,1)}, bf16[48,768]{1,0:T(8,128)(2,1)S(1)}, u32[]{:S(2)}, u32[]{:S(2)}) collective-permute-start(bf16[48,768]{1,0:T(8,128)(2,1)} %get-tuple-element.245), channel_id=1, source_target_pairs={{0,2},{1,3},{2,0},{3,1},{4,6},{5,7},{6,4},{7,5},{8,10},{9,11},{10,... | collective-permute-start | bytes 221192 | tf_op jit(solution)/shard_map/ppermute | solution.py:752
  304.8 9.7 %collective-permute-start.34 = (bf16[48,768]{1,0:T(8,128)(2,1)}, bf16[48,768]{1,0:T(8,128)(2,1)S(1)}, u32[]{:S(2)}, u32[]{:S(2)}) collective-permute-start(bf16[48,768]{1,0:T(8,128)(2,1)} %get-tuple-element.246), channel_id=1, source_target_pairs={{0,4},{1,5},{2,6},{3,7},{4,0},{5,1},{6,2},{7,3},{8,12},{9,13},{10,... | collective-permute-start | bytes 221192 | tf_op jit(solution)/shard_map/ppermute | solution.py:752
  306.6 9.6 %collective-permute-start.35 = (bf16[48,768]{1,0:T(8,128)(2,1)}, bf16[48,768]{1,0:T(8,128)(2,1)S(1)}, u32[]{:S(2)}, u32[]{:S(2)}) collective-permute-start(bf16[48,768]{1,0:T(8,128)(2,1)} %get-tuple-element.247), channel_id=1, source_target_pairs={{0,6},{1,7},{2,4},{3,5},{4,2},{5,3},{6,0},{7,1},{8,14},{9,15},{10,... | collective-permute-start | bytes 221192 | tf_op jit(solution)/shard_map/ppermute | solution.py:752
  307.9 10.5 %collective-permute-start.55 = (f32[21,768]{1,0:T(8,128)S(1)}, f32[21,768]{1,0:T(8,128)S(1)}, u32[]{:S(2)}, u32[]{:S(2)}) collective-permute-start(f32[21,768]{1,0:T(8,128)S(1)} %add.159), channel_id=1, source_target_pairs={{0,8},{8,0},{16,24},{24,16},{1,9},{9,1},{17,25},{25,17},{2,10},{10... | collective-permute-start | bytes 193544 | tf_op jit(solution)/shard_map/ppermute | solution.py:752
  311.6 14.2 %collective-permute-start.52 = (bf16[48,768]{1,0:T(8,128)(2,1)}, bf16[48,768]{1,0:T(8,128)(2,1)S(1)}, u32[]{:S(2)}, u32[]{:S(2)}) collective-permute-start(bf16[48,768]{1,0:T(8,128)(2,1)} %get-tuple-element.258), channel_id=1, source_target_pairs={{0,2},{1,3},{2,0},{3,1},{4,6},{5,7},{6,4},{7,5},{8,10},{9,11},{10,... | collective-permute-start | bytes 221192 | tf_op jit(solution)/shard_map/ppermute | solution.py:752
  312.4 15.0 %collective-permute-start.53 = (bf16[48,768]{1,0:T(8,128)(2,1)}, bf16[48,768]{1,0:T(8,128)(2,1)S(1)}, u32[]{:S(2)}, u32[]{:S(2)}) collective-permute-start(bf16[48,768]{1,0:T(8,128)(2,1)} %get-tuple-element.259), channel_id=1, source_target_pairs={{0,4},{1,5},{2,6},{3,7},{4,0},{5,1},{6,2},{7,3},{8,12},{9,13},{10,... | collective-permute-start | bytes 221192 | tf_op jit(solution)/shard_map/ppermute | solution.py:752
  314.6 12.8 %collective-permute-start.54 = (bf16[48,768]{1,0:T(8,128)(2,1)}, bf16[48,768]{1,0:T(8,128)(2,1)S(1)}, u32[]{:S(2)}, u32[]{:S(2)}) collective-permute-start(bf16[48,768]{1,0:T(8,128)(2,1)} %get-tuple-element.260), channel_id=1, source_target_pairs={{0,6},{1,7},{2,4},{3,5},{4,2},{5,3},{6,0},{7,1},{8,14},{9,15},{10,... | collective-permute-start | bytes 221192 | tf_op jit(solution)/shard_map/ppermute | solution.py:752
  318.5 14.0 %collective-permute-start.36 = (bf16[48,768]{1,0:T(8,128)(2,1)}, bf16[48,768]{1,0:T(8,128)(2,1)S(1)}, u32[]{:S(2)}, u32[]{:S(2)}) collective-permute-start(bf16[48,768]{1,0:T(8,128)(2,1)} %share.9.refs_0_), channel_id=1, source_target_pairs={{0,2},{1,3},{2,0},{3,1},{4,6},{5,7},{6,4},{7,5},{8,10},{9,11},{10,... | collective-permute-start | bytes 221192 | tf_op jit(solution)/shard_map/ppermute | solution.py:752
  323.0 11.1 %collective-permute-start.37 = (bf16[48,768]{1,0:T(8,128)(2,1)}, bf16[48,768]{1,0:T(8,128)(2,1)S(1)}, u32[]{:S(2)}, u32[]{:S(2)}) collective-permute-start(bf16[48,768]{1,0:T(8,128)(2,1)} %share.9.refs_0_), channel_id=1, source_target_pairs={{0,4},{1,5},{2,6},{3,7},{4,0},{5,1},{6,2},{7,3},{8,12},{9,13},{10,... | collective-permute-start | bytes 221192 | tf_op jit(solution)/shard_map/ppermute | solution.py:752
  329.7 9.9 %collective-permute-start.57 = (bf16[48,768]{1,0:T(8,128)(2,1)}, bf16[48,768]{1,0:T(8,128)(2,1)S(1)}, u32[]{:S(2)}, u32[]{:S(2)}) collective-permute-start(bf16[48,768]{1,0:T(8,128)(2,1)} %share.11.refs_0_), channel_id=1, source_target_pairs={{0,2},{1,3},{2,0},{3,1},{4,6},{5,7},{6,4},{7,5},{8,10},{9,11},{10,... | collective-permute-start | bytes 221192 | tf_op jit(solution)/shard_map/ppermute | solution.py:752
  329.7 10.9 %collective-permute-start.58 = (bf16[48,768]{1,0:T(8,128)(2,1)}, bf16[48,768]{1,0:T(8,128)(2,1)S(1)}, u32[]{:S(2)}, u32[]{:S(2)}) collective-permute-start(bf16[48,768]{1,0:T(8,128)(2,1)} %share.11.refs_0_), channel_id=1, source_target_pairs={{0,4},{1,5},{2,6},{3,7},{4,0},{5,1},{6,2},{7,3},{8,12},{9,13},{10,... | collective-permute-start | bytes 221192 | tf_op jit(solution)/shard_map/ppermute | solution.py:752
  337.1 19.5 %collective-permute-start.39 = (bf16[192,768]{1,0:T(8,128)(2,1)}, bf16[192,768]{1,0:T(8,128)(2,1)S(1)}, u32[]{:S(2)}, u32[]{:S(2)}) collective-permute-start(bf16[192,768]{1,0:T(8,128)(2,1)} %join.4.refs_0_), channel_id=1, source_target_pairs={{0,8},{8,0},{16,24},{24,16},{1,9},{9,1},{17,25},{25,17},{2,10},{10... | collective-permute-start | bytes 884744 | tf_op jit(solution)/shard_map/ppermute | solution.py:752
  339.0 22.2 %collective-permute-start.40 = (bf16[192,768]{1,0:T(8,128)(2,1)}, bf16[192,768]{1,0:T(8,128)(2,1)S(1)}, u32[]{:S(2)}, u32[]{:S(2)}) collective-permute-start(bf16[192,768]{1,0:T(8,128)(2,1)} %join.4.refs_0_), channel_id=1, source_target_pairs={{0,16},{8,24},{16,0},{24,8},{1,17},{9,25},{17,1},{25,9},{2,18},{10... | collective-permute-start | bytes 884744 | tf_op jit(solution)/shard_map/ppermute | solution.py:752
  339.6 21.7 %collective-permute-start.41 = (bf16[192,768]{1,0:T(8,128)(2,1)}, bf16[192,768]{1,0:T(8,128)(2,1)S(1)}, u32[]{:S(2)}, u32[]{:S(2)}) collective-permute-start(bf16[192,768]{1,0:T(8,128)(2,1)} %join.4.refs_0_), channel_id=1, source_target_pairs={{0,24},{8,16},{16,8},{24,0},{1,25},{9,17},{17,9},{25,1},{2,26},{10... | collective-permute-start | bytes 884744 | tf_op jit(solution)/shard_map/ppermute | solution.py:752
  343.6 17.7 %collective-permute-start.60 = (bf16[192,768]{1,0:T(8,128)(2,1)}, bf16[192,768]{1,0:T(8,128)(2,1)S(1)}, u32[]{:S(2)}, u32[]{:S(2)}) collective-permute-start(bf16[192,768]{1,0:T(8,128)(2,1)} %join.5.refs_0_), channel_id=1, source_target_pairs={{0,8},{8,0},{16,24},{24,16},{1,9},{9,1},{17,25},{25,17},{2,10},{10... | collective-permute-start | bytes 884744 | tf_op jit(solution)/shard_map/ppermute | solution.py:752
  345.5 15.8 %collective-permute-start.61 = (bf16[192,768]{1,0:T(8,128)(2,1)}, bf16[192,768]{1,0:T(8,128)(2,1)S(1)}, u32[]{:S(2)}, u32[]{:S(2)}) collective-permute-start(bf16[192,768]{1,0:T(8,128)(2,1)} %join.5.refs_0_), channel_id=1, source_target_pairs={{0,16},{8,24},{16,0},{24,8},{1,17},{9,25},{17,1},{25,9},{2,18},{10... | collective-permute-start | bytes 884744 | tf_op jit(solution)/shard_map/ppermute | solution.py:752
  369.7 8.8 %collective-permute-start.63 = (bf16[768,768]{1,0:T(8,128)(2,1)}, bf16[768,768]{1,0:T(8,128)(2,1)S(1)}, u32[]{:S(2)}, u32[]{:S(2)}) collective-permute-start(bf16[768,768]{1,0:T(8,128)(2,1)} %join.6.own_ref), channel_id=1, source_target_pairs={{0,1},{1,0},{2,3},{3,2},{4,5},{5,4},{6,7},{7,6},{8,9},{9,8},{10,11... | collective-permute-start | bytes 3538952 | tf_op jit(solution)/shard_map/ppermute | solution.py:752
  (84 other events, 658.2 us)

commit v3 on v2

--- a/solution.py
+++ b/solution.py
@@ -14,6 +14,7 @@
 EPSILON = 1e-06
 NEGATIVE = -1000000000.0
 TILE = 128
+BUCKETS = 32
 LANES = 128
 HALF = 64
 LINE = 4 * TILE
@@ -102,9 +103,7 @@
 
 def home_rows(expert_ref, column, refs, plan):
     block_rows = plan.block_rows
-    rows = jnp.concatenate(
-        [ref[first : first + block_rows, :] for ref, first in plan.take(refs)], axis=0
-    )
+    rows = jnp.concatenate([ref[...] for ref in plan.by_distance(refs)], axis=0)
     place = iota((1, rows.shape[0]), 1)
     wanted = place
     for distance in range(plan.blocks):
@@ -305,9 +304,9 @@
 
     @pl.when(pl.program_id(0) == 0)
     def _():
-        for number, (ref, first) in enumerate(plan.take(up_refs)):
+        for number, ref in enumerate(plan.by_distance(up_refs)):
             rows = plan.block_rows
-            up_ref[number * rows : (number + 1) * rows, :] = ref[first : first + rows, :]
+            up_ref[number * rows : (number + 1) * rows, :] = ref[...]
 
     act_grad_ref[...] = dot(up_ref[...], out_ref[0], 1, 1).astype(BF)
 
@@ -322,7 +321,7 @@
         grid=(hidden // tile,),
         out_shape=[shape_of((rows, width), BF), shape_of((rows, hidden), BF)],
         in_specs=[pl.BlockSpec((1, tile, width), lambda f: (0, f, 0))]
-        + [whole(array.shape) for array in up_arrays],
+        + plan.specs(up_arrays),
         out_specs=[whole((rows, width)), pl.BlockSpec((rows, tile), lambda f: (0, f))],
         compiler_params=params(28),
         name="expert_activation_gradient",
@@ -341,17 +340,16 @@
     steps = len(plan.arrays)
     rows, hidden = act_ref.shape
     experts = router_ref.shape[0]
-    blocks = plan.take(row_refs)
+    blocks = plan.by_distance(row_refs)
     for number in range(steps):
 
         @pl.when(step == number)
         def _(number=number):
             each = len(blocks) // steps
             for place in range(each):
-                ref, first = blocks[number * each + place]
-                rows_ref[place * block_rows : (place + 1) * block_rows, :] = ref[
-                    first : first + block_rows, :
-                ]
+                rows_ref[place * block_rows : (place + 1) * block_rows, :] = blocks[
+                    number * each + place
+                ][...]
 
     own = iota((rows, experts), 1) == expert_ref[0]
     logits = dot(rows_ref[...], router_ref[...], 1, 1)
@@ -417,7 +415,7 @@
             whole((1, width, hidden)),
             whole((experts, width)),
         ]
-        + [whole(array.shape) for array in row_arrays],
+        + plan.specs(row_arrays),
         out_specs=[by_rows(some, columns) for columns in (hidden, hidden, width, width, 1, experts)]
         + [whole((count, width)) for count in plan.arrays],
         scratch_shapes=[pltpu.VMEM((some, width), BF)],
@@ -510,7 +508,7 @@
     )(act, expert_out, gate)
 
 
-ROW_STEPS = 4
+ROW_STEPS = 2
 
 
 def result_kernel(plan, expert_ref, length_ref, column_ref, resid_ref, *refs):
@@ -528,7 +526,7 @@
         grid=(ROW_STEPS,),
         out_shape=shape_of(resid.shape, BF),
         in_specs=[smem(), smem(), by_rows(rows, LANES), by_rows(rows, width)]
-        + [whole(array.shape) for array in arrays],
+        + plan.specs(arrays),
         out_specs=by_rows(rows, width),
         compiler_params=params(58),
         name="result",
@@ -579,7 +577,7 @@
             shape_of((1, width), F32),
         ],
         in_specs=[smem(), smem(), by_rows(rows, LANES), block, block, whole((width, width)), whole((width,))]
-        + [whole(array.shape) for array in arrays],
+        + plan.specs(arrays),
         out_specs=[block, block, block, whole((1, width))],
         compiler_params=params(58),
         name="expert_norm_backward",
@@ -587,10 +585,26 @@
 
 
 def backward_kernel(
-    qkv_ref, probs_ref, mixed_ref, grad_ref, attn_grad_ref, inverse_ref, back_ref, line_ref, score_s
+    core_ref,
+    qkv_ref,
+    probs_ref,
+    lefts_ref,
+    mixed_ref,
+    grad_ref,
+    attn_grad_ref,
+    inverse_ref,
+    back_ref,
+    line_ref,
+    *refs,
 ):
+    own_refs, other_refs, score_s, lefts_s, backs_s = refs[:2], refs[2:4], *refs[4:]
     seq_len = grad_ref.shape[0]
-    back_ref[3] = attn_grad_ref[...]
+
+    @pl.when(pl.program_id(0) == 0)
+    def _():
+        lefts_s[0] = lefts_ref[0].T
+        lefts_s[1] = lefts_ref[1].T
+
     tiles = seq_len // TILE
     query = qkv_ref[0, 0]
     key = qkv_ref[1, 0]
@@ -648,63 +662,105 @@
         spread = pltpu.roll(spread, 0, 1, stride=1, stride_axis=0)
         line_ref[0, half : half + 1, :LINE] = jnp.sum(spread, axis=0, keepdims=True)
     first = lane < HALF
-    back_ref[0] = (jnp.where(first, query_backs[0], query_backs[1]) * HALF ** (-0.5)).astype(BF)
-    for place, backs in ((1, key_backs), (2, value_backs)):
-        joined = jnp.concatenate([backs[0][:HALF], backs[1][HALF:]], axis=0)
-        back_ref[place] = joined.T.astype(BF)
-
-
-def backward_part(qkv, probs, lefts, mixed_grad, attn_grad, inverse):
+    backs = [(jnp.where(first, query_backs[0], query_backs[1]) * HALF ** (-0.5)).astype(BF)]
+    for halves in (key_backs, value_backs):
+        joined = jnp.concatenate([halves[0][:HALF], halves[1][HALF:]], axis=0)
+        backs.append(joined.T.astype(BF))
+    backs.append(attn_grad_ref[...])
+    for place, values in enumerate(backs):
+        if place < 3:
+            back_ref[place] = values
+
+    @pl.when(pl.program_id(0) % 2 == 0)
+    def _():
+        for place, values in enumerate(backs):
+            backs_s[place] = values
+
+    @pl.when(pl.program_id(0) % 2 == 1)
+    def _():
+        wides = [jnp.concatenate([backs_s[n], values], axis=1) for n, values in enumerate(backs)]
+        grads = [dot(lefts_s[n // 3], wide).astype(BF) for n, wide in enumerate(wides)]
+        for core in range(2):
+
+            @pl.when(core_ref[0] == core)
+            def _(core=core):
+                for target_refs, place in ((own_refs, core), (other_refs, 1 - core)):
+                    target_refs[0][...] = grads[place]
+                    target_refs[1][...] = grads[2 + place]
+
+
+def backward_part(core, qkv, probs, lefts, mixed_grad, attn_grad, inverse):
     _, seq_len, width = lefts.shape
     pairs = width // LANES
+    assert pairs % 2 == 0
     column = pl.BlockSpec((seq_len, LANES), lambda p: (0, p))
+    grad = pl.BlockSpec((width, 2 * LANES), lambda p: (0, p // 2))
     return pl.pallas_call(
         backward_kernel,
         grid=(pairs,),
         out_shape=[
-            shape_of((4, seq_len, width), BF),
+            shape_of((3, seq_len, width), BF),
             shape_of((pairs, 2, LINE + 2 * LANES), F32),
-        ],
+        ]
+        + [shape_of((width, width), BF)] * 4,
         in_specs=[
+            smem(),
             pl.BlockSpec((3, 1, seq_len, LANES), lambda p: (0, p, 0, 0)),
             pl.BlockSpec((2, seq_len, seq_len), lambda p: (p, 0, 0)),
+            whole(lefts.shape),
             pl.BlockSpec((1, seq_len, LANES), lambda p: (1, 0, p)),
             column,
             column,
             pl.BlockSpec((1, seq_len, LANES), lambda p: (p, 0, 0)),
         ],
         out_specs=[
-            pl.BlockSpec((4, seq_len, LANES), lambda p: (0, 0, p)),
+            pl.BlockSpec((3, seq_len, LANES), lambda p: (0, 0, p)),
             pl.BlockSpec((1, 2, LINE + 2 * LANES), lambda p: (p, 0, 0)),
+        ]
+        + [grad] * 4,
+        scratch_shapes=[
+            pltpu.VMEM((2, seq_len, seq_len), BF),
+            pltpu.VMEM((2, width, seq_len), BF),
+            pltpu.VMEM((4, seq_len, LANES), BF),
         ],
-        scratch_shapes=[pltpu.VMEM((2, seq_len, seq_len), BF)],
         compiler_params=params(58),
         name="attention_backward",
-    )(qkv, probs, lefts, mixed_grad, attn_grad, inverse)
-
-
-def projection_grad_kernel(left_places_ref, right_places_ref, left_ref, right_ref, out_ref):
-    out_ref[...] = dot(left_ref[0], right_ref[0], 0, 0).astype(BF)
-
-
-def projection_grad_part(left_places, right_places, lefts, rights):
-    _, seq_len, width = lefts.shape
-    count = left_places.shape[0]
-    return pl.pallas_call(
-        projection_grad_kernel,
-        grid_spec=pltpu.PrefetchScalarGridSpec(
-            num_scalar_prefetch=2,
-            grid=(count,),
-            in_specs=[
-                pl.BlockSpec((1, seq_len, width), lambda s, left, right: (left[s], 0, 0)),
-                pl.BlockSpec((1, seq_len, width), lambda s, left, right: (right[s], 0, 0)),
-            ],
-            out_specs=pl.BlockSpec((width, width), lambda s, left, right: (s, 0)),
-        ),
-        out_shape=shape_of((count * width, width), BF),
+    )(core, qkv, probs, lefts, lefts, mixed_grad, attn_grad, inverse)
+
+
+def extra_kernel(router_ref, gain_ref, line_ref, out_ref):
+    experts, width = router_ref.shape
+    heads, places = line_ref.shape
+    place = iota((places, width), 0)
+    bucket = iota((places, width), 1)
+    own = bucket_of(place - (2 * TILE - 1), BUCKETS, MAXDIST)
+    own = jnp.where(place >= LINE, BUCKETS // 2 - 1, own)
+    own = jnp.where(place >= LINE + LANES, BUCKETS - 1, own)
+    sums = lax.dot_general(
+        line_ref[...],
+        jnp.where(own == bucket, 1.0, 0.0),
+        (((1,), (0,)), ((), ())),
+        precision=lax.Precision.HIGHEST,
+        preferred_element_type=F32,
+    )
+    rows = [
+        router_ref[...],
+        jnp.broadcast_to(gain_ref[...], (8, width)),
+        sums,
+        jnp.zeros((out_ref.shape[0] - experts - 8 - heads, width), F32),
+    ]
+    out_ref[...] = jnp.concatenate(rows, axis=0).astype(BF)
+
+
+def extra_part(router_grad, gain_grad, lines):
+    experts, width = router_grad.shape
+    rows = -(-(experts + 8 + lines.shape[0]) // 16) * 16
+    return pl.pallas_call(
+        extra_kernel,
+        out_shape=shape_of((rows, width), BF),
         compiler_params=params(58),
-        name="projection_gradient",
-    )(left_places, right_places, lefts, rights)
+        name="extra_rows",
+    )(router_grad, gain_grad, lines)
 
 
 def token_grad_kernel(
@@ -788,13 +844,17 @@
             return arrays
         return [*arrays, *[swap(array, "expert", self.size, 1) for array in arrays]]
 
-    def take(self, refs):
+    def specs(self, arrays):
         if not self.paired:
-            return [(refs[0], 0)]
+            return [whole(array.shape) for array in arrays]
+        return [
+            pl.BlockSpec((self.block_rows, array.shape[1]), lambda *_, n=n: (2 * n // len(arrays), 0))
+            for n, array in enumerate(arrays)
+        ]
+
+    def by_distance(self, refs):
         half = len(refs) // 2
-        return [
-            place for pair in zip(refs[:half], refs[half:]) for place in zip(pair, (0, self.block_rows))
-        ]
+        return [ref for pair in zip(refs[:half], refs[half:]) for ref in pair] if self.paired else refs
 
 
 def stages_of(dp_size, expert_size):
@@ -815,34 +875,59 @@
     return sum(((index // bit) % 2) << n for n, bit in enumerate(bits))
 
 
-def share_kernel(inputs, place_ref, *refs):
+def share_kernel(inputs, extra, apart, place_ref, *refs):
     in_refs, out_refs = refs[:inputs], refs[inputs:]
-    for number, out_ref in enumerate(out_refs):
-        rows = out_ref.shape[0]
-        if len(out_refs) == 1:
-            part = slice(None)
+    extra_refs, out_refs = out_refs[: len(out_refs) - apart], out_refs[len(out_refs) - apart :]
+    last = in_refs[0].shape[0] - (0 if extra_refs else extra)
+    count = 1 if place_ref is None else len(out_refs)
+    rows = last // count
+    for number in range(count):
+        start = 0 if count == 1 else pl.multiple_of((place_ref[0] ^ number) * rows, rows)
+        total = sum(ref[pl.ds(start, rows), :].astype(F32) for ref in in_refs)
+        out_refs[number][:rows, :] = total.astype(BF)
+    if extra:
+        if extra_refs:
+            total = sum(ref[...].astype(F32) for ref in extra_refs).astype(BF)
         else:
-            part = pl.ds(pl.multiple_of((place_ref[0] ^ number) * rows, rows), rows)
-        out_ref[...] = sum(ref[part, :].astype(F32) for ref in in_refs).astype(BF)
-
-
-def share_one(parts, stage):
+            total = sum(ref[last:, :].astype(F32) for ref in in_refs).astype(BF)
+        if count > 1:
+            for out_ref in out_refs:
+                out_ref[rows:, :] = total
+        else:
+            out_refs[-1][...] = total
+
+
+def share(parts, stage, extra, extras=()):
     count = 1 if stage is None else 1 << len(stage[2])
-    place = jnp.int32(0) if stage is None else place_of(stage)
-    rows, width = parts[0].shape[0] // count, parts[0].shape[1]
+    place = None if stage is None else place_of(stage)
+    if parts[0].shape[0] // count % 16 and extras:
+        parts = [jnp.concatenate(pair, axis=0) for pair in zip(parts, extras)]
+        extras = ()
+    last, width = parts[0].shape[0] - (0 if extras else extra), parts[0].shape[1]
+    rows = last // count
+    shapes = [(rows + extra, width)] * count if count > 1 else [(rows, width)]
+    if count == 1 and extra:
+        shapes.append((extra, width))
     if rows % 16:
         total = sum(part.astype(F32) for part in parts).astype(BF)
+        if stage is None:
+            return [total[:last], total[last:]] if extra else [total]
         return [
-            lax.dynamic_slice_in_dim(total, (place ^ number) * rows, rows, 0)
+            jnp.concatenate(
+                [lax.dynamic_slice_in_dim(total, (place ^ number) * rows, rows, 0), total[last:]], axis=0
+            )
             for number in range(count)
         ]
-    return pl.pallas_call(
-        functools.partial(share_kernel, len(parts)),
-        out_shape=[shape_of((rows, width), BF)] * count,
-        in_specs=[smem()] + [pl.BlockSpec()] * len(parts),
+    kernel = functools.partial(share_kernel, len(parts), extra, len(shapes))
+    if stage is None:
+        kernel = functools.partial(kernel, None)
+    return pl.pallas_call(
+        kernel,
+        out_shape=[shape_of(shape, BF) for shape in shapes],
+        in_specs=[smem()] * (stage is not None) + [pl.BlockSpec()] * (len(parts) + len(extras)),
         compiler_params=params(58),
         name="share",
-    )(place.reshape(1), *parts)
+    )(*([] if stage is None else [place.reshape(1)]), *parts, *extras)
 
 
 def scatter(parts, stage):
@@ -886,38 +971,39 @@
     )(place.reshape(1), *parts)
 
 
-def widen_kernel(place_ref, own_ref, other_ref, *refs):
-    weight_refs, out_refs, gain_ref = refs[:-3], refs[-3:-1], refs[-1]
-    for number, out_ref in enumerate(out_refs):
-
-        @pl.when(place_ref[0] == number)
-        def _(out_ref=out_ref):
-            out_ref[...] = own_ref[...].astype(F32)
-
-        @pl.when(place_ref[0] != number)
-        def _(out_ref=out_ref):
-            out_ref[...] = other_ref[...].astype(F32)
+def assemble_kernel(count, places_ref, *refs):
+    own_refs, other_refs = refs[:count], refs[count : 2 * count]
+    weight_refs, out_refs, gain_ref = refs[2 * count : -3], refs[-3:-1], refs[-1]
+    source = places_ref[1] ^ pl.program_id(0)
+    for number in range(count):
+        for core in range(2):
+
+            @pl.when((source == number) & (places_ref[0] == core))
+            def _(number=number, core=core):
+                out_refs[core][...] = own_refs[number][...].astype(F32)
+                out_refs[1 - core][...] = other_refs[number][...].astype(F32)
 
     total = sum(
         jnp.sum(out_ref[...] * weight_ref[...].astype(F32), axis=1, keepdims=True)
         for out_ref, weight_ref in zip(out_refs, weight_refs)
     )
-    gain_ref[...] = jnp.broadcast_to(total, (total.shape[0], LANES)).T[:1]
-
-
-def widen(parts, stage, weights):
-    rows, width = parts[0].shape
-    some = 2 * LANES
-    block = by_rows(some, width)
-    return pl.pallas_call(
-        widen_kernel,
-        grid=(rows // some,),
-        out_shape=[shape_of(parts[0].shape, F32)] * 2 + [shape_of((1, rows), F32)],
-        in_specs=[smem()] + [block] * (2 + len(weights)),
-        out_specs=[block, block, pl.BlockSpec((1, some), lambda step: (0, step))],
+    gain_ref[...] = jnp.broadcast_to(total, gain_ref.shape)
+
+
+def assemble(own, other, stages, weights):
+    rows, width = own[0].shape
+    count = len(own)
+    block = by_rows(rows, width)
+    places = jnp.stack([place_of(stage) for stage in stages])
+    return pl.pallas_call(
+        functools.partial(assemble_kernel, count),
+        grid=(count,),
+        out_shape=[shape_of((count * rows, width), F32)] * 2 + [shape_of((count * rows, LANES), F32)],
+        in_specs=[smem()] + [whole((rows, width))] * (2 * count) + [block] * len(weights),
+        out_specs=[block, block, by_rows(rows, LANES)],
         compiler_params=params(58),
-        name="widen",
-    )(place_of(stage).reshape(1), *parts, *weights)
+        name="assemble",
+    )(places, *own, *other, *weights)
 
 
 def halving_order(bits):
@@ -946,8 +1032,8 @@
     expert_out,
 ):
     seq_count, seq_len, width = tokens.shape
-    assert seq_count == 1
     buckets, heads = bucket_head_bias.shape
+    assert seq_count == 1 and buckets == BUCKETS
     experts = router_weight.shape[1]
     capacity = max(2, 5 * seq_len // (4 * experts))
     plan = Plan(expert_size, capacity, experts)
@@ -1010,58 +1096,38 @@
     ]
     mixed_grad = after(mixed_grad, *seconds)
 
-    back, lines = backward_part(qkv, probs, lefts, mixed_grad, attn_grad, inverse_total)
-    back, result_there, arrived_seconds = lax.optimization_barrier(
-        (back, result_there, arrived_seconds)
-    )
-
-    sum_bucket = bucket_of(jnp.arange(LINE, dtype=jnp.int32) - (2 * TILE - 1), buckets, MAXDIST)
-    sum_indicator = sum_bucket[None, :] == jnp.arange(buckets, dtype=jnp.int32)[:, None]
-    lines = jnp.pad(
-        lines.reshape(heads, LINE + 2 * LANES), ((0, 0), (0, width - LINE - 2 * LANES))
-    )
-    small = jnp.concatenate([ffn_gain_grad, router_grad, lines], axis=0)
     stages = stages_of(dp_size, expert_size)
-    steps = [
-        (axis, size, bit)
-        for axis, size, bits in stages[2:] + stages[:1] + stages[1:2]
-        for bit in bits
-    ]
-
-    def sum_step(small):
-        if not steps:
-            return small
-        return small + swap(small, *steps.pop(0))
-
     core = place_of(stages[0])
+    back, lines, *grads = backward_part(
+        core.reshape(1), qkv, probs, lefts, mixed_grad, attn_grad, inverse_total
+    )
+    kept, sent = grads[:2], grads[2:]
+    back, sent, result_there, arrived_seconds = lax.optimization_barrier(
+        (back, sent, result_there, arrived_seconds)
+    )
+
+    there = [swap(values, *stages[0][:2], 1) for values in sent]
+    extra = extra_part(router_grad, ffn_gain_grad, lines.reshape(heads, -1))
+    extra_rows = [0, extra.shape[0]]
+    extras = [(), (extra, swap(extra, *stages[0][:2], 1))]
+    shares = []
+    for values, other, rows, more in zip(kept, there, extra_rows, extras):
+        parts = [values, other]
+        if shares:
+            parts = after(parts, shares[0])
+        shares.append(share(parts, stages[1], rows, more))
+    moved = [scatter(parts, stages[1]) for parts in shares]
+    token_grad = token_grad_part(after(back, *shares[1]), weights, rows_in, norm_gain, resid_grad)
+    moved[0], token_grad, result_there = lax.optimization_barrier(
+        (moved[0], token_grad, result_there)
+    )
     result_arrays = plan.finish(result_there)
-
-    def gradient(chunk, which, *others):
-        left, right = (0 * which, which) if chunk == 0 else (which, 2 + which)
-        args = lax.optimization_barrier(((lefts, back), others))[0]
-        return projection_grad_part(left.reshape(1), right.reshape(1), *args)
-
-    sent = [gradient(0, 1 - core)]
-    sent.append(gradient(1, 1 - core, sent[0]))
-    there = [swap(values, *stages[0][:2], 1) for values in sent]
-    kept = gradient(0, core, sent[1])
-    shares = [share_one([kept, there[0]], stages[1])]
-    kept = gradient(1, core, shares[0])
-    shares.append(share_one([kept, there[1]], stages[1]))
-    moved = [scatter(parts, stages[1]) for parts in shares]
-    later_back, small = lax.optimization_barrier((back, small, shares[1]))[:2]
-    token_grad = token_grad_part(later_back, weights, rows_in, norm_gain, resid_grad)
-    moved[0], token_grad = lax.optimization_barrier((moved[0], token_grad))
-    while len(steps) > len(stages[1][2]):
-        small = sum_step(small)
-    moved[1], small, result_arrays = lax.optimization_barrier((moved[1], small, result_arrays))
     for stage in stages[2:]:
-        shares = [share_one(parts, stage) for parts in moved]
+        shares = [share(parts, stage, rows) for parts, rows in zip(moved, extra_rows)]
         moved = [scatter(parts, stage) for parts in shares]
-        while steps:
-            small = sum_step(small)
-        moved[1], small = lax.optimization_barrier((moved[1], small))
-    chunks = [share_one(parts, None)[0] for parts in moved]
+    chunks = [share(parts, None, rows) for parts, rows in zip(moved, extra_rows)]
+    extra = chunks[1][1].astype(F32)
+    chunks = [chunk[0] for chunk in chunks]
     for stage in stages[:1:-1]:
         chunks = [join(gather(values, stage), stage) for values in chunks]
     there = [gather(values, stages[1]) for values in chunks]
@@ -1075,28 +1141,19 @@
         if rest:
             total = total + second.astype(F32)
         weight_sums.append(total)
-    there, weight_sums, result = lax.optimization_barrier((there, weight_sums, result))
+    last = [pieces.pop() for pieces in there]
+    over = [[swap(piece, *stages[0][:2], 1) for piece in pieces] for pieces in there]
+    last, weight_sums, result = lax.optimization_barrier((last, weight_sums, result))
+    for pieces, others, piece in zip(there, over, last):
+        pieces.append(piece)
+        others.append(swap(piece, *stages[0][:2], 1))
     expert_out_grad, expert_in_grad = weight_sums
-    chunks = [join(parts, stages[1]) for parts in there]
-    pairs_of = [gather(chunk, stages[0]) for chunk in chunks]
-    query_grad, key_grad, gain_sum = widen(pairs_of[0], stages[0], (query_weight, key_weight))
-    value_grad, output_grad, value_sum = widen(pairs_of[1], stages[0], (value_weight,))
-    norm_gain_grad = (gain_sum + value_sum).reshape(width) / norm_gain.astype(F32)
-
-    lines = small[1 + experts :]
-    bucket_grad = lax.dot_general(
-        sum_indicator.astype(F32),
-        lines[:, :LINE],
-        (((1,), (1,)), ((), ())),
-        precision=lax.Precision.HIGHEST,
-    )
-    far_sums = jnp.sum(lines[:, LINE : LINE + 2 * LANES].reshape(heads, 2, LANES), axis=-1)
-    bucket_row = jnp.arange(buckets, dtype=jnp.int32)[:, None]
-    bucket_grad = bucket_grad + jnp.where(
-        bucket_row == buckets // 2 - 1,
-        far_sums[None, :, 0],
-        jnp.where(bucket_row == buckets - 1, far_sums[None, :, 1], 0.0),
-    )
+    (query_grad, key_grad, gain_sum), (value_grad, output_grad, value_sum) = [
+        assemble(own, other, stages[:2], some)
+        for own, other, some in zip(there, over, ((query_weight, key_weight), (value_weight,)))
+    ]
+    norm_gain_grad = (gain_sum + value_sum)[:, 0] / norm_gain.astype(F32)
+
     return (
         result.reshape(tokens.shape),
         token_grad.reshape(tokens.shape),
@@ -1105,9 +1162,9 @@
         key_grad,
         value_grad,
         output_grad,
-        bucket_grad,
-        small[0],
-        small[1 : 1 + experts].T,
+        extra[experts + 8 : experts + 8 + heads, :buckets].T,
+        extra[experts],
+        extra[:experts].T,
         expert_in_grad,
         expert_out_grad,
     )

time: 390 us -> 380 us (0.974)
  Pallas kernels: 211 us -> 197 us
  waiting for transfers between devices: 44.7 us -> 50.5 us
  starting transfers between devices: 91.4 us -> 86.2 us
    pallas_call x13 -> x10, Pallas kernels: 69.5 us -> 63.6 us  [the longest x1 37.3 us: backward_part(): pl.pallas_call(backward_kernel, grid=(pairs,), out_shape=[shape_of((3, se...]
    ppermute x65 -> x67, waiting for transfers between devices: 44.7 us -> 50.5 us  [swap(): lax.ppermute(values, axis, [(place, place ^ distance) for place in range(...]
    ppermute x65 -> x67, starting transfers between devices: 91.4 us -> 86.2 us  [swap(): lax.ppermute(values, axis, [(place, place ^ distance) for place in range(...]
    pallas_call x4 -> x2, Pallas kernels: 8.09 us -> 3.44 us  [join(): pl.pallas_call(join_kernel, out_shape=shape_of((rows * len(parts), width)...]
    unnamed x134 -> x142, local copies, waits for them, and re-layouts: 25.8 us -> 26.3 us
  transfers between devices with their start and end apart: 65 -> 67, of which waited for: 14 -> 17; matrix products, arithmetic and copies ran while one was open for 3% -> 3% of each run, Pallas kernels for 41% -> 41%
where the time goes in v3:
time: 380 us; the launch traced here: 376 us
  Pallas kernels  197 us (52%)
  starting transfers between devices  86.2 us (23%)
  waiting for transfers between devices  50.5 us (13%)
  local copies, waits for them, and re-layouts  28.9 us (8%)
  other arithmetic  10.2 us (3%)
    ppermute x67, starting transfers between devices, swap(): lax.ppermute(values, axis, [(place, place ^ distance) for place in range(...  86.2 us
    ppermute x67, waiting for transfers between devices, swap(): lax.ppermute(values, axis, [(place, place ^ distance) for place in range(...  50.5 us
    pallas_call x1, Pallas kernels, backward_part(): pl.pallas_call(backward_kernel, grid=(pairs,), out_shape=[shape_of((3, se...  37.3 us
    pallas_call x1, Pallas kernels, forward_part(): pl.pallas_call(functools.partial(forward_kernel, plan), grid=(pairs,), ou...  36.5 us
    unnamed x142, local copies, waits for them, and re-layouts  26.3 us
    pallas_call x1, Pallas kernels, expert_part(): pl.pallas_call(functools.partial(expert_kernel, plan), grid=(steps,), out...  24.6 us
    pallas_call x3, Pallas kernels, weight_grad_part(): pl.pallas_call(functools.partial(weight_grad_kernel, transposed, len(term...  17.6 us
    pallas_call x6, Pallas kernels, share(): pl.pallas_call(kernel, out_shape=[shape_of(shape, BF) for shape in shapes...  13.5 us
  transfers between devices with their start and end apart: 67, of which 17 were waited for; matrix products, arithmetic and copies ran while one was open for 3% of the time, Pallas kernels for 41%

profile of v3, /device:TPU:0, one launch (start us, length us, event | category | flops | bytes accessed | tf_op | source)
XLA Modules:
  0.0 376.2 jit_solution(2291630714130814681)
XLA Ops:
  1.3 5.2 %slots.1 = (s32[1,1024]{1,0:T(1,128)}, s32[1024,128]{1,0:T(8,128)}, bf16[320,768]{1,0:T(8,128)(2,1)}, bf16[320,768]{1,0:T(8,128)(2,1)}, bf16[320,768]{1,0:T(8,128)(2,1)}, /*index=5*/bf16[320,768]{1,0:T(8,128)(2,1)}) custom-call(s32[1]{0:T(128)} %bitcast.3.expert_ref, s32[1]{0:T(128)S(6)} %copy.28.length_ref, s32[1,1024]{1,0:T(1,128)} %routes_ref.1, ...), custom_call_target="tpu_custom_call" | custom-call | tf_op jit(solution)/shard_map/slots/pallas_call | solution.py:136
  6.5 3.0 collective-permute-start
  9.6 2.6 collective-permute-start.1
  12.2 36.5 %attention_forward.1 = (bf16[12,1024,1024]{2,1,0:T(8,128)(2,1)}, bf16[3,6,1024,128]{3,2,1,0:T(8,128)(2,1)}, bf16[2,1024,768]{2,1,0:T(8,128)(2,1)}, f32[6,1024,12...) custom-call(s32[1]{0:T(128)} %bitcast.3.expert_ref, ...), custom_call_target="tpu_custom_call" | custom-call | tf_op jit(solution)/shard_map/attention_forward/pallas_call | solution.py:259
  49.8 6.8 %collective-permute-start.7 = (bf16[320,768]{1,0:T(8,128)(2,1)}, bf16[320,768]{1,0:T(8,128)(2,1)S(1)}, u32[]{:S(2)}, u32[]{:S(2)}) collective-permute-start(bf16[320,768]{1,0:T(8,128)(2,1)} %get-tuple-element.159), channel_id=1, source_target_pairs={{0,2},{1,3},{2,0},{3,1},{4,6},{5,7},{6,4},{7,5},{8,10},{9,11},{10,... | collective-permute-start | bytes 1474568 | tf_op jit(solution)/shard_map/ppermute | solution.py:808
  57.4 1.8 collective-permute-start.8
  61.4 2.3 copy-done.2
  65.8 9.5 %expert_activation_gradient.1 = (bf16[1280,768]{1,0:T(8,128)(2,1)S(1)}, bf16[1280,3072]{1,0:T(8,128)(2,1)S(1)}) custom-call(bf16[1,3072,768]{2,1,0:T(8,128)(2,1)S(1)} %copy-done.2, bf16[320,768]{1,0:T(8,128)(2,1)S(1)} %copy-done.15, bf16[320,768]{1,0:T(8,128)(2,1)S(1)} %collective-permute-done.refs_1_, bf16[320,768]{1,0:T(8,128)(2,1)S(1)} %collective-permute-done.1.refs_2_, ...), custom_call_target="tpu_custom_call" | custom-call | tf_op jit(solution)/shard_map/expert_activation_gradient/pallas_call | solution.py:319
  75.3 3.1 copy-done.3
  79.7 13.9 %collective-permute-done.8.refs_2_ = bf16[320,768]{1,0:T(8,128)(2,1)S(1)} collective-permute-done((bf16[320,768]{1,0:T(8,128)(2,1)}, bf16[320,768]{1,0:T(8,128)(2,1)S(1)}, u32[]{:S(2)}, u32[]{:S(2)}) %collective-permute-start.8) | collective-permute-done | bytes 491552 | tf_op jit(solution)/shard_map/ppermute | solution.py:808
  98.7 24.6 %expert_rows.1 = (bf16[1280,3072]{1,0:T(8,128)(2,1)}, bf16[1280,3072]{1,0:T(8,128)(2,1)}, bf16[1280,768]{1,0:T(8,128)(2,1)S(1)}, bf16[1280,768]{1,0:T(8,128)(2,1...) custom-call(s32[1]{0:T(128)} %bitcast.3.expert_ref, ...), custom_call_target="tpu_custom_call" | custom-call | tf_op jit(solution)/shard_map/expert_rows/pallas_call | solution.py:399
  123.3 3.5 copy-done.1
  126.8 4.3 %expert_weight_gradients.5 = bf16[2,768,768]{2,1,0:T(8,128)(2,1)S(1)} custom-call(s32[2]{0:T(128)S(1)} %get-tuple-element.264.refs_0_, bf16[1280,3072]{1,0:T(8,128)(2,1)S(1)} %copy-done.1, bf16[1280,768]{1,0:T(8,128)(2,1)S(1)} %get-tuple-element.169.refs_5_.refs_2_), custom_call_target="tpu_custom_call" | custom-call | tf_op jit(solution)/shard_map/expert_weight_gradients/pallas_call | solution.py:465
  131.2 1.6 collective-permute-start.22
  132.8 4.3 %expert_weight_gradients.4 = bf16[2,768,768]{2,1,0:T(8,128)(2,1)S(1)} custom-call(s32[2]{0:T(128)S(1)} %get-tuple-element.266.refs_0_, bf16[1280,3072]{1,0:T(8,128)(2,1)S(1)} %copy-done, bf16[1280,768]{1,0:T(8,128)(2,1)S(1)} %copy-done.4), custom_call_target="tpu_custom_call" | custom-call | tf_op jit(solution)/shard_map/expert_weight_gradients/pallas_call | solution.py:465
  138.7 9.9 %collective-permute-start.14 = (bf16[320,768]{1,0:T(8,128)(2,1)S(1)}, bf16[320,768]{1,0:T(8,128)(2,1)S(1)}, u32[]{:S(2)}, u32[]{:S(2)}) collective-permute-start(bf16[320,768]{1,0:T(8,128)(2,1)S(1)} %get-tuple-element.174), channel_id=1, source_target_pairs={{0,2},{1,3},{2,0},{3,1},{4,6},{5,7},{6,4},{7,5},{8,10},{9,11},{10,... | collective-permute-start | bytes 1474568 | tf_op jit(solution)/shard_map/ppermute | solution.py:808
  151.0 8.0 %expert_output.1 = (bf16[320,768]{1,0:T(8,128)(2,1)S(1)}, bf16[320,768]{1,0:T(8,128)(2,1)}, bf16[320,768]{1,0:T(8,128)(2,1)}, bf16[320,768]{1,0:T(8,128)(2,1)S(1)}) custom-call(bf16[1280,3072]{1,0:T(8,128)(2,1)S(1)} %copy-done, bf16[1,3072,768]{2,1,0:T(8,128)(2,1)S(1)} %bitcast.17, f32[1280,1]{1,0:T(8,128)S(1)} %get-tuple-element.177.gate_ref), custom_call_target="tpu_custom_call" | custom-call | tf_op jit(solution)/shard_map/expert_output/pallas_call | solution.py:496
  159.0 8.9 %expert_weight_gradients.3 = (bf16[2,768,768]{2,1,0:T(8,128)(2,1)S(1)}, bf16[2,768,768]{2,1,0:T(8,128)(2,1)S(1)}) custom-call(s32[2]{0:T(128)S(1)} %get-tuple-element.267.refs_0_, s32[2]{0:T(128)S(1)} %get-tuple-element.265.refs_1_, bf16[1280,3072]{1,0:T(8,128)(2,1)S(1)} %copy-done, bf16[1280,3072]{1,0:T(8,128)(2,1)} %get-tuple-element.167.refs_3_.refs_1_, ...), custom_call_target="tpu_custom_call" | custom-call | tf_op jit(solution)/shard_map/expert_weight_gradients/pallas_call | solution.py:465
  170.8 13.9 %collective-permute-done.15.refs_2_ = bf16[320,768]{1,0:T(8,128)(2,1)S(1)} collective-permute-done((bf16[320,768]{1,0:T(8,128)(2,1)S(1)}, bf16[320,768]{1,0:T(8,128)(2,1)S(1)}, u32[]{:S(2)}, u32[]{:S(2)}) %collective-permute-start.15) | collective-permute-done | bytes 491552 | tf_op jit(solution)/shard_map/ppermute | solution.py:808
  190.3 4.3 %later_sums.1 = (bf16[1,768,768]{2,1,0:T(8,128)(2,1)}, bf16[1,768,768]{2,1,0:T(8,128)(2,1)}) custom-call(bf16[2,768,768]{2,1,0:T(8,128)(2,1)} %copy-done.5, bf16[2,768,768]{2,1,0:T(8,128)(2,1)} %copy-done.7, bf16[2,768,768]{2,1,0:T(8,128)(2,1)} %collective-permute-done.21.refs_2_, bf16[2,768,768]{2,1,0:T(8,128)(2,1)} %collective-permute-done.22.refs_3_), custom_call_target="tpu_custom_call" | custom-call | tf_op jit(solution)/shard_map/later_sums/pallas_call | solution.py:441
  196.6 9.9 %collective-permute-start.23 = (bf16[320,768]{1,0:T(8,128)(2,1)}, bf16[320,768]{1,0:T(8,128)(2,1)}, u32[]{:S(2)}, u32[]{:S(2)}) collective-permute-start(bf16[320,768]{1,0:T(8,128)(2,1)} %get-tuple-element.199), channel_id=1, source_target_pairs={{0,2},{1,3},{2,0},{3,1},{4,6},{5,7},{6,4},{7,5},{8,10},{9,11},{10,... | collective-permute-start | bytes 1474568 | tf_op jit(solution)/shard_map/ppermute | solution.py:808
  209.0 9.5 %expert_norm_backward.1 = (f32[1024,768]{1,0:T(8,128)}, bf16[1024,768]{1,0:T(8,128)(2,1)}, bf16[1024,768]{1,0:T(8,128)(2,1)}, f32[1,768]{1,0:T(1,128)}) custom-call(s32[1]{0:T(128)} %bitcast.3.expert_ref, s32[1]{0:T(128)S(6)} %copy.28.length_ref, s32[1024,128]{1,0:T(8,128)} %get-tuple-element.142.column_ref, f32[1024,768]{1,0:T(8,128)} %get-tuple-element.246.resid_ref, ...), custom_call_target="tpu_custom_call" | custom-call | tf_op jit(solution)/shard_map/expert_norm_backward/pallas_call | solution.py:570
  218.5 37.3 %attention_backward.1 = (bf16[3,1024,768]{2,1,0:T(8,128)(2,1)}, f32[6,2,768]{2,1,0:T(2,128)}, bf16[768,768]{1,0:T(8,128)(2,1)}, bf16[768,768]{1,0:T(8,128)(2,1)}...) custom-call(s32[1]{0:T(128)} %bitcast.2.core_ref, bf16[3,6,1024,128]{3,2,1,0:T(8,128)(2,1)} %get-tuple-element.139.qkv_ref, ...), custom_call_target="tpu_custom_call" | custom-call | tf_op jit(solution)/shard_map/attention_backward/pallas_call | solution.py:698
  256.5 2.7 collective-permute-done.28.refs_1_
  259.2 2.8 share.6
  267.2 2.2 extra_rows.1.refs_2_
  271.4 2.9 share.7
  277.8 9.4 %token_gradient.1 = f32[1024,768]{1,0:T(8,128)} custom-call(bf16[3,1024,768]{2,1,0:T(8,128)(2,1)} %get-tuple-element.219.back_ref, bf16[768,768]{1,0:T(8,128)(2,1)} %refs_8_.2, bf16[768,768]{1,0:T(8,128)(2,1)} %refs_9_.1, bf16[768,768]{1,0:T(8,128)(2,1)} %refs_8_.3, bf16[1024,768]{1,0:T(8,128)(2,1)} %bitcast.20, bf16[768]{0:T(1024)(128)(2,1)} %gain_ref.3, ...), custom_call_target="tpu_custom_call" | custom-call | tf_op jit(solution)/shard_map/token_gradient/pallas_call | solution.py:794
  287.2 2.2 share.8
  290.4 1.9 collective-permute-start.35
  292.4 2.3 collective-permute-done.34.refs_1_
  294.7 2.4 collective-permute-start.36
  297.2 3.9 %collective-permute-done.36.refs_3_ = bf16[48,768]{1,0:T(8,128)(2,1)S(1)} collective-permute-done((bf16[48,768]{1,0:T(8,128)(2,1)}, bf16[48,768]{1,0:T(8,128)(2,1)S(1)}, u32[]{:S(2)}, u32[]{:S(2)}) %collective-permute-start.36) | collective-permute-done | bytes 73760 | tf_op jit(solution)/shard_map/ppermute | solution.py:808
  301.7 1.7 share.9.refs_0_
  303.3 3.0 collective-permute-start.38
  309.2 2.2 share.10
  311.4 3.0 collective-permute-start.45
  317.0 1.7 join.2.refs_0_
  322.4 1.8 share.11
  328.8 3.2 collective-permute-start.49
  333.6 1.6 collective-permute-done.49.refs_3_
  336.3 1.7 join.3.refs_0_
  339.3 3.4 convert_add_fusion
  345.5 3.7 collective-permute-done.50.refs_3_
  349.2 3.6 convert_add_fusion.1
  352.8 5.4 %result.1 = bf16[1024,768]{1,0:T(8,128)(2,1)} custom-call(s32[1]{0:T(128)} %bitcast.3.expert_ref, s32[1]{0:T(128)S(6)} %copy.28.length_ref, s32[1024,128]{1,0:T(8,128)} %get-tuple-element.142.column_ref, f32[1024,768]{1,0:T(8,128)} %get-tuple-element.246.resid_ref, bf16[320,768]{1,0:T(8,128)(2,1)} %copy-done.10, ...), custom_call_target="tpu_custom_call" | custom-call | tf_op jit(solution)/shard_map/result/pallas_call | solution.py:524
  361.8 5.5 %assemble.2 = (f32[768,768]{1,0:T(8,128)}, f32[768,768]{1,0:T(8,128)}, f32[768,128]{1,0:T(8,128)}) custom-call(s32[2]{0:T(128)} %pad_add_fusion.places_ref, bf16[192,768]{1,0:T(8,128)(2,1)} %join.2.refs_0_, bf16[192,768]{1,0:T(8,128)(2,1)} %copy-done.41, bf16[192,768]{1,0:T(8,128)(2,1)} %collective-permute-done.56.refs_2_, bf16[192,768]{1,0:T(8,128)(2,1)} %copy-done.40, ...), custom_call_target="tpu_custom_call" | custom-call | tf_op jit(solution)/shard_map/assemble/pallas_call | solution.py:998
  369.0 5.1 %assemble.3 = (f32[768,768]{1,0:T(8,128)}, f32[768,768]{1,0:T(8,128)}, f32[768,128]{1,0:T(8,128)}) custom-call(s32[2]{0:T(128)} %pad_add_fusion.places_ref, bf16[192,768]{1,0:T(8,128)(2,1)} %join.3.refs_0_, bf16[192,768]{1,0:T(8,128)(2,1)} %copy-done.47, bf16[192,768]{1,0:T(8,128)(2,1)} %copy-done.48, bf16[192,768]{1,0:T(8,128)(2,1)} %collective-permute-done.50.refs_3_, ...), custom_call_target="tpu_custom_call" | custom-call | tf_op jit(solution)/shard_map/assemble/pallas_call | solution.py:998
  (267 shorter events, 69.7 us)
Async XLA Ops:
  6.5 42.2 %collective-permute-start = (bf16[320,768]{1,0:T(8,128)(2,1)}, bf16[320,768]{1,0:T(8,128)(2,1)S(1)}, u32[]{:S(2)}, u32[]{:S(2)}) collective-permute-start(bf16[320,768]{1,0:T(8,128)(2,1)} %get-tuple-element.149), channel_id=1, source_target_pairs={{0,2},{1,3},{2,0},{3,1},{4,6},{5,7},{6,4},{7,5},{8,10},{9,11},{10,... | collective-permute-start | bytes 1474568 | tf_op jit(solution)/shard_map/ppermute | solution.py:808
  9.6 39.1 %collective-permute-start.1 = (bf16[320,768]{1,0:T(8,128)(2,1)}, bf16[320,768]{1,0:T(8,128)(2,1)S(1)}, u32[]{:S(2)}, u32[]{:S(2)}) collective-permute-start(bf16[320,768]{1,0:T(8,128)(2,1)} %get-tuple-element.150), channel_id=1, source_target_pairs={{0,4},{1,5},{2,6},{3,7},{4,0},{5,1},{6,2},{7,3},{8,12},{9,13},{10,... | collective-permute-start | bytes 1474568 | tf_op jit(solution)/shard_map/ppermute | solution.py:808
  12.2 36.6 %collective-permute-start.2 = (bf16[320,768]{1,0:T(8,128)(2,1)}, bf16[320,768]{1,0:T(8,128)(2,1)S(1)}, u32[]{:S(2)}, u32[]{:S(2)}) collective-permute-start(bf16[320,768]{1,0:T(8,128)(2,1)} %get-tuple-element.151), channel_id=1, source_target_pairs={{0,6},{1,7},{2,4},{3,5},{4,2},{5,3},{6,0},{7,1},{8,14},{9,15},{10,... | collective-permute-start | bytes 1474568 | tf_op jit(solution)/shard_map/ppermute | solution.py:808
  48.7 7.9 %collective-permute-start.3 = (bf16[320,768]{1,0:T(8,128)(2,1)S(1)}, bf16[320,768]{1,0:T(8,128)(2,1)S(1)}, u32[]{:S(2)}, u32[]{:S(2)}) collective-permute-start(bf16[320,768]{1,0:T(8,128)(2,1)S(1)} %copy-done.15), channel_id=1, source_target_pairs={{0,1},{1,0},{2,3},{3,2},{4,5},{5,4},{6,7},{7,6},{8,9},{9,8},{10,11... | collective-permute-start | bytes 1474568 | tf_op jit(solution)/shard_map/ppermute | solution.py:808
  48.8 10.4 %collective-permute-start.4 = (bf16[320,768]{1,0:T(8,128)(2,1)S(1)}, bf16[320,768]{1,0:T(8,128)(2,1)S(1)}, u32[]{:S(2)}, u32[]{:S(2)}) collective-permute-start(bf16[320,768]{1,0:T(8,128)(2,1)S(1)} %collective-permute-done.refs_1_), channel_id=1, source_target_pairs={{0,1},{1,0},{2,3},{3,2},{4,5},{5,4},{6,7},{7,6},{8,9},{9,8},{10,11... | collective-permute-start | bytes 1474568 | tf_op jit(solution)/shard_map/ppermute | solution.py:808
  49.3 12.0 %collective-permute-start.5 = (bf16[320,768]{1,0:T(8,128)(2,1)S(1)}, bf16[320,768]{1,0:T(8,128)(2,1)}, u32[]{:S(2)}, u32[]{:S(2)}) collective-permute-start(bf16[320,768]{1,0:T(8,128)(2,1)S(1)} %collective-permute-done.1.refs_2_), channel_id=1, source_target_pairs={{0,1},{1,0},{2,3},{3,2},{4,5},{5,4},{6,7},{7,6},{8,9},{9,8},{10,11... | collective-permute-start | bytes 1474568 | tf_op jit(solution)/shard_map/ppermute | solution.py:808
  49.4 12.0 %collective-permute-start.6 = (bf16[320,768]{1,0:T(8,128)(2,1)S(1)}, bf16[320,768]{1,0:T(8,128)(2,1)}, u32[]{:S(2)}, u32[]{:S(2)}) collective-permute-start(bf16[320,768]{1,0:T(8,128)(2,1)S(1)} %collective-permute-done.2.refs_3_), channel_id=1, source_target_pairs={{0,1},{1,0},{2,3},{3,2},{4,5},{5,4},{6,7},{7,6},{8,9},{9,8},{10,11... | collective-permute-start | bytes 1474568 | tf_op jit(solution)/shard_map/ppermute | solution.py:808
  49.8 29.9 %collective-permute-start.7 = (bf16[320,768]{1,0:T(8,128)(2,1)}, bf16[320,768]{1,0:T(8,128)(2,1)S(1)}, u32[]{:S(2)}, u32[]{:S(2)}) collective-permute-start(bf16[320,768]{1,0:T(8,128)(2,1)} %get-tuple-element.159), channel_id=1, source_target_pairs={{0,2},{1,3},{2,0},{3,1},{4,6},{5,7},{6,4},{7,5},{8,10},{9,11},{10,... | collective-permute-start | bytes 1474568 | tf_op jit(solution)/shard_map/ppermute | solution.py:808
  57.4 36.3 %collective-permute-start.8 = (bf16[320,768]{1,0:T(8,128)(2,1)}, bf16[320,768]{1,0:T(8,128)(2,1)S(1)}, u32[]{:S(2)}, u32[]{:S(2)}) collective-permute-start(bf16[320,768]{1,0:T(8,128)(2,1)} %get-tuple-element.160), channel_id=1, source_target_pairs={{0,4},{1,5},{2,6},{3,7},{4,0},{5,1},{6,2},{7,3},{8,12},{9,13},{10,... | collective-permute-start | bytes 1474568 | tf_op jit(solution)/shard_map/ppermute | solution.py:808
  60.0 33.7 %collective-permute-start.9 = (bf16[320,768]{1,0:T(8,128)(2,1)}, bf16[320,768]{1,0:T(8,128)(2,1)S(1)}, u32[]{:S(2)}, u32[]{:S(2)}) collective-permute-start(bf16[320,768]{1,0:T(8,128)(2,1)} %get-tuple-element.161), channel_id=1, source_target_pairs={{0,6},{1,7},{2,4},{3,5},{4,2},{5,3},{6,0},{7,1},{8,14},{9,15},{10,... | collective-permute-start | bytes 1474568 | tf_op jit(solution)/shard_map/ppermute | solution.py:808
  131.2 57.5 %collective-permute-start.22 = (bf16[2,768,768]{2,1,0:T(8,128)(2,1)S(1)}, bf16[2,768,768]{2,1,0:T(8,128)(2,1)}, u32[]{:S(2)}, u32[]{:S(2)}) collective-permute-start(bf16[2,768,768]{2,1,0:T(8,128)(2,1)S(1)} %expert_weight_gradients.5), channel_id=1, source_target_pairs={{0,16},{8,24},{16,0},{24,8},{1,17},{9,25},{17,1},{25,9},{2,18},{10... | collective-permute-start | bytes 7077896 | tf_op jit(solution)/shard_map/ppermute | solution.py:808
  137.1 53.2 %collective-permute-start.21 = (bf16[2,768,768]{2,1,0:T(8,128)(2,1)S(1)}, bf16[2,768,768]{2,1,0:T(8,128)(2,1)}, u32[]{:S(2)}, u32[]{:S(2)}) collective-permute-start(bf16[2,768,768]{2,1,0:T(8,128)(2,1)S(1)} %expert_weight_gradients.4), channel_id=1, source_target_pairs={{0,8},{8,0},{16,24},{24,16},{1,9},{9,1},{17,25},{25,17},{2,10},{10... | collective-permute-start | bytes 7077896 | tf_op jit(solution)/shard_map/ppermute | solution.py:808
  138.7 32.1 %collective-permute-start.14 = (bf16[320,768]{1,0:T(8,128)(2,1)S(1)}, bf16[320,768]{1,0:T(8,128)(2,1)S(1)}, u32[]{:S(2)}, u32[]{:S(2)}) collective-permute-start(bf16[320,768]{1,0:T(8,128)(2,1)S(1)} %get-tuple-element.174), channel_id=1, source_target_pairs={{0,2},{1,3},{2,0},{3,1},{4,6},{5,7},{6,4},{7,5},{8,10},{9,11},{10,... | collective-permute-start | bytes 1474568 | tf_op jit(solution)/shard_map/ppermute | solution.py:808
  148.5 36.1 %collective-permute-start.15 = (bf16[320,768]{1,0:T(8,128)(2,1)S(1)}, bf16[320,768]{1,0:T(8,128)(2,1)S(1)}, u32[]{:S(2)}, u32[]{:S(2)}) collective-permute-start(bf16[320,768]{1,0:T(8,128)(2,1)S(1)} %get-tuple-element.175), channel_id=1, source_target_pairs={{0,4},{1,5},{2,6},{3,7},{4,0},{5,1},{6,2},{7,3},{8,12},{9,13},{10,... | collective-permute-start | bytes 1474568 | tf_op jit(solution)/shard_map/ppermute | solution.py:808
  149.5 35.1 %collective-permute-start.16 = (bf16[320,768]{1,0:T(8,128)(2,1)S(1)}, bf16[320,768]{1,0:T(8,128)(2,1)S(1)}, u32[]{:S(2)}, u32[]{:S(2)}) collective-permute-start(bf16[320,768]{1,0:T(8,128)(2,1)S(1)} %get-tuple-element.176), channel_id=1, source_target_pairs={{0,6},{1,7},{2,4},{3,5},{4,2},{5,3},{6,0},{7,1},{8,14},{9,15},{10,... | collective-permute-start | bytes 1474568 | tf_op jit(solution)/shard_map/ppermute | solution.py:808
  194.6 61.3 %collective-permute-start.26 = (bf16[1,768,768]{2,1,0:T(8,128)(2,1)}, bf16[1,768,768]{2,1,0:T(8,128)(2,1)}, u32[]{:S(2)}, u32[]{:S(2)}) collective-permute-start(bf16[1,768,768]{2,1,0:T(8,128)(2,1)} %get-tuple-element.189), channel_id=1, source_target_pairs={{0,16},{8,24},{16,0},{24,8},{1,17},{9,25},{17,1},{25,9},{2,18},{10... | collective-permute-start | bytes 3538952 | tf_op jit(solution)/shard_map/ppermute | solution.py:808
  195.2 60.7 %collective-permute-start.27 = (bf16[1,768,768]{2,1,0:T(8,128)(2,1)}, bf16[1,768,768]{2,1,0:T(8,128)(2,1)}, u32[]{:S(2)}, u32[]{:S(2)}) collective-permute-start(bf16[1,768,768]{2,1,0:T(8,128)(2,1)} %get-tuple-element.190), channel_id=1, source_target_pairs={{0,8},{8,0},{16,24},{24,16},{1,9},{9,1},{17,25},{25,17},{2,10},{10... | collective-permute-start | bytes 3538952 | tf_op jit(solution)/shard_map/ppermute | solution.py:808
  196.6 59.2 %collective-permute-start.23 = (bf16[320,768]{1,0:T(8,128)(2,1)}, bf16[320,768]{1,0:T(8,128)(2,1)}, u32[]{:S(2)}, u32[]{:S(2)}) collective-permute-start(bf16[320,768]{1,0:T(8,128)(2,1)} %get-tuple-element.199), channel_id=1, source_target_pairs={{0,2},{1,3},{2,0},{3,1},{4,6},{5,7},{6,4},{7,5},{8,10},{9,11},{10,... | collective-permute-start | bytes 1474568 | tf_op jit(solution)/shard_map/ppermute | solution.py:808
  206.5 49.4 %collective-permute-start.24 = (bf16[320,768]{1,0:T(8,128)(2,1)}, bf16[320,768]{1,0:T(8,128)(2,1)}, u32[]{:S(2)}, u32[]{:S(2)}) collective-permute-start(bf16[320,768]{1,0:T(8,128)(2,1)} %get-tuple-element.200), channel_id=1, source_target_pairs={{0,4},{1,5},{2,6},{3,7},{4,0},{5,1},{6,2},{7,3},{8,12},{9,13},{10,... | collective-permute-start | bytes 1474568 | tf_op jit(solution)/shard_map/ppermute | solution.py:808
  207.5 48.3 %collective-permute-start.25 = (bf16[320,768]{1,0:T(8,128)(2,1)S(1)}, bf16[320,768]{1,0:T(8,128)(2,1)}, u32[]{:S(2)}, u32[]{:S(2)}) collective-permute-start(bf16[320,768]{1,0:T(8,128)(2,1)S(1)} %get-tuple-element.201), channel_id=1, source_target_pairs={{0,6},{1,7},{2,4},{3,5},{4,2},{5,3},{6,0},{7,1},{8,14},{9,15},{10,... | collective-permute-start | bytes 1474568 | tf_op jit(solution)/shard_map/ppermute | solution.py:808
  256.0 13.4 %collective-permute-start.32 = (bf16[768,768]{1,0:T(8,128)(2,1)}, bf16[768,768]{1,0:T(8,128)(2,1)}, u32[]{:S(2)}, u32[]{:S(2)}) collective-permute-start(bf16[768,768]{1,0:T(8,128)(2,1)} %get-tuple-element.209), channel_id=1, source_target_pairs={{0,1},{1,0},{2,3},{3,2},{4,5},{5,4},{6,7},{7,6},{8,9},{9,8},{10,11... | collective-permute-start | bytes 3538952 | tf_op jit(solution)/shard_map/ppermute | solution.py:808
  262.0 14.4 %collective-permute-start.29 = (bf16[192,768]{1,0:T(8,128)(2,1)}, bf16[192,768]{1,0:T(8,128)(2,1)S(1)}, u32[]{:S(2)}, u32[]{:S(2)}) collective-permute-start(bf16[192,768]{1,0:T(8,128)(2,1)} %get-tuple-element.204), channel_id=1, source_target_pairs={{0,8},{8,0},{16,24},{24,16},{1,9},{9,1},{17,25},{25,17},{2,10},{10... | collective-permute-start | bytes 884744 | tf_op jit(solution)/shard_map/ppermute | solution.py:808
  262.5 24.7 %collective-permute-start.30 = (bf16[192,768]{1,0:T(8,128)(2,1)}, bf16[192,768]{1,0:T(8,128)(2,1)}, u32[]{:S(2)}, u32[]{:S(2)}) collective-permute-start(bf16[192,768]{1,0:T(8,128)(2,1)} %get-tuple-element.205), channel_id=1, source_target_pairs={{0,16},{8,24},{16,0},{24,8},{1,17},{9,25},{17,1},{25,9},{2,18},{10... | collective-permute-start | bytes 884744 | tf_op jit(solution)/shard_map/ppermute | solution.py:808
  264.1 23.2 %collective-permute-start.31 = (bf16[192,768]{1,0:T(8,128)(2,1)}, bf16[192,768]{1,0:T(8,128)(2,1)}, u32[]{:S(2)}, u32[]{:S(2)}) collective-permute-start(bf16[192,768]{1,0:T(8,128)(2,1)} %get-tuple-element.206), channel_id=1, source_target_pairs={{0,24},{8,16},{16,8},{24,0},{1,25},{9,17},{17,9},{25,1},{2,26},{10... | collective-permute-start | bytes 884744 | tf_op jit(solution)/shard_map/ppermute | solution.py:808
  274.3 32.1 %collective-permute-start.41 = (bf16[224,768]{1,0:T(8,128)(2,1)}, bf16[224,768]{1,0:T(8,128)(2,1)S(1)}, u32[]{:S(2)}, u32[]{:S(2)}) collective-permute-start(bf16[224,768]{1,0:T(8,128)(2,1)} %get-tuple-element.216), channel_id=1, source_target_pairs={{0,8},{8,0},{16,24},{24,16},{1,9},{9,1},{17,25},{25,17},{2,10},{10... | collective-permute-start | bytes 1032200 | tf_op jit(solution)/shard_map/ppermute | solution.py:808
  274.8 32.9 %collective-permute-start.42 = (bf16[224,768]{1,0:T(8,128)(2,1)}, bf16[224,768]{1,0:T(8,128)(2,1)S(1)}, u32[]{:S(2)}, u32[]{:S(2)}) collective-permute-start(bf16[224,768]{1,0:T(8,128)(2,1)} %get-tuple-element.217), channel_id=1, source_target_pairs={{0,16},{8,24},{16,0},{24,8},{1,17},{9,25},{17,1},{25,9},{2,18},{10... | collective-permute-start | bytes 1032200 | tf_op jit(solution)/shard_map/ppermute | solution.py:808
  276.4 31.4 %collective-permute-start.43 = (bf16[224,768]{1,0:T(8,128)(2,1)}, bf16[224,768]{1,0:T(8,128)(2,1)S(1)}, u32[]{:S(2)}, u32[]{:S(2)}) collective-permute-start(bf16[224,768]{1,0:T(8,128)(2,1)} %get-tuple-element.218), channel_id=1, source_target_pairs={{0,24},{8,16},{16,8},{24,0},{1,25},{9,17},{17,9},{25,1},{2,26},{10... | collective-permute-start | bytes 1032200 | tf_op jit(solution)/shard_map/ppermute | solution.py:808
  303.3 11.0 %collective-permute-start.37 = (bf16[48,768]{1,0:T(8,128)(2,1)}, bf16[48,768]{1,0:T(8,128)(2,1)S(1)}, u32[]{:S(2)}, u32[]{:S(2)}) collective-permute-start(bf16[48,768]{1,0:T(8,128)(2,1)} %share.9.refs_0_), channel_id=1, source_target_pairs={{0,2},{1,3},{2,0},{3,1},{4,6},{5,7},{6,4},{7,5},{8,10},{9,11},{10,... | collective-permute-start | bytes 221192 | tf_op jit(solution)/shard_map/ppermute | solution.py:808
  303.3 12.4 %collective-permute-start.38 = (bf16[48,768]{1,0:T(8,128)(2,1)}, bf16[48,768]{1,0:T(8,128)(2,1)S(1)}, u32[]{:S(2)}, u32[]{:S(2)}) collective-permute-start(bf16[48,768]{1,0:T(8,128)(2,1)} %share.9.refs_0_), channel_id=1, source_target_pairs={{0,4},{1,5},{2,6},{3,7},{4,0},{5,1},{6,2},{7,3},{8,12},{9,13},{10,... | collective-permute-start | bytes 221192 | tf_op jit(solution)/shard_map/ppermute | solution.py:808
  306.4 9.4 %collective-permute-start.39 = (bf16[48,768]{1,0:T(8,128)(2,1)}, bf16[48,768]{1,0:T(8,128)(2,1)S(1)}, u32[]{:S(2)}, u32[]{:S(2)}) collective-permute-start(bf16[48,768]{1,0:T(8,128)(2,1)} %share.9.refs_0_), channel_id=1, source_target_pairs={{0,6},{1,7},{2,4},{3,5},{4,2},{5,3},{6,0},{7,1},{8,14},{9,15},{10,... | collective-permute-start | bytes 221192 | tf_op jit(solution)/shard_map/ppermute | solution.py:808
  311.4 10.3 %collective-permute-start.44 = (bf16[80,768]{1,0:T(8,128)(2,1)}, bf16[80,768]{1,0:T(8,128)(2,1)S(1)}, u32[]{:S(2)}, u32[]{:S(2)}) collective-permute-start(bf16[80,768]{1,0:T(8,128)(2,1)} %get-tuple-element.234), channel_id=1, source_target_pairs={{0,2},{1,3},{2,0},{3,1},{4,6},{5,7},{6,4},{7,5},{8,10},{9,11},{10,... | collective-permute-start | bytes 368648 | tf_op jit(solution)/shard_map/ppermute | solution.py:808
  311.4 10.3 %collective-permute-start.45 = (bf16[80,768]{1,0:T(8,128)(2,1)}, bf16[80,768]{1,0:T(8,128)(2,1)S(1)}, u32[]{:S(2)}, u32[]{:S(2)}) collective-permute-start(bf16[80,768]{1,0:T(8,128)(2,1)} %get-tuple-element.235), channel_id=1, source_target_pairs={{0,4},{1,5},{2,6},{3,7},{4,0},{5,1},{6,2},{7,3},{8,12},{9,13},{10,... | collective-permute-start | bytes 368648 | tf_op jit(solution)/shard_map/ppermute | solution.py:808
  318.7 16.4 %collective-permute-start.40 = (bf16[192,768]{1,0:T(8,128)(2,1)}, bf16[192,768]{1,0:T(8,128)(2,1)S(1)}, u32[]{:S(2)}, u32[]{:S(2)}) collective-permute-start(bf16[192,768]{1,0:T(8,128)(2,1)} %join.2.refs_0_), channel_id=1, source_target_pairs={{0,24},{8,16},{16,8},{24,0},{1,25},{9,17},{17,9},{25,1},{2,26},{10... | collective-permute-start | bytes 884744 | tf_op jit(solution)/shard_map/ppermute | solution.py:808
  320.2 15.4 %collective-permute-start.55 = (bf16[192,768]{1,0:T(8,128)(2,1)}, bf16[192,768]{1,0:T(8,128)(2,1)S(1)}, u32[]{:S(2)}, u32[]{:S(2)}) collective-permute-start(bf16[192,768]{1,0:T(8,128)(2,1)} %join.2.refs_0_), channel_id=1, source_target_pairs={{0,8},{8,0},{16,24},{24,16},{1,9},{9,1},{17,25},{25,17},{2,10},{10... | collective-permute-start | bytes 884744 | tf_op jit(solution)/shard_map/ppermute | solution.py:808
  325.4 12.7 %collective-permute-start.56 = (bf16[192,768]{1,0:T(8,128)(2,1)}, bf16[192,768]{1,0:T(8,128)(2,1)}, u32[]{:S(2)}, u32[]{:S(2)}) collective-permute-start(bf16[192,768]{1,0:T(8,128)(2,1)} %join.2.refs_0_), channel_id=1, source_target_pairs={{0,16},{8,24},{16,0},{24,8},{1,17},{9,25},{17,1},{25,9},{2,18},{10... | collective-permute-start | bytes 884744 | tf_op jit(solution)/shard_map/ppermute | solution.py:808
  333.5 9.2 %collective-permute-start.51 = (bf16[320,768]{1,0:T(8,128)(2,1)S(1)}, bf16[320,768]{1,0:T(8,128)(2,1)S(1)}, u32[]{:S(2)}, u32[]{:S(2)}) collective-permute-start(bf16[320,768]{1,0:T(8,128)(2,1)S(1)} %get-tuple-element.247.refs_0_), channel_id=1, source_target_pairs={{0,1},{1,0},{2,3},{3,2},{4,5},{5,4},{6,7},{7,6},{8,9},{9,8},{10,11... | collective-permute-start | bytes 1474568 | tf_op jit(solution)/shard_map/ppermute | solution.py:808
  335.1 9.4 %collective-permute-start.53 = (bf16[320,768]{1,0:T(8,128)(2,1)}, bf16[320,768]{1,0:T(8,128)(2,1)S(1)}, u32[]{:S(2)}, u32[]{:S(2)}) collective-permute-start(bf16[320,768]{1,0:T(8,128)(2,1)} %collective-permute-done.24.refs_2_), channel_id=1, source_target_pairs={{0,1},{1,0},{2,3},{3,2},{4,5},{5,4},{6,7},{7,6},{8,9},{9,8},{10,11... | collective-permute-start | bytes 1474568 | tf_op jit(solution)/shard_map/ppermute | solution.py:808
  335.6 9.7 %collective-permute-start.54 = (bf16[320,768]{1,0:T(8,128)(2,1)}, bf16[320,768]{1,0:T(8,128)(2,1)S(1)}, u32[]{:S(2)}, u32[]{:S(2)}) collective-permute-start(bf16[320,768]{1,0:T(8,128)(2,1)} %collective-permute-done.25.refs_3_), channel_id=1, source_target_pairs={{0,1},{1,0},{2,3},{3,2},{4,5},{5,4},{6,7},{7,6},{8,9},{9,8},{10,11... | collective-permute-start | bytes 1474568 | tf_op jit(solution)/shard_map/ppermute | solution.py:808
  338.1 11.1 %collective-permute-start.50 = (bf16[192,768]{1,0:T(8,128)(2,1)}, bf16[192,768]{1,0:T(8,128)(2,1)}, u32[]{:S(2)}, u32[]{:S(2)}) collective-permute-start(bf16[192,768]{1,0:T(8,128)(2,1)} %join.3.refs_0_), channel_id=1, source_target_pairs={{0,24},{8,16},{16,8},{24,0},{1,25},{9,17},{17,9},{25,1},{2,26},{10... | collective-permute-start | bytes 884744 | tf_op jit(solution)/shard_map/ppermute | solution.py:808
  342.7 15.5 %collective-permute-start.57 = (bf16[192,768]{1,0:T(8,128)(2,1)S(1)}, bf16[192,768]{1,0:T(8,128)(2,1)S(1)}, u32[]{:S(2)}, u32[]{:S(2)}) collective-permute-start(bf16[192,768]{1,0:T(8,128)(2,1)S(1)} %copy-done.23), channel_id=1, source_target_pairs={{0,1},{1,0},{2,3},{3,2},{4,5},{5,4},{6,7},{7,6},{8,9},{9,8},{10,11... | collective-permute-start | bytes 884744 | tf_op jit(solution)/shard_map/ppermute | solution.py:808
  342.9 15.9 %collective-permute-start.61 = (bf16[192,768]{1,0:T(8,128)(2,1)S(1)}, bf16[192,768]{1,0:T(8,128)(2,1)S(1)}, u32[]{:S(2)}, u32[]{:S(2)}) collective-permute-start(bf16[192,768]{1,0:T(8,128)(2,1)S(1)} %copy-done.24), channel_id=1, source_target_pairs={{0,8},{8,0},{16,24},{24,16},{1,9},{9,1},{17,25},{25,17},{2,10},{10... | collective-permute-start | bytes 884744 | tf_op jit(solution)/shard_map/ppermute | solution.py:808
  344.5 14.4 %collective-permute-start.62 = (bf16[192,768]{1,0:T(8,128)(2,1)S(1)}, bf16[192,768]{1,0:T(8,128)(2,1)S(1)}, u32[]{:S(2)}, u32[]{:S(2)}) collective-permute-start(bf16[192,768]{1,0:T(8,128)(2,1)S(1)} %copy-done.24), channel_id=1, source_target_pairs={{0,16},{8,24},{16,0},{24,8},{1,17},{9,25},{17,1},{25,9},{2,18},{10... | collective-permute-start | bytes 884744 | tf_op jit(solution)/shard_map/ppermute | solution.py:808
  345.4 14.0 %collective-permute-start.58 = (bf16[192,768]{1,0:T(8,128)(2,1)S(1)}, bf16[192,768]{1,0:T(8,128)(2,1)S(1)}, u32[]{:S(2)}, u32[]{:S(2)}) collective-permute-start(bf16[192,768]{1,0:T(8,128)(2,1)S(1)} %collective-permute-done.55.refs_1_), channel_id=1, source_target_pairs={{0,1},{1,0},{2,3},{3,2},{4,5},{5,4},{6,7},{7,6},{8,9},{9,8},{10,11... | collective-permute-start | bytes 884744 | tf_op jit(solution)/shard_map/ppermute | solution.py:808
  349.2 10.3 %collective-permute-start.59 = (bf16[192,768]{1,0:T(8,128)(2,1)}, bf16[192,768]{1,0:T(8,128)(2,1)S(1)}, u32[]{:S(2)}, u32[]{:S(2)}) collective-permute-start(bf16[192,768]{1,0:T(8,128)(2,1)} %collective-permute-done.56.refs_2_), channel_id=1, source_target_pairs={{0,1},{1,0},{2,3},{3,2},{4,5},{5,4},{6,7},{7,6},{8,9},{9,8},{10,11... | collective-permute-start | bytes 884744 | tf_op jit(solution)/shard_map/ppermute | solution.py:808
  358.2 9.1 %collective-permute-start.63 = (bf16[192,768]{1,0:T(8,128)(2,1)S(1)}, bf16[192,768]{1,0:T(8,128)(2,1)S(1)}, u32[]{:S(2)}, u32[]{:S(2)}) collective-permute-start(bf16[192,768]{1,0:T(8,128)(2,1)S(1)} %copy-done.24), channel_id=1, source_target_pairs={{0,1},{1,0},{2,3},{3,2},{4,5},{5,4},{6,7},{7,6},{8,9},{9,8},{10,11... | collective-permute-start | bytes 884744 | tf_op jit(solution)/shard_map/ppermute | solution.py:808
  358.9 8.5 %collective-permute-start.66 = (bf16[192,768]{1,0:T(8,128)(2,1)}, bf16[192,768]{1,0:T(8,128)(2,1)S(1)}, u32[]{:S(2)}, u32[]{:S(2)}) collective-permute-start(bf16[192,768]{1,0:T(8,128)(2,1)} %collective-permute-done.50.refs_3_), channel_id=1, source_target_pairs={{0,1},{1,0},{2,3},{3,2},{4,5},{5,4},{6,7},{7,6},{8,9},{9,8},{10,11... | collective-permute-start | bytes 884744 | tf_op jit(solution)/shard_map/ppermute | solution.py:808
  359.4 8.0 %collective-permute-start.64 = (bf16[192,768]{1,0:T(8,128)(2,1)S(1)}, bf16[192,768]{1,0:T(8,128)(2,1)S(1)}, u32[]{:S(2)}, u32[]{:S(2)}) collective-permute-start(bf16[192,768]{1,0:T(8,128)(2,1)S(1)} %collective-permute-done.61.refs_1_), channel_id=1, source_target_pairs={{0,1},{1,0},{2,3},{3,2},{4,5},{5,4},{6,7},{7,6},{8,9},{9,8},{10,11... | collective-permute-start | bytes 884744 | tf_op jit(solution)/shard_map/ppermute | solution.py:808
  359.5 7.9 %collective-permute-start.65 = (bf16[192,768]{1,0:T(8,128)(2,1)S(1)}, bf16[192,768]{1,0:T(8,128)(2,1)S(1)}, u32[]{:S(2)}, u32[]{:S(2)}) collective-permute-start(bf16[192,768]{1,0:T(8,128)(2,1)S(1)} %collective-permute-done.62.refs_2_), channel_id=1, source_target_pairs={{0,1},{1,0},{2,3},{3,2},{4,5},{5,4},{6,7},{7,6},{8,9},{9,8},{10,11... | collective-permute-start | bytes 884744 | tf_op jit(solution)/shard_map/ppermute | solution.py:808
  (90 other events, 801.2 us)

commit v4 on v3

--- a/solution.py
+++ b/solution.py
@@ -328,16 +328,15 @@
     )(expert_out, *up_arrays)
 
 
-def expert_kernel(plan, expert_ref, up_ref, act_grad_ref, in_ref, router_ref, *refs):
-    count = len(plan.arrays)
-    row_refs = refs[: -(7 + count)]
+def expert_kernel(plan, inputs, count, expert_ref, up_ref, act_grad_ref, in_ref, router_ref, *refs):
+    row_refs = refs[:inputs]
     act_ref, slope_ref, scaled_ref, rows_grad_ref, gate_ref, logit_grad_ref = refs[
         -(7 + count) : -(1 + count)
     ]
     back_refs, rows_ref = refs[-(1 + count) : -1], refs[-1]
     block_rows = plan.block_rows
     step = pl.program_id(0)
-    steps = len(plan.arrays)
+    steps = count
     rows, hidden = act_ref.shape
     experts = router_ref.shape[0]
     blocks = plan.by_distance(row_refs)
@@ -390,14 +389,18 @@
             back_refs[number][...] = back
 
 
-def expert_part(expert, up_rows, act_grad, expert_in, router, row_arrays, plan):
+def expert_part(expert, up_rows, act_grad, expert_in, router, row_arrays, plan, first, previous):
     rows, width = up_rows.shape
     hidden = expert_in.shape[2]
     experts = router.shape[0]
-    steps = len(plan.arrays)
-    some = rows // steps
-    return pl.pallas_call(
-        functools.partial(expert_kernel, plan),
+    some = rows // len(plan.arrays)
+    steps = len(row_arrays) // 2 if plan.paired else 1
+
+    def block(columns):
+        return pl.BlockSpec((some, columns), lambda r: (first + r, 0))
+
+    return pl.pallas_call(
+        functools.partial(expert_kernel, plan, len(row_arrays), steps),
         grid=(steps,),
         out_shape=[
             shape_of((rows, hidden), BF),
@@ -407,21 +410,23 @@
             shape_of((rows, 1), F32),
             shape_of((rows, experts), BF),
         ]
-        + [shape_of((count, width), BF) for count in plan.arrays],
+        + [shape_of((count, width), BF) for count in plan.arrays[:steps]],
         in_specs=[
             smem(),
-            by_rows(some, width),
-            by_rows(some, hidden),
+            block(width),
+            block(hidden),
             whole((1, width, hidden)),
             whole((experts, width)),
         ]
-        + plan.specs(row_arrays),
-        out_specs=[by_rows(some, columns) for columns in (hidden, hidden, width, width, 1, experts)]
-        + [whole((count, width)) for count in plan.arrays],
+        + plan.specs(row_arrays)
+        + [pl.BlockSpec(memory_space=pl.ANY)] * len(previous),
+        out_specs=[block(columns) for columns in (hidden, hidden, width, width, 1, experts)]
+        + [whole((count, width)) for count in plan.arrays[:steps]],
+        input_output_aliases={5 + len(row_arrays) + n: n for n in range(len(previous))},
         scratch_shapes=[pltpu.VMEM((some, width), BF)],
         compiler_params=params(44),
         name="expert_rows",
-    )(expert, up_rows, act_grad, expert_in, router, *row_arrays)
+    )(expert, up_rows, act_grad, expert_in, router, *row_arrays, *previous)
 
 
 def later_sums_kernel(*refs):
@@ -1059,10 +1064,24 @@
     row_send, up_there = lax.optimization_barrier((row_send, up_there))
     row_there = plan.cross(row_send)
     up_rows, act_grad = expert_up_part(plan.finish(up_there), expert_out, plan)
-    row_there = lax.optimization_barrier((row_there, act_grad))[0]
-    act, slope, scaled_rows, rows_grad, gate, logit_grad, *back_send = expert_part(
-        expert, up_rows, act_grad, expert_in, router_weight.T, plan.finish(row_there), plan
-    )
+    cut = len(row_there) - 1 if plan.paired else len(row_there)
+    values, back_send = (), []
+    for first, some in ((0, row_there[:cut]), (cut, row_there[cut:])):
+        if some:
+            some = lax.optimization_barrier((some, values[4] if values else act_grad))[0]
+            outs = expert_part(
+                expert,
+                up_rows,
+                act_grad,
+                expert_in,
+                router_weight.T,
+                plan.finish(some),
+                plan,
+                first,
+                values,
+            )
+            values, back_send = outs[:6], back_send + list(outs[6:])
+    act, slope, scaled_rows, rows_grad, gate, logit_grad = values
     router_grad = dot(logit_grad, scaled_rows, 0, 0)
     back_there = plan.cross(back_send)
 

time: 380 us -> 371 us (0.976)
  starting transfers between devices: 86.2 us -> 66.3 us
  waiting for transfers between devices: 50.5 us -> 57.3 us
  Pallas kernels: 197 us -> 203 us
    ppermute x67, starting transfers between devices: 86.2 us -> 66.3 us  [swap(): lax.ppermute(values, axis, [(place, place ^ distance) for place in range(...]
    ppermute x67, waiting for transfers between devices: 50.5 us -> 57.3 us  [swap(): lax.ppermute(values, axis, [(place, place ^ distance) for place in range(...]
    pallas_call x1 -> x2, Pallas kernels: 24.6 us -> 28.2 us  [expert_part(): pl.pallas_call(functools.partial(expert_kernel, plan, len(row_arrays), st...]
    unnamed x142 -> x152, local copies, waits for them, and re-layouts: 26.3 us -> 25 us
  transfers between devices with their start and end apart: 67 -> 67, of which waited for: 17 -> 19; matrix products, arithmetic and copies ran while one was open for 3% -> 3% of each run, Pallas kernels for 41% -> 47%
where the time goes in v4:
time: 371 us; the launch traced here: 367 us
  Pallas kernels  203 us (55%)
  starting transfers between devices  66.3 us (18%)
  waiting for transfers between devices  57.3 us (15%)
  local copies, waits for them, and re-layouts  27.6 us (7%)
  other arithmetic  10.1 us (3%)
    ppermute x67, starting transfers between devices, swap(): lax.ppermute(values, axis, [(place, place ^ distance) for place in range(...  66.3 us
    ppermute x67, waiting for transfers between devices, swap(): lax.ppermute(values, axis, [(place, place ^ distance) for place in range(...  57.3 us
    pallas_call x1, Pallas kernels, backward_part(): pl.pallas_call(backward_kernel, grid=(pairs,), out_shape=[shape_of((3, se...  37.5 us
    pallas_call x1, Pallas kernels, forward_part(): pl.pallas_call(functools.partial(forward_kernel, plan), grid=(pairs,), ou...  36.8 us
    pallas_call x2, Pallas kernels, expert_part(): pl.pallas_call(functools.partial(expert_kernel, plan, len(row_arrays), st...  28.2 us
    unnamed x152, local copies, waits for them, and re-layouts  25 us
    pallas_call x3, Pallas kernels, weight_grad_part(): pl.pallas_call(functools.partial(weight_grad_kernel, transposed, len(term...  18.6 us
    pallas_call x6, Pallas kernels, share(): pl.pallas_call(kernel, out_shape=[shape_of(shape, BF) for shape in shapes...  13.5 us
  transfers between devices with their start and end apart: 67, of which 19 were waited for; matrix products, arithmetic and copies ran while one was open for 3% of the time, Pallas kernels for 47%

profile of v4, /device:TPU:0, one launch (start us, length us, event | category | flops | bytes accessed | tf_op | source)
XLA Modules:
  0.0 367.1 jit_solution(18135081215242431803)
XLA Ops:
  1.3 5.2 %slots.1 = (s32[1,1024]{1,0:T(1,128)}, s32[1024,128]{1,0:T(8,128)}, bf16[320,768]{1,0:T(8,128)(2,1)}, bf16[320,768]{1,0:T(8,128)(2,1)}, bf16[320,768]{1,0:T(8,128)(2,1)}, /*index=5*/bf16[320,768]{1,0:T(8,128)(2,1)}) custom-call(s32[1]{0:T(128)} %bitcast.3.expert_ref, s32[1]{0:T(128)S(6)} %copy.40.length_ref, s32[1,1024]{1,0:T(1,128)} %routes_ref.1, ...), custom_call_target="tpu_custom_call" | custom-call | tf_op jit(solution)/shard_map/slots/pallas_call | solution.py:136
  6.5 3.0 collective-permute-start
  9.6 2.6 collective-permute-start.1
  12.2 36.8 %attention_forward.1 = (bf16[12,1024,1024]{2,1,0:T(8,128)(2,1)}, bf16[3,6,1024,128]{3,2,1,0:T(8,128)(2,1)}, bf16[2,1024,768]{2,1,0:T(8,128)(2,1)}, f32[6,1024,12...) custom-call(s32[1]{0:T(128)} %bitcast.3.expert_ref, ...), custom_call_target="tpu_custom_call" | custom-call | tf_op jit(solution)/shard_map/attention_forward/pallas_call | solution.py:259
  50.1 6.6 %collective-permute-start.8 = (bf16[320,768]{1,0:T(8,128)(2,1)}, bf16[320,768]{1,0:T(8,128)(2,1)}, u32[]{:S(2)}, u32[]{:S(2)}) collective-permute-start(bf16[320,768]{1,0:T(8,128)(2,1)} %get-tuple-element.166), channel_id=1, source_target_pairs={{0,2},{1,3},{2,0},{3,1},{4,6},{5,7},{6,4},{7,5},{8,10},{9,11},{10,... | collective-permute-start | bytes 1474568 | tf_op jit(solution)/shard_map/ppermute | solution.py:813
  58.6 9.6 %expert_activation_gradient.1 = (bf16[1280,768]{1,0:T(8,128)(2,1)S(1)}, bf16[1280,3072]{1,0:T(8,128)(2,1)S(1)}) custom-call(bf16[1,3072,768]{2,1,0:T(8,128)(2,1)S(1)} %copy-done.3, bf16[320,768]{1,0:T(8,128)(2,1)S(1)} %copy-done.14, bf16[320,768]{1,0:T(8,128)(2,1)S(1)} %collective-permute-done.refs_1_, bf16[320,768]{1,0:T(8,128)(2,1)S(1)} %collective-permute-done.1.refs_2_, ...), custom_call_target="tpu_custom_call" | custom-call | tf_op jit(solution)/shard_map/expert_activation_gradient/pallas_call | solution.py:319
  68.1 3.2 copy-done.2
  72.6 6.3 %collective-permute-done.8.refs_1_ = bf16[320,768]{1,0:T(8,128)(2,1)} collective-permute-done((bf16[320,768]{1,0:T(8,128)(2,1)}, bf16[320,768]{1,0:T(8,128)(2,1)}, u32[]{:S(2)}, u32[]{:S(2)}) %collective-permute-start.8) | collective-permute-done | bytes 491552 | tf_op jit(solution)/shard_map/ppermute | solution.py:813
  78.9 2.5 collective-permute-done.9.refs_2_
  81.9 2.5 collective-permute-start.7
  89.8 19.8 %expert_rows.2 = (bf16[1280,3072]{1,0:T(8,128)(2,1)}, bf16[1280,3072]{1,0:T(8,128)(2,1)}, bf16[1280,768]{1,0:T(8,128)(2,1)S(1)}, bf16[1280,768]{1,0:T(8,128)(2,1...) custom-call(s32[1]{0:T(128)} %bitcast.3.expert_ref, ...), custom_call_target="tpu_custom_call" | custom-call | tf_op jit(solution)/shard_map/expert_rows/pallas_call | solution.py:402
  111.6 8.4 %expert_rows.3 = (bf16[1280,3072]{1,0:T(8,128)(2,1)}, bf16[1280,3072]{1,0:T(8,128)(2,1)}, bf16[1280,768]{1,0:T(8,128)(2,1)S(1)}, bf16[1280,768]{1,0:T(8,128)(2,1...) custom-call(s32[1]{0:T(128)} %bitcast.3.expert_ref, ...), custom_call_target="tpu_custom_call", output_to_operand_aliasing={{0}: (7, {}), {1}: (8, {}), {2}: (9, {}), {3}: (10, {}), {4... | custom-call | tf_op jit(solution)/shard_map/expert_rows/pallas_call | solution.py:402
  121.3 3.2 copy-done.1
  124.5 5.5 %expert_weight_gradients.5 = bf16[2,768,768]{2,1,0:T(8,128)(2,1)} custom-call(s32[2]{0:T(128)S(1)} %get-tuple-element.276.refs_0_, bf16[1280,3072]{1,0:T(8,128)(2,1)S(1)} %copy-done.1, bf16[1280,768]{1,0:T(8,128)(2,1)S(1)} %get-tuple-element.181.refs_5_.refs_2_), custom_call_target="tpu_custom_call" | custom-call | tf_op jit(solution)/shard_map/expert_weight_gradients/pallas_call | solution.py:470
  131.6 4.3 %expert_weight_gradients.4 = bf16[2,768,768]{2,1,0:T(8,128)(2,1)S(1)} custom-call(s32[2]{0:T(128)S(1)} %get-tuple-element.278.refs_0_, bf16[1280,3072]{1,0:T(8,128)(2,1)S(1)} %copy-done, bf16[1280,768]{1,0:T(8,128)(2,1)S(1)} %copy-done.5), custom_call_target="tpu_custom_call" | custom-call | tf_op jit(solution)/shard_map/expert_weight_gradients/pallas_call | solution.py:470
  137.5 2.1 collective-permute-start.15
  139.6 2.3 collective-permute-start.16
  141.9 8.2 %expert_output.1 = (bf16[320,768]{1,0:T(8,128)(2,1)S(1)}, bf16[320,768]{1,0:T(8,128)(2,1)}, bf16[320,768]{1,0:T(8,128)(2,1)}, bf16[320,768]{1,0:T(8,128)(2,1)}) custom-call(bf16[1280,3072]{1,0:T(8,128)(2,1)S(1)} %copy-done, bf16[1,3072,768]{2,1,0:T(8,128)(2,1)S(1)} %bitcast.17, f32[1280,1]{1,0:T(8,128)S(1)} %get-tuple-element.189.gate_ref), custom_call_target="tpu_custom_call" | custom-call | tf_op jit(solution)/shard_map/expert_output/pallas_call | solution.py:501
  150.1 8.7 %expert_weight_gradients.3 = (bf16[2,768,768]{2,1,0:T(8,128)(2,1)S(1)}, bf16[2,768,768]{2,1,0:T(8,128)(2,1)S(1)}) custom-call(s32[2]{0:T(128)S(1)} %get-tuple-element.279.refs_0_, s32[2]{0:T(128)S(1)} %get-tuple-element.277.refs_1_, bf16[1280,3072]{1,0:T(8,128)(2,1)S(1)} %copy-done, bf16[1280,3072]{1,0:T(8,128)(2,1)} %get-tuple-element.179.refs_3_.refs_1_, ...), custom_call_target="tpu_custom_call" | custom-call | tf_op jit(solution)/shard_map/expert_weight_gradients/pallas_call | solution.py:470
  161.6 12.0 %collective-permute-done.15.refs_2_ = bf16[320,768]{1,0:T(8,128)(2,1)S(1)} collective-permute-done((bf16[320,768]{1,0:T(8,128)(2,1)S(1)}, bf16[320,768]{1,0:T(8,128)(2,1)S(1)}, u32[]{:S(2)}, u32[]{:S(2)}) %collective-permute-start.15) | collective-permute-done | bytes 491552 | tf_op jit(solution)/shard_map/ppermute | solution.py:813
  177.7 6.0 %collective-permute-done.22.refs_3_ = bf16[2,768,768]{2,1,0:T(8,128)(2,1)} collective-permute-done((bf16[2,768,768]{2,1,0:T(8,128)(2,1)}, bf16[2,768,768]{2,1,0:T(8,128)(2,1)}, u32[]{:S(2)}, u32[]{:S(2)}) %collective-permute-start.22) | collective-permute-done | bytes 2359328 | tf_op jit(solution)/shard_map/ppermute | solution.py:813
  183.7 5.5 %collective-permute-done.21.refs_2_ = bf16[2,768,768]{2,1,0:T(8,128)(2,1)} collective-permute-done((bf16[2,768,768]{2,1,0:T(8,128)(2,1)S(1)}, bf16[2,768,768]{2,1,0:T(8,128)(2,1)}, u32[]{:S(2)}, u32[]{:S(2)}) %collective-permute-start.21) | collective-permute-done | bytes 2359328 | tf_op jit(solution)/shard_map/ppermute | solution.py:813
  189.2 4.3 %later_sums.1 = (bf16[1,768,768]{2,1,0:T(8,128)(2,1)}, bf16[1,768,768]{2,1,0:T(8,128)(2,1)}) custom-call(bf16[2,768,768]{2,1,0:T(8,128)(2,1)} %copy-done.8, bf16[2,768,768]{2,1,0:T(8,128)(2,1)} %copy-done.10, bf16[2,768,768]{2,1,0:T(8,128)(2,1)} %collective-permute-done.21.refs_2_, bf16[2,768,768]{2,1,0:T(8,128)(2,1)} %collective-permute-done.22.refs_3_), custom_call_target="tpu_custom_call" | custom-call | tf_op jit(solution)/shard_map/later_sums/pallas_call | solution.py:446
  195.5 2.0 collective-permute-start.24
  197.6 2.4 collective-permute-start.25
  199.9 9.5 %expert_norm_backward.1 = (f32[1024,768]{1,0:T(8,128)}, bf16[1024,768]{1,0:T(8,128)(2,1)}, bf16[1024,768]{1,0:T(8,128)(2,1)}, f32[1,768]{1,0:T(1,128)}) custom-call(s32[1]{0:T(128)} %bitcast.3.expert_ref, s32[1]{0:T(128)S(6)} %copy.40.length_ref, s32[1024,128]{1,0:T(8,128)} %get-tuple-element.148.column_ref, f32[1024,768]{1,0:T(8,128)} %get-tuple-element.258.resid_ref, ...), custom_call_target="tpu_custom_call" | custom-call | tf_op jit(solution)/shard_map/expert_norm_backward/pallas_call | solution.py:575
  209.5 37.5 %attention_backward.1 = (bf16[3,1024,768]{2,1,0:T(8,128)(2,1)}, f32[6,2,768]{2,1,0:T(2,128)}, bf16[768,768]{1,0:T(8,128)(2,1)}, bf16[768,768]{1,0:T(8,128)(2,1)}...) custom-call(s32[1]{0:T(128)} %bitcast.2.core_ref, bf16[3,6,1024,128]{3,2,1,0:T(8,128)(2,1)} %get-tuple-element.145.qkv_ref, ...), custom_call_target="tpu_custom_call" | custom-call | tf_op jit(solution)/shard_map/attention_backward/pallas_call | solution.py:703
  247.6 2.7 collective-permute-done.28.refs_1_
  250.3 2.8 share.6
  258.3 2.2 extra_rows.1.refs_2_
  262.5 2.9 share.7
  268.9 9.4 %token_gradient.1 = f32[1024,768]{1,0:T(8,128)} custom-call(bf16[3,1024,768]{2,1,0:T(8,128)(2,1)} %get-tuple-element.231.back_ref, bf16[768,768]{1,0:T(8,128)(2,1)} %refs_8_.2, bf16[768,768]{1,0:T(8,128)(2,1)} %refs_9_.1, bf16[768,768]{1,0:T(8,128)(2,1)} %refs_8_.3, bf16[1024,768]{1,0:T(8,128)(2,1)} %bitcast.21, bf16[768]{0:T(1024)(128)(2,1)} %gain_ref.3, ...), custom_call_target="tpu_custom_call" | custom-call | tf_op jit(solution)/shard_map/token_gradient/pallas_call | solution.py:799
  278.4 2.1 share.8
  280.5 2.0 collective-permute-start.35
  282.5 2.6 collective-permute-done.34.refs_1_
  287.6 4.0 %collective-permute-done.36.refs_3_ = bf16[48,768]{1,0:T(8,128)(2,1)S(1)} collective-permute-done((bf16[48,768]{1,0:T(8,128)(2,1)}, bf16[48,768]{1,0:T(8,128)(2,1)S(1)}, u32[]{:S(2)}, u32[]{:S(2)}) %collective-permute-start.36) | collective-permute-done | bytes 73760 | tf_op jit(solution)/shard_map/ppermute | solution.py:813
  293.8 2.0 collective-permute-start.38
  295.8 2.4 collective-permute-start.39
  299.7 2.2 share.10
  301.9 2.0 collective-permute-start.45
  303.9 2.4 collective-permute-start.46
  323.5 2.2 collective-permute-done.49.refs_3_
  329.8 3.4 convert_add_fusion
  336.0 3.7 %collective-permute-done.50.refs_3_ = bf16[192,768]{1,0:T(8,128)(2,1)S(1)} collective-permute-done((bf16[192,768]{1,0:T(8,128)(2,1)}, bf16[192,768]{1,0:T(8,128)(2,1)S(1)}, u32[]{:S(2)}, u32[]{:S(2)}) %collective-permute-start.50) | collective-permute-done | bytes 294944 | tf_op jit(solution)/shard_map/ppermute | solution.py:813
  340.4 3.6 convert_add_fusion.1
  344.0 5.5 %result.1 = bf16[1024,768]{1,0:T(8,128)(2,1)} custom-call(s32[1]{0:T(128)} %bitcast.3.expert_ref, s32[1]{0:T(128)S(6)} %copy.40.length_ref, s32[1024,128]{1,0:T(8,128)} %get-tuple-element.148.column_ref, f32[1024,768]{1,0:T(8,128)} %get-tuple-element.258.resid_ref, bf16[320,768]{1,0:T(8,128)(2,1)} %copy-done.12, bf16[320,768]{1,0:T(8,128)(2,1)} %copy-done.28, ...), custom_call_target="tpu_custom_call" | custom-call | tf_op jit(solution)/shard_map/result/pallas_call | solution.py:529
  352.8 5.5 %assemble.2 = (f32[768,768]{1,0:T(8,128)}, f32[768,768]{1,0:T(8,128)}, f32[768,128]{1,0:T(8,128)}) custom-call(s32[2]{0:T(128)} %pad_add_fusion.places_ref, bf16[192,768]{1,0:T(8,128)(2,1)} %join.2.refs_0_, bf16[192,768]{1,0:T(8,128)(2,1)} %collective-permute-done.55.refs_1_, bf16[192,768]{1,0:T(8,128)(2,1)} %collective-permute-done.56.refs_2_, ...), custom_call_target="tpu_custom_call" | custom-call | tf_op jit(solution)/shard_map/assemble/pallas_call | solution.py:1003
  359.9 5.1 %assemble.3 = (f32[768,768]{1,0:T(8,128)}, f32[768,768]{1,0:T(8,128)}, f32[768,128]{1,0:T(8,128)}) custom-call(s32[2]{0:T(128)} %pad_add_fusion.places_ref, bf16[192,768]{1,0:T(8,128)(2,1)} %join.3.refs_0_, bf16[192,768]{1,0:T(8,128)(2,1)} %copy-done.52, bf16[192,768]{1,0:T(8,128)(2,1)} %copy-done.53, bf16[192,768]{1,0:T(8,128)(2,1)} %copy-done.50, ...), custom_call_target="tpu_custom_call" | custom-call | tf_op jit(solution)/shard_map/assemble/pallas_call | solution.py:1003
  (278 shorter events, 74.1 us)
Async XLA Ops:
  6.5 42.4 %collective-permute-start = (bf16[320,768]{1,0:T(8,128)(2,1)}, bf16[320,768]{1,0:T(8,128)(2,1)S(1)}, u32[]{:S(2)}, u32[]{:S(2)}) collective-permute-start(bf16[320,768]{1,0:T(8,128)(2,1)} %get-tuple-element.155), channel_id=1, source_target_pairs={{0,2},{1,3},{2,0},{3,1},{4,6},{5,7},{6,4},{7,5},{8,10},{9,11},{10,... | collective-permute-start | bytes 1474568 | tf_op jit(solution)/shard_map/ppermute | solution.py:813
  9.6 39.4 %collective-permute-start.1 = (bf16[320,768]{1,0:T(8,128)(2,1)}, bf16[320,768]{1,0:T(8,128)(2,1)S(1)}, u32[]{:S(2)}, u32[]{:S(2)}) collective-permute-start(bf16[320,768]{1,0:T(8,128)(2,1)} %get-tuple-element.156), channel_id=1, source_target_pairs={{0,4},{1,5},{2,6},{3,7},{4,0},{5,1},{6,2},{7,3},{8,12},{9,13},{10,... | collective-permute-start | bytes 1474568 | tf_op jit(solution)/shard_map/ppermute | solution.py:813
  12.1 36.8 %collective-permute-start.2 = (bf16[320,768]{1,0:T(8,128)(2,1)}, bf16[320,768]{1,0:T(8,128)(2,1)}, u32[]{:S(2)}, u32[]{:S(2)}) collective-permute-start(bf16[320,768]{1,0:T(8,128)(2,1)} %get-tuple-element.157), channel_id=1, source_target_pairs={{0,6},{1,7},{2,4},{3,5},{4,2},{5,3},{6,0},{7,1},{8,14},{9,15},{10,... | collective-permute-start | bytes 1474568 | tf_op jit(solution)/shard_map/ppermute | solution.py:813
  49.1 9.4 %collective-permute-start.4 = (bf16[320,768]{1,0:T(8,128)(2,1)S(1)}, bf16[320,768]{1,0:T(8,128)(2,1)S(1)}, u32[]{:S(2)}, u32[]{:S(2)}) collective-permute-start(bf16[320,768]{1,0:T(8,128)(2,1)S(1)} %collective-permute-done.refs_1_), channel_id=1, source_target_pairs={{0,1},{1,0},{2,3},{3,2},{4,5},{5,4},{6,7},{7,6},{8,9},{9,8},{10,11... | collective-permute-start | bytes 1474568 | tf_op jit(solution)/shard_map/ppermute | solution.py:813
  49.6 9.0 %collective-permute-start.5 = (bf16[320,768]{1,0:T(8,128)(2,1)S(1)}, bf16[320,768]{1,0:T(8,128)(2,1)S(1)}, u32[]{:S(2)}, u32[]{:S(2)}) collective-permute-start(bf16[320,768]{1,0:T(8,128)(2,1)S(1)} %collective-permute-done.1.refs_2_), channel_id=1, source_target_pairs={{0,1},{1,0},{2,3},{3,2},{4,5},{5,4},{6,7},{7,6},{8,9},{9,8},{10,11... | collective-permute-start | bytes 1474568 | tf_op jit(solution)/shard_map/ppermute | solution.py:813
  49.7 8.9 %collective-permute-start.6 = (bf16[320,768]{1,0:T(8,128)(2,1)}, bf16[320,768]{1,0:T(8,128)(2,1)S(1)}, u32[]{:S(2)}, u32[]{:S(2)}) collective-permute-start(bf16[320,768]{1,0:T(8,128)(2,1)} %collective-permute-done.2.refs_3_), channel_id=1, source_target_pairs={{0,1},{1,0},{2,3},{3,2},{4,5},{5,4},{6,7},{7,6},{8,9},{9,8},{10,11... | collective-permute-start | bytes 1474568 | tf_op jit(solution)/shard_map/ppermute | solution.py:813
  50.1 28.8 %collective-permute-start.8 = (bf16[320,768]{1,0:T(8,128)(2,1)}, bf16[320,768]{1,0:T(8,128)(2,1)}, u32[]{:S(2)}, u32[]{:S(2)}) collective-permute-start(bf16[320,768]{1,0:T(8,128)(2,1)} %get-tuple-element.166), channel_id=1, source_target_pairs={{0,2},{1,3},{2,0},{3,1},{4,6},{5,7},{6,4},{7,5},{8,10},{9,11},{10,... | collective-permute-start | bytes 1474568 | tf_op jit(solution)/shard_map/ppermute | solution.py:813
  56.7 24.7 %collective-permute-start.9 = (bf16[320,768]{1,0:T(8,128)(2,1)}, bf16[320,768]{1,0:T(8,128)(2,1)}, u32[]{:S(2)}, u32[]{:S(2)}) collective-permute-start(bf16[320,768]{1,0:T(8,128)(2,1)} %get-tuple-element.167), channel_id=1, source_target_pairs={{0,4},{1,5},{2,6},{3,7},{4,0},{5,1},{6,2},{7,3},{8,12},{9,13},{10,... | collective-permute-start | bytes 1474568 | tf_op jit(solution)/shard_map/ppermute | solution.py:813
  81.9 27.7 %collective-permute-start.7 = (bf16[320,768]{1,0:T(8,128)(2,1)}, bf16[320,768]{1,0:T(8,128)(2,1)S(1)}, u32[]{:S(2)}, u32[]{:S(2)}) collective-permute-start(bf16[320,768]{1,0:T(8,128)(2,1)} %get-tuple-element.164), channel_id=1, source_target_pairs={{0,6},{1,7},{2,4},{3,5},{4,2},{5,3},{6,0},{7,1},{8,14},{9,15},{10,... | collective-permute-start | bytes 1474568 | tf_op jit(solution)/shard_map/ppermute | solution.py:813
  130.0 53.7 %collective-permute-start.22 = (bf16[2,768,768]{2,1,0:T(8,128)(2,1)}, bf16[2,768,768]{2,1,0:T(8,128)(2,1)}, u32[]{:S(2)}, u32[]{:S(2)}) collective-permute-start(bf16[2,768,768]{2,1,0:T(8,128)(2,1)} %expert_weight_gradients.5), channel_id=1, source_target_pairs={{0,16},{8,24},{16,0},{24,8},{1,17},{9,25},{17,1},{25,9},{2,18},{10... | collective-permute-start | bytes 7077896 | tf_op jit(solution)/shard_map/ppermute | solution.py:813
  135.9 53.3 %collective-permute-start.21 = (bf16[2,768,768]{2,1,0:T(8,128)(2,1)S(1)}, bf16[2,768,768]{2,1,0:T(8,128)(2,1)}, u32[]{:S(2)}, u32[]{:S(2)}) collective-permute-start(bf16[2,768,768]{2,1,0:T(8,128)(2,1)S(1)} %expert_weight_gradients.4), channel_id=1, source_target_pairs={{0,8},{8,0},{16,24},{24,16},{1,9},{9,1},{17,25},{25,17},{2,10},{10... | collective-permute-start | bytes 7077896 | tf_op jit(solution)/shard_map/ppermute | solution.py:813
  137.5 24.2 %collective-permute-start.14 = (bf16[320,768]{1,0:T(8,128)(2,1)S(1)}, bf16[320,768]{1,0:T(8,128)(2,1)S(1)}, u32[]{:S(2)}, u32[]{:S(2)}) collective-permute-start(bf16[320,768]{1,0:T(8,128)(2,1)S(1)} %copy-done.25), channel_id=1, source_target_pairs={{0,2},{1,3},{2,0},{3,1},{4,6},{5,7},{6,4},{7,5},{8,10},{9,11},{10,... | collective-permute-start | bytes 1474568 | tf_op jit(solution)/shard_map/ppermute | solution.py:813
  137.5 36.2 %collective-permute-start.15 = (bf16[320,768]{1,0:T(8,128)(2,1)S(1)}, bf16[320,768]{1,0:T(8,128)(2,1)S(1)}, u32[]{:S(2)}, u32[]{:S(2)}) collective-permute-start(bf16[320,768]{1,0:T(8,128)(2,1)S(1)} %copy-done.23), channel_id=1, source_target_pairs={{0,4},{1,5},{2,6},{3,7},{4,0},{5,1},{6,2},{7,3},{8,12},{9,13},{10,... | collective-permute-start | bytes 1474568 | tf_op jit(solution)/shard_map/ppermute | solution.py:813
  139.6 34.0 %collective-permute-start.16 = (bf16[320,768]{1,0:T(8,128)(2,1)}, bf16[320,768]{1,0:T(8,128)(2,1)S(1)}, u32[]{:S(2)}, u32[]{:S(2)}) collective-permute-start(bf16[320,768]{1,0:T(8,128)(2,1)} %get-tuple-element.188), channel_id=1, source_target_pairs={{0,6},{1,7},{2,4},{3,5},{4,2},{5,3},{6,0},{7,1},{8,14},{9,15},{10,... | collective-permute-start | bytes 1474568 | tf_op jit(solution)/shard_map/ppermute | solution.py:813
  193.5 53.5 %collective-permute-start.26 = (bf16[1,768,768]{2,1,0:T(8,128)(2,1)}, bf16[1,768,768]{2,1,0:T(8,128)(2,1)}, u32[]{:S(2)}, u32[]{:S(2)}) collective-permute-start(bf16[1,768,768]{2,1,0:T(8,128)(2,1)} %get-tuple-element.201), channel_id=1, source_target_pairs={{0,16},{8,24},{16,0},{24,8},{1,17},{9,25},{17,1},{25,9},{2,18},{10... | collective-permute-start | bytes 3538952 | tf_op jit(solution)/shard_map/ppermute | solution.py:813
  194.0 53.0 %collective-permute-start.27 = (bf16[1,768,768]{2,1,0:T(8,128)(2,1)}, bf16[1,768,768]{2,1,0:T(8,128)(2,1)}, u32[]{:S(2)}, u32[]{:S(2)}) collective-permute-start(bf16[1,768,768]{2,1,0:T(8,128)(2,1)} %get-tuple-element.202), channel_id=1, source_target_pairs={{0,8},{8,0},{16,24},{24,16},{1,9},{9,1},{17,25},{25,17},{2,10},{10... | collective-permute-start | bytes 3538952 | tf_op jit(solution)/shard_map/ppermute | solution.py:813
  195.5 51.4 %collective-permute-start.23 = (bf16[320,768]{1,0:T(8,128)(2,1)}, bf16[320,768]{1,0:T(8,128)(2,1)S(1)}, u32[]{:S(2)}, u32[]{:S(2)}) collective-permute-start(bf16[320,768]{1,0:T(8,128)(2,1)} %get-tuple-element.211), channel_id=1, source_target_pairs={{0,2},{1,3},{2,0},{3,1},{4,6},{5,7},{6,4},{7,5},{8,10},{9,11},{10,... | collective-permute-start | bytes 1474568 | tf_op jit(solution)/shard_map/ppermute | solution.py:813
  195.5 51.4 %collective-permute-start.24 = (bf16[320,768]{1,0:T(8,128)(2,1)}, bf16[320,768]{1,0:T(8,128)(2,1)}, u32[]{:S(2)}, u32[]{:S(2)}) collective-permute-start(bf16[320,768]{1,0:T(8,128)(2,1)} %get-tuple-element.212), channel_id=1, source_target_pairs={{0,4},{1,5},{2,6},{3,7},{4,0},{5,1},{6,2},{7,3},{8,12},{9,13},{10,... | collective-permute-start | bytes 1474568 | tf_op jit(solution)/shard_map/ppermute | solution.py:813
  197.6 49.4 %collective-permute-start.25 = (bf16[320,768]{1,0:T(8,128)(2,1)}, bf16[320,768]{1,0:T(8,128)(2,1)}, u32[]{:S(2)}, u32[]{:S(2)}) collective-permute-start(bf16[320,768]{1,0:T(8,128)(2,1)} %get-tuple-element.213), channel_id=1, source_target_pairs={{0,6},{1,7},{2,4},{3,5},{4,2},{5,3},{6,0},{7,1},{8,14},{9,15},{10,... | collective-permute-start | bytes 1474568 | tf_op jit(solution)/shard_map/ppermute | solution.py:813
  247.1 13.3 %collective-permute-start.32 = (bf16[768,768]{1,0:T(8,128)(2,1)}, bf16[768,768]{1,0:T(8,128)(2,1)}, u32[]{:S(2)}, u32[]{:S(2)}) collective-permute-start(bf16[768,768]{1,0:T(8,128)(2,1)} %get-tuple-element.221), channel_id=1, source_target_pairs={{0,1},{1,0},{2,3},{3,2},{4,5},{5,4},{6,7},{7,6},{8,9},{9,8},{10,11... | collective-permute-start | bytes 3538952 | tf_op jit(solution)/shard_map/ppermute | solution.py:813
  253.1 14.4 %collective-permute-start.29 = (bf16[192,768]{1,0:T(8,128)(2,1)}, bf16[192,768]{1,0:T(8,128)(2,1)}, u32[]{:S(2)}, u32[]{:S(2)}) collective-permute-start(bf16[192,768]{1,0:T(8,128)(2,1)} %get-tuple-element.216), channel_id=1, source_target_pairs={{0,8},{8,0},{16,24},{24,16},{1,9},{9,1},{17,25},{25,17},{2,10},{10... | collective-permute-start | bytes 884744 | tf_op jit(solution)/shard_map/ppermute | solution.py:813
  253.6 24.7 %collective-permute-start.30 = (bf16[192,768]{1,0:T(8,128)(2,1)}, bf16[192,768]{1,0:T(8,128)(2,1)}, u32[]{:S(2)}, u32[]{:S(2)}) collective-permute-start(bf16[192,768]{1,0:T(8,128)(2,1)} %get-tuple-element.217), channel_id=1, source_target_pairs={{0,16},{8,24},{16,0},{24,8},{1,17},{9,25},{17,1},{25,9},{2,18},{10... | collective-permute-start | bytes 884744 | tf_op jit(solution)/shard_map/ppermute | solution.py:813
  255.1 23.2 %collective-permute-start.31 = (bf16[192,768]{1,0:T(8,128)(2,1)}, bf16[192,768]{1,0:T(8,128)(2,1)}, u32[]{:S(2)}, u32[]{:S(2)}) collective-permute-start(bf16[192,768]{1,0:T(8,128)(2,1)} %get-tuple-element.218), channel_id=1, source_target_pairs={{0,24},{8,16},{16,8},{24,0},{1,25},{9,17},{17,9},{25,1},{2,26},{10... | collective-permute-start | bytes 884744 | tf_op jit(solution)/shard_map/ppermute | solution.py:813
  265.4 30.4 %collective-permute-start.41 = (bf16[224,768]{1,0:T(8,128)(2,1)}, bf16[224,768]{1,0:T(8,128)(2,1)S(1)}, u32[]{:S(2)}, u32[]{:S(2)}) collective-permute-start(bf16[224,768]{1,0:T(8,128)(2,1)} %get-tuple-element.228), channel_id=1, source_target_pairs={{0,8},{8,0},{16,24},{24,16},{1,9},{9,1},{17,25},{25,17},{2,10},{10... | collective-permute-start | bytes 1032200 | tf_op jit(solution)/shard_map/ppermute | solution.py:813
  265.9 32.3 %collective-permute-start.42 = (bf16[224,768]{1,0:T(8,128)(2,1)}, bf16[224,768]{1,0:T(8,128)(2,1)S(1)}, u32[]{:S(2)}, u32[]{:S(2)}) collective-permute-start(bf16[224,768]{1,0:T(8,128)(2,1)} %get-tuple-element.229), channel_id=1, source_target_pairs={{0,16},{8,24},{16,0},{24,8},{1,17},{9,25},{17,1},{25,9},{2,18},{10... | collective-permute-start | bytes 1032200 | tf_op jit(solution)/shard_map/ppermute | solution.py:813
  267.4 30.8 %collective-permute-start.43 = (bf16[224,768]{1,0:T(8,128)(2,1)}, bf16[224,768]{1,0:T(8,128)(2,1)S(1)}, u32[]{:S(2)}, u32[]{:S(2)}) collective-permute-start(bf16[224,768]{1,0:T(8,128)(2,1)} %get-tuple-element.230), channel_id=1, source_target_pairs={{0,24},{8,16},{16,8},{24,0},{1,25},{9,17},{17,9},{25,1},{2,26},{10... | collective-permute-start | bytes 1032200 | tf_op jit(solution)/shard_map/ppermute | solution.py:813
  293.8 10.1 %collective-permute-start.37 = (bf16[48,768]{1,0:T(8,128)(2,1)}, bf16[48,768]{1,0:T(8,128)(2,1)S(1)}, u32[]{:S(2)}, u32[]{:S(2)}) collective-permute-start(bf16[48,768]{1,0:T(8,128)(2,1)} %share.9.refs_0_), channel_id=1, source_target_pairs={{0,2},{1,3},{2,0},{3,1},{4,6},{5,7},{6,4},{7,5},{8,10},{9,11},{10,... | collective-permute-start | bytes 221192 | tf_op jit(solution)/shard_map/ppermute | solution.py:813
  293.8 12.5 %collective-permute-start.38 = (bf16[48,768]{1,0:T(8,128)(2,1)}, bf16[48,768]{1,0:T(8,128)(2,1)S(1)}, u32[]{:S(2)}, u32[]{:S(2)}) collective-permute-start(bf16[48,768]{1,0:T(8,128)(2,1)} %share.9.refs_0_), channel_id=1, source_target_pairs={{0,4},{1,5},{2,6},{3,7},{4,0},{5,1},{6,2},{7,3},{8,12},{9,13},{10,... | collective-permute-start | bytes 221192 | tf_op jit(solution)/shard_map/ppermute | solution.py:813
  295.8 10.4 %collective-permute-start.39 = (bf16[48,768]{1,0:T(8,128)(2,1)}, bf16[48,768]{1,0:T(8,128)(2,1)S(1)}, u32[]{:S(2)}, u32[]{:S(2)}) collective-permute-start(bf16[48,768]{1,0:T(8,128)(2,1)} %share.9.refs_0_), channel_id=1, source_target_pairs={{0,6},{1,7},{2,4},{3,5},{4,2},{5,3},{6,0},{7,1},{8,14},{9,15},{10,... | collective-permute-start | bytes 221192 | tf_op jit(solution)/shard_map/ppermute | solution.py:813
  301.9 10.4 %collective-permute-start.44 = (bf16[80,768]{1,0:T(8,128)(2,1)}, bf16[80,768]{1,0:T(8,128)(2,1)S(1)}, u32[]{:S(2)}, u32[]{:S(2)}) collective-permute-start(bf16[80,768]{1,0:T(8,128)(2,1)} %get-tuple-element.246), channel_id=1, source_target_pairs={{0,2},{1,3},{2,0},{3,1},{4,6},{5,7},{6,4},{7,5},{8,10},{9,11},{10,... | collective-permute-start | bytes 368648 | tf_op jit(solution)/shard_map/ppermute | solution.py:813
  301.9 10.4 %collective-permute-start.45 = (bf16[80,768]{1,0:T(8,128)(2,1)}, bf16[80,768]{1,0:T(8,128)(2,1)S(1)}, u32[]{:S(2)}, u32[]{:S(2)}) collective-permute-start(bf16[80,768]{1,0:T(8,128)(2,1)} %get-tuple-element.247), channel_id=1, source_target_pairs={{0,4},{1,5},{2,6},{3,7},{4,0},{5,1},{6,2},{7,3},{8,12},{9,13},{10,... | collective-permute-start | bytes 368648 | tf_op jit(solution)/shard_map/ppermute | solution.py:813
  303.9 8.4 %collective-permute-start.46 = (bf16[80,768]{1,0:T(8,128)(2,1)}, bf16[80,768]{1,0:T(8,128)(2,1)S(1)}, u32[]{:S(2)}, u32[]{:S(2)}) collective-permute-start(bf16[80,768]{1,0:T(8,128)(2,1)} %get-tuple-element.248), channel_id=1, source_target_pairs={{0,6},{1,7},{2,4},{3,5},{4,2},{5,3},{6,0},{7,1},{8,14},{9,15},{10,... | collective-permute-start | bytes 368648 | tf_op jit(solution)/shard_map/ppermute | solution.py:813
  309.3 16.4 %collective-permute-start.40 = (bf16[192,768]{1,0:T(8,128)(2,1)}, bf16[192,768]{1,0:T(8,128)(2,1)S(1)}, u32[]{:S(2)}, u32[]{:S(2)}) collective-permute-start(bf16[192,768]{1,0:T(8,128)(2,1)} %join.2.refs_0_), channel_id=1, source_target_pairs={{0,24},{8,16},{16,8},{24,0},{1,25},{9,17},{17,9},{25,1},{2,26},{10... | collective-permute-start | bytes 884744 | tf_op jit(solution)/shard_map/ppermute | solution.py:813
  310.7 15.5 %collective-permute-start.55 = (bf16[192,768]{1,0:T(8,128)(2,1)}, bf16[192,768]{1,0:T(8,128)(2,1)}, u32[]{:S(2)}, u32[]{:S(2)}) collective-permute-start(bf16[192,768]{1,0:T(8,128)(2,1)} %join.2.refs_0_), channel_id=1, source_target_pairs={{0,8},{8,0},{16,24},{24,16},{1,9},{9,1},{17,25},{25,17},{2,10},{10... | collective-permute-start | bytes 884744 | tf_op jit(solution)/shard_map/ppermute | solution.py:813
  315.9 12.7 %collective-permute-start.56 = (bf16[192,768]{1,0:T(8,128)(2,1)}, bf16[192,768]{1,0:T(8,128)(2,1)}, u32[]{:S(2)}, u32[]{:S(2)}) collective-permute-start(bf16[192,768]{1,0:T(8,128)(2,1)} %join.2.refs_0_), channel_id=1, source_target_pairs={{0,16},{8,24},{16,0},{24,8},{1,17},{9,25},{17,1},{25,9},{2,18},{10... | collective-permute-start | bytes 884744 | tf_op jit(solution)/shard_map/ppermute | solution.py:813
  323.5 9.7 %collective-permute-start.51 = (bf16[320,768]{1,0:T(8,128)(2,1)S(1)}, bf16[320,768]{1,0:T(8,128)(2,1)S(1)}, u32[]{:S(2)}, u32[]{:S(2)}) collective-permute-start(bf16[320,768]{1,0:T(8,128)(2,1)S(1)} %get-tuple-element.259.refs_0_), channel_id=1, source_target_pairs={{0,1},{1,0},{2,3},{3,2},{4,5},{5,4},{6,7},{7,6},{8,9},{9,8},{10,11... | collective-permute-start | bytes 1474568 | tf_op jit(solution)/shard_map/ppermute | solution.py:813
  325.7 7.8 %collective-permute-start.52 = (bf16[320,768]{1,0:T(8,128)(2,1)S(1)}, bf16[320,768]{1,0:T(8,128)(2,1)S(1)}, u32[]{:S(2)}, u32[]{:S(2)}) collective-permute-start(bf16[320,768]{1,0:T(8,128)(2,1)S(1)} %collective-permute-done.23.refs_1_), channel_id=1, source_target_pairs={{0,1},{1,0},{2,3},{3,2},{4,5},{5,4},{6,7},{7,6},{8,9},{9,8},{10,11... | collective-permute-start | bytes 1474568 | tf_op jit(solution)/shard_map/ppermute | solution.py:813
  325.7 9.2 %collective-permute-start.53 = (bf16[320,768]{1,0:T(8,128)(2,1)}, bf16[320,768]{1,0:T(8,128)(2,1)S(1)}, u32[]{:S(2)}, u32[]{:S(2)}) collective-permute-start(bf16[320,768]{1,0:T(8,128)(2,1)} %collective-permute-done.24.refs_2_), channel_id=1, source_target_pairs={{0,1},{1,0},{2,3},{3,2},{4,5},{5,4},{6,7},{7,6},{8,9},{9,8},{10,11... | collective-permute-start | bytes 1474568 | tf_op jit(solution)/shard_map/ppermute | solution.py:813
  326.2 9.7 %collective-permute-start.54 = (bf16[320,768]{1,0:T(8,128)(2,1)}, bf16[320,768]{1,0:T(8,128)(2,1)S(1)}, u32[]{:S(2)}, u32[]{:S(2)}) collective-permute-start(bf16[320,768]{1,0:T(8,128)(2,1)} %collective-permute-done.25.refs_3_), channel_id=1, source_target_pairs={{0,1},{1,0},{2,3},{3,2},{4,5},{5,4},{6,7},{7,6},{8,9},{9,8},{10,11... | collective-permute-start | bytes 1474568 | tf_op jit(solution)/shard_map/ppermute | solution.py:813
  328.7 11.0 %collective-permute-start.50 = (bf16[192,768]{1,0:T(8,128)(2,1)}, bf16[192,768]{1,0:T(8,128)(2,1)S(1)}, u32[]{:S(2)}, u32[]{:S(2)}) collective-permute-start(bf16[192,768]{1,0:T(8,128)(2,1)} %join.3.refs_0_), channel_id=1, source_target_pairs={{0,24},{8,16},{16,8},{24,0},{1,25},{9,17},{17,9},{25,1},{2,26},{10... | collective-permute-start | bytes 884744 | tf_op jit(solution)/shard_map/ppermute | solution.py:813
  333.2 16.3 %collective-permute-start.57 = (bf16[192,768]{1,0:T(8,128)(2,1)S(1)}, bf16[192,768]{1,0:T(8,128)(2,1)S(1)}, u32[]{:S(2)}, u32[]{:S(2)}) collective-permute-start(bf16[192,768]{1,0:T(8,128)(2,1)S(1)} %copy-done.26), channel_id=1, source_target_pairs={{0,1},{1,0},{2,3},{3,2},{4,5},{5,4},{6,7},{7,6},{8,9},{9,8},{10,11... | collective-permute-start | bytes 884744 | tf_op jit(solution)/shard_map/ppermute | solution.py:813
  333.5 16.1 %collective-permute-start.61 = (bf16[192,768]{1,0:T(8,128)(2,1)S(1)}, bf16[192,768]{1,0:T(8,128)(2,1)S(1)}, u32[]{:S(2)}, u32[]{:S(2)}) collective-permute-start(bf16[192,768]{1,0:T(8,128)(2,1)S(1)} %copy-done.27), channel_id=1, source_target_pairs={{0,8},{8,0},{16,24},{24,16},{1,9},{9,1},{17,25},{25,17},{2,10},{10... | collective-permute-start | bytes 884744 | tf_op jit(solution)/shard_map/ppermute | solution.py:813
  335.0 15.2 %collective-permute-start.62 = (bf16[192,768]{1,0:T(8,128)(2,1)S(1)}, bf16[192,768]{1,0:T(8,128)(2,1)S(1)}, u32[]{:S(2)}, u32[]{:S(2)}) collective-permute-start(bf16[192,768]{1,0:T(8,128)(2,1)S(1)} %copy-done.27), channel_id=1, source_target_pairs={{0,16},{8,24},{16,0},{24,8},{1,17},{9,25},{17,1},{25,9},{2,18},{10... | collective-permute-start | bytes 884744 | tf_op jit(solution)/shard_map/ppermute | solution.py:813
  336.0 14.3 %collective-permute-start.58 = (bf16[192,768]{1,0:T(8,128)(2,1)}, bf16[192,768]{1,0:T(8,128)(2,1)S(1)}, u32[]{:S(2)}, u32[]{:S(2)}) collective-permute-start(bf16[192,768]{1,0:T(8,128)(2,1)} %collective-permute-done.55.refs_1_), channel_id=1, source_target_pairs={{0,1},{1,0},{2,3},{3,2},{4,5},{5,4},{6,7},{7,6},{8,9},{9,8},{10,11... | collective-permute-start | bytes 884744 | tf_op jit(solution)/shard_map/ppermute | solution.py:813
  339.7 11.1 %collective-permute-start.59 = (bf16[192,768]{1,0:T(8,128)(2,1)}, bf16[192,768]{1,0:T(8,128)(2,1)S(1)}, u32[]{:S(2)}, u32[]{:S(2)}) collective-permute-start(bf16[192,768]{1,0:T(8,128)(2,1)} %collective-permute-done.56.refs_2_), channel_id=1, source_target_pairs={{0,1},{1,0},{2,3},{3,2},{4,5},{5,4},{6,7},{7,6},{8,9},{9,8},{10,11... | collective-permute-start | bytes 884744 | tf_op jit(solution)/shard_map/ppermute | solution.py:813
  349.5 8.8 %collective-permute-start.63 = (bf16[192,768]{1,0:T(8,128)(2,1)S(1)}, bf16[192,768]{1,0:T(8,128)(2,1)S(1)}, u32[]{:S(2)}, u32[]{:S(2)}) collective-permute-start(bf16[192,768]{1,0:T(8,128)(2,1)S(1)} %copy-done.27), channel_id=1, source_target_pairs={{0,1},{1,0},{2,3},{3,2},{4,5},{5,4},{6,7},{7,6},{8,9},{9,8},{10,11... | collective-permute-start | bytes 884744 | tf_op jit(solution)/shard_map/ppermute | solution.py:813
  350.2 8.1 %collective-permute-start.66 = (bf16[192,768]{1,0:T(8,128)(2,1)S(1)}, bf16[192,768]{1,0:T(8,128)(2,1)S(1)}, u32[]{:S(2)}, u32[]{:S(2)}) collective-permute-start(bf16[192,768]{1,0:T(8,128)(2,1)S(1)} %copy-done.51), channel_id=1, source_target_pairs={{0,1},{1,0},{2,3},{3,2},{4,5},{5,4},{6,7},{7,6},{8,9},{9,8},{10,11... | collective-permute-start | bytes 884744 | tf_op jit(solution)/shard_map/ppermute | solution.py:813
  350.3 8.1 %collective-permute-start.64 = (bf16[192,768]{1,0:T(8,128)(2,1)S(1)}, bf16[192,768]{1,0:T(8,128)(2,1)S(1)}, u32[]{:S(2)}, u32[]{:S(2)}) collective-permute-start(bf16[192,768]{1,0:T(8,128)(2,1)S(1)} %collective-permute-done.61.refs_1_), channel_id=1, source_target_pairs={{0,1},{1,0},{2,3},{3,2},{4,5},{5,4},{6,7},{7,6},{8,9},{9,8},{10,11... | collective-permute-start | bytes 884744 | tf_op jit(solution)/shard_map/ppermute | solution.py:813
  (95 other events, 894.2 us)

commit v5 on v4

--- a/solution.py
+++ b/solution.py
@@ -449,7 +449,7 @@
         out_shape=[shape_of((later, rows, columns), BF)] * len(keeps),
         in_specs=[block(count - later)] * (2 * len(keeps)),
         out_specs=[block(0)] * len(keeps),
-        compiler_params=params(58),
+        compiler_params=params(63),
         name="later_sums",
     )(*keeps, *theres)
 
@@ -533,7 +533,7 @@
         in_specs=[smem(), smem(), by_rows(rows, LANES), by_rows(rows, width)]
         + plan.specs(arrays),
         out_specs=by_rows(rows, width),
-        compiler_params=params(58),
+        compiler_params=params(63),
         name="result",
     )(expert, lengths, column, resid, *arrays)
 
@@ -584,7 +584,7 @@
         in_specs=[smem(), smem(), by_rows(rows, LANES), block, block, whole((width, width)), whole((width,))]
         + plan.specs(arrays),
         out_specs=[block, block, block, whole((1, width))],
-        compiler_params=params(58),
+        compiler_params=params(63),
         name="expert_norm_backward",
     )(expert, lengths, column, resid, cotangent, out_weight, gain, *arrays)
 
@@ -763,7 +763,7 @@
     return pl.pallas_call(
         extra_kernel,
         out_shape=shape_of((rows, width), BF),
-        compiler_params=params(58),
+        compiler_params=params(63),
         name="extra_rows",
     )(router_grad, gain_grad, lines)
 
@@ -804,7 +804,7 @@
         + [whole((width, width))] * 3
         + [block, whole((width,)), block],
         out_specs=block,
-        compiler_params=params(58),
+        compiler_params=params(63),
         name="token_gradient",
     )(back, *weights, tokens, gain, resid_grad)
 
@@ -930,7 +930,7 @@
         kernel,
         out_shape=[shape_of(shape, BF) for shape in shapes],
         in_specs=[smem()] * (stage is not None) + [pl.BlockSpec()] * (len(parts) + len(extras)),
-        compiler_params=params(58),
+        compiler_params=params(63),
         name="share",
     )(*([] if stage is None else [place.reshape(1)]), *parts, *extras)
 
@@ -971,7 +971,7 @@
         join_kernel,
         out_shape=shape_of((rows * len(parts), width), BF),
         in_specs=[smem()] + [pl.BlockSpec()] * len(parts),
-        compiler_params=params(58),
+        compiler_params=params(63),
         name="join",
     )(place.reshape(1), *parts)
 
@@ -1006,7 +1006,7 @@
         out_shape=[shape_of((count * rows, width), F32)] * 2 + [shape_of((count * rows, LANES), F32)],
         in_specs=[smem()] + [whole((rows, width))] * (2 * count) + [block] * len(weights),
         out_specs=[block, block, by_rows(rows, LANES)],
-        compiler_params=params(58),
+        compiler_params=params(63),
         name="assemble",
     )(places, *own, *other, *weights)
 

time: 371 us -> 363 us (0.978)
  local copies, waits for them, and re-layouts: 27.6 us -> 19.3 us
    unnamed x152 -> x94, local copies, waits for them, and re-layouts: 25 us -> 16.7 us
  transfers between devices with their start and end apart: 67 -> 67, of which waited for: 19 -> 21; matrix products, arithmetic and copies ran while one was open for 3% -> 4% of each run, Pallas kernels for 47% -> 48%
where the time goes in v5:
time: 363 us; the launch traced here: 360 us
  Pallas kernels  200 us (55%)
  starting transfers between devices  68 us (19%)
  waiting for transfers between devices  56.6 us (16%)
  local copies, waits for them, and re-layouts  19.3 us (5%)
  other arithmetic  10.6 us (3%)
    ppermute x67, starting transfers between devices, swap(): lax.ppermute(values, axis, [(place, place ^ distance) for place in range(...  68 us
    ppermute x67, waiting for transfers between devices, swap(): lax.ppermute(values, axis, [(place, place ^ distance) for place in range(...  56.6 us
    pallas_call x1, Pallas kernels, backward_part(): pl.pallas_call(backward_kernel, grid=(pairs,), out_shape=[shape_of((3, se...  37.5 us
    pallas_call x1, Pallas kernels, forward_part(): pl.pallas_call(functools.partial(forward_kernel, plan), grid=(pairs,), ou...  36.8 us
    pallas_call x2, Pallas kernels, expert_part(): pl.pallas_call(functools.partial(expert_kernel, plan, len(row_arrays), st...  28.2 us
    pallas_call x3, Pallas kernels, weight_grad_part(): pl.pallas_call(functools.partial(weight_grad_kernel, transposed, len(term...  17.6 us
    unnamed x94, local copies, waits for them, and re-layouts  16.7 us
    pallas_call x6, Pallas kernels, share(): pl.pallas_call(kernel, out_shape=[shape_of(shape, BF) for shape in shapes...  13.4 us
  transfers between devices with their start and end apart: 67, of which 21 were waited for; matrix products, arithmetic and copies ran while one was open for 4% of the time, Pallas kernels for 48%

profile of v5, /device:TPU:0, one launch (start us, length us, event | category | flops | bytes accessed | tf_op | source)
XLA Modules:
  0.0 359.5 jit_solution(11726717804851019805)
XLA Ops:
  1.3 5.2 %slots.1 = (s32[1,1024]{1,0:T(1,128)}, s32[1024,128]{1,0:T(8,128)}, bf16[320,768]{1,0:T(8,128)(2,1)}, bf16[320,768]{1,0:T(8,128)(2,1)}, bf16[320,768]{1,0:T(8,128)(2,1)}, /*index=5*/bf16[320,768]{1,0:T(8,128)(2,1)}) custom-call(s32[1]{0:T(128)} %bitcast.3.expert_ref, s32[1]{0:T(128)S(6)} %copy.40.length_ref, s32[1,1024]{1,0:T(1,128)} %routes_ref.1, ...), custom_call_target="tpu_custom_call" | custom-call | tf_op jit(solution)/shard_map/slots/pallas_call | solution.py:136
  6.5 3.0 collective-permute-start
  9.6 2.6 collective-permute-start.1
  12.2 36.8 %attention_forward.1 = (bf16[12,1024,1024]{2,1,0:T(8,128)(2,1)}, bf16[3,6,1024,128]{3,2,1,0:T(8,128)(2,1)}, bf16[2,1024,768]{2,1,0:T(8,128)(2,1)}, f32[6,1024,12...) custom-call(s32[1]{0:T(128)} %bitcast.3.expert_ref, ...), custom_call_target="tpu_custom_call" | custom-call | tf_op jit(solution)/shard_map/attention_forward/pallas_call | solution.py:259
  50.1 6.6 %collective-permute-start.8 = (bf16[320,768]{1,0:T(8,128)(2,1)}, bf16[320,768]{1,0:T(8,128)(2,1)}, u32[]{:S(2)}, u32[]{:S(2)}) collective-permute-start(bf16[320,768]{1,0:T(8,128)(2,1)} %get-tuple-element.166), channel_id=1, source_target_pairs={{0,2},{1,3},{2,0},{3,1},{4,6},{5,7},{6,4},{7,5},{8,10},{9,11},{10,... | collective-permute-start | bytes 1474568 | tf_op jit(solution)/shard_map/ppermute | solution.py:813
  56.7 1.8 collective-permute-start.9
  58.6 9.6 %expert_activation_gradient.1 = (bf16[1280,768]{1,0:T(8,128)(2,1)S(1)}, bf16[1280,3072]{1,0:T(8,128)(2,1)S(1)}) custom-call(bf16[1,3072,768]{2,1,0:T(8,128)(2,1)S(1)} %copy-done.4, bf16[320,768]{1,0:T(8,128)(2,1)S(1)} %copy-done.12, bf16[320,768]{1,0:T(8,128)(2,1)S(1)} %collective-permute-done.refs_1_, bf16[320,768]{1,0:T(8,128)(2,1)S(1)} %collective-permute-done.1.refs_2_, ...), custom_call_target="tpu_custom_call" | custom-call | tf_op jit(solution)/shard_map/expert_activation_gradient/pallas_call | solution.py:319
  68.1 3.1 copy-done.2
  72.5 6.4 %collective-permute-done.8.refs_1_ = bf16[320,768]{1,0:T(8,128)(2,1)} collective-permute-done((bf16[320,768]{1,0:T(8,128)(2,1)}, bf16[320,768]{1,0:T(8,128)(2,1)}, u32[]{:S(2)}, u32[]{:S(2)}) %collective-permute-start.8) | collective-permute-done | bytes 491552 | tf_op jit(solution)/shard_map/ppermute | solution.py:813
  78.9 2.5 collective-permute-done.9.refs_2_
  81.9 2.5 collective-permute-start.7
  84.9 19.8 %expert_rows.2 = (bf16[1280,3072]{1,0:T(8,128)(2,1)}, bf16[1280,3072]{1,0:T(8,128)(2,1)}, bf16[1280,768]{1,0:T(8,128)(2,1)S(1)}, bf16[1280,768]{1,0:T(8,128)(2,1...) custom-call(s32[1]{0:T(128)} %bitcast.3.expert_ref, ...), custom_call_target="tpu_custom_call" | custom-call | tf_op jit(solution)/shard_map/expert_rows/pallas_call | solution.py:402
  106.7 8.4 %expert_rows.3 = (bf16[1280,3072]{1,0:T(8,128)(2,1)}, bf16[1280,3072]{1,0:T(8,128)(2,1)}, bf16[1280,768]{1,0:T(8,128)(2,1)S(1)}, bf16[1280,768]{1,0:T(8,128)(2,1...) custom-call(s32[1]{0:T(128)} %bitcast.3.expert_ref, ...), custom_call_target="tpu_custom_call", output_to_operand_aliasing={{0}: (7, {}), {1}: (8, {}), {2}: (9, {}), {3}: (10, {}), {4... | custom-call | tf_op jit(solution)/shard_map/expert_rows/pallas_call | solution.py:402
  115.0 3.9 %copy-done.1 = bf16[1280,3072]{1,0:T(8,128)(2,1)S(1)} copy-done((bf16[1280,3072]{1,0:T(8,128)(2,1)S(1)}, bf16[1280,3072]{1,0:T(8,128)(2,1)}, u32[]{:S(2)}) %copy-start.1) | copy-done | bytes 7864344
  119.0 4.5 %expert_weight_gradients.5 = bf16[2,768,768]{2,1,0:T(8,128)(2,1)S(1)} custom-call(s32[2]{0:T(128)S(1)} %get-tuple-element.276.refs_0_, bf16[1280,3072]{1,0:T(8,128)(2,1)S(1)} %copy-done.1, bf16[1280,768]{1,0:T(8,128)(2,1)S(1)} %get-tuple-element.181.refs_5_.refs_2_), custom_call_target="tpu_custom_call" | custom-call | tf_op jit(solution)/shard_map/expert_weight_gradients/pallas_call | solution.py:470
  125.1 4.3 %expert_weight_gradients.4 = bf16[2,768,768]{2,1,0:T(8,128)(2,1)S(1)} custom-call(s32[2]{0:T(128)S(1)} %get-tuple-element.278.refs_0_, bf16[1280,3072]{1,0:T(8,128)(2,1)S(1)} %copy-done, bf16[1280,768]{1,0:T(8,128)(2,1)S(1)} %get-tuple-element.180.refs_4_.refs_2_), custom_call_target="tpu_custom_call" | custom-call | tf_op jit(solution)/shard_map/expert_weight_gradients/pallas_call | solution.py:470
  131.0 2.0 collective-permute-start.14
  135.4 7.0 %expert_output.1 = (bf16[320,768]{1,0:T(8,128)(2,1)S(1)}, bf16[320,768]{1,0:T(8,128)(2,1)S(1)}, bf16[320,768]{1,0:T(8,128)(2,1)S(1)}, bf16[320,768]{1,0:T(8,128)(2,1)S(1)}) custom-call(bf16[1280,3072]{1,0:T(8,128)(2,1)S(1)} %copy-done, bf16[1,3072,768]{2,1,0:T(8,128)(2,1)S(1)} %bitcast.17, f32[1280,1]{1,0:T(8,128)S(1)} %get-tuple-element.189.gate_ref), custom_call_target="tpu_custom_call" | custom-call | tf_op jit(solution)/shard_map/expert_output/pallas_call | solution.py:501
  142.4 8.7 %expert_weight_gradients.3 = (bf16[2,768,768]{2,1,0:T(8,128)(2,1)S(1)}, bf16[2,768,768]{2,1,0:T(8,128)(2,1)S(1)}) custom-call(s32[2]{0:T(128)S(1)} %get-tuple-element.279.refs_0_, s32[2]{0:T(128)S(1)} %get-tuple-element.277.refs_1_, bf16[1280,3072]{1,0:T(8,128)(2,1)S(1)} %copy-done, bf16[1280,3072]{1,0:T(8,128)(2,1)} %get-tuple-element.179.refs_3_.refs_1_, ...), custom_call_target="tpu_custom_call" | custom-call | tf_op jit(solution)/shard_map/expert_weight_gradients/pallas_call | solution.py:470
  154.0 15.0 %collective-permute-done.15.refs_2_ = bf16[320,768]{1,0:T(8,128)(2,1)S(1)} collective-permute-done((bf16[320,768]{1,0:T(8,128)(2,1)S(1)}, bf16[320,768]{1,0:T(8,128)(2,1)S(1)}, u32[]{:S(2)}, u32[]{:S(2)}) %collective-permute-start.15) | collective-permute-done | bytes 491552 | tf_op jit(solution)/shard_map/ppermute | solution.py:813
  173.1 3.7 %collective-permute-done.22.refs_3_ = bf16[2,768,768]{2,1,0:T(8,128)(2,1)S(1)} collective-permute-done((bf16[2,768,768]{2,1,0:T(8,128)(2,1)S(1)}, bf16[2,768,768]{2,1,0:T(8,128)(2,1)S(1)}, u32[]{:S(2)}, u32[]{:S(2)}) %collective-permute-start.22) | collective-permute-done | bytes 2359328 | tf_op jit(solution)/shard_map/ppermute | solution.py:813
  178.3 4.3 %collective-permute-done.21.refs_2_ = bf16[2,768,768]{2,1,0:T(8,128)(2,1)} collective-permute-done((bf16[2,768,768]{2,1,0:T(8,128)(2,1)S(1)}, bf16[2,768,768]{2,1,0:T(8,128)(2,1)}, u32[]{:S(2)}, u32[]{:S(2)}) %collective-permute-start.21) | collective-permute-done | bytes 2359328 | tf_op jit(solution)/shard_map/ppermute | solution.py:813
  182.6 4.3 %later_sums.1 = (bf16[1,768,768]{2,1,0:T(8,128)(2,1)}, bf16[1,768,768]{2,1,0:T(8,128)(2,1)}) custom-call(bf16[2,768,768]{2,1,0:T(8,128)(2,1)} %copy-done.7, bf16[2,768,768]{2,1,0:T(8,128)(2,1)} %copy-done.9, bf16[2,768,768]{2,1,0:T(8,128)(2,1)} %collective-permute-done.21.refs_2_, bf16[2,768,768]{2,1,0:T(8,128)(2,1)} %copy-done.17), custom_call_target="tpu_custom_call" | custom-call | tf_op jit(solution)/shard_map/later_sums/pallas_call | solution.py:446
  188.9 1.9 collective-permute-start.23
  193.3 9.5 %expert_norm_backward.1 = (f32[1024,768]{1,0:T(8,128)}, bf16[1024,768]{1,0:T(8,128)(2,1)}, bf16[1024,768]{1,0:T(8,128)(2,1)}, f32[1,768]{1,0:T(1,128)}) custom-call(s32[1]{0:T(128)} %bitcast.3.expert_ref, s32[1]{0:T(128)S(6)} %copy.40.length_ref, s32[1024,128]{1,0:T(8,128)} %get-tuple-element.148.column_ref, f32[1024,768]{1,0:T(8,128)} %get-tuple-element.258.resid_ref, ...), custom_call_target="tpu_custom_call" | custom-call | tf_op jit(solution)/shard_map/expert_norm_backward/pallas_call | solution.py:575
  202.8 37.5 %attention_backward.1 = (bf16[3,1024,768]{2,1,0:T(8,128)(2,1)}, f32[6,2,768]{2,1,0:T(2,128)}, bf16[768,768]{1,0:T(8,128)(2,1)}, bf16[768,768]{1,0:T(8,128)(2,1)}...) custom-call(s32[1]{0:T(128)} %bitcast.2.core_ref, bf16[3,6,1024,128]{3,2,1,0:T(8,128)(2,1)} %get-tuple-element.145.qkv_ref, ...), custom_call_target="tpu_custom_call" | custom-call | tf_op jit(solution)/shard_map/attention_backward/pallas_call | solution.py:703
  241.0 2.7 collective-permute-done.28.refs_1_
  243.7 2.8 share.6
  250.0 2.6 fusion.3.router_ref
  253.2 2.2 extra_rows.1.refs_2_
  257.5 2.9 share.7
  263.9 9.4 %token_gradient.1 = f32[1024,768]{1,0:T(8,128)} custom-call(bf16[3,1024,768]{2,1,0:T(8,128)(2,1)} %get-tuple-element.231.back_ref, bf16[768,768]{1,0:T(8,128)(2,1)} %refs_8_.2, bf16[768,768]{1,0:T(8,128)(2,1)} %refs_9_.1, bf16[768,768]{1,0:T(8,128)(2,1)} %refs_8_.3, bf16[1024,768]{1,0:T(8,128)(2,1)} %bitcast.21, bf16[768]{0:T(1024)(128)(2,1)} %gain_ref.3, ...), custom_call_target="tpu_custom_call" | custom-call | tf_op jit(solution)/shard_map/token_gradient/pallas_call | solution.py:799
  273.3 2.0 share.8
  276.4 2.0 collective-permute-start.35
  278.4 2.3 collective-permute-done.34.refs_1_
  283.2 3.9 %collective-permute-done.36.refs_3_ = bf16[48,768]{1,0:T(8,128)(2,1)S(1)} collective-permute-done((bf16[48,768]{1,0:T(8,128)(2,1)}, bf16[48,768]{1,0:T(8,128)(2,1)S(1)}, u32[]{:S(2)}, u32[]{:S(2)}) %collective-permute-start.36) | collective-permute-done | bytes 73760 | tf_op jit(solution)/shard_map/ppermute | solution.py:813
  289.4 2.3 collective-permute-start.38
  291.7 2.1 collective-permute-start.39
  293.8 2.2 share.10
  296.0 2.3 collective-permute-start.45
  298.3 2.1 collective-permute-start.46
  316.6 2.0 collective-permute-done.48.refs_2_
  324.6 3.8 %convert_add_fusion = f32[1,768,768]{2,1,0:T(8,128)} fusion(bf16[1,768,768]{2,1,0:T(8,128)(2,1)} %collective-permute-done.27, bf16[2,768,768]{2,1,0:T(8,128)(2,1)} %copy-done.17, bf16[2,768,768]{2,1,0:T(8,128)(2,1)} %copy-done.9), kind=kLoop, calls=%fused_computation | loop fusion | flops 2949120 | bytes 5898240 | tf_op jit(solution)/shard_map/add | solution.py:1161
  330.4 3.5 collective-permute-done.50.refs_3_
  334.6 3.6 convert_add_fusion.1
  338.1 5.5 %result.1 = bf16[1024,768]{1,0:T(8,128)(2,1)} custom-call(s32[1]{0:T(128)} %bitcast.3.expert_ref, s32[1]{0:T(128)S(6)} %copy.40.length_ref, s32[1024,128]{1,0:T(8,128)} %get-tuple-element.148.column_ref, f32[1024,768]{1,0:T(8,128)} %get-tuple-element.258.resid_ref, bf16[320,768]{1,0:T(8,128)(2,1)} %copy-done.10, ...), custom_call_target="tpu_custom_call" | custom-call | tf_op jit(solution)/shard_map/result/pallas_call | solution.py:529
  346.7 5.5 %assemble.2 = (f32[768,768]{1,0:T(8,128)}, f32[768,768]{1,0:T(8,128)}, f32[768,128]{1,0:T(8,128)}) custom-call(s32[2]{0:T(128)} %pad_add_fusion.places_ref, bf16[192,768]{1,0:T(8,128)(2,1)} %join.2.refs_0_, bf16[192,768]{1,0:T(8,128)(2,1)} %collective-permute-done.55.refs_1_, bf16[192,768]{1,0:T(8,128)(2,1)} %collective-permute-done.56.refs_2_, ...), custom_call_target="tpu_custom_call" | custom-call | tf_op jit(solution)/shard_map/assemble/pallas_call | solution.py:1003
  352.3 5.2 %assemble.3 = (f32[768,768]{1,0:T(8,128)}, f32[768,768]{1,0:T(8,128)}, f32[768,128]{1,0:T(8,128)}) custom-call(s32[2]{0:T(128)} %pad_add_fusion.places_ref, bf16[192,768]{1,0:T(8,128)(2,1)} %join.3.refs_0_, bf16[192,768]{1,0:T(8,128)(2,1)} %collective-permute-done.61.refs_1_, bf16[192,768]{1,0:T(8,128)(2,1)} %collective-permute-done.62.refs_2_, ...), custom_call_target="tpu_custom_call" | custom-call | tf_op jit(solution)/shard_map/assemble/pallas_call | solution.py:1003
  (220 shorter events, 69.5 us)
Async XLA Ops:
  6.5 42.4 %collective-permute-start = (bf16[320,768]{1,0:T(8,128)(2,1)}, bf16[320,768]{1,0:T(8,128)(2,1)S(1)}, u32[]{:S(2)}, u32[]{:S(2)}) collective-permute-start(bf16[320,768]{1,0:T(8,128)(2,1)} %get-tuple-element.155), channel_id=1, source_target_pairs={{0,2},{1,3},{2,0},{3,1},{4,6},{5,7},{6,4},{7,5},{8,10},{9,11},{10,... | collective-permute-start | bytes 1474568 | tf_op jit(solution)/shard_map/ppermute | solution.py:813
  9.6 39.4 %collective-permute-start.1 = (bf16[320,768]{1,0:T(8,128)(2,1)}, bf16[320,768]{1,0:T(8,128)(2,1)S(1)}, u32[]{:S(2)}, u32[]{:S(2)}) collective-permute-start(bf16[320,768]{1,0:T(8,128)(2,1)} %get-tuple-element.156), channel_id=1, source_target_pairs={{0,4},{1,5},{2,6},{3,7},{4,0},{5,1},{6,2},{7,3},{8,12},{9,13},{10,... | collective-permute-start | bytes 1474568 | tf_op jit(solution)/shard_map/ppermute | solution.py:813
  12.1 36.8 %collective-permute-start.2 = (bf16[320,768]{1,0:T(8,128)(2,1)}, bf16[320,768]{1,0:T(8,128)(2,1)}, u32[]{:S(2)}, u32[]{:S(2)}) collective-permute-start(bf16[320,768]{1,0:T(8,128)(2,1)} %get-tuple-element.157), channel_id=1, source_target_pairs={{0,6},{1,7},{2,4},{3,5},{4,2},{5,3},{6,0},{7,1},{8,14},{9,15},{10,... | collective-permute-start | bytes 1474568 | tf_op jit(solution)/shard_map/ppermute | solution.py:813
  49.1 9.5 %collective-permute-start.4 = (bf16[320,768]{1,0:T(8,128)(2,1)S(1)}, bf16[320,768]{1,0:T(8,128)(2,1)S(1)}, u32[]{:S(2)}, u32[]{:S(2)}) collective-permute-start(bf16[320,768]{1,0:T(8,128)(2,1)S(1)} %collective-permute-done.refs_1_), channel_id=1, source_target_pairs={{0,1},{1,0},{2,3},{3,2},{4,5},{5,4},{6,7},{7,6},{8,9},{9,8},{10,11... | collective-permute-start | bytes 1474568 | tf_op jit(solution)/shard_map/ppermute | solution.py:813
  49.6 9.0 %collective-permute-start.5 = (bf16[320,768]{1,0:T(8,128)(2,1)S(1)}, bf16[320,768]{1,0:T(8,128)(2,1)S(1)}, u32[]{:S(2)}, u32[]{:S(2)}) collective-permute-start(bf16[320,768]{1,0:T(8,128)(2,1)S(1)} %collective-permute-done.1.refs_2_), channel_id=1, source_target_pairs={{0,1},{1,0},{2,3},{3,2},{4,5},{5,4},{6,7},{7,6},{8,9},{9,8},{10,11... | collective-permute-start | bytes 1474568 | tf_op jit(solution)/shard_map/ppermute | solution.py:813
  49.7 8.9 %collective-permute-start.6 = (bf16[320,768]{1,0:T(8,128)(2,1)}, bf16[320,768]{1,0:T(8,128)(2,1)S(1)}, u32[]{:S(2)}, u32[]{:S(2)}) collective-permute-start(bf16[320,768]{1,0:T(8,128)(2,1)} %collective-permute-done.2.refs_3_), channel_id=1, source_target_pairs={{0,1},{1,0},{2,3},{3,2},{4,5},{5,4},{6,7},{7,6},{8,9},{9,8},{10,11... | collective-permute-start | bytes 1474568 | tf_op jit(solution)/shard_map/ppermute | solution.py:813
  50.1 28.8 %collective-permute-start.8 = (bf16[320,768]{1,0:T(8,128)(2,1)}, bf16[320,768]{1,0:T(8,128)(2,1)}, u32[]{:S(2)}, u32[]{:S(2)}) collective-permute-start(bf16[320,768]{1,0:T(8,128)(2,1)} %get-tuple-element.166), channel_id=1, source_target_pairs={{0,2},{1,3},{2,0},{3,1},{4,6},{5,7},{6,4},{7,5},{8,10},{9,11},{10,... | collective-permute-start | bytes 1474568 | tf_op jit(solution)/shard_map/ppermute | solution.py:813
  56.7 24.7 %collective-permute-start.9 = (bf16[320,768]{1,0:T(8,128)(2,1)}, bf16[320,768]{1,0:T(8,128)(2,1)}, u32[]{:S(2)}, u32[]{:S(2)}) collective-permute-start(bf16[320,768]{1,0:T(8,128)(2,1)} %get-tuple-element.167), channel_id=1, source_target_pairs={{0,4},{1,5},{2,6},{3,7},{4,0},{5,1},{6,2},{7,3},{8,12},{9,13},{10,... | collective-permute-start | bytes 1474568 | tf_op jit(solution)/shard_map/ppermute | solution.py:813
  81.9 22.8 %collective-permute-start.7 = (bf16[320,768]{1,0:T(8,128)(2,1)}, bf16[320,768]{1,0:T(8,128)(2,1)S(1)}, u32[]{:S(2)}, u32[]{:S(2)}) collective-permute-start(bf16[320,768]{1,0:T(8,128)(2,1)} %get-tuple-element.164), channel_id=1, source_target_pairs={{0,6},{1,7},{2,4},{3,5},{4,2},{5,3},{6,0},{7,1},{8,14},{9,15},{10,... | collective-permute-start | bytes 1474568 | tf_op jit(solution)/shard_map/ppermute | solution.py:813
  123.5 53.3 %collective-permute-start.22 = (bf16[2,768,768]{2,1,0:T(8,128)(2,1)S(1)}, bf16[2,768,768]{2,1,0:T(8,128)(2,1)S(1)}, u32[]{:S(2)}, u32[]{:S(2)}) collective-permute-start(bf16[2,768,768]{2,1,0:T(8,128)(2,1)S(1)} %expert_weight_gradients.5), channel_id=1, source_target_pairs={{0,16},{8,24},{16,0},{24,8},{1,17},{9,25},{17,1},{25,9},{2,18},{10... | collective-permute-start | bytes 7077896 | tf_op jit(solution)/shard_map/ppermute | solution.py:813
  129.4 53.2 %collective-permute-start.21 = (bf16[2,768,768]{2,1,0:T(8,128)(2,1)S(1)}, bf16[2,768,768]{2,1,0:T(8,128)(2,1)}, u32[]{:S(2)}, u32[]{:S(2)}) collective-permute-start(bf16[2,768,768]{2,1,0:T(8,128)(2,1)S(1)} %expert_weight_gradients.4), channel_id=1, source_target_pairs={{0,8},{8,0},{16,24},{24,16},{1,9},{9,1},{17,25},{25,17},{2,10},{10... | collective-permute-start | bytes 7077896 | tf_op jit(solution)/shard_map/ppermute | solution.py:813
  131.0 23.1 %collective-permute-start.14 = (bf16[320,768]{1,0:T(8,128)(2,1)S(1)}, bf16[320,768]{1,0:T(8,128)(2,1)S(1)}, u32[]{:S(2)}, u32[]{:S(2)}) collective-permute-start(bf16[320,768]{1,0:T(8,128)(2,1)S(1)} %get-tuple-element.186), channel_id=1, source_target_pairs={{0,2},{1,3},{2,0},{3,1},{4,6},{5,7},{6,4},{7,5},{8,10},{9,11},{10,... | collective-permute-start | bytes 1474568 | tf_op jit(solution)/shard_map/ppermute | solution.py:813
  132.9 36.1 %collective-permute-start.15 = (bf16[320,768]{1,0:T(8,128)(2,1)S(1)}, bf16[320,768]{1,0:T(8,128)(2,1)S(1)}, u32[]{:S(2)}, u32[]{:S(2)}) collective-permute-start(bf16[320,768]{1,0:T(8,128)(2,1)S(1)} %get-tuple-element.187), channel_id=1, source_target_pairs={{0,4},{1,5},{2,6},{3,7},{4,0},{5,1},{6,2},{7,3},{8,12},{9,13},{10,... | collective-permute-start | bytes 1474568 | tf_op jit(solution)/shard_map/ppermute | solution.py:813
  134.0 35.1 %collective-permute-start.16 = (bf16[320,768]{1,0:T(8,128)(2,1)S(1)}, bf16[320,768]{1,0:T(8,128)(2,1)S(1)}, u32[]{:S(2)}, u32[]{:S(2)}) collective-permute-start(bf16[320,768]{1,0:T(8,128)(2,1)S(1)} %get-tuple-element.188), channel_id=1, source_target_pairs={{0,6},{1,7},{2,4},{3,5},{4,2},{5,3},{6,0},{7,1},{8,14},{9,15},{10,... | collective-permute-start | bytes 1474568 | tf_op jit(solution)/shard_map/ppermute | solution.py:813
  186.9 53.5 %collective-permute-start.26 = (bf16[1,768,768]{2,1,0:T(8,128)(2,1)}, bf16[1,768,768]{2,1,0:T(8,128)(2,1)}, u32[]{:S(2)}, u32[]{:S(2)}) collective-permute-start(bf16[1,768,768]{2,1,0:T(8,128)(2,1)} %get-tuple-element.201), channel_id=1, source_target_pairs={{0,16},{8,24},{16,0},{24,8},{1,17},{9,25},{17,1},{25,9},{2,18},{10... | collective-permute-start | bytes 3538952 | tf_op jit(solution)/shard_map/ppermute | solution.py:813
  187.4 53.0 %collective-permute-start.27 = (bf16[1,768,768]{2,1,0:T(8,128)(2,1)}, bf16[1,768,768]{2,1,0:T(8,128)(2,1)}, u32[]{:S(2)}, u32[]{:S(2)}) collective-permute-start(bf16[1,768,768]{2,1,0:T(8,128)(2,1)} %get-tuple-element.202), channel_id=1, source_target_pairs={{0,8},{8,0},{16,24},{24,16},{1,9},{9,1},{17,25},{25,17},{2,10},{10... | collective-permute-start | bytes 3538952 | tf_op jit(solution)/shard_map/ppermute | solution.py:813
  188.9 51.4 %collective-permute-start.23 = (bf16[320,768]{1,0:T(8,128)(2,1)}, bf16[320,768]{1,0:T(8,128)(2,1)}, u32[]{:S(2)}, u32[]{:S(2)}) collective-permute-start(bf16[320,768]{1,0:T(8,128)(2,1)} %copy-done.16), channel_id=1, source_target_pairs={{0,2},{1,3},{2,0},{3,1},{4,6},{5,7},{6,4},{7,5},{8,10},{9,11},{10,... | collective-permute-start | bytes 1474568 | tf_op jit(solution)/shard_map/ppermute | solution.py:813
  190.9 49.5 %collective-permute-start.24 = (bf16[320,768]{1,0:T(8,128)(2,1)}, bf16[320,768]{1,0:T(8,128)(2,1)}, u32[]{:S(2)}, u32[]{:S(2)}) collective-permute-start(bf16[320,768]{1,0:T(8,128)(2,1)} %copy-done.15), channel_id=1, source_target_pairs={{0,4},{1,5},{2,6},{3,7},{4,0},{5,1},{6,2},{7,3},{8,12},{9,13},{10,... | collective-permute-start | bytes 1474568 | tf_op jit(solution)/shard_map/ppermute | solution.py:813
  192.0 48.4 %collective-permute-start.25 = (bf16[320,768]{1,0:T(8,128)(2,1)}, bf16[320,768]{1,0:T(8,128)(2,1)}, u32[]{:S(2)}, u32[]{:S(2)}) collective-permute-start(bf16[320,768]{1,0:T(8,128)(2,1)} %copy-done.14), channel_id=1, source_target_pairs={{0,6},{1,7},{2,4},{3,5},{4,2},{5,3},{6,0},{7,1},{8,14},{9,15},{10,... | collective-permute-start | bytes 1474568 | tf_op jit(solution)/shard_map/ppermute | solution.py:813
  240.5 14.9 %collective-permute-start.32 = (bf16[768,768]{1,0:T(8,128)(2,1)}, bf16[768,768]{1,0:T(8,128)(2,1)}, u32[]{:S(2)}, u32[]{:S(2)}) collective-permute-start(bf16[768,768]{1,0:T(8,128)(2,1)} %get-tuple-element.221), channel_id=1, source_target_pairs={{0,1},{1,0},{2,3},{3,2},{4,5},{5,4},{6,7},{7,6},{8,9},{9,8},{10,11... | collective-permute-start | bytes 3538952 | tf_op jit(solution)/shard_map/ppermute | solution.py:813
  246.5 15.9 %collective-permute-start.29 = (bf16[192,768]{1,0:T(8,128)(2,1)}, bf16[192,768]{1,0:T(8,128)(2,1)}, u32[]{:S(2)}, u32[]{:S(2)}) collective-permute-start(bf16[192,768]{1,0:T(8,128)(2,1)} %get-tuple-element.216), channel_id=1, source_target_pairs={{0,8},{8,0},{16,24},{24,16},{1,9},{9,1},{17,25},{25,17},{2,10},{10... | collective-permute-start | bytes 884744 | tf_op jit(solution)/shard_map/ppermute | solution.py:813
  247.1 26.3 %collective-permute-start.30 = (bf16[192,768]{1,0:T(8,128)(2,1)}, bf16[192,768]{1,0:T(8,128)(2,1)}, u32[]{:S(2)}, u32[]{:S(2)}) collective-permute-start(bf16[192,768]{1,0:T(8,128)(2,1)} %get-tuple-element.217), channel_id=1, source_target_pairs={{0,16},{8,24},{16,0},{24,8},{1,17},{9,25},{17,1},{25,9},{2,18},{10... | collective-permute-start | bytes 884744 | tf_op jit(solution)/shard_map/ppermute | solution.py:813
  248.6 24.7 %collective-permute-start.31 = (bf16[192,768]{1,0:T(8,128)(2,1)}, bf16[192,768]{1,0:T(8,128)(2,1)}, u32[]{:S(2)}, u32[]{:S(2)}) collective-permute-start(bf16[192,768]{1,0:T(8,128)(2,1)} %get-tuple-element.218), channel_id=1, source_target_pairs={{0,24},{8,16},{16,8},{24,0},{1,25},{9,17},{17,9},{25,1},{2,26},{10... | collective-permute-start | bytes 884744 | tf_op jit(solution)/shard_map/ppermute | solution.py:813
  260.4 31.3 %collective-permute-start.41 = (bf16[224,768]{1,0:T(8,128)(2,1)}, bf16[224,768]{1,0:T(8,128)(2,1)}, u32[]{:S(2)}, u32[]{:S(2)}) collective-permute-start(bf16[224,768]{1,0:T(8,128)(2,1)} %get-tuple-element.228), channel_id=1, source_target_pairs={{0,8},{8,0},{16,24},{24,16},{1,9},{9,1},{17,25},{25,17},{2,10},{10... | collective-permute-start | bytes 1032200 | tf_op jit(solution)/shard_map/ppermute | solution.py:813
  260.9 32.9 %collective-permute-start.42 = (bf16[224,768]{1,0:T(8,128)(2,1)}, bf16[224,768]{1,0:T(8,128)(2,1)}, u32[]{:S(2)}, u32[]{:S(2)}) collective-permute-start(bf16[224,768]{1,0:T(8,128)(2,1)} %get-tuple-element.229), channel_id=1, source_target_pairs={{0,16},{8,24},{16,0},{24,8},{1,17},{9,25},{17,1},{25,9},{2,18},{10... | collective-permute-start | bytes 1032200 | tf_op jit(solution)/shard_map/ppermute | solution.py:813
  262.4 31.3 %collective-permute-start.43 = (bf16[224,768]{1,0:T(8,128)(2,1)}, bf16[224,768]{1,0:T(8,128)(2,1)}, u32[]{:S(2)}, u32[]{:S(2)}) collective-permute-start(bf16[224,768]{1,0:T(8,128)(2,1)} %get-tuple-element.230), channel_id=1, source_target_pairs={{0,24},{8,16},{16,8},{24,0},{1,25},{9,17},{17,9},{25,1},{2,26},{10... | collective-permute-start | bytes 1032200 | tf_op jit(solution)/shard_map/ppermute | solution.py:813
  289.4 8.9 %collective-permute-start.37 = (bf16[48,768]{1,0:T(8,128)(2,1)}, bf16[48,768]{1,0:T(8,128)(2,1)S(1)}, u32[]{:S(2)}, u32[]{:S(2)}) collective-permute-start(bf16[48,768]{1,0:T(8,128)(2,1)} %share.9.refs_0_), channel_id=1, source_target_pairs={{0,2},{1,3},{2,0},{3,1},{4,6},{5,7},{6,4},{7,5},{8,10},{9,11},{10,... | collective-permute-start | bytes 221192 | tf_op jit(solution)/shard_map/ppermute | solution.py:813
  289.4 11.0 %collective-permute-start.38 = (bf16[48,768]{1,0:T(8,128)(2,1)}, bf16[48,768]{1,0:T(8,128)(2,1)S(1)}, u32[]{:S(2)}, u32[]{:S(2)}) collective-permute-start(bf16[48,768]{1,0:T(8,128)(2,1)} %share.9.refs_0_), channel_id=1, source_target_pairs={{0,4},{1,5},{2,6},{3,7},{4,0},{5,1},{6,2},{7,3},{8,12},{9,13},{10,... | collective-permute-start | bytes 221192 | tf_op jit(solution)/shard_map/ppermute | solution.py:813
  291.7 8.7 %collective-permute-start.39 = (bf16[48,768]{1,0:T(8,128)(2,1)}, bf16[48,768]{1,0:T(8,128)(2,1)S(1)}, u32[]{:S(2)}, u32[]{:S(2)}) collective-permute-start(bf16[48,768]{1,0:T(8,128)(2,1)} %share.9.refs_0_), channel_id=1, source_target_pairs={{0,6},{1,7},{2,4},{3,5},{4,2},{5,3},{6,0},{7,1},{8,14},{9,15},{10,... | collective-permute-start | bytes 221192 | tf_op jit(solution)/shard_map/ppermute | solution.py:813
  296.0 10.4 %collective-permute-start.44 = (bf16[80,768]{1,0:T(8,128)(2,1)}, bf16[80,768]{1,0:T(8,128)(2,1)S(1)}, u32[]{:S(2)}, u32[]{:S(2)}) collective-permute-start(bf16[80,768]{1,0:T(8,128)(2,1)} %get-tuple-element.246), channel_id=1, source_target_pairs={{0,2},{1,3},{2,0},{3,1},{4,6},{5,7},{6,4},{7,5},{8,10},{9,11},{10,... | collective-permute-start | bytes 368648 | tf_op jit(solution)/shard_map/ppermute | solution.py:813
  296.0 10.9 %collective-permute-start.45 = (bf16[80,768]{1,0:T(8,128)(2,1)}, bf16[80,768]{1,0:T(8,128)(2,1)}, u32[]{:S(2)}, u32[]{:S(2)}) collective-permute-start(bf16[80,768]{1,0:T(8,128)(2,1)} %get-tuple-element.247), channel_id=1, source_target_pairs={{0,4},{1,5},{2,6},{3,7},{4,0},{5,1},{6,2},{7,3},{8,12},{9,13},{10,... | collective-permute-start | bytes 368648 | tf_op jit(solution)/shard_map/ppermute | solution.py:813
  298.3 8.6 %collective-permute-start.46 = (bf16[80,768]{1,0:T(8,128)(2,1)}, bf16[80,768]{1,0:T(8,128)(2,1)}, u32[]{:S(2)}, u32[]{:S(2)}) collective-permute-start(bf16[80,768]{1,0:T(8,128)(2,1)} %get-tuple-element.248), channel_id=1, source_target_pairs={{0,6},{1,7},{2,4},{3,5},{4,2},{5,3},{6,0},{7,1},{8,14},{9,15},{10,... | collective-permute-start | bytes 368648 | tf_op jit(solution)/shard_map/ppermute | solution.py:813
  303.3 16.5 %collective-permute-start.40 = (bf16[192,768]{1,0:T(8,128)(2,1)}, bf16[192,768]{1,0:T(8,128)(2,1)S(1)}, u32[]{:S(2)}, u32[]{:S(2)}) collective-permute-start(bf16[192,768]{1,0:T(8,128)(2,1)} %join.2.refs_0_), channel_id=1, source_target_pairs={{0,24},{8,16},{16,8},{24,0},{1,25},{9,17},{17,9},{25,1},{2,26},{10... | collective-permute-start | bytes 884744 | tf_op jit(solution)/shard_map/ppermute | solution.py:813
  304.9 15.6 %collective-permute-start.55 = (bf16[192,768]{1,0:T(8,128)(2,1)}, bf16[192,768]{1,0:T(8,128)(2,1)}, u32[]{:S(2)}, u32[]{:S(2)}) collective-permute-start(bf16[192,768]{1,0:T(8,128)(2,1)} %join.2.refs_0_), channel_id=1, source_target_pairs={{0,8},{8,0},{16,24},{24,16},{1,9},{9,1},{17,25},{25,17},{2,10},{10... | collective-permute-start | bytes 884744 | tf_op jit(solution)/shard_map/ppermute | solution.py:813
  310.6 12.3 %collective-permute-start.56 = (bf16[192,768]{1,0:T(8,128)(2,1)}, bf16[192,768]{1,0:T(8,128)(2,1)}, u32[]{:S(2)}, u32[]{:S(2)}) collective-permute-start(bf16[192,768]{1,0:T(8,128)(2,1)} %join.2.refs_0_), channel_id=1, source_target_pairs={{0,16},{8,24},{16,0},{24,8},{1,17},{9,25},{17,1},{25,9},{2,18},{10... | collective-permute-start | bytes 884744 | tf_op jit(solution)/shard_map/ppermute | solution.py:813
  318.6 9.7 %collective-permute-start.51 = (bf16[320,768]{1,0:T(8,128)(2,1)S(1)}, bf16[320,768]{1,0:T(8,128)(2,1)}, u32[]{:S(2)}, u32[]{:S(2)}) collective-permute-start(bf16[320,768]{1,0:T(8,128)(2,1)S(1)} %get-tuple-element.259.refs_0_), channel_id=1, source_target_pairs={{0,1},{1,0},{2,3},{3,2},{4,5},{5,4},{6,7},{7,6},{8,9},{9,8},{10,11... | collective-permute-start | bytes 1474568 | tf_op jit(solution)/shard_map/ppermute | solution.py:813
  319.8 8.7 %collective-permute-start.52 = (bf16[320,768]{1,0:T(8,128)(2,1)}, bf16[320,768]{1,0:T(8,128)(2,1)}, u32[]{:S(2)}, u32[]{:S(2)}) collective-permute-start(bf16[320,768]{1,0:T(8,128)(2,1)} %collective-permute-done.23.refs_1_), channel_id=1, source_target_pairs={{0,1},{1,0},{2,3},{3,2},{4,5},{5,4},{6,7},{7,6},{8,9},{9,8},{10,11... | collective-permute-start | bytes 1474568 | tf_op jit(solution)/shard_map/ppermute | solution.py:813
  319.9 10.0 %collective-permute-start.53 = (bf16[320,768]{1,0:T(8,128)(2,1)}, bf16[320,768]{1,0:T(8,128)(2,1)}, u32[]{:S(2)}, u32[]{:S(2)}) collective-permute-start(bf16[320,768]{1,0:T(8,128)(2,1)} %collective-permute-done.24.refs_2_), channel_id=1, source_target_pairs={{0,1},{1,0},{2,3},{3,2},{4,5},{5,4},{6,7},{7,6},{8,9},{9,8},{10,11... | collective-permute-start | bytes 1474568 | tf_op jit(solution)/shard_map/ppermute | solution.py:813
  320.5 9.9 %collective-permute-start.54 = (bf16[320,768]{1,0:T(8,128)(2,1)}, bf16[320,768]{1,0:T(8,128)(2,1)}, u32[]{:S(2)}, u32[]{:S(2)}) collective-permute-start(bf16[320,768]{1,0:T(8,128)(2,1)} %collective-permute-done.25.refs_3_), channel_id=1, source_target_pairs={{0,1},{1,0},{2,3},{3,2},{4,5},{5,4},{6,7},{7,6},{8,9},{9,8},{10,11... | collective-permute-start | bytes 1474568 | tf_op jit(solution)/shard_map/ppermute | solution.py:813
  322.9 11.0 %collective-permute-start.50 = (bf16[192,768]{1,0:T(8,128)(2,1)}, bf16[192,768]{1,0:T(8,128)(2,1)S(1)}, u32[]{:S(2)}, u32[]{:S(2)}) collective-permute-start(bf16[192,768]{1,0:T(8,128)(2,1)} %join.3.refs_0_), channel_id=1, source_target_pairs={{0,24},{8,16},{16,8},{24,0},{1,25},{9,17},{17,9},{25,1},{2,26},{10... | collective-permute-start | bytes 884744 | tf_op jit(solution)/shard_map/ppermute | solution.py:813
  328.3 15.3 %collective-permute-start.57 = (bf16[192,768]{1,0:T(8,128)(2,1)S(1)}, bf16[192,768]{1,0:T(8,128)(2,1)S(1)}, u32[]{:S(2)}, u32[]{:S(2)}) collective-permute-start(bf16[192,768]{1,0:T(8,128)(2,1)S(1)} %copy-done.18), channel_id=1, source_target_pairs={{0,1},{1,0},{2,3},{3,2},{4,5},{5,4},{6,7},{7,6},{8,9},{9,8},{10,11... | collective-permute-start | bytes 884744 | tf_op jit(solution)/shard_map/ppermute | solution.py:813
  328.5 15.2 %collective-permute-start.61 = (bf16[192,768]{1,0:T(8,128)(2,1)}, bf16[192,768]{1,0:T(8,128)(2,1)}, u32[]{:S(2)}, u32[]{:S(2)}) collective-permute-start(bf16[192,768]{1,0:T(8,128)(2,1)} %join.3.refs_0_), channel_id=1, source_target_pairs={{0,8},{8,0},{16,24},{24,16},{1,9},{9,1},{17,25},{25,17},{2,10},{10... | collective-permute-start | bytes 884744 | tf_op jit(solution)/shard_map/ppermute | solution.py:813
  329.9 14.3 %collective-permute-start.62 = (bf16[192,768]{1,0:T(8,128)(2,1)}, bf16[192,768]{1,0:T(8,128)(2,1)}, u32[]{:S(2)}, u32[]{:S(2)}) collective-permute-start(bf16[192,768]{1,0:T(8,128)(2,1)} %join.3.refs_0_), channel_id=1, source_target_pairs={{0,16},{8,24},{16,0},{24,8},{1,17},{9,25},{17,1},{25,9},{2,18},{10... | collective-permute-start | bytes 884744 | tf_op jit(solution)/shard_map/ppermute | solution.py:813
  330.4 13.9 %collective-permute-start.58 = (bf16[192,768]{1,0:T(8,128)(2,1)}, bf16[192,768]{1,0:T(8,128)(2,1)}, u32[]{:S(2)}, u32[]{:S(2)}) collective-permute-start(bf16[192,768]{1,0:T(8,128)(2,1)} %collective-permute-done.55.refs_1_), channel_id=1, source_target_pairs={{0,1},{1,0},{2,3},{3,2},{4,5},{5,4},{6,7},{7,6},{8,9},{9,8},{10,11... | collective-permute-start | bytes 884744 | tf_op jit(solution)/shard_map/ppermute | solution.py:813
  333.9 10.9 %collective-permute-start.59 = (bf16[192,768]{1,0:T(8,128)(2,1)}, bf16[192,768]{1,0:T(8,128)(2,1)}, u32[]{:S(2)}, u32[]{:S(2)}) collective-permute-start(bf16[192,768]{1,0:T(8,128)(2,1)} %collective-permute-done.56.refs_2_), channel_id=1, source_target_pairs={{0,1},{1,0},{2,3},{3,2},{4,5},{5,4},{6,7},{7,6},{8,9},{9,8},{10,11... | collective-permute-start | bytes 884744 | tf_op jit(solution)/shard_map/ppermute | solution.py:813
  343.6 8.6 %collective-permute-start.63 = (bf16[192,768]{1,0:T(8,128)(2,1)}, bf16[192,768]{1,0:T(8,128)(2,1)}, u32[]{:S(2)}, u32[]{:S(2)}) collective-permute-start(bf16[192,768]{1,0:T(8,128)(2,1)} %join.3.refs_0_), channel_id=1, source_target_pairs={{0,1},{1,0},{2,3},{3,2},{4,5},{5,4},{6,7},{7,6},{8,9},{9,8},{10,11... | collective-permute-start | bytes 884744 | tf_op jit(solution)/shard_map/ppermute | solution.py:813
  344.2 8.1 %collective-permute-start.66 = (bf16[192,768]{1,0:T(8,128)(2,1)}, bf16[192,768]{1,0:T(8,128)(2,1)}, u32[]{:S(2)}, u32[]{:S(2)}) collective-permute-start(bf16[192,768]{1,0:T(8,128)(2,1)} %copy-done.31), channel_id=1, source_target_pairs={{0,1},{1,0},{2,3},{3,2},{4,5},{5,4},{6,7},{7,6},{8,9},{9,8},{10,11... | collective-permute-start | bytes 884744 | tf_op jit(solution)/shard_map/ppermute | solution.py:813
  344.3 8.0 %collective-permute-start.64 = (bf16[192,768]{1,0:T(8,128)(2,1)}, bf16[192,768]{1,0:T(8,128)(2,1)}, u32[]{:S(2)}, u32[]{:S(2)}) collective-permute-start(bf16[192,768]{1,0:T(8,128)(2,1)} %collective-permute-done.61.refs_1_), channel_id=1, source_target_pairs={{0,1},{1,0},{2,3},{3,2},{4,5},{5,4},{6,7},{7,6},{8,9},{9,8},{10,11... | collective-permute-start | bytes 884744 | tf_op jit(solution)/shard_map/ppermute | solution.py:813
  (66 other events, 699.3 us)

commit v6 on v5

--- a/solution.py
+++ b/solution.py
@@ -158,8 +158,8 @@
     gain_two_ref,
     *refs,
 ):
-    probs_ref, qkv_ref, lefts_ref, inverse_ref, resid_ref = refs[:5]
-    send_refs = refs[5:-3]
+    probs_ref, qkv_ref, lefts_ref, mixed_ref, inverse_ref, resid_ref = refs[:6]
+    send_refs = refs[6:-3]
     qkv_s, mixed_s, line_s = refs[-3:]
     pair = pl.program_id(0)
     pairs = pl.num_programs(0)
@@ -177,7 +177,7 @@
             line_s[number, 0:2, :] = lines[2 * number : 2 * number + 2]
         rows = tokens_ref[...].astype(F32)
         normed = (rows * inverse_rms(rows) * gain_one_ref[...].astype(F32).reshape(1, width)).astype(BF)
-        lefts_ref[0] = normed
+        lefts_ref[0] = normed.T
         for part, weight_ref in enumerate((query_weight_ref, key_weight_ref, value_weight_ref)):
             values = dot(normed, weight_ref[...])
             for number in range(width // LANES):
@@ -245,7 +245,8 @@
     @pl.when(pair == pairs - 1)
     def _():
         mixed_all = jnp.concatenate([mixed_s[number] for number in range(width // LANES)], axis=1)
-        lefts_ref[1] = mixed_all
+        lefts_ref[1] = mixed_all.T
+        mixed_ref[...] = mixed_all
         resid = tokens_ref[...].astype(F32) + dot(mixed_all, out_weight_ref[...])
         resid_ref[...] = resid
         normed = (resid * inverse_rms(resid) * gain_two_ref[...].astype(F32).reshape(1, width)).astype(BF)
@@ -262,7 +263,8 @@
         out_shape=[
             shape_of((2 * pairs, seq_len, seq_len), BF),
             shape_of((3, pairs, seq_len, LANES), BF),
-            shape_of((2, seq_len, width), BF),
+            shape_of((2, width, seq_len), BF),
+            shape_of((seq_len, width), BF),
             shape_of((pairs, seq_len, LANES), F32),
             shape_of((seq_len, width), F32),
         ]
@@ -283,7 +285,8 @@
         out_specs=[
             pl.BlockSpec((2, seq_len, seq_len), lambda p: (p, 0, 0)),
             pl.BlockSpec((3, 1, seq_len, LANES), lambda p: (0, p, 0, 0)),
-            whole((2, seq_len, width)),
+            whole((2, width, seq_len)),
+            whole((seq_len, width)),
             pl.BlockSpec((1, seq_len, LANES), lambda p: (p, 0, 0)),
             whole((seq_len, width)),
         ]
@@ -602,13 +605,8 @@
     line_ref,
     *refs,
 ):
-    own_refs, other_refs, score_s, lefts_s, backs_s = refs[:2], refs[2:4], *refs[4:]
+    own_refs, other_refs, score_s, backs_s = refs[:2], refs[2:4], *refs[4:]
     seq_len = grad_ref.shape[0]
-
-    @pl.when(pl.program_id(0) == 0)
-    def _():
-        lefts_s[0] = lefts_ref[0].T
-        lefts_s[1] = lefts_ref[1].T
 
     tiles = seq_len // TILE
     query = qkv_ref[0, 0]
@@ -617,7 +615,7 @@
     lane = iota((seq_len, LANES), 1)
     row_tile = iota((seq_len, LANES), 0) // TILE
     scaled = grad_ref[...].astype(F32) * inverse_ref[0]
-    product = scaled * mixed_ref[0].astype(F32)
+    product = scaled * mixed_ref[...].astype(F32)
     scaled_low = scaled.astype(BF)
     key_wide = jnp.concatenate([key, jnp.where(lane == row_tile, 1.0, 0.0).astype(BF)], axis=1)
     backward_rows = jnp.where(iota((TILE, TILE), 0) + iota((TILE, TILE), 1) == TILE - 1, 1.0, 0.0)
@@ -684,7 +682,7 @@
     @pl.when(pl.program_id(0) % 2 == 1)
     def _():
         wides = [jnp.concatenate([backs_s[n], values], axis=1) for n, values in enumerate(backs)]
-        grads = [dot(lefts_s[n // 3], wide).astype(BF) for n, wide in enumerate(wides)]
+        grads = [dot(lefts_ref[n // 3], wide).astype(BF) for n, wide in enumerate(wides)]
         for core in range(2):
 
             @pl.when(core_ref[0] == core)
@@ -694,8 +692,8 @@
                     target_refs[1][...] = grads[2 + place]
 
 
-def backward_part(core, qkv, probs, lefts, mixed_grad, attn_grad, inverse):
-    _, seq_len, width = lefts.shape
+def backward_part(core, qkv, probs, lefts, mixed, mixed_grad, attn_grad, inverse):
+    seq_len, width = mixed.shape
     pairs = width // LANES
     assert pairs % 2 == 0
     column = pl.BlockSpec((seq_len, LANES), lambda p: (0, p))
@@ -713,7 +711,7 @@
             pl.BlockSpec((3, 1, seq_len, LANES), lambda p: (0, p, 0, 0)),
             pl.BlockSpec((2, seq_len, seq_len), lambda p: (p, 0, 0)),
             whole(lefts.shape),
-            pl.BlockSpec((1, seq_len, LANES), lambda p: (1, 0, p)),
+            column,
             column,
             column,
             pl.BlockSpec((1, seq_len, LANES), lambda p: (p, 0, 0)),
@@ -725,12 +723,11 @@
         + [grad] * 4,
         scratch_shapes=[
             pltpu.VMEM((2, seq_len, seq_len), BF),
-            pltpu.VMEM((2, width, seq_len), BF),
             pltpu.VMEM((4, seq_len, LANES), BF),
         ],
         compiler_params=params(58),
         name="attention_backward",
-    )(core, qkv, probs, lefts, lefts, mixed_grad, attn_grad, inverse)
+    )(core, qkv, probs, lefts, mixed, mixed_grad, attn_grad, inverse)
 
 
 def extra_kernel(router_ref, gain_ref, line_ref, out_ref):
@@ -1050,7 +1047,7 @@
 
     slot, column, *up_send = slots_part(expert, lengths, routes, upstream, capacity, experts, plan)
     up_there = plan.cross(up_send)
-    probs, qkv, lefts, inverse_total, resid, *row_send = forward_part(
+    probs, qkv, lefts, mixed, inverse_total, resid, *row_send = forward_part(
         expert,
         lengths,
         slot,
@@ -1118,7 +1115,7 @@
     stages = stages_of(dp_size, expert_size)
     core = place_of(stages[0])
     back, lines, *grads = backward_part(
-        core.reshape(1), qkv, probs, lefts, mixed_grad, attn_grad, inverse_total
+        core.reshape(1), qkv, probs, lefts, mixed, mixed_grad, attn_grad, inverse_total
     )
     kept, sent = grads[:2], grads[2:]
     back, sent, result_there, arrived_seconds = lax.optimization_barrier(

time: 363 us -> 362 us (level)
  no operation moved by 1% of the time
where the time goes in v6:
time: 362 us; the launch traced here: 359 us
  Pallas kernels  200 us (55%)
  starting transfers between devices  67.3 us (19%)
  waiting for transfers between devices  56.7 us (16%)
  local copies, waits for them, and re-layouts  19.4 us (5%)
  other arithmetic  10.5 us (3%)
    ppermute x67, starting transfers between devices, swap(): lax.ppermute(values, axis, [(place, place ^ distance) for place in range(...  67.3 us
    ppermute x67, waiting for transfers between devices, swap(): lax.ppermute(values, axis, [(place, place ^ distance) for place in range(...  56.7 us
    pallas_call x1, Pallas kernels, forward_part(): pl.pallas_call(functools.partial(forward_kernel, plan), grid=(pairs,), ou...  37.5 us
    pallas_call x1, Pallas kernels, backward_part(): pl.pallas_call(backward_kernel, grid=(pairs,), out_shape=[shape_of((3, se...  36.8 us
    pallas_call x2, Pallas kernels, expert_part(): pl.pallas_call(functools.partial(expert_kernel, plan, len(row_arrays), st...  28.2 us
    pallas_call x3, Pallas kernels, weight_grad_part(): pl.pallas_call(functools.partial(weight_grad_kernel, transposed, len(term...  17.6 us
    unnamed x94, local copies, waits for them, and re-layouts  16.8 us
    pallas_call x6, Pallas kernels, share(): pl.pallas_call(kernel, out_shape=[shape_of(shape, BF) for shape in shapes...  13.4 us
  transfers between devices with their start and end apart: 67, of which 21 were waited for; matrix products, arithmetic and copies ran while one was open for 4% of the time, Pallas kernels for 48%

profile of v6, /device:TPU:0, one launch (start us, length us, event | category | flops | bytes accessed | tf_op | source)
XLA Modules:
  0.0 358.9 jit_solution(2706573319876503579)
XLA Ops:
  1.3 5.2 %slots.1 = (s32[1,1024]{1,0:T(1,128)}, s32[1024,128]{1,0:T(8,128)}, bf16[320,768]{1,0:T(8,128)(2,1)}, bf16[320,768]{1,0:T(8,128)(2,1)}, bf16[320,768]{1,0:T(8,128)(2,1)}, /*index=5*/bf16[320,768]{1,0:T(8,128)(2,1)}) custom-call(s32[1]{0:T(128)} %bitcast.3.expert_ref, s32[1]{0:T(128)S(6)} %copy.40.length_ref, s32[1,1024]{1,0:T(1,128)} %routes_ref.1, ...), custom_call_target="tpu_custom_call" | custom-call | tf_op jit(solution)/shard_map/slots/pallas_call | solution.py:136
  6.5 3.0 collective-permute-start
  9.6 2.6 collective-permute-start.1
  12.2 37.5 %attention_forward.1 = (bf16[12,1024,1024]{2,1,0:T(8,128)(2,1)}, bf16[3,6,1024,128]{3,2,1,0:T(8,128)(2,1)}, bf16[2,768,1024]{2,1,0:T(8,128)(2,1)}, bf16[1024,768...) custom-call(s32[1]{0:T(128)} %bitcast.3.expert_ref, ...), custom_call_target="tpu_custom_call" | custom-call | tf_op jit(solution)/shard_map/attention_forward/pallas_call | solution.py:260
  50.8 5.9 %collective-permute-start.8 = (bf16[320,768]{1,0:T(8,128)(2,1)}, bf16[320,768]{1,0:T(8,128)(2,1)}, u32[]{:S(2)}, u32[]{:S(2)}) collective-permute-start(bf16[320,768]{1,0:T(8,128)(2,1)} %get-tuple-element.168), channel_id=1, source_target_pairs={{0,2},{1,3},{2,0},{3,1},{4,6},{5,7},{6,4},{7,5},{8,10},{9,11},{10,... | collective-permute-start | bytes 1474568 | tf_op jit(solution)/shard_map/ppermute | solution.py:810
  56.7 1.8 collective-permute-start.9
  58.6 9.6 %expert_activation_gradient.1 = (bf16[1280,768]{1,0:T(8,128)(2,1)S(1)}, bf16[1280,3072]{1,0:T(8,128)(2,1)S(1)}) custom-call(bf16[1,3072,768]{2,1,0:T(8,128)(2,1)S(1)} %copy-done.4, bf16[320,768]{1,0:T(8,128)(2,1)S(1)} %copy-done.12, bf16[320,768]{1,0:T(8,128)(2,1)S(1)} %collective-permute-done.refs_1_, bf16[320,768]{1,0:T(8,128)(2,1)S(1)} %collective-permute-done.1.refs_2_, ...), custom_call_target="tpu_custom_call" | custom-call | tf_op jit(solution)/shard_map/expert_activation_gradient/pallas_call | solution.py:322
  68.1 3.1 copy-done.2
  72.5 6.4 %collective-permute-done.8.refs_1_ = bf16[320,768]{1,0:T(8,128)(2,1)} collective-permute-done((bf16[320,768]{1,0:T(8,128)(2,1)}, bf16[320,768]{1,0:T(8,128)(2,1)}, u32[]{:S(2)}, u32[]{:S(2)}) %collective-permute-start.8) | collective-permute-done | bytes 491552 | tf_op jit(solution)/shard_map/ppermute | solution.py:810
  78.9 2.5 collective-permute-done.9.refs_2_
  81.9 2.5 collective-permute-start.7
  84.9 19.8 %expert_rows.2 = (bf16[1280,3072]{1,0:T(8,128)(2,1)}, bf16[1280,3072]{1,0:T(8,128)(2,1)}, bf16[1280,768]{1,0:T(8,128)(2,1)S(1)}, bf16[1280,768]{1,0:T(8,128)(2,1...) custom-call(s32[1]{0:T(128)} %bitcast.3.expert_ref, ...), custom_call_target="tpu_custom_call" | custom-call | tf_op jit(solution)/shard_map/expert_rows/pallas_call | solution.py:405
  106.7 8.4 %expert_rows.3 = (bf16[1280,3072]{1,0:T(8,128)(2,1)}, bf16[1280,3072]{1,0:T(8,128)(2,1)}, bf16[1280,768]{1,0:T(8,128)(2,1)S(1)}, bf16[1280,768]{1,0:T(8,128)(2,1...) custom-call(s32[1]{0:T(128)} %bitcast.3.expert_ref, ...), custom_call_target="tpu_custom_call", output_to_operand_aliasing={{0}: (7, {}), {1}: (8, {}), {2}: (9, {}), {3}: (10, {}), {4... | custom-call | tf_op jit(solution)/shard_map/expert_rows/pallas_call | solution.py:405
  115.0 3.9 %copy-done.1 = bf16[1280,3072]{1,0:T(8,128)(2,1)S(1)} copy-done((bf16[1280,3072]{1,0:T(8,128)(2,1)S(1)}, bf16[1280,3072]{1,0:T(8,128)(2,1)}, u32[]{:S(2)}) %copy-start.1) | copy-done | bytes 7864344
  119.0 4.5 %expert_weight_gradients.5 = bf16[2,768,768]{2,1,0:T(8,128)(2,1)S(1)} custom-call(s32[2]{0:T(128)S(1)} %get-tuple-element.278.refs_0_, bf16[1280,3072]{1,0:T(8,128)(2,1)S(1)} %copy-done.1, bf16[1280,768]{1,0:T(8,128)(2,1)S(1)} %get-tuple-element.183.refs_5_.refs_2_), custom_call_target="tpu_custom_call" | custom-call | tf_op jit(solution)/shard_map/expert_weight_gradients/pallas_call | solution.py:473
  125.1 4.3 %expert_weight_gradients.4 = bf16[2,768,768]{2,1,0:T(8,128)(2,1)S(1)} custom-call(s32[2]{0:T(128)S(1)} %get-tuple-element.280.refs_0_, bf16[1280,3072]{1,0:T(8,128)(2,1)S(1)} %copy-done, bf16[1280,768]{1,0:T(8,128)(2,1)S(1)} %get-tuple-element.182.refs_4_.refs_2_), custom_call_target="tpu_custom_call" | custom-call | tf_op jit(solution)/shard_map/expert_weight_gradients/pallas_call | solution.py:473
  131.0 2.0 collective-permute-start.14
  135.4 7.0 %expert_output.1 = (bf16[320,768]{1,0:T(8,128)(2,1)S(1)}, bf16[320,768]{1,0:T(8,128)(2,1)S(1)}, bf16[320,768]{1,0:T(8,128)(2,1)S(1)}, bf16[320,768]{1,0:T(8,128)(2,1)S(1)}) custom-call(bf16[1280,3072]{1,0:T(8,128)(2,1)S(1)} %copy-done, bf16[1,3072,768]{2,1,0:T(8,128)(2,1)S(1)} %bitcast.17, f32[1280,1]{1,0:T(8,128)S(1)} %get-tuple-element.191.gate_ref), custom_call_target="tpu_custom_call" | custom-call | tf_op jit(solution)/shard_map/expert_output/pallas_call | solution.py:504
  142.4 8.7 %expert_weight_gradients.3 = (bf16[2,768,768]{2,1,0:T(8,128)(2,1)S(1)}, bf16[2,768,768]{2,1,0:T(8,128)(2,1)S(1)}) custom-call(s32[2]{0:T(128)S(1)} %get-tuple-element.281.refs_0_, s32[2]{0:T(128)S(1)} %get-tuple-element.279.refs_1_, bf16[1280,3072]{1,0:T(8,128)(2,1)S(1)} %copy-done, bf16[1280,3072]{1,0:T(8,128)(2,1)} %get-tuple-element.181.refs_3_.refs_1_, ...), custom_call_target="tpu_custom_call" | custom-call | tf_op jit(solution)/shard_map/expert_weight_gradients/pallas_call | solution.py:473
  154.0 15.0 %collective-permute-done.15.refs_2_ = bf16[320,768]{1,0:T(8,128)(2,1)S(1)} collective-permute-done((bf16[320,768]{1,0:T(8,128)(2,1)S(1)}, bf16[320,768]{1,0:T(8,128)(2,1)S(1)}, u32[]{:S(2)}, u32[]{:S(2)}) %collective-permute-start.15) | collective-permute-done | bytes 491552 | tf_op jit(solution)/shard_map/ppermute | solution.py:810
  173.1 3.7 %collective-permute-done.22.refs_3_ = bf16[2,768,768]{2,1,0:T(8,128)(2,1)S(1)} collective-permute-done((bf16[2,768,768]{2,1,0:T(8,128)(2,1)S(1)}, bf16[2,768,768]{2,1,0:T(8,128)(2,1)S(1)}, u32[]{:S(2)}, u32[]{:S(2)}) %collective-permute-start.22) | collective-permute-done | bytes 2359328 | tf_op jit(solution)/shard_map/ppermute | solution.py:810
  178.3 4.3 %collective-permute-done.21.refs_2_ = bf16[2,768,768]{2,1,0:T(8,128)(2,1)} collective-permute-done((bf16[2,768,768]{2,1,0:T(8,128)(2,1)S(1)}, bf16[2,768,768]{2,1,0:T(8,128)(2,1)}, u32[]{:S(2)}, u32[]{:S(2)}) %collective-permute-start.21) | collective-permute-done | bytes 2359328 | tf_op jit(solution)/shard_map/ppermute | solution.py:810
  182.6 4.3 %later_sums.1 = (bf16[1,768,768]{2,1,0:T(8,128)(2,1)}, bf16[1,768,768]{2,1,0:T(8,128)(2,1)}) custom-call(bf16[2,768,768]{2,1,0:T(8,128)(2,1)} %copy-done.7, bf16[2,768,768]{2,1,0:T(8,128)(2,1)} %copy-done.9, bf16[2,768,768]{2,1,0:T(8,128)(2,1)} %collective-permute-done.21.refs_2_, bf16[2,768,768]{2,1,0:T(8,128)(2,1)} %copy-done.17), custom_call_target="tpu_custom_call" | custom-call | tf_op jit(solution)/shard_map/later_sums/pallas_call | solution.py:449
  188.9 1.9 collective-permute-start.23
  193.3 9.5 %expert_norm_backward.1 = (f32[1024,768]{1,0:T(8,128)}, bf16[1024,768]{1,0:T(8,128)(2,1)}, bf16[1024,768]{1,0:T(8,128)(2,1)}, f32[1,768]{1,0:T(1,128)}) custom-call(s32[1]{0:T(128)} %bitcast.3.expert_ref, s32[1]{0:T(128)S(6)} %copy.40.length_ref, s32[1024,128]{1,0:T(8,128)} %get-tuple-element.150.column_ref, f32[1024,768]{1,0:T(8,128)} %get-tuple-element.260.resid_ref, ...), custom_call_target="tpu_custom_call" | custom-call | tf_op jit(solution)/shard_map/expert_norm_backward/pallas_call | solution.py:578
  202.8 36.8 %attention_backward.1 = (bf16[3,1024,768]{2,1,0:T(8,128)(2,1)}, f32[6,2,768]{2,1,0:T(2,128)}, bf16[768,768]{1,0:T(8,128)(2,1)}, bf16[768,768]{1,0:T(8,128)(2,1)}...) custom-call(s32[1]{0:T(128)} %bitcast.2.core_ref, bf16[3,6,1024,128]{3,2,1,0:T(8,128)(2,1)} %get-tuple-element.146.qkv_ref, ...), custom_call_target="tpu_custom_call" | custom-call | tf_op jit(solution)/shard_map/attention_backward/pallas_call | solution.py:701
  240.3 2.7 collective-permute-done.28.refs_1_
  243.0 2.8 share.6
  249.3 2.6 fusion.3.router_ref
  252.5 2.2 extra_rows.1.refs_2_
  256.8 2.9 share.7
  263.2 9.4 %token_gradient.1 = f32[1024,768]{1,0:T(8,128)} custom-call(bf16[3,1024,768]{2,1,0:T(8,128)(2,1)} %get-tuple-element.233.back_ref, bf16[768,768]{1,0:T(8,128)(2,1)} %refs_8_.2, bf16[768,768]{1,0:T(8,128)(2,1)} %refs_9_.1, bf16[768,768]{1,0:T(8,128)(2,1)} %refs_8_.3, bf16[1024,768]{1,0:T(8,128)(2,1)} %bitcast.21, bf16[768]{0:T(1024)(128)(2,1)} %gain_ref.3, ...), custom_call_target="tpu_custom_call" | custom-call | tf_op jit(solution)/shard_map/token_gradient/pallas_call | solution.py:796
  272.6 2.0 share.8
  275.7 2.0 collective-permute-start.35
  277.7 2.3 collective-permute-done.34.refs_1_
  282.5 3.9 %collective-permute-done.36.refs_3_ = bf16[48,768]{1,0:T(8,128)(2,1)S(1)} collective-permute-done((bf16[48,768]{1,0:T(8,128)(2,1)}, bf16[48,768]{1,0:T(8,128)(2,1)S(1)}, u32[]{:S(2)}, u32[]{:S(2)}) %collective-permute-start.36) | collective-permute-done | bytes 73760 | tf_op jit(solution)/shard_map/ppermute | solution.py:810
  288.7 2.3 collective-permute-start.38
  291.0 2.1 collective-permute-start.39
  293.1 2.2 share.10
  295.3 2.3 collective-permute-start.45
  297.6 2.1 collective-permute-start.46
  315.8 2.1 collective-permute-done.48.refs_2_
  323.9 3.8 %convert_add_fusion = f32[1,768,768]{2,1,0:T(8,128)} fusion(bf16[1,768,768]{2,1,0:T(8,128)(2,1)} %collective-permute-done.27, bf16[2,768,768]{2,1,0:T(8,128)(2,1)} %copy-done.17, bf16[2,768,768]{2,1,0:T(8,128)(2,1)} %copy-done.9), kind=kLoop, calls=%fused_computation | loop fusion | flops 2949120 | bytes 5898240 | tf_op jit(solution)/shard_map/add | solution.py:1158
  329.7 3.5 collective-permute-done.50.refs_3_
  333.9 3.6 convert_add_fusion.1
  337.5 5.5 %result.1 = bf16[1024,768]{1,0:T(8,128)(2,1)} custom-call(s32[1]{0:T(128)} %bitcast.3.expert_ref, s32[1]{0:T(128)S(6)} %copy.40.length_ref, s32[1024,128]{1,0:T(8,128)} %get-tuple-element.150.column_ref, f32[1024,768]{1,0:T(8,128)} %get-tuple-element.260.resid_ref, bf16[320,768]{1,0:T(8,128)(2,1)} %copy-done.10, ...), custom_call_target="tpu_custom_call" | custom-call | tf_op jit(solution)/shard_map/result/pallas_call | solution.py:532
  346.1 5.5 %assemble.2 = (f32[768,768]{1,0:T(8,128)}, f32[768,768]{1,0:T(8,128)}, f32[768,128]{1,0:T(8,128)}) custom-call(s32[2]{0:T(128)} %pad_add_fusion.places_ref, bf16[192,768]{1,0:T(8,128)(2,1)} %join.2.refs_0_, bf16[192,768]{1,0:T(8,128)(2,1)} %collective-permute-done.55.refs_1_, bf16[192,768]{1,0:T(8,128)(2,1)} %collective-permute-done.56.refs_2_, ...), custom_call_target="tpu_custom_call" | custom-call | tf_op jit(solution)/shard_map/assemble/pallas_call | solution.py:1000
  351.7 5.2 %assemble.3 = (f32[768,768]{1,0:T(8,128)}, f32[768,768]{1,0:T(8,128)}, f32[768,128]{1,0:T(8,128)}) custom-call(s32[2]{0:T(128)} %pad_add_fusion.places_ref, bf16[192,768]{1,0:T(8,128)(2,1)} %join.3.refs_0_, bf16[192,768]{1,0:T(8,128)(2,1)} %collective-permute-done.61.refs_1_, bf16[192,768]{1,0:T(8,128)(2,1)} %collective-permute-done.62.refs_2_, ...), custom_call_target="tpu_custom_call" | custom-call | tf_op jit(solution)/shard_map/assemble/pallas_call | solution.py:1000
  (220 shorter events, 69.5 us)
Async XLA Ops:
  6.5 43.1 %collective-permute-start = (bf16[320,768]{1,0:T(8,128)(2,1)}, bf16[320,768]{1,0:T(8,128)(2,1)S(1)}, u32[]{:S(2)}, u32[]{:S(2)}) collective-permute-start(bf16[320,768]{1,0:T(8,128)(2,1)} %get-tuple-element.157), channel_id=1, source_target_pairs={{0,2},{1,3},{2,0},{3,1},{4,6},{5,7},{6,4},{7,5},{8,10},{9,11},{10,... | collective-permute-start | bytes 1474568 | tf_op jit(solution)/shard_map/ppermute | solution.py:810
  9.6 40.1 %collective-permute-start.1 = (bf16[320,768]{1,0:T(8,128)(2,1)}, bf16[320,768]{1,0:T(8,128)(2,1)S(1)}, u32[]{:S(2)}, u32[]{:S(2)}) collective-permute-start(bf16[320,768]{1,0:T(8,128)(2,1)} %get-tuple-element.158), channel_id=1, source_target_pairs={{0,4},{1,5},{2,6},{3,7},{4,0},{5,1},{6,2},{7,3},{8,12},{9,13},{10,... | collective-permute-start | bytes 1474568 | tf_op jit(solution)/shard_map/ppermute | solution.py:810
  12.1 37.5 %collective-permute-start.2 = (bf16[320,768]{1,0:T(8,128)(2,1)}, bf16[320,768]{1,0:T(8,128)(2,1)}, u32[]{:S(2)}, u32[]{:S(2)}) collective-permute-start(bf16[320,768]{1,0:T(8,128)(2,1)} %get-tuple-element.159), channel_id=1, source_target_pairs={{0,6},{1,7},{2,4},{3,5},{4,2},{5,3},{6,0},{7,1},{8,14},{9,15},{10,... | collective-permute-start | bytes 1474568 | tf_op jit(solution)/shard_map/ppermute | solution.py:810
  49.8 8.8 %collective-permute-start.4 = (bf16[320,768]{1,0:T(8,128)(2,1)S(1)}, bf16[320,768]{1,0:T(8,128)(2,1)S(1)}, u32[]{:S(2)}, u32[]{:S(2)}) collective-permute-start(bf16[320,768]{1,0:T(8,128)(2,1)S(1)} %collective-permute-done.refs_1_), channel_id=1, source_target_pairs={{0,1},{1,0},{2,3},{3,2},{4,5},{5,4},{6,7},{7,6},{8,9},{9,8},{10,11... | collective-permute-start | bytes 1474568 | tf_op jit(solution)/shard_map/ppermute | solution.py:810
  50.3 8.3 %collective-permute-start.5 = (bf16[320,768]{1,0:T(8,128)(2,1)S(1)}, bf16[320,768]{1,0:T(8,128)(2,1)S(1)}, u32[]{:S(2)}, u32[]{:S(2)}) collective-permute-start(bf16[320,768]{1,0:T(8,128)(2,1)S(1)} %collective-permute-done.1.refs_2_), channel_id=1, source_target_pairs={{0,1},{1,0},{2,3},{3,2},{4,5},{5,4},{6,7},{7,6},{8,9},{9,8},{10,11... | collective-permute-start | bytes 1474568 | tf_op jit(solution)/shard_map/ppermute | solution.py:810
  50.4 8.2 %collective-permute-start.6 = (bf16[320,768]{1,0:T(8,128)(2,1)}, bf16[320,768]{1,0:T(8,128)(2,1)S(1)}, u32[]{:S(2)}, u32[]{:S(2)}) collective-permute-start(bf16[320,768]{1,0:T(8,128)(2,1)} %collective-permute-done.2.refs_3_), channel_id=1, source_target_pairs={{0,1},{1,0},{2,3},{3,2},{4,5},{5,4},{6,7},{7,6},{8,9},{9,8},{10,11... | collective-permute-start | bytes 1474568 | tf_op jit(solution)/shard_map/ppermute | solution.py:810
  50.8 28.1 %collective-permute-start.8 = (bf16[320,768]{1,0:T(8,128)(2,1)}, bf16[320,768]{1,0:T(8,128)(2,1)}, u32[]{:S(2)}, u32[]{:S(2)}) collective-permute-start(bf16[320,768]{1,0:T(8,128)(2,1)} %get-tuple-element.168), channel_id=1, source_target_pairs={{0,2},{1,3},{2,0},{3,1},{4,6},{5,7},{6,4},{7,5},{8,10},{9,11},{10,... | collective-permute-start | bytes 1474568 | tf_op jit(solution)/shard_map/ppermute | solution.py:810
  56.7 24.7 %collective-permute-start.9 = (bf16[320,768]{1,0:T(8,128)(2,1)}, bf16[320,768]{1,0:T(8,128)(2,1)}, u32[]{:S(2)}, u32[]{:S(2)}) collective-permute-start(bf16[320,768]{1,0:T(8,128)(2,1)} %get-tuple-element.169), channel_id=1, source_target_pairs={{0,4},{1,5},{2,6},{3,7},{4,0},{5,1},{6,2},{7,3},{8,12},{9,13},{10,... | collective-permute-start | bytes 1474568 | tf_op jit(solution)/shard_map/ppermute | solution.py:810
  81.9 22.8 %collective-permute-start.7 = (bf16[320,768]{1,0:T(8,128)(2,1)}, bf16[320,768]{1,0:T(8,128)(2,1)S(1)}, u32[]{:S(2)}, u32[]{:S(2)}) collective-permute-start(bf16[320,768]{1,0:T(8,128)(2,1)} %get-tuple-element.166), channel_id=1, source_target_pairs={{0,6},{1,7},{2,4},{3,5},{4,2},{5,3},{6,0},{7,1},{8,14},{9,15},{10,... | collective-permute-start | bytes 1474568 | tf_op jit(solution)/shard_map/ppermute | solution.py:810
  123.5 53.3 %collective-permute-start.22 = (bf16[2,768,768]{2,1,0:T(8,128)(2,1)S(1)}, bf16[2,768,768]{2,1,0:T(8,128)(2,1)S(1)}, u32[]{:S(2)}, u32[]{:S(2)}) collective-permute-start(bf16[2,768,768]{2,1,0:T(8,128)(2,1)S(1)} %expert_weight_gradients.5), channel_id=1, source_target_pairs={{0,16},{8,24},{16,0},{24,8},{1,17},{9,25},{17,1},{25,9},{2,18},{10... | collective-permute-start | bytes 7077896 | tf_op jit(solution)/shard_map/ppermute | solution.py:810
  129.4 53.2 %collective-permute-start.21 = (bf16[2,768,768]{2,1,0:T(8,128)(2,1)S(1)}, bf16[2,768,768]{2,1,0:T(8,128)(2,1)}, u32[]{:S(2)}, u32[]{:S(2)}) collective-permute-start(bf16[2,768,768]{2,1,0:T(8,128)(2,1)S(1)} %expert_weight_gradients.4), channel_id=1, source_target_pairs={{0,8},{8,0},{16,24},{24,16},{1,9},{9,1},{17,25},{25,17},{2,10},{10... | collective-permute-start | bytes 7077896 | tf_op jit(solution)/shard_map/ppermute | solution.py:810
  131.0 23.1 %collective-permute-start.14 = (bf16[320,768]{1,0:T(8,128)(2,1)S(1)}, bf16[320,768]{1,0:T(8,128)(2,1)S(1)}, u32[]{:S(2)}, u32[]{:S(2)}) collective-permute-start(bf16[320,768]{1,0:T(8,128)(2,1)S(1)} %get-tuple-element.188), channel_id=1, source_target_pairs={{0,2},{1,3},{2,0},{3,1},{4,6},{5,7},{6,4},{7,5},{8,10},{9,11},{10,... | collective-permute-start | bytes 1474568 | tf_op jit(solution)/shard_map/ppermute | solution.py:810
  132.9 36.1 %collective-permute-start.15 = (bf16[320,768]{1,0:T(8,128)(2,1)S(1)}, bf16[320,768]{1,0:T(8,128)(2,1)S(1)}, u32[]{:S(2)}, u32[]{:S(2)}) collective-permute-start(bf16[320,768]{1,0:T(8,128)(2,1)S(1)} %get-tuple-element.189), channel_id=1, source_target_pairs={{0,4},{1,5},{2,6},{3,7},{4,0},{5,1},{6,2},{7,3},{8,12},{9,13},{10,... | collective-permute-start | bytes 1474568 | tf_op jit(solution)/shard_map/ppermute | solution.py:810
  134.0 35.1 %collective-permute-start.16 = (bf16[320,768]{1,0:T(8,128)(2,1)S(1)}, bf16[320,768]{1,0:T(8,128)(2,1)S(1)}, u32[]{:S(2)}, u32[]{:S(2)}) collective-permute-start(bf16[320,768]{1,0:T(8,128)(2,1)S(1)} %get-tuple-element.190), channel_id=1, source_target_pairs={{0,6},{1,7},{2,4},{3,5},{4,2},{5,3},{6,0},{7,1},{8,14},{9,15},{10,... | collective-permute-start | bytes 1474568 | tf_op jit(solution)/shard_map/ppermute | solution.py:810
  186.9 52.8 %collective-permute-start.26 = (bf16[1,768,768]{2,1,0:T(8,128)(2,1)}, bf16[1,768,768]{2,1,0:T(8,128)(2,1)}, u32[]{:S(2)}, u32[]{:S(2)}) collective-permute-start(bf16[1,768,768]{2,1,0:T(8,128)(2,1)} %get-tuple-element.203), channel_id=1, source_target_pairs={{0,16},{8,24},{16,0},{24,8},{1,17},{9,25},{17,1},{25,9},{2,18},{10... | collective-permute-start | bytes 3538952 | tf_op jit(solution)/shard_map/ppermute | solution.py:810
  187.4 52.3 %collective-permute-start.27 = (bf16[1,768,768]{2,1,0:T(8,128)(2,1)}, bf16[1,768,768]{2,1,0:T(8,128)(2,1)}, u32[]{:S(2)}, u32[]{:S(2)}) collective-permute-start(bf16[1,768,768]{2,1,0:T(8,128)(2,1)} %get-tuple-element.204), channel_id=1, source_target_pairs={{0,8},{8,0},{16,24},{24,16},{1,9},{9,1},{17,25},{25,17},{2,10},{10... | collective-permute-start | bytes 3538952 | tf_op jit(solution)/shard_map/ppermute | solution.py:810
  188.9 50.8 %collective-permute-start.23 = (bf16[320,768]{1,0:T(8,128)(2,1)}, bf16[320,768]{1,0:T(8,128)(2,1)}, u32[]{:S(2)}, u32[]{:S(2)}) collective-permute-start(bf16[320,768]{1,0:T(8,128)(2,1)} %copy-done.16), channel_id=1, source_target_pairs={{0,2},{1,3},{2,0},{3,1},{4,6},{5,7},{6,4},{7,5},{8,10},{9,11},{10,... | collective-permute-start | bytes 1474568 | tf_op jit(solution)/shard_map/ppermute | solution.py:810
  190.9 48.8 %collective-permute-start.24 = (bf16[320,768]{1,0:T(8,128)(2,1)}, bf16[320,768]{1,0:T(8,128)(2,1)}, u32[]{:S(2)}, u32[]{:S(2)}) collective-permute-start(bf16[320,768]{1,0:T(8,128)(2,1)} %copy-done.15), channel_id=1, source_target_pairs={{0,4},{1,5},{2,6},{3,7},{4,0},{5,1},{6,2},{7,3},{8,12},{9,13},{10,... | collective-permute-start | bytes 1474568 | tf_op jit(solution)/shard_map/ppermute | solution.py:810
  192.0 47.8 %collective-permute-start.25 = (bf16[320,768]{1,0:T(8,128)(2,1)}, bf16[320,768]{1,0:T(8,128)(2,1)}, u32[]{:S(2)}, u32[]{:S(2)}) collective-permute-start(bf16[320,768]{1,0:T(8,128)(2,1)} %copy-done.14), channel_id=1, source_target_pairs={{0,6},{1,7},{2,4},{3,5},{4,2},{5,3},{6,0},{7,1},{8,14},{9,15},{10,... | collective-permute-start | bytes 1474568 | tf_op jit(solution)/shard_map/ppermute | solution.py:810
  239.8 14.9 %collective-permute-start.32 = (bf16[768,768]{1,0:T(8,128)(2,1)}, bf16[768,768]{1,0:T(8,128)(2,1)}, u32[]{:S(2)}, u32[]{:S(2)}) collective-permute-start(bf16[768,768]{1,0:T(8,128)(2,1)} %get-tuple-element.223), channel_id=1, source_target_pairs={{0,1},{1,0},{2,3},{3,2},{4,5},{5,4},{6,7},{7,6},{8,9},{9,8},{10,11... | collective-permute-start | bytes 3538952 | tf_op jit(solution)/shard_map/ppermute | solution.py:810
  245.8 16.0 %collective-permute-start.29 = (bf16[192,768]{1,0:T(8,128)(2,1)}, bf16[192,768]{1,0:T(8,128)(2,1)}, u32[]{:S(2)}, u32[]{:S(2)}) collective-permute-start(bf16[192,768]{1,0:T(8,128)(2,1)} %get-tuple-element.218), channel_id=1, source_target_pairs={{0,8},{8,0},{16,24},{24,16},{1,9},{9,1},{17,25},{25,17},{2,10},{10... | collective-permute-start | bytes 884744 | tf_op jit(solution)/shard_map/ppermute | solution.py:810
  246.4 26.2 %collective-permute-start.30 = (bf16[192,768]{1,0:T(8,128)(2,1)}, bf16[192,768]{1,0:T(8,128)(2,1)}, u32[]{:S(2)}, u32[]{:S(2)}) collective-permute-start(bf16[192,768]{1,0:T(8,128)(2,1)} %get-tuple-element.219), channel_id=1, source_target_pairs={{0,16},{8,24},{16,0},{24,8},{1,17},{9,25},{17,1},{25,9},{2,18},{10... | collective-permute-start | bytes 884744 | tf_op jit(solution)/shard_map/ppermute | solution.py:810
  247.9 24.7 %collective-permute-start.31 = (bf16[192,768]{1,0:T(8,128)(2,1)}, bf16[192,768]{1,0:T(8,128)(2,1)}, u32[]{:S(2)}, u32[]{:S(2)}) collective-permute-start(bf16[192,768]{1,0:T(8,128)(2,1)} %get-tuple-element.220), channel_id=1, source_target_pairs={{0,24},{8,16},{16,8},{24,0},{1,25},{9,17},{17,9},{25,1},{2,26},{10... | collective-permute-start | bytes 884744 | tf_op jit(solution)/shard_map/ppermute | solution.py:810
  259.7 31.3 %collective-permute-start.41 = (bf16[224,768]{1,0:T(8,128)(2,1)}, bf16[224,768]{1,0:T(8,128)(2,1)}, u32[]{:S(2)}, u32[]{:S(2)}) collective-permute-start(bf16[224,768]{1,0:T(8,128)(2,1)} %get-tuple-element.230), channel_id=1, source_target_pairs={{0,8},{8,0},{16,24},{24,16},{1,9},{9,1},{17,25},{25,17},{2,10},{10... | collective-permute-start | bytes 1032200 | tf_op jit(solution)/shard_map/ppermute | solution.py:810
  260.3 32.9 %collective-permute-start.42 = (bf16[224,768]{1,0:T(8,128)(2,1)}, bf16[224,768]{1,0:T(8,128)(2,1)}, u32[]{:S(2)}, u32[]{:S(2)}) collective-permute-start(bf16[224,768]{1,0:T(8,128)(2,1)} %get-tuple-element.231), channel_id=1, source_target_pairs={{0,16},{8,24},{16,0},{24,8},{1,17},{9,25},{17,1},{25,9},{2,18},{10... | collective-permute-start | bytes 1032200 | tf_op jit(solution)/shard_map/ppermute | solution.py:810
  261.8 31.3 %collective-permute-start.43 = (bf16[224,768]{1,0:T(8,128)(2,1)}, bf16[224,768]{1,0:T(8,128)(2,1)}, u32[]{:S(2)}, u32[]{:S(2)}) collective-permute-start(bf16[224,768]{1,0:T(8,128)(2,1)} %get-tuple-element.232), channel_id=1, source_target_pairs={{0,24},{8,16},{16,8},{24,0},{1,25},{9,17},{17,9},{25,1},{2,26},{10... | collective-permute-start | bytes 1032200 | tf_op jit(solution)/shard_map/ppermute | solution.py:810
  288.7 8.9 %collective-permute-start.37 = (bf16[48,768]{1,0:T(8,128)(2,1)}, bf16[48,768]{1,0:T(8,128)(2,1)S(1)}, u32[]{:S(2)}, u32[]{:S(2)}) collective-permute-start(bf16[48,768]{1,0:T(8,128)(2,1)} %share.9.refs_0_), channel_id=1, source_target_pairs={{0,2},{1,3},{2,0},{3,1},{4,6},{5,7},{6,4},{7,5},{8,10},{9,11},{10,... | collective-permute-start | bytes 221192 | tf_op jit(solution)/shard_map/ppermute | solution.py:810
  288.7 11.0 %collective-permute-start.38 = (bf16[48,768]{1,0:T(8,128)(2,1)}, bf16[48,768]{1,0:T(8,128)(2,1)S(1)}, u32[]{:S(2)}, u32[]{:S(2)}) collective-permute-start(bf16[48,768]{1,0:T(8,128)(2,1)} %share.9.refs_0_), channel_id=1, source_target_pairs={{0,4},{1,5},{2,6},{3,7},{4,0},{5,1},{6,2},{7,3},{8,12},{9,13},{10,... | collective-permute-start | bytes 221192 | tf_op jit(solution)/shard_map/ppermute | solution.py:810
  291.0 8.7 %collective-permute-start.39 = (bf16[48,768]{1,0:T(8,128)(2,1)}, bf16[48,768]{1,0:T(8,128)(2,1)S(1)}, u32[]{:S(2)}, u32[]{:S(2)}) collective-permute-start(bf16[48,768]{1,0:T(8,128)(2,1)} %share.9.refs_0_), channel_id=1, source_target_pairs={{0,6},{1,7},{2,4},{3,5},{4,2},{5,3},{6,0},{7,1},{8,14},{9,15},{10,... | collective-permute-start | bytes 221192 | tf_op jit(solution)/shard_map/ppermute | solution.py:810
  295.3 10.4 %collective-permute-start.44 = (bf16[80,768]{1,0:T(8,128)(2,1)}, bf16[80,768]{1,0:T(8,128)(2,1)S(1)}, u32[]{:S(2)}, u32[]{:S(2)}) collective-permute-start(bf16[80,768]{1,0:T(8,128)(2,1)} %get-tuple-element.248), channel_id=1, source_target_pairs={{0,2},{1,3},{2,0},{3,1},{4,6},{5,7},{6,4},{7,5},{8,10},{9,11},{10,... | collective-permute-start | bytes 368648 | tf_op jit(solution)/shard_map/ppermute | solution.py:810
  295.3 10.9 %collective-permute-start.45 = (bf16[80,768]{1,0:T(8,128)(2,1)}, bf16[80,768]{1,0:T(8,128)(2,1)}, u32[]{:S(2)}, u32[]{:S(2)}) collective-permute-start(bf16[80,768]{1,0:T(8,128)(2,1)} %get-tuple-element.249), channel_id=1, source_target_pairs={{0,4},{1,5},{2,6},{3,7},{4,0},{5,1},{6,2},{7,3},{8,12},{9,13},{10,... | collective-permute-start | bytes 368648 | tf_op jit(solution)/shard_map/ppermute | solution.py:810
  297.6 8.6 %collective-permute-start.46 = (bf16[80,768]{1,0:T(8,128)(2,1)}, bf16[80,768]{1,0:T(8,128)(2,1)}, u32[]{:S(2)}, u32[]{:S(2)}) collective-permute-start(bf16[80,768]{1,0:T(8,128)(2,1)} %get-tuple-element.250), channel_id=1, source_target_pairs={{0,6},{1,7},{2,4},{3,5},{4,2},{5,3},{6,0},{7,1},{8,14},{9,15},{10,... | collective-permute-start | bytes 368648 | tf_op jit(solution)/shard_map/ppermute | solution.py:810
  302.7 16.5 %collective-permute-start.40 = (bf16[192,768]{1,0:T(8,128)(2,1)}, bf16[192,768]{1,0:T(8,128)(2,1)S(1)}, u32[]{:S(2)}, u32[]{:S(2)}) collective-permute-start(bf16[192,768]{1,0:T(8,128)(2,1)} %join.2.refs_0_), channel_id=1, source_target_pairs={{0,24},{8,16},{16,8},{24,0},{1,25},{9,17},{17,9},{25,1},{2,26},{10... | collective-permute-start | bytes 884744 | tf_op jit(solution)/shard_map/ppermute | solution.py:810
  304.2 15.6 %collective-permute-start.55 = (bf16[192,768]{1,0:T(8,128)(2,1)}, bf16[192,768]{1,0:T(8,128)(2,1)}, u32[]{:S(2)}, u32[]{:S(2)}) collective-permute-start(bf16[192,768]{1,0:T(8,128)(2,1)} %join.2.refs_0_), channel_id=1, source_target_pairs={{0,8},{8,0},{16,24},{24,16},{1,9},{9,1},{17,25},{25,17},{2,10},{10... | collective-permute-start | bytes 884744 | tf_op jit(solution)/shard_map/ppermute | solution.py:810
  309.9 12.3 %collective-permute-start.56 = (bf16[192,768]{1,0:T(8,128)(2,1)}, bf16[192,768]{1,0:T(8,128)(2,1)}, u32[]{:S(2)}, u32[]{:S(2)}) collective-permute-start(bf16[192,768]{1,0:T(8,128)(2,1)} %join.2.refs_0_), channel_id=1, source_target_pairs={{0,16},{8,24},{16,0},{24,8},{1,17},{9,25},{17,1},{25,9},{2,18},{10... | collective-permute-start | bytes 884744 | tf_op jit(solution)/shard_map/ppermute | solution.py:810
  317.9 9.8 %collective-permute-start.51 = (bf16[320,768]{1,0:T(8,128)(2,1)S(1)}, bf16[320,768]{1,0:T(8,128)(2,1)}, u32[]{:S(2)}, u32[]{:S(2)}) collective-permute-start(bf16[320,768]{1,0:T(8,128)(2,1)S(1)} %get-tuple-element.261.refs_0_), channel_id=1, source_target_pairs={{0,1},{1,0},{2,3},{3,2},{4,5},{5,4},{6,7},{7,6},{8,9},{9,8},{10,11... | collective-permute-start | bytes 1474568 | tf_op jit(solution)/shard_map/ppermute | solution.py:810
  319.2 8.7 %collective-permute-start.52 = (bf16[320,768]{1,0:T(8,128)(2,1)}, bf16[320,768]{1,0:T(8,128)(2,1)}, u32[]{:S(2)}, u32[]{:S(2)}) collective-permute-start(bf16[320,768]{1,0:T(8,128)(2,1)} %collective-permute-done.23.refs_1_), channel_id=1, source_target_pairs={{0,1},{1,0},{2,3},{3,2},{4,5},{5,4},{6,7},{7,6},{8,9},{9,8},{10,11... | collective-permute-start | bytes 1474568 | tf_op jit(solution)/shard_map/ppermute | solution.py:810
  319.2 10.0 %collective-permute-start.53 = (bf16[320,768]{1,0:T(8,128)(2,1)}, bf16[320,768]{1,0:T(8,128)(2,1)}, u32[]{:S(2)}, u32[]{:S(2)}) collective-permute-start(bf16[320,768]{1,0:T(8,128)(2,1)} %collective-permute-done.24.refs_2_), channel_id=1, source_target_pairs={{0,1},{1,0},{2,3},{3,2},{4,5},{5,4},{6,7},{7,6},{8,9},{9,8},{10,11... | collective-permute-start | bytes 1474568 | tf_op jit(solution)/shard_map/ppermute | solution.py:810
  319.8 9.9 %collective-permute-start.54 = (bf16[320,768]{1,0:T(8,128)(2,1)}, bf16[320,768]{1,0:T(8,128)(2,1)}, u32[]{:S(2)}, u32[]{:S(2)}) collective-permute-start(bf16[320,768]{1,0:T(8,128)(2,1)} %collective-permute-done.25.refs_3_), channel_id=1, source_target_pairs={{0,1},{1,0},{2,3},{3,2},{4,5},{5,4},{6,7},{7,6},{8,9},{9,8},{10,11... | collective-permute-start | bytes 1474568 | tf_op jit(solution)/shard_map/ppermute | solution.py:810
  322.2 11.0 %collective-permute-start.50 = (bf16[192,768]{1,0:T(8,128)(2,1)}, bf16[192,768]{1,0:T(8,128)(2,1)S(1)}, u32[]{:S(2)}, u32[]{:S(2)}) collective-permute-start(bf16[192,768]{1,0:T(8,128)(2,1)} %join.3.refs_0_), channel_id=1, source_target_pairs={{0,24},{8,16},{16,8},{24,0},{1,25},{9,17},{17,9},{25,1},{2,26},{10... | collective-permute-start | bytes 884744 | tf_op jit(solution)/shard_map/ppermute | solution.py:810
  327.7 15.2 %collective-permute-start.57 = (bf16[192,768]{1,0:T(8,128)(2,1)S(1)}, bf16[192,768]{1,0:T(8,128)(2,1)S(1)}, u32[]{:S(2)}, u32[]{:S(2)}) collective-permute-start(bf16[192,768]{1,0:T(8,128)(2,1)S(1)} %copy-done.18), channel_id=1, source_target_pairs={{0,1},{1,0},{2,3},{3,2},{4,5},{5,4},{6,7},{7,6},{8,9},{9,8},{10,11... | collective-permute-start | bytes 884744 | tf_op jit(solution)/shard_map/ppermute | solution.py:810
  327.9 15.1 %collective-permute-start.61 = (bf16[192,768]{1,0:T(8,128)(2,1)}, bf16[192,768]{1,0:T(8,128)(2,1)}, u32[]{:S(2)}, u32[]{:S(2)}) collective-permute-start(bf16[192,768]{1,0:T(8,128)(2,1)} %join.3.refs_0_), channel_id=1, source_target_pairs={{0,8},{8,0},{16,24},{24,16},{1,9},{9,1},{17,25},{25,17},{2,10},{10... | collective-permute-start | bytes 884744 | tf_op jit(solution)/shard_map/ppermute | solution.py:810
  329.2 14.3 %collective-permute-start.62 = (bf16[192,768]{1,0:T(8,128)(2,1)}, bf16[192,768]{1,0:T(8,128)(2,1)}, u32[]{:S(2)}, u32[]{:S(2)}) collective-permute-start(bf16[192,768]{1,0:T(8,128)(2,1)} %join.3.refs_0_), channel_id=1, source_target_pairs={{0,16},{8,24},{16,0},{24,8},{1,17},{9,25},{17,1},{25,9},{2,18},{10... | collective-permute-start | bytes 884744 | tf_op jit(solution)/shard_map/ppermute | solution.py:810
  329.7 13.9 %collective-permute-start.58 = (bf16[192,768]{1,0:T(8,128)(2,1)}, bf16[192,768]{1,0:T(8,128)(2,1)}, u32[]{:S(2)}, u32[]{:S(2)}) collective-permute-start(bf16[192,768]{1,0:T(8,128)(2,1)} %collective-permute-done.55.refs_1_), channel_id=1, source_target_pairs={{0,1},{1,0},{2,3},{3,2},{4,5},{5,4},{6,7},{7,6},{8,9},{9,8},{10,11... | collective-permute-start | bytes 884744 | tf_op jit(solution)/shard_map/ppermute | solution.py:810
  333.2 10.9 %collective-permute-start.59 = (bf16[192,768]{1,0:T(8,128)(2,1)}, bf16[192,768]{1,0:T(8,128)(2,1)}, u32[]{:S(2)}, u32[]{:S(2)}) collective-permute-start(bf16[192,768]{1,0:T(8,128)(2,1)} %collective-permute-done.56.refs_2_), channel_id=1, source_target_pairs={{0,1},{1,0},{2,3},{3,2},{4,5},{5,4},{6,7},{7,6},{8,9},{9,8},{10,11... | collective-permute-start | bytes 884744 | tf_op jit(solution)/shard_map/ppermute | solution.py:810
  343.0 8.7 %collective-permute-start.63 = (bf16[192,768]{1,0:T(8,128)(2,1)}, bf16[192,768]{1,0:T(8,128)(2,1)}, u32[]{:S(2)}, u32[]{:S(2)}) collective-permute-start(bf16[192,768]{1,0:T(8,128)(2,1)} %join.3.refs_0_), channel_id=1, source_target_pairs={{0,1},{1,0},{2,3},{3,2},{4,5},{5,4},{6,7},{7,6},{8,9},{9,8},{10,11... | collective-permute-start | bytes 884744 | tf_op jit(solution)/shard_map/ppermute | solution.py:810
  343.5 8.1 %collective-permute-start.66 = (bf16[192,768]{1,0:T(8,128)(2,1)}, bf16[192,768]{1,0:T(8,128)(2,1)}, u32[]{:S(2)}, u32[]{:S(2)}) collective-permute-start(bf16[192,768]{1,0:T(8,128)(2,1)} %copy-done.31), channel_id=1, source_target_pairs={{0,1},{1,0},{2,3},{3,2},{4,5},{5,4},{6,7},{7,6},{8,9},{9,8},{10,11... | collective-permute-start | bytes 884744 | tf_op jit(solution)/shard_map/ppermute | solution.py:810
  343.6 8.0 %collective-permute-start.64 = (bf16[192,768]{1,0:T(8,128)(2,1)}, bf16[192,768]{1,0:T(8,128)(2,1)}, u32[]{:S(2)}, u32[]{:S(2)}) collective-permute-start(bf16[192,768]{1,0:T(8,128)(2,1)} %collective-permute-done.61.refs_1_), channel_id=1, source_target_pairs={{0,1},{1,0},{2,3},{3,2},{4,5},{5,4},{6,7},{7,6},{8,9},{9,8},{10,11... | collective-permute-start | bytes 884744 | tf_op jit(solution)/shard_map/ppermute | solution.py:810
  (66 other events, 698.1 us)
